TPU v7x, 32 devices: a whole 2x2x4 slice. The times are simulated.
32 devices in a mesh: dp: 2 (over x), ctx: 16 (over z, y, core).
Axes of the slice: x: 2, y: 2, z: 4, core: 2. Of those that a mesh axis runs over, the one named last changes fastest.
Arguments:
- grad_out: bfloat16 [2, 2048, 2048], P('dp', 'ctx'), may hold values from -6 to 6
- saved_input: bfloat16 [2, 2048, 2048], P('dp', 'ctx'), may hold values from -6 to 6
- gate_value: bfloat16 [2, 2048, 2048], P('dp', 'ctx'), may hold values from -6 to 6
- filter_taps: bfloat16 [2048, 2048], P(None, 'ctx'), may hold values from -0.125 to 0.125
- skip_gain: float32 [2048], replicated, may hold values from 0.1 to 1.9
- lang_ids: int32 [2, 2048], P('dp', 'ctx'), may hold values from 0 to 15
- doc_ids: int32 [2, 2048], P('dp', 'ctx'), may hold values from 0 to 31, never falling along the last dimension, each value on 1 to 512 neighbouring positions
- dro_weight: float32 [16], replicated, may hold values from 0.25 to 4
Outputs:
- d_input: bfloat16 [2, 2048, 2048], P('dp', 'ctx')
- d_gate: bfloat16 [2, 2048, 2048], P('dp', 'ctx')
- d_filter: float32 [2048, 2048], P('ctx', 'dp')
Inputs may be any that keep to these rules, and one draw needn't show every extreme that they name: `doc_ids`: in each sequence the document numbers never fall, and every number from 0 to 31 occurs.
All inputs are finite; a program needn't handle non-finite values.
Results may differ from a plain program's by a relative error of at most 0.017.
Values may be sent and summed in bfloat16 or wider, within the bound.
No kernel may reach another device: no remote copies, remote signals or barrier semaphores. Data moves between devices by JAX's collectives and lax.ppermute only.
A program may use at most 128 MiB of HBM per device.

v0:
```python
import math

import jax
import jax.numpy as jnp
from jax import lax
from jax.sharding import PartitionSpec as P

NDOCS = 32


highest = lax.Precision.HIGHEST


def angles(first, second, period):
    return 2.0 * math.pi / period * (first * second % period).astype(jnp.float32)


def spectral_tables(length):
    size = 2 * length
    rows = size // 128
    half = length // 128
    outer = angles(
        jnp.arange(half, dtype=jnp.int32)[:, None], jnp.arange(rows, dtype=jnp.int32)[None, :], rows
    )
    twist = angles(
        jnp.arange(rows, dtype=jnp.int32)[:, None], jnp.arange(128, dtype=jnp.int32)[None, :], size
    )
    inner = angles(
        jnp.arange(128, dtype=jnp.int32)[:, None], jnp.arange(128, dtype=jnp.int32)[None, :], 128
    )
    return (
        jnp.cos(outer),
        jnp.sin(outer),
        jnp.cos(twist),
        jnp.sin(twist),
        jnp.cos(inner),
        jnp.sin(inner),
    )


def forward(signal, tables):
    cos_out, sin_out, cos_tw, sin_tw, cos_in, sin_in = tables
    count = signal.shape[0]
    shaped = signal.reshape(count, cos_out.shape[0], 128)
    first_re = jnp.einsum("cpn,pk->ckn", shaped, cos_out, precision=highest)
    first_im = -jnp.einsum("cpn,pk->ckn", shaped, sin_out, precision=highest)
    turned_re = first_re * cos_tw + first_im * sin_tw
    turned_im = first_im * cos_tw - first_re * sin_tw
    spec_re = jnp.einsum("ckn,nm->ckm", turned_re, cos_in, precision=highest) + jnp.einsum(
        "ckn,nm->ckm", turned_im, sin_in, precision=highest
    )
    spec_im = jnp.einsum("ckn,nm->ckm", turned_im, cos_in, precision=highest) - jnp.einsum(
        "ckn,nm->ckm", turned_re, sin_in, precision=highest
    )
    return (spec_re, spec_im)


def inverse(spec_re, spec_im, tables):
    cos_out, sin_out, cos_tw, sin_tw, cos_in, sin_in = tables
    count = spec_re.shape[0]
    size = spec_re.shape[1] * 128
    part_re = jnp.einsum("ckm,mn->ckn", spec_re, cos_in, precision=highest) - jnp.einsum(
        "ckm,mn->ckn", spec_im, sin_in, precision=highest
    )
    part_im = jnp.einsum("ckm,mn->ckn", spec_im, cos_in, precision=highest) + jnp.einsum(
        "ckm,mn->ckn", spec_re, sin_in, precision=highest
    )
    turned_re = part_re * cos_tw - part_im * sin_tw
    turned_im = part_im * cos_tw + part_re * sin_tw
    signal = jnp.einsum("ckn,pk->cpn", turned_re, cos_out, precision=highest) - jnp.einsum(
        "ckn,pk->cpn", turned_im, sin_out, precision=highest
    )
    return signal.reshape(count, cos_out.shape[0] * 128) / size


def local(grad_out, saved_input, gate_value, filter_taps, skip_gain, lang_ids, doc_ids, dro_weight):
    tokens = grad_out.shape[1]
    channels = grad_out.shape[2]
    pieces = lax.axis_size("ctx")
    length = tokens * pieces
    span = channels // pieces
    lang_hot = lang_ids[0][:, None] == jnp.arange(dro_weight.shape[0], dtype=jnp.int32)[None, :]
    group_weight = jnp.sum(
        jnp.where(lang_hot, dro_weight[None, :], jnp.zeros_like(dro_weight)[None, :]), axis=1
    )
    doc_hot = (doc_ids[0][:, None] == jnp.arange(NDOCS, dtype=jnp.int32)[None, :]).astype(
        jnp.float32
    )
    counts = lax.psum(jnp.sum(doc_hot, axis=0), "ctx")
    doc_len = jnp.sum(doc_hot * counts[None, :], axis=1)
    mean_len = length / NDOCS
    scale = group_weight * (2.0 * mean_len) / (doc_len + mean_len)
    grad_scaled = grad_out[0].astype(jnp.float32) * scale[:, None]
    grad_conv = (grad_scaled * gate_value[0].astype(jnp.float32)).astype(jnp.bfloat16)
    tables = spectral_tables(length)
    skip_local = lax.dynamic_slice_in_dim(skip_gain, lax.axis_index("ctx") * span, span)[:, None]
    input_slab = saved_input[0].T
    grad_slab = grad_conv.T
    members = lax.axis_size("dp")
    share = span // members
    blocks = filter_taps.reshape(pieces, span, tokens)
    own_taps = lax.dynamic_slice_in_dim(blocks, lax.axis_index("dp") * share, share, 1).reshape(
        pieces * share, tokens
    )
    input_pen, grad_pen, filter_pen = (
        lax.all_to_all(input_slab, "ctx", split_axis=0, concat_axis=1, tiled=True),
        lax.all_to_all(grad_slab, "ctx", split_axis=0, concat_axis=1, tiled=True),
        lax.all_to_all(own_taps, "ctx", split_axis=0, concat_axis=1, tiled=True),
    )
    share_re, share_im = forward(filter_pen.astype(jnp.float32), tables)
    filt_re, filt_im = (
        lax.all_gather(share_re.astype(jnp.bfloat16), "dp", axis=0, tiled=True).astype(
            share_re.dtype
        ),
        lax.all_gather(share_im.astype(jnp.bfloat16), "dp", axis=0, tiled=True).astype(
            share_im.dtype
        ),
    )
    input_full = input_pen.astype(jnp.float32)
    grad_full = grad_pen.astype(jnp.float32)
    input_re, input_im = forward(input_full, tables)
    grad_re, grad_im = forward(grad_full, tables)
    mixed = inverse(
        filt_re * input_re - filt_im * input_im, filt_re * input_im + filt_im * input_re, tables
    )
    mixed_pen = (mixed + skip_local * input_full).astype(jnp.bfloat16)
    back = inverse(
        filt_re * grad_re + filt_im * grad_im, filt_re * grad_im - filt_im * grad_re, tables
    )
    mixed_slab = lax.all_to_all(mixed_pen, "ctx", split_axis=1, concat_axis=0, tiled=True)
    input_back = lax.all_to_all(
        (back + skip_local * grad_full).astype(jnp.bfloat16),
        "ctx",
        split_axis=1,
        concat_axis=0,
        tiled=True,
    )
    lagged = inverse(
        input_re * grad_re + input_im * grad_im, input_re * grad_im - input_im * grad_re, tables
    )
    filter_grad = lax.psum_scatter(
        lagged.astype(jnp.bfloat16), "dp", scatter_dimension=1, tiled=True
    ).astype(jnp.float32)
    d_gate = (grad_scaled * mixed_slab.T.astype(jnp.float32)).astype(jnp.bfloat16)
    return (input_back.T[None], d_gate[None], filter_grad)


def solution(mesh):
    return jax.shard_map(
        local,
        mesh=mesh,
        in_specs=(
            P("dp", "ctx", None),
            P("dp", "ctx", None),
            P("dp", "ctx", None),
            P(None, "ctx"),
            P(),
            P("dp", "ctx"),
            P("dp", "ctx"),
            P(),
        ),
        out_specs=(P("dp", "ctx", None), P("dp", "ctx", None), P("ctx", "dp")),
        check_vma=False,
    )
```

profile of v0, /device:TPU:0, one launch (start us, length us, event | category | flops | bytes accessed | tf_op | source)
XLA Modules:
  0.0 239.6 jit_solution(15899880237634695635)
XLA Ops:
  8.9 7.4 %all-to-all-start = ((bf16[16,64,128]{2,1,0:T(8,128)(2,1)}), bf16[16,64,128]{2,1,0:T(8,128)(2,1)S(1)}, u32[]{:S(2)}, u32[]{:S(2)}) async-start(bf16[16,64,128]{2,1,0:T(8,128)(2,1)} %constant_dynamic-slice_fusion), calls=%async_computation | async-start | bytes 524288 | tf_op jit(solution)/shard_map/all_to_all | solution.py:108
  16.5 9.9 %all-to-all-done = bf16[16,64,128]{2,1,0:T(8,128)(2,1)S(1)} async-done(((bf16[16,64,128]{2,1,0:T(8,128)(2,1)}), bf16[16,64,128]{2,1,0:T(8,128)(2,1)S(1)}, u32[]{:S(2)}, u32[]{:S(2)}) %all-to-all-start) | async-done | bytes 262176 | tf_op jit(solution)/shard_map/all_to_all | solution.py:108
  32.1 3.6 %all-to-all-start.3 = ((bf16[16,128,128]{2,1,0:T(8,128)(2,1)}), bf16[16,128,128]{2,1,0:T(8,128)(2,1)S(1)}, u32[]{:S(2)}, u32[]{:S(2)}) async-start(bf16[16,128,128]{2,1,0:T(8,128)(2,1)} %bitcast.24), calls=%async_computation.3 | async-start | bytes 1048576 | tf_op jit(solution)/shard_map/all_to_all | solution.py:106
  39.9 10.1 %all-to-all-done.3 = bf16[16,128,128]{2,1,0:T(8,128)(2,1)S(1)} async-done(((bf16[16,128,128]{2,1,0:T(8,128)(2,1)}), bf16[16,128,128]{2,1,0:T(8,128)(2,1)S(1)}, u32[]{:S(2)}, u32[]{:S(2)}) %all-to-all-start.3) | async-done | bytes 524320 | tf_op jit(solution)/shard_map/all_to_all | solution.py:106
  52.7 3.6 %fusion.18 = f32[128,32,128]{2,0,1:T(8,128)S(1)} fusion(f32[128,32,128]{2,1,0:T(8,128)S(1)} %get-tuple-element.19), kind=kOutput, calls=%fused_computation.38 | convolution fusion | flops 805535744 | bytes 4194304 | tf_op jit(solution)/shard_map/ckn,nm->ckm/dot_general | solution.py:49
  56.3 3.8 %fusion.16 = f32[128,32,128]{2,0,1:T(8,128)S(1)} fusion(f32[128,32,128]{2,1,0:T(8,128)S(1)} %get-tuple-element.19), kind=kOutput, calls=%fused_computation.36 | convolution fusion | flops 805535744 | bytes 4194304 | tf_op jit(solution)/shard_map/ckn,nm->ckm/dot_general | solution.py:52
  60.1 3.6 %fusion.38 = f32[128,32,128]{2,0,1:T(8,128)S(1)} fusion(f32[128,32,128]{2,0,1:T(8,128)S(1)} %fusion.18, f32[128,32,128]{2,1,0:T(8,128)S(1)} %get-tuple-element.18), kind=kOutput, calls=%fused_computation.54 | convolution fusion | flops 806060032 | bytes 6291456 | tf_op jit(solution)/shard_map/ckn,nm->ckm/dot_general | solution.py:49
  63.7 4.9 %fusion.41 = f32[128,32,128]{2,0,1:T(8,128)} fusion(f32[128,32,128]{2,0,1:T(8,128)S(1)} %fusion.16, f32[128,32,128]{2,1,0:T(8,128)S(1)} %get-tuple-element.18), kind=kOutput, calls=%fused_computation.55 | convolution fusion | flops 806060032 | bytes 6291456 | tf_op jit(solution)/shard_map/ckn,nm->ckm/dot_general | solution.py:52
  68.7 5.6 %all-gather.5.cloned.1.call-done = bf16[128,32,128]{2,1,0:T(8,128)(2,1)} async-done(((bf16[64,32,128]{2,1,0:T(8,128)(2,1)}), bf16[128,32,128]{2,1,0:T(8,128)(2,1)}) %all-gather.5.cloned.1.call-update) | async-done | bytes 1048592 | tf_op jit(solution)/shard_map/all_gather | solution.py:115
  74.3 5.3 %fusion.129 = f32[128,32,128]{2,0,1:T(8,128)S(1)} fusion(f32[128,32,128]{2,0,1:T(8,128)} %fusion.41, f32[128,32,128]{2,0,1:T(8,128)S(1)} %fusion.38, bf16[128,32,128]{2,1,0:T(8,128)(2,1)} %all-gather.5.cloned.1.call-done, bf16[128,32,128]{2,1,0:T(8,128)(2,1)} %all-gather.3.cloned.1.call-done), kind=kOutput, calls=%fused_computation.133 | convolution fusion | flops 808157184 | bytes 8388608 | tf_op jit(solution)/shard_map/ckm,mn->ckn/dot_general | solution.py:65
  79.6 3.4 %fusion.131 = f32[128,32,128]{2,0,1:T(8,128)S(1)} fusion(f32[128,32,128]{2,0,1:T(8,128)S(1)} %fusion.38, f32[128,32,128]{2,0,1:T(8,128)S(1)} %copy-done.2, bf16[128,32,128]{2,1,0:T(8,128)(2,1)S(1)} %copy-done.6, bf16[128,32,128]{2,1,0:T(8,128)(2,1)S(1)} %copy-done.4), kind=kOutput, calls=%fused_computation.135 | convolution fusion | flops 808157184 | bytes 8388608 | tf_op jit(solution)/shard_map/ckm,mn->ckn/dot_general | solution.py:62
  83.0 3.0 %convolution_subtract_fusion.1 = f32[128,32,128]{2,0,1:T(8,128)S(1)} fusion(f32[128,32,128]{2,0,1:T(8,128)S(1)} %fusion.131, f32[128,32,128]{2,0,1:T(8,128)S(1)} %copy-done.2, f32[128,32,128]{2,0,1:T(8,128)S(1)} %fusion.38, bf16[128,32,128]{2,1,0:T(8,128)(2,1)S(1)} %copy-done.6, bf16[128,32,128]{2,1,0:T(8,128)(2,1)S(1)} %copy-done.4), kind=kOutput, calls=%fused_computation.59 | convolution fusion | flops 808681472 | bytes 10485760 | tf_op jit(solution)/shard_map/ckm,mn->ckn/dot_general | solution.py:62
  86.0 3.2 %multiply_subtract_fusion.2 = (f32[128,32,128]{2,0,1:T(8,128)S(1)}, f32[128,32,128]{2,0,1:T(8,128)S(1)}) fusion(f32[128,32,128]{2,0,1:T(8,128)S(1)} %convolution_subtract_fusion.1, f32[32,128]{1,0:T(8,128)S(1)} %get-tuple-element.29, f32[32,128]{1,0:T(8,128)S(1)} %get-tuple-element.30, f32[128,32,128]{2,0,1:T(8,128)S(1)} %fusion.129, ...), kind=kOutput, calls=%fused_computation.29 | convolution fusion | flops 811827200 | bytes 14712832 | tf_op jit(solution)/shard_map/ckm,mn->ckn/dot_general | solution.py:65
  89.3 2.3 fusion.8
  91.5 2.8 %fusion.77 = bf16[128,16,128]{2,1,0:T(8,128)(2,1)S(1)} fusion(f32[16,128,128]{2,0,1:T(8,128)S(1)} %fusion.8, f32[128,32,128]{2,0,1:T(8,128)S(1)} %get-tuple-element.16, f32[128]{0:T(128)S(1)} %dynamic_slice.7, bf16[16,128,128]{2,1,0:T(8,128)(2,1)S(1)} %all-to-all-done.3), kind=kOutput, calls=%fused_computation.76 | convolution fusion | flops 102243328 | bytes 4194816 | tf_op jit(solution)/shard_map/ckn,pk->cpn/dot_general | solution.py:70
  95.3 5.6 %all-to-all-start.4 = ((bf16[128,16,128]{2,0,1:T(8,128)(2,1)}), bf16[128,16,128]{2,0,1:T(8,128)(2,1)S(1)}, u32[]{:S(2)}, u32[]{:S(2)}) async-start(bf16[128,16,128]{2,0,1:T(8,128)(2,1)} %copy.136), calls=%async_computation.4 | async-start | bytes 1048576 | tf_op jit(solution)/shard_map/all_to_all | solution.py:130
  104.2 34.0 %psum.7 = f32[32]{0:T(128)S(1)} all-reduce(f32[32]{0:T(128)S(1)} %convert_reduce_fusion), channel_id=1, replica_groups=mesh['dp'=2,'ctx'=16] {'ctx'}, use_global_device_ids=true, to_apply=%region_2.3 | all-reduce | flops 32 | bytes 256 | tf_op jit(solution)/shard_map/psum | solution.py:89
  139.8 17.1 %all_to_all.71 = bf16[16,128,128]{2,1,0:T(8,128)(2,1)S(1)} all-to-all(bf16[16,128,128]{2,1,0:T(8,128)(2,1)S(1)} %bitcast.185), channel_id=1, replica_groups=mesh['dp'=2,'ctx'=16] {'ctx'}, dimensions={0} | all-to-all | bytes 1048576 | tf_op jit(solution)/shard_map/all_to_all | solution.py:107
  159.5 3.6 %fusion.24 = f32[128,32,128]{2,0,1:T(8,128)S(1)} fusion(f32[128,32,128]{2,1,0:T(8,128)S(1)} %get-tuple-element.23), kind=kOutput, calls=%fused_computation.44 | convolution fusion | flops 805535744 | bytes 4194304 | tf_op jit(solution)/shard_map/ckn,nm->ckm/dot_general | solution.py:52
  163.1 3.6 %fusion.26 = f32[128,32,128]{2,0,1:T(8,128)S(1)} fusion(f32[128,32,128]{2,1,0:T(8,128)S(1)} %get-tuple-element.23), kind=kOutput, calls=%fused_computation.46 | convolution fusion | flops 805535744 | bytes 4194304 | tf_op jit(solution)/shard_map/ckn,nm->ckm/dot_general | solution.py:49
  166.7 4.0 %fusion.35 = f32[128,32,128]{2,0,1:T(8,128)S(1)} fusion(f32[128,32,128]{2,0,1:T(8,128)S(1)} %fusion.24, f32[128,32,128]{2,1,0:T(8,128)S(1)} %get-tuple-element.22), kind=kOutput, calls=%fused_computation.53 | convolution fusion | flops 806060032 | bytes 6291456 | tf_op jit(solution)/shard_map/ckn,nm->ckm/dot_general | solution.py:52
  170.8 4.2 %multiply_subtract_fusion.1 = (f32[128,32,128]{2,0,1:T(8,128)S(1)}, f32[128,32,128]{2,0,1:T(8,128)S(1)}, f32[128,32,128]{2,0,1:T(8,128)S(1)}) fusion(f32[128,32,128]{2,0,1:T(8,128)S(1)} %copy-done.3, f32[128,32,128]{2,0,1:T(8,128)S(1)} %fusion.38, f32[128,32,128]{2,0,1:T(8,128)S(1)} %fusion.35, f32[128,32,128]{2,0,1:T(8,128)S(1)} %fusion.26, ...), kind=kOutput, calls=%fused_computation.26 | convolution fusion | flops 809205760 | bytes 16777216 | tf_op jit(solution)/shard_map/ckn,nm->ckm/dot_general | solution.py:49
  181.5 3.3 %fusion.135 = f32[128,32,128]{2,0,1:T(8,128)S(1)} fusion(f32[128,32,128]{2,0,1:T(8,128)S(1)} %fusion.35, f32[128,32,128]{2,0,1:T(8,128)S(1)} %get-tuple-element.28, bf16[128,32,128]{2,1,0:T(8,128)(2,1)S(1)} %copy-done.7, bf16[128,32,128]{2,1,0:T(8,128)(2,1)S(1)} %copy-done.5), kind=kOutput, calls=%fused_computation.139 | convolution fusion | flops 808157184 | bytes 8388608 | tf_op jit(solution)/shard_map/ckm,mn->ckn/dot_general | solution.py:65
  184.8 3.1 %fusion.137 = f32[128,32,128]{2,0,1:T(8,128)S(1)} fusion(f32[128,32,128]{2,0,1:T(8,128)S(1)} %get-tuple-element.28, f32[128,32,128]{2,0,1:T(8,128)S(1)} %fusion.35, bf16[128,32,128]{2,1,0:T(8,128)(2,1)S(1)} %copy-done.7, bf16[128,32,128]{2,1,0:T(8,128)(2,1)S(1)} %copy-done.5), kind=kOutput, calls=%fused_computation.141 | convolution fusion | flops 808157184 | bytes 8388608 | tf_op jit(solution)/shard_map/ckm,mn->ckn/dot_general | solution.py:62
  187.9 3.1 %convolution_add_fusion.2 = f32[128,32,128]{2,0,1:T(8,128)S(1)} fusion(f32[128,32,128]{2,0,1:T(8,128)S(1)} %fusion.135, f32[128,32,128]{2,0,1:T(8,128)S(1)} %get-tuple-element.28, f32[128,32,128]{2,0,1:T(8,128)S(1)} %fusion.35, bf16[128,32,128]{2,1,0:T(8,128)(2,1)S(1)} %copy-done.7, bf16[128,32,128]{2,1,0:T(8,128)(2,1)S(1)} %copy-done.5), kind=kOutput, calls=%fused_computation.60 | convolution fusion | flops 808681472 | bytes 10485760 | tf_op jit(solution)/shard_map/ckm,mn->ckn/dot_general | solution.py:65
  191.0 3.1 %convolution_subtract_fusion.2 = f32[128,32,128]{2,0,1:T(8,128)S(1)} fusion(f32[128,32,128]{2,0,1:T(8,128)S(1)} %fusion.137, f32[128,32,128]{2,0,1:T(8,128)S(1)} %fusion.35, f32[128,32,128]{2,0,1:T(8,128)S(1)} %get-tuple-element.28, bf16[128,32,128]{2,1,0:T(8,128)(2,1)S(1)} %copy-done.7, bf16[128,32,128]{2,1,0:T(8,128)(2,1)S(1)} %copy-done.5), kind=kOutput, calls=%fused_computation.61 | convolution fusion | flops 808681472 | bytes 10485760 | tf_op jit(solution)/shard_map/ckm,mn->ckn/dot_general | solution.py:62
  194.2 4.4 %multiply_subtract_fusion = (f32[128,32,128]{2,0,1:T(8,128)S(1)}, f32[128,32,128]{2,0,1:T(8,128)S(1)}, f32[128,32,128]{2,0,1:T(8,128)}, f32[128,32,128]{2,0,1:T(8,128)S(1)}) fusion(f32[128,32,128]{2,0,1:T(8,128)S(1)} %convolution_subtract_fusion, f32[32,128]{1,0:T(8,128)S(1)} %get-tuple-element.29, f32[32,128]{1,0:T(8,128)S(1)} %get-tuple-element.30, ...), kind=kOutput, calls=%fused_computation.25 | convolution fusion | flops 812351488 | bytes 18907136 | tf_op jit(solution)/shard_map/ckm,mn->ckn/dot_general | solution.py:65
  200.9 2.3 fusion.82
  204.2 3.8 %fusion.12 = f32[16,128,128]{2,0,1:T(8,128)S(1)} fusion(f32[128,32,128]{2,0,1:T(8,128)} %get-tuple-element.26), kind=kOutput, calls=%fused_computation.20 | convolution fusion | flops 100670464 | bytes 3145728 | tf_op jit(solution)/shard_map/ckn,pk->cpn/dot_general | solution.py:70
  208.0 2.6 %fusion.74 = bf16[128,16,128]{2,1,0:T(8,128)(2,1)S(1)} fusion(f32[16,128,128]{2,0,1:T(8,128)S(1)} %fusion.12, f32[128,32,128]{2,0,1:T(8,128)S(1)} %get-tuple-element.27, f32[128]{0:T(128)S(1)} %dynamic_slice.7, bf16[16,128,128]{2,1,0:T(8,128)(2,1)S(1)} %all_to_all.71), kind=kOutput, calls=%fused_computation.75 | convolution fusion | flops 102243328 | bytes 4194816 | tf_op jit(solution)/shard_map/ckn,pk->cpn/dot_general | solution.py:70
  211.6 4.0 %all-to-all-start.2 = ((bf16[128,16,128]{2,0,1:T(8,128)(2,1)}), bf16[128,16,128]{2,0,1:T(8,128)(2,1)S(1)}, u32[]{:S(2)}, u32[]{:S(2)}) async-start(bf16[128,16,128]{2,0,1:T(8,128)(2,1)} %copy.127), calls=%async_computation.2 | async-start | bytes 1048576 | tf_op jit(solution)/shard_map/all_to_all | solution.py:131
  216.6 13.5 %all-to-all-done.2 = bf16[128,16,128]{2,0,1:T(8,128)(2,1)S(1)} async-done(((bf16[128,16,128]{2,0,1:T(8,128)(2,1)}), bf16[128,16,128]{2,0,1:T(8,128)(2,1)S(1)}, u32[]{:S(2)}, u32[]{:S(2)}) %all-to-all-start.2) | async-done | bytes 524320 | tf_op jit(solution)/shard_map/all_to_all | solution.py:131
  (66 shorter events, 37.2 us)
Async XLA Ops:
  7.2 1.1 copy-start
  8.9 17.4 %all-to-all-start = ((bf16[16,64,128]{2,1,0:T(8,128)(2,1)}), bf16[16,64,128]{2,1,0:T(8,128)(2,1)S(1)}, u32[]{:S(2)}, u32[]{:S(2)}) async-start(bf16[16,64,128]{2,1,0:T(8,128)(2,1)} %constant_dynamic-slice_fusion), calls=%async_computation | async-start | bytes 524288 | tf_op jit(solution)/shard_map/all_to_all | solution.py:108
  16.3 52.3 %all-gather.3.cloned.1.call-start = ((), (), s32[]{:S(2)}) async-start(), calls=%async_computation.6 | async-start | bytes 1572864 | tf_op jit(solution)/shard_map/all_gather | solution.py:112
  29.0 2.1 copy-start.8
  32.1 18.0 %all-to-all-start.3 = ((bf16[16,128,128]{2,1,0:T(8,128)(2,1)}), bf16[16,128,128]{2,1,0:T(8,128)(2,1)S(1)}, u32[]{:S(2)}, u32[]{:S(2)}) async-start(bf16[16,128,128]{2,1,0:T(8,128)(2,1)} %bitcast.24), calls=%async_computation.3 | async-start | bytes 1048576 | tf_op jit(solution)/shard_map/all_to_all | solution.py:106
  35.6 38.6 %all-gather.5.cloned.1.call-start = ((), (), s32[]{:S(2)}) async-start(), calls=%async_computation.7 | async-start | bytes 1572864 | tf_op jit(solution)/shard_map/all_gather | solution.py:115
  74.3 5.3 %copy-start.2 = (f32[128,32,128]{2,0,1:T(8,128)S(1)}, f32[128,32,128]{2,0,1:T(8,128)}, u32[]{:S(2)}) copy-start(f32[128,32,128]{2,0,1:T(8,128)} %fusion.41) | copy-start | bytes 6291460
  74.3 5.3 %copy-start.4 = (bf16[128,32,128]{2,1,0:T(8,128)(2,1)S(1)}, bf16[128,32,128]{2,1,0:T(8,128)(2,1)}, u32[]{:S(2)}) copy-start(bf16[128,32,128]{2,1,0:T(8,128)(2,1)} %all-gather.3.cloned.1.call-done) | copy-start | bytes 3145732
  74.3 5.3 %copy-start.6 = (bf16[128,32,128]{2,1,0:T(8,128)(2,1)S(1)}, bf16[128,32,128]{2,1,0:T(8,128)(2,1)}, u32[]{:S(2)}) copy-start(bf16[128,32,128]{2,1,0:T(8,128)(2,1)} %all-gather.5.cloned.1.call-done) | copy-start | bytes 3145732
  94.4 6.7 %copy-start.9 = (bf16[1,128,2048]{2,1,0:T(8,128)(2,1)S(1)}, bf16[1,128,2048]{2,1,0:T(8,128)(2,1)}, u32[]{:S(2)}) copy-start(bf16[1,128,2048]{2,1,0:T(8,128)(2,1)} %param.8) | copy-start | bytes 1572868
  94.4 9.7 %copy-start.10 = (s32[1,128]{1,0:T(1,128)S(1)}, s32[1,128]{1,0:T(1,128)}, u32[]{:S(2)}) copy-start(s32[1,128]{1,0:T(1,128)} %param.14) | copy-start | bytes 1540
  94.4 43.9 %copy-start.11 = (f32[16]{0:T(128)S(1)}, f32[16]{0:T(128)}, u32[]{:S(2)}) copy-start(f32[16]{0:T(128)} %param.15) | copy-start | bytes 196
  94.4 43.8 %copy-start.12 = (s32[1,128]{1,0:T(1,128)S(1)}, s32[1,128]{1,0:T(1,128)}, u32[]{:S(2)}) copy-start(s32[1,128]{1,0:T(1,128)} %param.13) | copy-start | bytes 1540
  95.3 43.0 %all-to-all-start.4 = ((bf16[128,16,128]{2,0,1:T(8,128)(2,1)}), bf16[128,16,128]{2,0,1:T(8,128)(2,1)S(1)}, u32[]{:S(2)}, u32[]{:S(2)}) async-start(bf16[128,16,128]{2,0,1:T(8,128)(2,1)} %copy.136), calls=%async_computation.4 | async-start | bytes 1048576 | tf_op jit(solution)/shard_map/all_to_all | solution.py:130
  101.0 130.1 %reduce-scatter.2.cloned.1.call-start = ((), (), s32[]{:S(2)}) async-start(), calls=%async_computation.8 | async-start | bytes 786432 | tf_op jit(solution)/shard_map/reduce_scatter | solution.py:141
  166.7 4.0 %copy-start.3 = (f32[128,32,128]{2,0,1:T(8,128)S(1)}, f32[128,32,128]{2,0,1:T(8,128)}, u32[]{:S(2)}) copy-start(f32[128,32,128]{2,0,1:T(8,128)} %fusion.41) | copy-start | bytes 6291460
  179.3 2.1 copy-start.5
  179.3 2.1 copy-start.7
  210.6 22.2 %copy-start.1 = (bf16[2048,128]{1,0:T(8,128)(2,1)S(1)}, bf16[2048,128]{1,0:T(8,128)(2,1)}, u32[]{:S(2)}) copy-start(bf16[2048,128]{1,0:T(8,128)(2,1)} %param.11) | copy-start | bytes 1572868
  211.6 18.5 %all-to-all-start.2 = ((bf16[128,16,128]{2,0,1:T(8,128)(2,1)}), bf16[128,16,128]{2,0,1:T(8,128)(2,1)S(1)}, u32[]{:S(2)}, u32[]{:S(2)}) async-start(bf16[128,16,128]{2,0,1:T(8,128)(2,1)} %copy.127), calls=%async_computation.2 | async-start | bytes 1048576 | tf_op jit(solution)/shard_map/all_to_all | solution.py:131
Sparse Core Ops, SparseCore 0:
  31.2 19.5 all-gather.2
  52.9 21.2 all-gather.4
  204.3 12.9 reduce-scatter.1
where the time goes:
time: 244 us; the launch traced here: 240 us
  matrix products  99 us (41%)
  blocking collectives  51 us (21%)
  waiting for transfers between devices  39.2 us (16%)
  starting transfers between devices  20.9 us (9%)
  between operations  14.4 us (6%)
  local copies, waits for them, and re-layouts  11.4 us (5%)
  other arithmetic  3.65 us (1%)
    psum x1, blocking collectives, local(): counts = lax.psum(jnp.sum(doc_hot, axis=0), 'ctx')  34 us
    all_to_all x1, blocking collectives, local(): lax.all_to_all(grad_slab, 'ctx', split_axis=0, concat_axis=1, tiled=True)  17.1 us
    all_to_all x1, waiting for transfers between devices, local(): lax.all_to_all((back + skip_local * grad_full).astype(jnp.bfloat16), 'ctx...  13.5 us
    dot_general x3, matrix products, forward(): jnp.einsum('ckn,nm->ckm', turned_re, sin_in, precision=highest)  11 us
    dot_general x3, matrix products, inverse(): jnp.einsum('ckm,mn->ckn', spec_re, sin_in, precision=highest)  10.8 us
    dot_general x3, matrix products, inverse(): jnp.einsum('ckm,mn->ckn', spec_im, cos_in, precision=highest)  10.7 us
    all_to_all x1, waiting for transfers between devices, local(): lax.all_to_all(input_slab, 'ctx', split_axis=0, concat_axis=1, tiled=True)  10.1 us
    all_to_all x1, waiting for transfers between devices, local(): lax.all_to_all(own_taps, 'ctx', split_axis=0, concat_axis=1, tiled=True)  9.91 us
  transfers between devices with their start and end apart: 7, of which 4 were waited for; matrix products, arithmetic and copies ran while one was open for 15% of the time, Pallas kernels for 0%

commit v1 on v0

v1 whole, which is shorter than its diff:
```python
import functools
import math

import jax
import jax.numpy as jnp
import numpy as np
from jax import lax
from jax.experimental import pallas as pl
from jax.experimental.pallas import tpu as pltpu
from jax.sharding import PartitionSpec as P

NDOCS = 32
ROWS = 16
VMEM = pl.BlockSpec(memory_space=pltpu.VMEM)
SMEM = pl.BlockSpec(memory_space=pltpu.SMEM)
f32 = jnp.float32
bf16 = jnp.bfloat16


def inner_tables(pieces, tokens):
    size = 2 * pieces * tokens
    m = np.arange(pieces)[:, None, None]
    k = np.arange(tokens)[None, :, None]
    q = np.arange(tokens)[None, None, :]
    turn = (q * (4 * m + 1 + 4 * pieces * k)) % (2 * size)
    angle = math.pi / size * turn
    cos, sin = np.cos(angle), np.sin(angle)
    ahead = np.concatenate(
        [np.concatenate([cos, sin], axis=2), np.concatenate([-sin, cos], axis=2)], axis=1
    )
    behind = np.swapaxes(ahead, 1, 2) * (2.0 / size)
    return jnp.asarray(ahead, bf16), jnp.asarray(behind, bf16)


def turned(value, turns):
    re, im = value
    turns = turns % 1.0
    if turns == 0.0:
        return value
    if turns == 0.25:
        return (-im, re)
    if turns == 0.5:
        return (-re, -im)
    if turns == 0.75:
        return (im, -re)
    cos, sin = math.cos(2.0 * math.pi * turns), math.sin(2.0 * math.pi * turns)
    if (turns * 8.0) % 1.0 == 0.0:
        root = math.sqrt(0.5)
        plus, minus = (re + im) * root, (re - im) * root
        if turns == 0.125:
            return (minus, plus)
        if turns == 0.375:
            return (-plus, minus)
        if turns == 0.625:
            return (-minus, -plus)
        return (plus, -minus)
    return (re * cos - im * sin, re * sin + im * cos)


def dft(values, sign):
    count = len(values)
    if count == 1:
        return values
    even, odd = dft(values[0::2], sign), dft(values[1::2], sign)
    first, second = [], []
    for k in range(count // 2):
        a, b = even[k], turned(odd[k], sign * k / count)
        first.append((a[0] + b[0], a[1] + b[1]))
        second.append((a[0] - b[0], a[1] - b[1]))
    return first + second


def outer_forward(reals):
    count = len(reals)
    values = [(reals[0], jnp.zeros_like(reals[0]))]
    for j in range(1, count):
        angle = -math.pi * j / (2 * count)
        values.append((reals[j] * math.cos(angle), reals[j] * math.sin(angle)))
    return dft(values, -1.0)


def outer_inverse(values):
    count = len(values)
    out = []
    for j, (re, im) in enumerate(dft(values, 1.0)):
        angle = math.pi * j / (2 * count)
        out.append(re if j == 0 else re * math.cos(angle) - im * math.sin(angle))
    return out


def chunked(total, body):
    def step(i, carry):
        body(pl.multiple_of(i * ROWS, ROWS))
        return carry

    lax.fori_loop(0, total // ROWS, step, 0)


def each_piece(pieces, body, group=4):
    def step(i, carry):
        for g in range(group):
            body(i * group + g)
        return carry

    lax.fori_loop(0, pieces // group, step, 0)


def dot(a, b):
    return lax.dot_general(a, b, (((1,), (0,)), ((), ())), preferred_element_type=f32)


def prep_kernel(pieces, span, grad_ref, gate_ref, doc_ref, lang_ref, out_ref):
    tokens = grad_ref.shape[0]
    split = tokens // span
    tile = lax.broadcasted_iota(jnp.int32, (ROWS, span), 0)
    rows = jnp.zeros((ROWS, span), f32)
    for a in range(split):
        part = slice(a * span, (a + 1) * span)
        rows = jnp.where(tile == a, doc_ref[:, part].astype(f32), rows)
        rows = jnp.where(tile == split + a, lang_ref[:, part].astype(f32), rows)
    rows = rows.astype(bf16)
    for i in range(pieces):
        part = slice(i * span, (i + 1) * span)
        out_ref[i, :tokens, :] = (
            grad_ref[:, part].astype(f32) * gate_ref[:, part].astype(f32)
        ).astype(bf16)
        out_ref[i, tokens:, :] = rows


def filter_kernel(taps_ref, ahead_ref, spec_ref, mid_ref):
    pieces, span, tokens = taps_ref.shape

    def outer(row):
        rows = pl.ds(row, ROWS)
        out = outer_forward([taps_ref[j, rows, :].astype(f32) for j in range(pieces)])
        for m, (re, im) in enumerate(out):
            mid_ref[m, rows, :tokens] = re.astype(bf16)
            mid_ref[m, rows, tokens:] = im.astype(bf16)

    chunked(span, outer)

    def inner(m):
        spec_ref[m] = lax.dot_general(
            ahead_ref[m], mid_ref[m], (((1,), (1,)), ((), ())), preferred_element_type=f32
        )

    each_piece(pieces, inner)


def to_middle(load, mid_ref, tokens, pieces):
    def outer(row):
        out = outer_forward([load(j, row) for j in range(pieces)])
        for m, (re, im) in enumerate(out):
            mid_ref[m, pl.ds(row, ROWS), :] = re.astype(bf16)
            mid_ref[m, pl.ds(tokens + row, ROWS), :] = im.astype(bf16)

    chunked(tokens, outer)


def from_middle(back_ref, store, tokens, pieces):
    def outer(row):
        out = outer_inverse(
            [
                (back_ref[m, pl.ds(row, ROWS), :], back_ref[m, pl.ds(tokens + row, ROWS), :])
                for m in range(pieces)
            ]
        )
        for j in range(pieces):
            store(j, row, out[j])

    chunked(tokens, outer)


def mixed_kernel(
    in_ref, filt_ref, skip_ref, ahead_ref, behind_ref, out_ref, spec_ref, mid_ref, back_ref
):
    pieces, tokens, _ = in_ref.shape

    def load(j, row):
        return in_ref[j, pl.ds(row, ROWS), :].astype(f32)

    to_middle(load, mid_ref, tokens, pieces)

    def inner(m):
        spec = dot(ahead_ref[m], mid_ref[m])
        spec_ref[m] = spec
        filt = filt_ref[m]
        re, im = spec[:tokens], spec[tokens:]
        fre, fim = filt[:tokens], filt[tokens:]
        prod = jnp.concatenate([fre * re - fim * im, fre * im + fim * re], axis=0).astype(bf16)
        back_ref[m] = dot(behind_ref[m], prod)

    each_piece(pieces, inner)
    skip = skip_ref[...]

    def store(j, row, value):
        out_ref[j, pl.ds(row, ROWS), :] = (value + skip * load(j, row)).astype(bf16)

    from_middle(back_ref, store, tokens, pieces)


def input_kernel(
    mean_len,
    grad_ref,
    filt_ref,
    skip_ref,
    dro_ref,
    ahead_ref,
    behind_ref,
    out_ref,
    spec_ref,
    scale_ref,
    mid_ref,
    back_ref,
    doc_ref,
    lang_ref,
):
    pieces, tall, span = grad_ref.shape
    tokens = tall - ROWS
    split = tokens // span
    for j in range(pieces):
        rows = grad_ref[j, tokens:, :].astype(f32)
        for a in range(split):
            doc_ref[a, j : j + 1, :] = rows[a : a + 1]
            lang_ref[a, j : j + 1, :] = rows[split + a : split + a + 1]
    docs, langs = doc_ref[...], lang_ref[...]
    doc_len = jnp.zeros_like(docs)
    for d in range(NDOCS):
        hot = (docs == float(d)).astype(f32)
        count = jnp.sum(jnp.sum(hot, axis=0), axis=(0, 1), keepdims=True)
        doc_len = doc_len + hot * count[None]
    weight = jnp.zeros_like(langs)
    for g in range(dro_ref.shape[0]):
        weight = jnp.where(langs == float(g), dro_ref[g], weight)
    scale = weight * (2.0 * mean_len) / (doc_len + mean_len)
    for a in range(split):
        scale_ref[a * span : (a + 1) * span, :] = scale[a].T

    def load(j, row):
        rows = pl.ds(row, ROWS)
        return grad_ref[j, rows, :].astype(f32) * scale_ref[rows, j : j + 1]

    to_middle(load, mid_ref, tokens, pieces)

    def inner(m):
        spec = dot(ahead_ref[m], mid_ref[m])
        spec_ref[m] = spec
        filt = filt_ref[m]
        re, im = spec[:tokens], spec[tokens:]
        fre, fim = filt[:tokens], filt[tokens:]
        prod = jnp.concatenate([fre * re + fim * im, fre * im - fim * re], axis=0).astype(bf16)
        back_ref[m] = dot(behind_ref[m], prod)

    each_piece(pieces, inner)
    skip = skip_ref[...]

    def store(j, row, value):
        out_ref[j, pl.ds(row, ROWS), :] = (value + skip * load(j, row)).astype(bf16)

    from_middle(back_ref, store, tokens, pieces)


def lags_kernel(in_ref, grad_ref, behind_ref, out_ref, back_ref, lag_ref):
    pieces, tall, span = in_ref.shape
    tokens = tall // 2
    held = out_ref.shape[2] // tokens

    def inner(m):
        x, g = in_ref[m], grad_ref[m]
        xre, xim, gre, gim = x[:tokens], x[tokens:], g[:tokens], g[tokens:]
        prod = jnp.concatenate([xre * gre + xim * gim, xre * gim - xim * gre], axis=0)
        back_ref[m] = dot(behind_ref[m], prod.astype(bf16))

    each_piece(pieces, inner)

    def store(j, row, value):
        lag_ref[j, pl.ds(row, ROWS), :] = value

    from_middle(back_ref, store, tokens, pieces)
    for j in range(pieces):
        place = (j % held) * tokens
        out_ref[j // held, :, place : place + tokens] = lag_ref[j].T.astype(bf16)


def gate_kernel(own_ref, grad_ref, scale_ref, mixed_ref, out_ref):
    pieces, tokens, span = mixed_ref.shape
    lane = lax.broadcasted_iota(jnp.int32, (tokens, pieces), 1)
    scale = jnp.sum(
        jnp.where(lane == own_ref[0], scale_ref[...], jnp.zeros((tokens, pieces), f32)),
        axis=1,
        keepdims=True,
    )
    for i in range(pieces):
        part = slice(i * span, (i + 1) * span)
        out_ref[:, part] = (
            grad_ref[:, part].astype(f32) * scale * mixed_ref[i].astype(f32)
        ).astype(bf16)


def call(kernel, out, ins, scratch=(), limit=24, cost=(0, 0)):
    return pl.pallas_call(
        kernel,
        out_shape=out,
        in_specs=ins,
        out_specs=jax.tree.map(lambda _: VMEM, out),
        scratch_shapes=scratch,
        compiler_params=pltpu.CompilerParams(vmem_limit_bytes=limit << 20),
        cost_estimate=pl.CostEstimate(flops=cost[0], bytes_accessed=cost[1], transcendentals=0),
    )


def local(grad_out, saved_input, gate_value, filter_taps, skip_gain, lang_ids, doc_ids, dro_weight):
    tokens = grad_out.shape[1]
    channels = grad_out.shape[2]
    pieces = lax.axis_size("ctx")
    members = lax.axis_size("dp")
    length = tokens * pieces
    span = channels // pieces
    mean_len = length / NDOCS
    own = lax.axis_index("ctx")
    ahead, behind = inner_tables(pieces, tokens)
    skip = lax.dynamic_slice_in_dim(skip_gain, own * span, span)[None, :]
    exchange = functools.partial(
        lax.all_to_all, axis_name="ctx", split_axis=0, concat_axis=0, tiled=True
    )
    block = jax.ShapeDtypeStruct((pieces, tokens, span), bf16)
    spectrum = jax.ShapeDtypeStruct((pieces, 2 * tokens, span), f32)
    middle = pltpu.VMEM((pieces, 2 * tokens, span), bf16)
    turned_back = pltpu.VMEM((pieces, 2 * tokens, span), f32)
    macs = pieces * (2 * tokens) ** 2 * span

    taps = exchange(filter_taps.reshape(pieces, span, tokens))
    inputs = exchange(saved_input[0].reshape(tokens, pieces, span).transpose(1, 0, 2))
    grads = call(
        functools.partial(prep_kernel, pieces, span),
        jax.ShapeDtypeStruct((pieces, tokens + ROWS, span), bf16),
        [VMEM] * 4,
        cost=(0, 4 << 20),
    )(grad_out[0], gate_value[0], doc_ids, lang_ids)
    grads = exchange(grads)
    filt = call(
        filter_kernel,
        spectrum,
        [VMEM] * 2,
        [pltpu.VMEM((pieces, span, 2 * tokens), bf16)],
        cost=(2 * macs, 4 << 20),
    )(taps, ahead)
    mixed, input_spec = call(
        mixed_kernel,
        (block, spectrum),
        [VMEM] * 5,
        [middle, turned_back],
        cost=(4 * macs, 8 << 20),
    )(inputs, filt, skip, ahead, behind)
    mixed = exchange(mixed)
    back, grad_spec, scale = call(
        functools.partial(input_kernel, mean_len),
        (block, spectrum, jax.ShapeDtypeStruct((tokens, pieces), f32)),
        [VMEM, VMEM, VMEM, SMEM, VMEM, VMEM],
        [
            middle,
            turned_back,
            pltpu.VMEM((tokens // span, pieces, span), f32),
            pltpu.VMEM((tokens // span, pieces, span), f32),
        ],
        cost=(4 * macs, 8 << 20),
    )(grads, filt, skip, dro_weight, ahead, behind)
    back = exchange(back)
    lagged = call(
        lags_kernel,
        jax.ShapeDtypeStruct((members, span, length // members), bf16),
        [VMEM] * 3,
        [turned_back, pltpu.VMEM((pieces, tokens, span), f32)],
        cost=(2 * macs, 6 << 20),
    )(input_spec, grad_spec, behind)
    lagged = lax.all_to_all(lagged, "dp", split_axis=0, concat_axis=0, tiled=True)
    d_gate = call(
        gate_kernel,
        jax.ShapeDtypeStruct((tokens, channels), bf16),
        [SMEM, VMEM, VMEM, VMEM],
        cost=(0, 4 << 20),
    )(own.reshape(1), grad_out[0], scale, mixed)
    d_input = back.transpose(1, 0, 2).reshape(tokens, channels)
    d_filter = jnp.sum(lagged.astype(f32), axis=0)
    return (d_input[None], d_gate[None], d_filter)


def solution(mesh):
    return jax.shard_map(
        local,
        mesh=mesh,
        in_specs=(
            P("dp", "ctx", None),
            P("dp", "ctx", None),
            P("dp", "ctx", None),
            P(None, "ctx"),
            P(),
            P("dp", "ctx"),
            P("dp", "ctx"),
            P(),
        ),
        out_specs=(P("dp", "ctx", None), P("dp", "ctx", None), P("ctx", "dp")),
        check_vma=False,
    )
```

time: 244 us -> 123 us (0.50); the launches traced: 240 us -> 122 us
  matrix products: 99 us -> 0 us
  blocking collectives: 51 us -> 29.9 us
  Pallas kernels: 0 us -> 16.1 us
  between operations: 14.4 us -> 0.83 us
  waiting for transfers between devices: 39.2 us -> 43.2 us
  other arithmetic: 3.65 us -> 0.88 us
    dot_general x36 -> x0, matrix products: 99 us -> none  [the longest x3 11 us: forward(): jnp.einsum('ckn,nm->ckm', turned_re, sin_in, precision=highest)]
    psum x1 -> x0, blocking collectives: 34 us -> none  [local(): counts = lax.psum(jnp.sum(doc_hot, axis=0), 'ctx')]
    pallas_call x0 -> x6, Pallas kernels: none -> 16.1 us  [the longest x1 6.36 us: local(): call(functools.partial(input_kernel, mean_len), (block, spectrum, jax.Sha...]
    all_to_all x1 -> x2, blocking collectives: 17.1 us -> 29.9 us  [the longest x1 19 us: local(): mixed = exchange(mixed)]
    all_to_all x4, waiting for transfers between devices: 33.5 us -> 43.2 us  [the longest x1 13.5 us: local(): exchange(saved_input[0].reshape(tokens, pieces, span).transpose(1, 0, 2))]
    all_gather x2 -> x0, waiting for transfers between devices: 5.6 us -> none  [the longest x1 5.6 us: local(): lax.all_gather(share_im.astype(jnp.bfloat16), 'dp', axis=0, tiled=True)]
    convert_element_type x2 -> x0, other arithmetic: 3.27 us -> none  [the longest x1 1.79 us: local(): filter_grad = lax.psum_scatter(lagged.astype(jnp.bfloat16), 'dp', scatter...]
    unnamed x32 -> x36, local copies, waits for them, and re-layouts: 8.08 us -> 10.2 us
  transfers between devices with their start and end apart: 7 -> 4, of which waited for: 4 -> 4; matrix products, arithmetic and copies ran while one was open for 15% -> 3% of each run, Pallas kernels for 0% -> 6%
where the time goes in v1:
time: 123 us; the launch traced here: 122 us
  waiting for transfers between devices  43.2 us (35%)
  blocking collectives  29.9 us (24%)
  starting transfers between devices  19.8 us (16%)
  Pallas kernels  16.1 us (13%)
  local copies, waits for them, and re-layouts  11.6 us (9%)
    all_to_all x1, blocking collectives, local(): mixed = exchange(mixed)  19 us
    all_to_all x1, waiting for transfers between devices, local(): exchange(saved_input[0].reshape(tokens, pieces, span).transpose(1, 0, 2))  13.5 us
    all_to_all x1, waiting for transfers between devices, local(): back = exchange(back)  12.5 us
    all_to_all x1, waiting for transfers between devices, local(): taps = exchange(filter_taps.reshape(pieces, span, tokens))  12.1 us
    all_to_all x1, blocking collectives, local(): lax.all_to_all(lagged, 'dp', split_axis=0, concat_axis=0, tiled=True)  11 us
    unnamed x36, local copies, waits for them, and re-layouts  10.2 us
    all_to_all x1, starting transfers between devices, local(): taps = exchange(filter_taps.reshape(pieces, span, tokens))  7.53 us
    pallas_call x1, Pallas kernels, local(): call(functools.partial(input_kernel, mean_len), (block, spectrum, jax.Sha...  6.36 us
  transfers between devices with their start and end apart: 4, of which 4 were waited for; matrix products, arithmetic and copies ran while one was open for 3% of the time, Pallas kernels for 6%

profile of v1, /device:TPU:0, one launch (start us, length us, event | category | flops | bytes accessed | tf_op | source)
XLA Modules:
  0.0 122.4 jit_solution(3755521598518582088)
XLA Ops:
  0.6 0.0 copy-start
  0.6 0.0 copy-start.9
  0.7 7.5 %all-to-all-start.1 = ((bf16[16,128,128]{2,1,0:T(8,128)(2,1)}), bf16[16,128,128]{2,1,0:T(8,128)(2,1)S(1)}, u32[]{:S(2)}, u32[]{:S(2)}) async-start(bf16[16,128,128]{2,1,0:T(8,128)(2,1)} %bitcast.17), calls=%async_computation.1 | async-start | bytes 1048576 | tf_op jit(solution)/shard_map/all_to_all | solution.py:332
  8.2 1.3 %copy.14 = bf16[1,128,2048]{1,2,0:T(8,128)(2,1)S(1)} copy(bf16[1,128,2048]{2,1,0:T(8,128)(2,1)} %param.11) | data formatting | bytes 1048576 | tf_op args[1]
  9.5 1.0 copy.15
  10.6 12.1 %all-to-all-done.1.taps_ref = bf16[16,128,128]{2,1,0:T(8,128)(2,1)S(1)} async-done(((bf16[16,128,128]{2,1,0:T(8,128)(2,1)}), bf16[16,128,128]{2,1,0:T(8,128)(2,1)S(1)}, u32[]{:S(2)}, u32[]{:S(2)}) %all-to-all-start.1) | async-done | bytes 524320 | tf_op jit(solution)/shard_map/all_to_all | solution.py:332
  22.7 4.1 %all-to-all-start.3 = ((bf16[16,128,128]{2,1,0:T(8,128)(2,1)}), bf16[16,128,128]{2,1,0:T(8,128)(2,1)S(1)}, u32[]{:S(2)}, u32[]{:S(2)}) async-start(bf16[16,128,128]{2,1,0:T(8,128)(2,1)} %bitcast.8), calls=%async_computation.3 | async-start | bytes 1048576 | tf_op jit(solution)/shard_map/all_to_all | solution.py:333
  26.8 1.0 shard_map.121
  27.8 13.5 %all-to-all-done.3.in_ref = bf16[16,128,128]{2,1,0:T(8,128)(2,1)S(1)} async-done(((bf16[16,128,128]{2,1,0:T(8,128)(2,1)}), bf16[16,128,128]{2,1,0:T(8,128)(2,1)S(1)}, u32[]{:S(2)}, u32[]{:S(2)}) %all-to-all-start.3) | async-done | bytes 524320 | tf_op jit(solution)/shard_map/all_to_all | solution.py:333
  41.3 4.1 %all-to-all-start = ((bf16[16,144,128]{2,1,0:T(8,128)(2,1)}), bf16[16,144,128]{2,1,0:T(8,128)(2,1)S(1)}, u32[]{:S(2)}, u32[]{:S(2)}) async-start(bf16[16,144,128]{2,1,0:T(8,128)(2,1)} %shard_map.121), calls=%async_computation | async-start | bytes 1179648 | tf_op jit(solution)/shard_map/all_to_all | solution.py:340
  45.4 0.1 dynamic-slice_bitcast_fusion.skip_ref
  45.5 1.6 %copy-done.2 = bf16[16,256,256]{2,1,0:T(8,128)(2,1)S(1)} copy-done((bf16[16,256,256]{2,1,0:T(8,128)(2,1)S(1)}, bf16[16,256,256]{2,1,0:T(8,128)(2,1)}, u32[]{:S(2)}) %copy-start.2) | copy-done | bytes 2097176
  47.1 1.8 %shard_map.122.filt_ref = f32[16,256,128]{2,1,0:T(8,128)S(1)} custom-call(bf16[16,128,128]{2,1,0:T(8,128)(2,1)S(1)} %all-to-all-done.1.taps_ref, bf16[16,256,256]{2,1,0:T(8,128)(2,1)S(1)} %copy-done.2), custom_call_target="tpu_custom_call" | custom-call | flops 268435456 | bytes 4194304 | tf_op jit(solution)/shard_map/pallas_call | solution.py:341
  48.9 0.4 copy-done.3
  49.3 0.1 copy-done.12
  49.4 3.8 %shard_map.124 = (bf16[16,128,128]{2,1,0:T(8,128)(2,1)S(1)}, f32[16,256,128]{2,1,0:T(8,128)S(1)}) custom-call(bf16[16,128,128]{2,1,0:T(8,128)(2,1)S(1)} %copy-done.12, f32[16,256,128]{2,1,0:T(8,128)S(1)} %shard_map.122.filt_ref, f32[1,128]{1,0:T(1,128)S(1)} %dynamic-slice_bitcast_fusion.skip_ref, bf16[16,256,256]{2,1,0:T(8,128)(2,1)S(1)} %copy-done.3, ...), custom_call_target="tpu_custom_call" | custom-call | flops 536870912 | bytes 8388608 | tf_op jit(solution)/shard_map/pallas_call | solution.py:348
  53.2 1.3 %copy-done.5 = f32[16,256,128]{2,1,0:T(8,128)} copy-done((f32[16,256,128]{2,1,0:T(8,128)}, f32[16,256,128]{2,1,0:T(8,128)S(1)}, u32[]{:S(2)}) %copy-start.5) | copy-done | bytes 2097176
  54.6 1.3 %copy-done.7 = f32[16,256,128]{2,1,0:T(8,128)} copy-done((f32[16,256,128]{2,1,0:T(8,128)}, f32[16,256,128]{2,1,0:T(8,128)S(1)}, u32[]{:S(2)}) %copy-start.7) | copy-done | bytes 2097176
  55.9 5.0 %all-to-all-done.grad_ref = bf16[16,144,128]{2,1,0:T(8,128)(2,1)S(1)} async-done(((bf16[16,144,128]{2,1,0:T(8,128)(2,1)}), bf16[16,144,128]{2,1,0:T(8,128)(2,1)S(1)}, u32[]{:S(2)}, u32[]{:S(2)}) %all-to-all-start) | async-done | bytes 589856 | tf_op jit(solution)/shard_map/all_to_all | solution.py:340
  60.9 1.6 %copy-done.4 = bf16[16,256,256]{2,1,0:T(8,128)(2,1)S(1)} copy-done((bf16[16,256,256]{2,1,0:T(8,128)(2,1)S(1)}, bf16[16,256,256]{2,1,0:T(8,128)(2,1)}, u32[]{:S(2)}) %copy-start.4) | copy-done | bytes 2097176
  62.5 1.6 %copy-done.6 = f32[16,256,128]{2,1,0:T(8,128)S(1)} copy-done((f32[16,256,128]{2,1,0:T(8,128)S(1)}, f32[16,256,128]{2,1,0:T(8,128)}, u32[]{:S(2)}) %copy-start.6) | copy-done | bytes 2097176
  64.1 6.4 %shard_map.123 = (bf16[16,128,128]{2,1,0:T(8,128)(2,1)}, f32[16,256,128]{2,1,0:T(8,128)S(1)}, f32[128,16]{1,0:T(8,128)S(1)}) custom-call(bf16[16,144,128]{2,1,0:T(8,128)(2,1)S(1)} %all-to-all-done.grad_ref, f32[16,256,128]{2,1,0:T(8,128)S(1)} %copy-done.6, f32[1,128]{1,0:T(1,128)S(1)} %dynamic-slice_bitcast_fusion.skip_ref, f32[16]{0:T(128)S(1)} %copy-done.16, ...), custom_call_target="tpu_custom_call" | custom-call | flops 536870912 | bytes 8388608 | tf_op jit(solution)/shard_map/pallas_call | solution.py:356
  70.5 2.1 %shard_map.126 = bf16[2,128,1024]{2,1,0:T(8,128)(2,1)S(1)} custom-call(f32[16,256,128]{2,1,0:T(8,128)S(1)} %copy-done.8, f32[16,256,128]{2,1,0:T(8,128)S(1)} %get-tuple-element.12.grad_ref, bf16[16,256,256]{2,1,0:T(8,128)(2,1)S(1)} %copy-done.1), custom_call_target="tpu_custom_call" | custom-call | flops 268435456 | bytes 6291456 | tf_op jit(solution)/shard_map/pallas_call | solution.py:369
  72.5 0.0 copy-start.10
  72.6 11.0 %all_to_all.30 = bf16[2,128,1024]{2,1,0:T(8,128)(2,1)S(1)} all-to-all(bf16[2,128,1024]{2,1,0:T(8,128)(2,1)S(1)} %shard_map.126), channel_id=1, replica_groups=mesh['dp'=2,'ctx'=16] {'dp'}, dimensions={0} | all-to-all | bytes 1048576 | tf_op jit(solution)/shard_map/all_to_all | solution.py:376
  83.5 19.0 %all_to_all.31.mixed_ref = bf16[16,128,128]{2,1,0:T(8,128)(2,1)S(1)} all-to-all(bf16[16,128,128]{2,1,0:T(8,128)(2,1)S(1)} %get-tuple-element.10), channel_id=1, replica_groups=mesh['dp'=2,'ctx'=16] {'ctx'}, dimensions={0} | all-to-all | bytes 1048576 | tf_op jit(solution)/shard_map/all_to_all | solution.py:355
  102.5 4.1 %all-to-all-start.2 = ((bf16[16,128,128]{2,1,0:T(8,128)(2,1)}), bf16[16,128,128]{2,1,0:T(8,128)(2,1)S(1)}, u32[]{:S(2)}, u32[]{:S(2)}) async-start(bf16[16,128,128]{2,1,0:T(8,128)(2,1)} %get-tuple-element.8), calls=%async_computation.2 | async-start | bytes 1048576 | tf_op jit(solution)/shard_map/all_to_all | solution.py:368
  106.6 0.9 convert_reduce_fusion
  107.5 1.0 shard_map.125
  108.5 12.5 %all-to-all-done.2 = bf16[16,128,128]{2,1,0:T(8,128)(2,1)S(1)} async-done(((bf16[16,128,128]{2,1,0:T(8,128)(2,1)}), bf16[16,128,128]{2,1,0:T(8,128)(2,1)S(1)}, u32[]{:S(2)}, u32[]{:S(2)}) %all-to-all-start.2) | async-done | bytes 524320 | tf_op jit(solution)/shard_map/all_to_all | solution.py:368
  121.1 0.3 copy.13
  121.4 1.0 copy.16
  (24 shorter events, 0.0 us)
Async XLA Ops:
  0.6 44.8 %copy-start = (f32[2048]{0:T(1024)S(1)}, f32[2048]{0:T(1024)}, u32[]{:S(2)}) copy-start(f32[2048]{0:T(1024)} %param.14) | copy-start | bytes 24580
  0.6 26.2 %copy-start.9 = (bf16[1,128,2048]{2,1,0:T(8,128)(2,1)S(1)}, bf16[1,128,2048]{2,1,0:T(8,128)(2,1)}, u32[]{:S(2)}) copy-start(bf16[1,128,2048]{2,1,0:T(8,128)(2,1)} %param.10) | copy-start | bytes 1572868
  0.7 26.2 %copy-start.13 = (bf16[1,128,2048]{2,1,0:T(8,128)(2,1)S(1)}, bf16[1,128,2048]{2,1,0:T(8,128)(2,1)}, u32[]{:S(2)}) copy-start(bf16[1,128,2048]{2,1,0:T(8,128)(2,1)} %param.12) | copy-start | bytes 1572868
  0.7 26.2 %copy-start.14 = (s32[1,128]{1,0:T(1,128)S(1)}, s32[1,128]{1,0:T(1,128)}, u32[]{:S(2)}) copy-start(s32[1,128]{1,0:T(1,128)} %doc_ref.1) | copy-start | bytes 1540
  0.7 26.2 %copy-start.15 = (s32[1,128]{1,0:T(1,128)S(1)}, s32[1,128]{1,0:T(1,128)}, u32[]{:S(2)}) copy-start(s32[1,128]{1,0:T(1,128)} %lang_ref.1) | copy-start | bytes 1540
  0.7 22.0 %all-to-all-start.1 = ((bf16[16,128,128]{2,1,0:T(8,128)(2,1)}), bf16[16,128,128]{2,1,0:T(8,128)(2,1)S(1)}, u32[]{:S(2)}, u32[]{:S(2)}) async-start(bf16[16,128,128]{2,1,0:T(8,128)(2,1)} %bitcast.17), calls=%async_computation.1 | async-start | bytes 1048576 | tf_op jit(solution)/shard_map/all_to_all | solution.py:332
  22.7 18.6 %all-to-all-start.3 = ((bf16[16,128,128]{2,1,0:T(8,128)(2,1)}), bf16[16,128,128]{2,1,0:T(8,128)(2,1)S(1)}, u32[]{:S(2)}, u32[]{:S(2)}) async-start(bf16[16,128,128]{2,1,0:T(8,128)(2,1)} %bitcast.8), calls=%async_computation.3 | async-start | bytes 1048576 | tf_op jit(solution)/shard_map/all_to_all | solution.py:333
  41.3 4.1 %copy-start.11 = (bf16[16,128,128]{2,1,0:T(8,128)(2,1)}, bf16[16,128,128]{2,1,0:T(8,128)(2,1)S(1)}, u32[]{:S(2)}) copy-start(bf16[16,128,128]{2,1,0:T(8,128)(2,1)S(1)} %all-to-all-done.3.in_ref) | copy-start | bytes 1572868
  41.3 19.7 %all-to-all-start = ((bf16[16,144,128]{2,1,0:T(8,128)(2,1)}), bf16[16,144,128]{2,1,0:T(8,128)(2,1)S(1)}, u32[]{:S(2)}, u32[]{:S(2)}) async-start(bf16[16,144,128]{2,1,0:T(8,128)(2,1)} %shard_map.121), calls=%async_computation | async-start | bytes 1179648 | tf_op jit(solution)/shard_map/all_to_all | solution.py:340
  45.5 1.6 %copy-start.2 = (bf16[16,256,256]{2,1,0:T(8,128)(2,1)S(1)}, bf16[16,256,256]{2,1,0:T(8,128)(2,1)}, u32[]{:S(2)}) copy-start(bf16[16,256,256]{2,1,0:T(8,128)(2,1)} %constant.16.clone.ahead_ref) | copy-start | bytes 6291460
  47.1 1.8 %copy-start.1 = (bf16[16,256,256]{2,1,0:T(8,128)(2,1)S(1)}, bf16[16,256,256]{2,1,0:T(8,128)(2,1)}, u32[]{:S(2)}) copy-start(bf16[16,256,256]{2,1,0:T(8,128)(2,1)} %constant.17.clone.behind_ref) | copy-start | bytes 6291460
  47.1 2.2 %copy-start.3 = (bf16[16,256,256]{2,1,0:T(8,128)(2,1)S(1)}, bf16[16,256,256]{2,1,0:T(8,128)(2,1)}, u32[]{:S(2)}) copy-start(bf16[16,256,256]{2,1,0:T(8,128)(2,1)} %constant.16.clone.ahead_ref) | copy-start | bytes 6291460
  47.1 2.3 %copy-start.12 = (bf16[16,128,128]{2,1,0:T(8,128)(2,1)S(1)}, bf16[16,128,128]{2,1,0:T(8,128)(2,1)}, u32[]{:S(2)}) copy-start(bf16[16,128,128]{2,1,0:T(8,128)(2,1)} %copy-done.11) | copy-start | bytes 1572868
  49.4 11.6 %copy-start.16 = (f32[16]{0:T(128)S(1)}, f32[16]{0:T(128)}, u32[]{:S(2)}) copy-start(f32[16]{0:T(128)} %dro_ref.1) | copy-start | bytes 196
  53.2 1.3 %copy-start.5 = (f32[16,256,128]{2,1,0:T(8,128)}, f32[16,256,128]{2,1,0:T(8,128)S(1)}, u32[]{:S(2)}) copy-start(f32[16,256,128]{2,1,0:T(8,128)S(1)} %shard_map.122.filt_ref) | copy-start | bytes 6291460
  54.6 1.3 %copy-start.7 = (f32[16,256,128]{2,1,0:T(8,128)}, f32[16,256,128]{2,1,0:T(8,128)S(1)}, u32[]{:S(2)}) copy-start(f32[16,256,128]{2,1,0:T(8,128)S(1)} %get-tuple-element.11.in_ref) | copy-start | bytes 6291460
  60.9 1.6 %copy-start.4 = (bf16[16,256,256]{2,1,0:T(8,128)(2,1)S(1)}, bf16[16,256,256]{2,1,0:T(8,128)(2,1)}, u32[]{:S(2)}) copy-start(bf16[16,256,256]{2,1,0:T(8,128)(2,1)} %constant.16.clone.ahead_ref) | copy-start | bytes 6291460
  62.5 1.6 %copy-start.6 = (f32[16,256,128]{2,1,0:T(8,128)S(1)}, f32[16,256,128]{2,1,0:T(8,128)}, u32[]{:S(2)}) copy-start(f32[16,256,128]{2,1,0:T(8,128)} %copy-done.5) | copy-start | bytes 6291460
  64.1 6.4 %copy-start.8 = (f32[16,256,128]{2,1,0:T(8,128)S(1)}, f32[16,256,128]{2,1,0:T(8,128)}, u32[]{:S(2)}) copy-start(f32[16,256,128]{2,1,0:T(8,128)} %copy-done.7) | copy-start | bytes 6291460
  72.5 34.9 %copy-start.10 = (bf16[1,128,2048]{2,1,0:T(8,128)(2,1)S(1)}, bf16[1,128,2048]{2,1,0:T(8,128)(2,1)}, u32[]{:S(2)}) copy-start(bf16[1,128,2048]{2,1,0:T(8,128)(2,1)} %param.10) | copy-start | bytes 1572868
  102.5 18.6 %all-to-all-start.2 = ((bf16[16,128,128]{2,1,0:T(8,128)(2,1)}), bf16[16,128,128]{2,1,0:T(8,128)(2,1)S(1)}, u32[]{:S(2)}, u32[]{:S(2)}) async-start(bf16[16,128,128]{2,1,0:T(8,128)(2,1)} %get-tuple-element.8), calls=%async_computation.2 | async-start | bytes 1048576 | tf_op jit(solution)/shard_map/all_to_all | solution.py:368

commit v2 on v1

v2 whole, which is shorter than its diff:
```python
import functools
import math

import jax
import jax.numpy as jnp
import numpy as np
from jax import lax
from jax.experimental import pallas as pl
from jax.experimental.pallas import tpu as pltpu
from jax.sharding import PartitionSpec as P

NDOCS = 32
ROWS = 16
VMEM = pl.BlockSpec(memory_space=pltpu.VMEM)
SMEM = pl.BlockSpec(memory_space=pltpu.SMEM)
f32 = jnp.float32
bf16 = jnp.bfloat16


def inner_tables(pieces, tokens):
    size = 2 * pieces * tokens
    m = np.arange(pieces)[:, None, None]
    k = np.arange(tokens)[None, :, None]
    q = np.arange(tokens)[None, None, :]
    turn = (q * (4 * m + 1 + 4 * pieces * k)) % (2 * size)
    angle = math.pi / size * turn
    cos, sin = np.cos(angle), np.sin(angle)
    ahead = np.concatenate(
        [np.concatenate([cos, sin], axis=2), np.concatenate([-sin, cos], axis=2)], axis=1
    )
    behind = np.swapaxes(ahead, 1, 2) * (2.0 / size)
    return jnp.asarray(ahead, bf16), jnp.asarray(behind, bf16)


def turned(value, turns):
    re, im = value
    turns = turns % 1.0
    if turns == 0.0:
        return value
    if turns == 0.25:
        return (-im, re)
    if turns == 0.5:
        return (-re, -im)
    if turns == 0.75:
        return (im, -re)
    cos, sin = math.cos(2.0 * math.pi * turns), math.sin(2.0 * math.pi * turns)
    if (turns * 8.0) % 1.0 == 0.0:
        root = math.sqrt(0.5)
        plus, minus = (re + im) * root, (re - im) * root
        if turns == 0.125:
            return (minus, plus)
        if turns == 0.375:
            return (-plus, minus)
        if turns == 0.625:
            return (-minus, -plus)
        return (plus, -minus)
    return (re * cos - im * sin, re * sin + im * cos)


def dft(values, sign):
    count = len(values)
    if count == 1:
        return values
    even, odd = dft(values[0::2], sign), dft(values[1::2], sign)
    first, second = [], []
    for k in range(count // 2):
        a, b = even[k], turned(odd[k], sign * k / count)
        first.append((a[0] + b[0], a[1] + b[1]))
        second.append((a[0] - b[0], a[1] - b[1]))
    return first + second


def outer_forward(reals):
    count = len(reals)
    values = [(reals[0], jnp.zeros_like(reals[0]))]
    for j in range(1, count):
        angle = -math.pi * j / (2 * count)
        values.append((reals[j] * math.cos(angle), reals[j] * math.sin(angle)))
    return dft(values, -1.0)


def outer_inverse(values):
    count = len(values)
    out = []
    for j, (re, im) in enumerate(dft(values, 1.0)):
        angle = math.pi * j / (2 * count)
        out.append(re if j == 0 else re * math.cos(angle) - im * math.sin(angle))
    return out


def chunked(total, body):
    def step(i, carry):
        body(pl.multiple_of(i * ROWS, ROWS))
        return carry

    lax.fori_loop(0, total // ROWS, step, 0)


def each_piece(pieces, body, group=4):
    def step(i, carry):
        for g in range(group):
            body(i * group + g)
        return carry

    lax.fori_loop(0, pieces // group, step, 0)


def dot(a, b):
    return lax.dot_general(a, b, (((1,), (0,)), ((), ())), preferred_element_type=f32)


def places(pieces, tokens, span):
    beside = max(1, tokens // span)

    def place(index, start):
        row = start + (index // beside) * tokens
        column = (index % beside) * span
        return row, slice(column, column + span)

    tall = -(-2 // beside) * tokens
    return place, tall


def prep_kernel(pieces, span, input_ref, grad_ref, gate_ref, taps_ref, doc_ref, lang_ref, out_ref):
    tokens = grad_ref.shape[0]
    place, tall = places(pieces, tokens, span)
    tile = lax.broadcasted_iota(jnp.int32, (ROWS, tokens), 0)
    ids = jnp.where(tile == 0, doc_ref[...], lang_ref[...]).astype(f32).astype(bf16)
    in_row, in_lanes = place(0, span)
    grad_row, grad_lanes = place(1, span)
    for i in range(pieces):
        part = slice(i * span, (i + 1) * span)
        out_ref[i, :span, :] = taps_ref[part, :]
        out_ref[i, in_row : in_row + tokens, in_lanes] = input_ref[:, part]
        out_ref[i, grad_row : grad_row + tokens, grad_lanes] = (
            grad_ref[:, part].astype(f32) * gate_ref[:, part].astype(f32)
        ).astype(bf16)
        out_ref[i, span + tall :, :] = ids


def token_scale(message_ref, scale_ref, dro_ref, ids, mean_len, doc_ref, lang_ref):
    for j in range(message_ref.shape[0]):
        rows = message_ref[j, ids:, :].astype(f32)
        doc_ref[j : j + 1, :] = rows[0:1]
        lang_ref[j : j + 1, :] = rows[1:2]
    docs, langs = doc_ref[...], lang_ref[...]
    doc_len = jnp.zeros_like(docs)
    for d in range(NDOCS):
        hot = (docs == float(d)).astype(f32)
        doc_len = doc_len + hot * jnp.sum(hot, axis=(0, 1), keepdims=True)
    weight = jnp.zeros_like(langs)
    for g in range(dro_ref.shape[0]):
        weight = jnp.where(langs == float(g), dro_ref[g], weight)
    scale_ref[...] = (weight * (2.0 * mean_len) / (doc_len + mean_len)).T


def conv_kernel(
    mean_len,
    message_ref,
    skip_ref,
    dro_ref,
    ahead_ref,
    behind_ref,
    out_ref,
    cross_ref,
    scale_ref,
    taps_mid_ref,
    mid_ref,
    back_ref,
    doc_ref,
    lang_ref,
):
    pieces = message_ref.shape[0]
    tokens = message_ref.shape[2]
    span = skip_ref.shape[1]
    place, tall = places(pieces, tokens, span)
    token_scale(message_ref, scale_ref, dro_ref, span + tall, mean_len, doc_ref, lang_ref)

    def outer_taps(row):
        rows = pl.ds(row, ROWS)
        out = outer_forward([message_ref[j, rows, :].astype(f32) for j in range(pieces)])
        for m, (re, im) in enumerate(out):
            taps_mid_ref[m, rows, :tokens] = re.astype(bf16)
            taps_mid_ref[m, rows, tokens:] = im.astype(bf16)

    chunked(span, outer_taps)

    def load(side, j, row):
        start, lanes = place(side, span)
        value = message_ref[j, pl.ds(start + row, ROWS), lanes].astype(f32)
        return value * scale_ref[pl.ds(row, ROWS), j : j + 1] if side else value

    sides = (slice(0, span), slice(span, 2 * span))

    def outer(side):
        def body(row):
            out = outer_forward([load(side, j, row) for j in range(pieces)])
            for m, (re, im) in enumerate(out):
                mid_ref[m, pl.ds(row, ROWS), sides[side]] = re.astype(bf16)
                mid_ref[m, pl.ds(tokens + row, ROWS), sides[side]] = im.astype(bf16)

        chunked(tokens, body)

    outer(0)
    outer(1)

    def inner(m):
        filt = lax.dot_general(
            ahead_ref[m], taps_mid_ref[m], (((1,), (1,)), ((), ())), preferred_element_type=f32
        )
        spec = dot(ahead_ref[m], mid_ref[m])
        fre, fim = filt[:tokens], filt[tokens:]
        xre, xim = spec[:tokens, sides[0]], spec[tokens:, sides[0]]
        gre, gim = spec[:tokens, sides[1]], spec[tokens:, sides[1]]
        cross_ref[m, :tokens, :] = (xre * gre + xim * gim).astype(bf16)
        cross_ref[m, tokens:, :] = (xre * gim - xim * gre).astype(bf16)
        mixed = jnp.concatenate([fre * xre - fim * xim, fre * xim + fim * xre], axis=0)
        back = jnp.concatenate([fre * gre + fim * gim, fre * gim - fim * gre], axis=0)
        both = jnp.concatenate([mixed.astype(bf16), back.astype(bf16)], axis=1)
        back_ref[m] = dot(behind_ref[m], both)

    each_piece(pieces, inner)
    skip = skip_ref[...]

    def outer_back(side):
        start, lanes = place(side, 0)

        def body(row):
            out = outer_inverse(
                [
                    (
                        back_ref[m, pl.ds(row, ROWS), sides[side]],
                        back_ref[m, pl.ds(tokens + row, ROWS), sides[side]],
                    )
                    for m in range(pieces)
                ]
            )
            for j in range(pieces):
                out_ref[j, pl.ds(start + row, ROWS), lanes] = (
                    out[j] + skip * load(side, j, row)
                ).astype(bf16)

        chunked(tokens, body)

    outer_back(0)
    outer_back(1)


def lags_kernel(own_ref, cross_ref, behind_ref, keep_ref, send_ref, back_ref, lag_ref):
    pieces, tall, span = cross_ref.shape
    tokens = tall // 2
    held = keep_ref.shape[1] // tokens
    members = pieces // held

    def inner(m):
        back_ref[m] = dot(behind_ref[m], cross_ref[m])

    each_piece(pieces, inner)

    def body(row):
        out = outer_inverse(
            [
                (back_ref[m, pl.ds(row, ROWS), :], back_ref[m, pl.ds(tokens + row, ROWS), :])
                for m in range(pieces)
            ]
        )
        for j in range(pieces):
            lag_ref[j, pl.ds(row, ROWS), :] = out[j]

    chunked(tokens, body)
    for j in range(held):
        part = slice(j * tokens, (j + 1) * tokens)
        keep_ref[:, part] = lag_ref[own_ref[0] * held + j].T
        for r in range(1, members):
            other = lax.rem(own_ref[0] + r, members)
            send_ref[r - 1, :, part] = lag_ref[other * held + j].T.astype(bf16)


def final_kernel(own_ref, grad_ref, scale_ref, message_ref, gate_ref, input_ref):
    pieces = message_ref.shape[0]
    tokens, channels = grad_ref.shape
    span = channels // pieces
    place, _ = places(pieces, tokens, span)
    lane = lax.broadcasted_iota(jnp.int32, (tokens, pieces), 1)
    scale = jnp.sum(
        jnp.where(lane == own_ref[0], scale_ref[...], jnp.zeros((tokens, pieces), f32)),
        axis=1,
        keepdims=True,
    )
    mixed_row, mixed_lanes = place(0, 0)
    back_row, back_lanes = place(1, 0)
    for i in range(pieces):
        part = slice(i * span, (i + 1) * span)
        mixed = message_ref[i, mixed_row : mixed_row + tokens, mixed_lanes].astype(f32)
        gate_ref[:, part] = (grad_ref[:, part].astype(f32) * scale * mixed).astype(bf16)
        input_ref[:, part] = message_ref[i, back_row : back_row + tokens, back_lanes]


def call(kernel, out, ins, scratch=(), limit=24, cost=(0, 0)):
    return pl.pallas_call(
        kernel,
        out_shape=out,
        in_specs=ins,
        out_specs=jax.tree.map(lambda _: VMEM, out),
        scratch_shapes=scratch,
        compiler_params=pltpu.CompilerParams(vmem_limit_bytes=limit << 20),
        cost_estimate=pl.CostEstimate(flops=cost[0], bytes_accessed=cost[1], transcendentals=0),
    )


def local(grad_out, saved_input, gate_value, filter_taps, skip_gain, lang_ids, doc_ids, dro_weight):
    tokens = grad_out.shape[1]
    channels = grad_out.shape[2]
    pieces = lax.axis_size("ctx")
    members = lax.axis_size("dp")
    length = tokens * pieces
    span = channels // pieces
    mean_len = length / NDOCS
    own = lax.axis_index("ctx")
    ahead, behind = inner_tables(pieces, tokens)
    skip = lax.dynamic_slice_in_dim(skip_gain, own * span, span)[None, :]
    exchange = functools.partial(
        lax.all_to_all, axis_name="ctx", split_axis=0, concat_axis=0, tiled=True
    )
    tall = places(pieces, tokens, span)[1]
    macs = pieces * (2 * tokens) ** 2 * span

    message = call(
        functools.partial(prep_kernel, pieces, span),
        jax.ShapeDtypeStruct((pieces, span + tall + ROWS, tokens), bf16),
        [VMEM] * 6,
        cost=(0, 4 << 20),
    )(saved_input[0], grad_out[0], gate_value[0], filter_taps, doc_ids, lang_ids)
    message = exchange(message)
    message, cross, scale = call(
        functools.partial(conv_kernel, mean_len),
        (
            jax.ShapeDtypeStruct((pieces, tall, tokens), bf16),
            jax.ShapeDtypeStruct((pieces, 2 * tokens, span), bf16),
            jax.ShapeDtypeStruct((tokens, pieces), f32),
        ),
        [VMEM, VMEM, SMEM, VMEM, VMEM],
        [
            pltpu.VMEM((pieces, span, 2 * tokens), bf16),
            pltpu.VMEM((pieces, 2 * tokens, 2 * span), bf16),
            pltpu.VMEM((pieces, 2 * tokens, 2 * span), f32),
            pltpu.VMEM((pieces, tokens), f32),
            pltpu.VMEM((pieces, tokens), f32),
        ],
        cost=(10 * macs, 8 << 20),
    )(message, skip, dro_weight, ahead, behind)
    message = exchange(message)
    keep, send = call(
        lags_kernel,
        (
            jax.ShapeDtypeStruct((span, length // members), f32),
            jax.ShapeDtypeStruct((members - 1, span, length // members), bf16),
        ),
        [SMEM, VMEM, VMEM],
        [
            pltpu.VMEM((pieces, 2 * tokens, span), f32),
            pltpu.VMEM((pieces, tokens, span), f32),
        ],
        cost=(2 * macs, 6 << 20),
    )(lax.axis_index("dp").reshape(1), cross, behind)
    d_filter = keep
    for r in range(1, members):
        ring = [(d, (d + r) % members) for d in range(members)]
        d_filter = d_filter + lax.ppermute(send[r - 1], "dp", ring).astype(f32)
    token_block = jax.ShapeDtypeStruct((tokens, channels), bf16)
    d_gate, d_input = call(
        final_kernel,
        (token_block, token_block),
        [SMEM, VMEM, VMEM, VMEM],
        cost=(0, 4 << 20),
    )(own.reshape(1), grad_out[0], scale, message)
    return (d_input[None], d_gate[None], d_filter)


def solution(mesh):
    return jax.shard_map(
        local,
        mesh=mesh,
        in_specs=(
            P("dp", "ctx", None),
            P("dp", "ctx", None),
            P("dp", "ctx", None),
            P(None, "ctx"),
            P(),
            P("dp", "ctx"),
            P("dp", "ctx"),
            P(),
        ),
        out_specs=(P("dp", "ctx", None), P("dp", "ctx", None), P("ctx", "dp")),
        check_vma=False,
    )
```

time: 123 us -> 99.4 us (0.81)
  blocking collectives: 29.9 us -> 0 us
  waiting for transfers between devices: 43.2 us -> 50.3 us
  Pallas kernels: 16.1 us -> 14.8 us
  starting transfers between devices: 19.8 us -> 18.5 us
    all_to_all x2 -> x0, blocking collectives: 29.9 us -> none  [the longest x1 19 us: local(): mixed = exchange(mixed)]
    ppermute x0 -> x1, waiting for transfers between devices: none -> 7.15 us  [local(): d_filter = d_filter + lax.ppermute(send[r - 1], 'dp', ring).astype(f32)]
    all_to_all x4 -> x2, starting transfers between devices: 19.8 us -> 16.9 us  [local(): message = exchange(message)]
    unnamed x36 -> x30, local copies, waits for them, and re-layouts: 10.2 us -> 12.5 us
    ppermute x0 -> x1, starting transfers between devices: none -> 1.55 us  [local(): d_filter = d_filter + lax.ppermute(send[r - 1], 'dp', ring).astype(f32)]
    pallas_call x5 -> x3, Pallas kernels: 15.1 us -> 14.5 us  [the longest x1 11.2 us: local(): call(functools.partial(conv_kernel, mean_len), (jax.ShapeDtypeStruct((pie...]
    all_to_all x4 -> x2, waiting for transfers between devices: 43.2 us -> 43.2 us  [local(): message = exchange(message)]
  transfers between devices with their start and end apart: 4 -> 3, of which waited for: 4 -> 3; matrix products, arithmetic and copies ran while one was open for 3% -> 1% of each run, Pallas kernels for 6% -> 2%
where the time goes in v2:
time: 99.4 us; the launch traced here: 97.7 us
  waiting for transfers between devices  50.3 us (51%)
  starting transfers between devices  18.5 us (19%)
  Pallas kernels  14.8 us (15%)
  local copies, waits for them, and re-layouts  12.5 us (13%)
    all_to_all x2, waiting for transfers between devices, local(): message = exchange(message)  43.2 us
    all_to_all x2, starting transfers between devices, local(): message = exchange(message)  16.9 us
    unnamed x30, local copies, waits for them, and re-layouts  12.5 us
    pallas_call x1, Pallas kernels, local(): call(functools.partial(conv_kernel, mean_len), (jax.ShapeDtypeStruct((pie...  11.2 us
    ppermute x1, waiting for transfers between devices, local(): d_filter = d_filter + lax.ppermute(send[r - 1], 'dp', ring).astype(f32)  7.15 us
    pallas_call x1, Pallas kernels, local(): call(lags_kernel, (jax.ShapeDtypeStruct((span, length // members), f32),...  2.05 us
  transfers between devices with their start and end apart: 3, of which 3 were waited for; matrix products, arithmetic and copies ran while one was open for 1% of the time, Pallas kernels for 2%

profile of v2, /device:TPU:0, one launch (start us, length us, event | category | flops | bytes accessed | tf_op | source)
XLA Modules:
  0.0 97.7 jit_solution(10298723466886498547)
XLA Ops:
  0.6 0.0 copy-start
  0.6 0.0 copy-start.4
  0.7 1.0 %copy-done.4 = bf16[1,128,2048]{2,1,0:T(8,128)(2,1)S(1)} copy-done((bf16[1,128,2048]{2,1,0:T(8,128)(2,1)S(1)}, bf16[1,128,2048]{2,1,0:T(8,128)(2,1)}, u32[]{:S(2)}) %copy-start.4) | copy-done | bytes 524312
  1.7 1.0 %copy-done.9 = bf16[1,128,2048]{2,1,0:T(8,128)(2,1)S(1)} copy-done((bf16[1,128,2048]{2,1,0:T(8,128)(2,1)S(1)}, bf16[1,128,2048]{2,1,0:T(8,128)(2,1)}, u32[]{:S(2)}) %copy-start.9) | copy-done | bytes 524312
  2.7 1.0 %copy-done.10 = bf16[1,128,2048]{2,1,0:T(8,128)(2,1)S(1)} copy-done((bf16[1,128,2048]{2,1,0:T(8,128)(2,1)S(1)}, bf16[1,128,2048]{2,1,0:T(8,128)(2,1)}, u32[]{:S(2)}) %copy-start.10) | copy-done | bytes 524312
  3.8 1.0 %copy-done.11 = bf16[2048,128]{1,0:T(8,128)(2,1)S(1)} copy-done((bf16[2048,128]{1,0:T(8,128)(2,1)S(1)}, bf16[2048,128]{1,0:T(8,128)(2,1)}, u32[]{:S(2)}) %copy-start.11) | copy-done | bytes 524312
  4.8 0.7 copy-done.12
  5.5 0.7 copy-done.13
  6.1 0.3 shard_map.121
  6.4 0.0 copy-start.2
  6.4 1.1 %copy-done.2 = bf16[16,400,128]{2,1,0:T(8,128)(2,1)} copy-done((bf16[16,400,128]{2,1,0:T(8,128)(2,1)}, bf16[16,400,128]{2,1,0:T(8,128)(2,1)S(1)}, u32[]{:S(2)}) %copy-start.2) | copy-done | bytes 1638424
  7.6 7.6 %all-to-all-start = ((bf16[16,400,128]{2,1,0:T(8,128)(2,1)}), bf16[16,400,128]{2,1,0:T(8,128)(2,1)}, u32[]{:S(2)}, u32[]{:S(2)}) async-start(bf16[16,400,128]{2,1,0:T(8,128)(2,1)} %copy-done.2), calls=%async_computation | async-start | bytes 3276800 | tf_op jit(solution)/shard_map/all_to_all | solution.py:334
  15.1 0.0 copy-done
  15.1 0.1 dynamic-slice_bitcast_fusion.skip_ref
  15.2 33.1 %all-to-all-done.message_ref = bf16[16,400,128]{2,1,0:T(8,128)(2,1)} async-done(((bf16[16,400,128]{2,1,0:T(8,128)(2,1)}), bf16[16,400,128]{2,1,0:T(8,128)(2,1)}, u32[]{:S(2)}, u32[]{:S(2)}) %all-to-all-start) | async-done | bytes 1638432 | tf_op jit(solution)/shard_map/all_to_all | solution.py:334
  48.3 0.0 copy-done.1
  48.3 0.0 copy-done.14
  48.3 1.6 %copy-done.3 = bf16[16,256,256]{2,1,0:T(8,128)(2,1)S(1)} copy-done((bf16[16,256,256]{2,1,0:T(8,128)(2,1)S(1)}, bf16[16,256,256]{2,1,0:T(8,128)(2,1)}, u32[]{:S(2)}) %copy-start.3) | copy-done | bytes 2097176
  49.9 11.2 %shard_map.122 = (bf16[16,256,128]{2,1,0:T(8,128)(2,1)S(1)}, bf16[16,256,128]{2,1,0:T(8,128)(2,1)S(1)}, f32[128,16]{1,0:T(8,128)S(1)}) custom-call(bf16[16,400,128]{2,1,0:T(8,128)(2,1)} %all-to-all-done.message_ref, f32[1,128]{1,0:T(1,128)S(1)} %dynamic-slice_bitcast_fusion.skip_ref, f32[16]{0:T(128)S(1)} %copy-done.14, bf16[16,256,256]{2,1,0:T(8,128)(2,1)S(1)} %copy-done.3, ...), custom_call_target="tpu_custom_call" | custom-call | flops 1342177280 | bytes 8388608 | tf_op jit(solution)/shard_map/pallas_call | solution.py:335
  61.2 0.0 copy-start.6
  61.2 1.0 %copy-done.6 = bf16[16,256,128]{2,1,0:T(8,128)(2,1)} copy-done((bf16[16,256,128]{2,1,0:T(8,128)(2,1)}, bf16[16,256,128]{2,1,0:T(8,128)(2,1)S(1)}, u32[]{:S(2)}) %copy-start.6) | copy-done | bytes 1048600
  62.2 1.0 copy-done.7
  63.1 9.4 %all-to-all-start.1 = ((bf16[16,256,128]{2,1,0:T(8,128)(2,1)}), bf16[16,256,128]{2,1,0:T(8,128)(2,1)S(1)}, u32[]{:S(2)}, u32[]{:S(2)}) async-start(bf16[16,256,128]{2,1,0:T(8,128)(2,1)} %copy-done.6), calls=%async_computation.1 | async-start | bytes 2097152 | tf_op jit(solution)/shard_map/all_to_all | solution.py:352
  72.5 0.0 copy-start.8
  72.5 1.2 %copy-done.8 = bf16[16,256,128]{2,1,0:T(8,128)(2,1)S(1)} copy-done((bf16[16,256,128]{2,1,0:T(8,128)(2,1)S(1)}, bf16[16,256,128]{2,1,0:T(8,128)(2,1)}, u32[]{:S(2)}) %copy-start.8) | copy-done | bytes 1048600
  73.7 2.1 %shard_map.124 = (f32[128,1024]{1,0:T(8,128)S(1)}, bf16[1,128,1024]{2,1,0:T(8,128)(2,1)S(1)}) custom-call(s32[1]{0:T(128)} %bitcast.7.own_ref, bf16[16,256,128]{2,1,0:T(8,128)(2,1)S(1)} %copy-done.8, bf16[16,256,256]{2,1,0:T(8,128)(2,1)S(1)} %copy-done.1), custom_call_target="tpu_custom_call" | custom-call | flops 268435456 | bytes 6291456 | tf_op jit(solution)/shard_map/pallas_call | solution.py:353
  75.8 1.6 %collective-permute-start = (bf16[128,1024]{1,0:T(8,128)(2,1)S(1)}, bf16[128,1024]{1,0:T(8,128)(2,1)S(1)}, u32[]{:S(2)}, u32[]{:S(2)}) collective-permute-start(bf16[128,1024]{1,0:T(8,128)(2,1)S(1)} %bitcast.14), channel_id=1, source_target_pairs={{0,16},{16,0},{1,17},{17,1},{2,18},{18,2},{3,19},{19,3},{4,20},{20... | collective-permute-start | bytes 786440 | tf_op jit(solution)/shard_map/ppermute | solution.py:369
  77.3 7.2 %collective-permute-done = bf16[128,1024]{1,0:T(8,128)(2,1)S(1)} collective-permute-done((bf16[128,1024]{1,0:T(8,128)(2,1)S(1)}, bf16[128,1024]{1,0:T(8,128)(2,1)S(1)}, u32[]{:S(2)}, u32[]{:S(2)}) %collective-permute-start) | collective-permute-done | bytes 262176 | tf_op jit(solution)/shard_map/ppermute | solution.py:369
  84.5 0.9 convert_add_fusion
  85.4 10.1 %all-to-all-done.1.message_ref = bf16[16,256,128]{2,1,0:T(8,128)(2,1)S(1)} async-done(((bf16[16,256,128]{2,1,0:T(8,128)(2,1)}), bf16[16,256,128]{2,1,0:T(8,128)(2,1)S(1)}, u32[]{:S(2)}, u32[]{:S(2)}) %all-to-all-start.1) | async-done | bytes 1048608 | tf_op jit(solution)/shard_map/all_to_all | solution.py:352
  95.4 1.0 %copy-done.5 = bf16[1,128,2048]{2,1,0:T(8,128)(2,1)S(1)} copy-done((bf16[1,128,2048]{2,1,0:T(8,128)(2,1)S(1)}, bf16[1,128,2048]{2,1,0:T(8,128)(2,1)}, u32[]{:S(2)}) %copy-start.5) | copy-done | bytes 524312
  96.5 1.2 %shard_map.123 = (bf16[128,2048]{1,0:T(8,128)(2,1)}, bf16[128,2048]{1,0:T(8,128)(2,1)}) custom-call(s32[1]{0:T(128)} %bitcast.own_ref, bf16[128,2048]{1,0:T(8,128)(2,1)S(1)} %bitcast.11, f32[128,16]{1,0:T(8,128)S(1)} %get-tuple-element.10.scale_ref, bf16[16,256,128]{2,1,0:T(8,128)(2,1)S(1)} %all-to-all-done.1.message_ref), custom_call_target="tpu_custom_call" | custom-call | bytes 4194304 | tf_op jit(solution)/shard_map/pallas_call | solution.py:371
  (10 shorter events, 0.0 us)
Async XLA Ops:
  0.6 14.5 %copy-start = (f32[2048]{0:T(1024)S(1)}, f32[2048]{0:T(1024)}, u32[]{:S(2)}) copy-start(f32[2048]{0:T(1024)} %param.14) | copy-start | bytes 24580
  0.6 1.0 %copy-start.4 = (bf16[1,128,2048]{2,1,0:T(8,128)(2,1)S(1)}, bf16[1,128,2048]{2,1,0:T(8,128)(2,1)}, u32[]{:S(2)}) copy-start(bf16[1,128,2048]{2,1,0:T(8,128)(2,1)} %param.10) | copy-start | bytes 1572868
  1.7 1.0 %copy-start.9 = (bf16[1,128,2048]{2,1,0:T(8,128)(2,1)S(1)}, bf16[1,128,2048]{2,1,0:T(8,128)(2,1)}, u32[]{:S(2)}) copy-start(bf16[1,128,2048]{2,1,0:T(8,128)(2,1)} %param.11) | copy-start | bytes 1572868
  2.7 1.0 %copy-start.10 = (bf16[1,128,2048]{2,1,0:T(8,128)(2,1)S(1)}, bf16[1,128,2048]{2,1,0:T(8,128)(2,1)}, u32[]{:S(2)}) copy-start(bf16[1,128,2048]{2,1,0:T(8,128)(2,1)} %param.12) | copy-start | bytes 1572868
  3.8 1.0 %copy-start.11 = (bf16[2048,128]{1,0:T(8,128)(2,1)S(1)}, bf16[2048,128]{1,0:T(8,128)(2,1)}, u32[]{:S(2)}) copy-start(bf16[2048,128]{1,0:T(8,128)(2,1)} %taps_ref.1) | copy-start | bytes 1572868
  4.8 0.7 copy-start.12
  5.5 0.7 copy-start.13
  6.4 1.2 %copy-start.2 = (bf16[16,400,128]{2,1,0:T(8,128)(2,1)}, bf16[16,400,128]{2,1,0:T(8,128)(2,1)S(1)}, u32[]{:S(2)}) copy-start(bf16[16,400,128]{2,1,0:T(8,128)(2,1)S(1)} %shard_map.121) | copy-start | bytes 4915204
  7.6 40.8 %copy-start.1 = (bf16[16,256,256]{2,1,0:T(8,128)(2,1)S(1)}, bf16[16,256,256]{2,1,0:T(8,128)(2,1)}, u32[]{:S(2)}) copy-start(bf16[16,256,256]{2,1,0:T(8,128)(2,1)} %constant.20.clone.behind_ref) | copy-start | bytes 6291460
  7.6 40.8 %copy-start.14 = (f32[16]{0:T(128)S(1)}, f32[16]{0:T(128)}, u32[]{:S(2)}) copy-start(f32[16]{0:T(128)} %dro_ref.1) | copy-start | bytes 196
  7.6 40.7 %all-to-all-start = ((bf16[16,400,128]{2,1,0:T(8,128)(2,1)}), bf16[16,400,128]{2,1,0:T(8,128)(2,1)}, u32[]{:S(2)}, u32[]{:S(2)}) async-start(bf16[16,400,128]{2,1,0:T(8,128)(2,1)} %copy-done.2), calls=%async_computation | async-start | bytes 3276800 | tf_op jit(solution)/shard_map/all_to_all | solution.py:334
  48.3 1.6 %copy-start.3 = (bf16[16,256,256]{2,1,0:T(8,128)(2,1)S(1)}, bf16[16,256,256]{2,1,0:T(8,128)(2,1)}, u32[]{:S(2)}) copy-start(bf16[16,256,256]{2,1,0:T(8,128)(2,1)} %constant.19.clone.ahead_ref) | copy-start | bytes 6291460
  61.2 1.0 %copy-start.6 = (bf16[16,256,128]{2,1,0:T(8,128)(2,1)}, bf16[16,256,128]{2,1,0:T(8,128)(2,1)S(1)}, u32[]{:S(2)}) copy-start(bf16[16,256,128]{2,1,0:T(8,128)(2,1)S(1)} %get-tuple-element.11) | copy-start | bytes 3145732
  62.2 1.0 copy-start.7
  63.1 32.3 %all-to-all-start.1 = ((bf16[16,256,128]{2,1,0:T(8,128)(2,1)}), bf16[16,256,128]{2,1,0:T(8,128)(2,1)S(1)}, u32[]{:S(2)}, u32[]{:S(2)}) async-start(bf16[16,256,128]{2,1,0:T(8,128)(2,1)} %copy-done.6), calls=%async_computation.1 | async-start | bytes 2097152 | tf_op jit(solution)/shard_map/all_to_all | solution.py:352
  72.5 1.2 %copy-start.8 = (bf16[16,256,128]{2,1,0:T(8,128)(2,1)S(1)}, bf16[16,256,128]{2,1,0:T(8,128)(2,1)}, u32[]{:S(2)}) copy-start(bf16[16,256,128]{2,1,0:T(8,128)(2,1)} %copy-done.7) | copy-start | bytes 3145732
  75.8 8.7 %collective-permute-start = (bf16[128,1024]{1,0:T(8,128)(2,1)S(1)}, bf16[128,1024]{1,0:T(8,128)(2,1)S(1)}, u32[]{:S(2)}, u32[]{:S(2)}) collective-permute-start(bf16[128,1024]{1,0:T(8,128)(2,1)S(1)} %bitcast.14), channel_id=1, source_target_pairs={{0,16},{16,0},{1,17},{17,1},{2,18},{18,2},{3,19},{19,3},{4,20},{20... | collective-permute-start | bytes 786440 | tf_op jit(solution)/shard_map/ppermute | solution.py:369
  95.4 1.0 %copy-start.5 = (bf16[1,128,2048]{2,1,0:T(8,128)(2,1)S(1)}, bf16[1,128,2048]{2,1,0:T(8,128)(2,1)}, u32[]{:S(2)}) copy-start(bf16[1,128,2048]{2,1,0:T(8,128)(2,1)} %param.10) | copy-start | bytes 1572868

commit v3 on v1

v3 whole, which is shorter than its diff:
```python
import functools
import math

import jax
import jax.numpy as jnp
import numpy as np
from jax import lax
from jax.experimental import pallas as pl
from jax.experimental.pallas import tpu as pltpu
from jax.sharding import PartitionSpec as P

NDOCS = 32
ROWS = 16
VMEM = pl.BlockSpec(memory_space=pltpu.VMEM)
SMEM = pl.BlockSpec(memory_space=pltpu.SMEM)
f32 = jnp.float32
bf16 = jnp.bfloat16


def inner_tables(pieces, tokens):
    size = 2 * pieces * tokens
    m = np.arange(pieces)[:, None, None]
    k = np.arange(tokens)[None, :, None]
    q = np.arange(tokens)[None, None, :]
    turn = (q * (4 * m + 1 + 4 * pieces * k)) % (2 * size)
    angle = math.pi / size * turn
    cos, sin = np.cos(angle), np.sin(angle)
    ahead = np.concatenate(
        [np.concatenate([cos, sin], axis=2), np.concatenate([-sin, cos], axis=2)], axis=1
    )
    behind = np.swapaxes(ahead, 1, 2) * (2.0 / size)
    return jnp.asarray(ahead, bf16), jnp.asarray(behind, bf16)


def turned(value, turns):
    re, im = value
    turns = turns % 1.0
    if turns == 0.0:
        return value
    if turns == 0.25:
        return (-im, re)
    if turns == 0.5:
        return (-re, -im)
    if turns == 0.75:
        return (im, -re)
    cos, sin = math.cos(2.0 * math.pi * turns), math.sin(2.0 * math.pi * turns)
    if (turns * 8.0) % 1.0 == 0.0:
        root = math.sqrt(0.5)
        plus, minus = (re + im) * root, (re - im) * root
        if turns == 0.125:
            return (minus, plus)
        if turns == 0.375:
            return (-plus, minus)
        if turns == 0.625:
            return (-minus, -plus)
        return (plus, -minus)
    return (re * cos - im * sin, re * sin + im * cos)


def dft(values, sign):
    count = len(values)
    if count == 1:
        return values
    even, odd = dft(values[0::2], sign), dft(values[1::2], sign)
    first, second = [], []
    for k in range(count // 2):
        a, b = even[k], turned(odd[k], sign * k / count)
        first.append((a[0] + b[0], a[1] + b[1]))
        second.append((a[0] - b[0], a[1] - b[1]))
    return first + second


def outer_forward(reals):
    count = len(reals)
    values = [(reals[0], jnp.zeros_like(reals[0]))]
    for j in range(1, count):
        angle = -math.pi * j / (2 * count)
        values.append((reals[j] * math.cos(angle), reals[j] * math.sin(angle)))
    return dft(values, -1.0)


def outer_inverse(values):
    count = len(values)
    out = []
    for j, (re, im) in enumerate(dft(values, 1.0)):
        angle = math.pi * j / (2 * count)
        out.append(re if j == 0 else re * math.cos(angle) - im * math.sin(angle))
    return out


def chunked(total, body):
    def step(i, carry):
        body(pl.multiple_of(i * ROWS, ROWS))
        return carry

    lax.fori_loop(0, total // ROWS, step, 0)


def each_piece(pieces, body, group=4):
    def step(i, carry):
        for g in range(group):
            body(i * group + g)
        return carry

    lax.fori_loop(0, pieces // group, step, 0)


def dot(a, b):
    return lax.dot_general(a, b, (((1,), (0,)), ((), ())), preferred_element_type=f32)


def relative(own_ref, r, count):
    return lax.rem(own_ref[0] + r, count)


def gathered(own_ref, chunk_refs, held_ref):
    count = len(chunk_refs)
    for r, ref in enumerate(chunk_refs):
        held_ref[relative(own_ref, count - r, count)] = ref[...]


def scattered(own_ref, held_ref, chunk_refs):
    count = len(chunk_refs)
    for r, ref in enumerate(chunk_refs):
        ref[...] = held_ref[relative(own_ref, r, count)]


def taps_out_kernel(pieces, span, own_ref, taps_ref, doc_ref, lang_ref, *out_refs):
    tile = lax.broadcasted_iota(jnp.int32, (ROWS, taps_ref.shape[1]), 0)
    ids = jnp.where(tile == 0, doc_ref[...], lang_ref[...]).astype(f32).astype(bf16)
    for r, ref in enumerate(out_refs):
        start = pl.multiple_of(relative(own_ref, r, pieces) * span, ROWS)
        ref[:span, :] = taps_ref[pl.ds(start, span), :]
        ref[span:, :] = ids


def input_out_kernel(pieces, span, own_ref, input_ref, *refs):
    held_ref = refs[pieces]
    for i in range(pieces):
        held_ref[i] = input_ref[:, i * span : (i + 1) * span]
    scattered(own_ref, held_ref, refs[:pieces])


def grad_out_kernel(pieces, span, own_ref, grad_ref, gate_ref, *refs):
    held_ref = refs[pieces]
    for i in range(pieces):
        part = slice(i * span, (i + 1) * span)
        held_ref[i] = (grad_ref[:, part].astype(f32) * gate_ref[:, part].astype(f32)).astype(bf16)
    scattered(own_ref, held_ref, refs[:pieces])


def token_scale(doc_ref, lang_ref, dro_ref, mean_len, scale_ref):
    docs, langs = doc_ref[...], lang_ref[...]
    doc_len = jnp.zeros_like(docs)
    for d in range(NDOCS):
        hot = (docs == float(d)).astype(f32)
        doc_len = doc_len + hot * jnp.sum(hot, axis=(0, 1), keepdims=True)
    weight = jnp.zeros_like(langs)
    for g in range(dro_ref.shape[0]):
        weight = jnp.where(langs == float(g), dro_ref[g], weight)
    scale_ref[...] = (weight * (2.0 * mean_len) / (doc_len + mean_len)).T


def filter_kernel(mean_len, pieces, own_ref, dro_ref, ahead_ref, *refs):
    chunks, (spec_ref, scale_ref, held_ref, mid_ref, doc_ref, lang_ref) = refs[:pieces], refs[pieces:]
    _, span, _ = mid_ref.shape
    tokens = scale_ref.shape[0]
    gathered(own_ref, chunks, held_ref)
    for j in range(pieces):
        rows = held_ref[j, span:, :].astype(f32)
        doc_ref[j : j + 1, :] = rows[0:1]
        lang_ref[j : j + 1, :] = rows[1:2]
    token_scale(doc_ref, lang_ref, dro_ref, mean_len, scale_ref)

    def outer(row):
        rows = pl.ds(row, ROWS)
        out = outer_forward([held_ref[j, rows, :].astype(f32) for j in range(pieces)])
        for m, (re, im) in enumerate(out):
            mid_ref[m, rows, :tokens] = re.astype(bf16)
            mid_ref[m, rows, tokens:] = im.astype(bf16)

    chunked(span, outer)

    def inner(m):
        spec_ref[m] = lax.dot_general(
            ahead_ref[m], mid_ref[m], (((1,), (1,)), ((), ())), preferred_element_type=f32
        ).astype(bf16)

    each_piece(pieces, inner)


def to_middle(load, mid_ref, tokens, pieces):
    def outer(row):
        out = outer_forward([load(j, row) for j in range(pieces)])
        for m, (re, im) in enumerate(out):
            mid_ref[m, pl.ds(row, ROWS), :] = re.astype(bf16)
            mid_ref[m, pl.ds(tokens + row, ROWS), :] = im.astype(bf16)

    chunked(tokens, outer)


def from_middle(back_ref, store, tokens, pieces):
    def outer(row):
        out = outer_inverse(
            [
                (back_ref[m, pl.ds(row, ROWS), :], back_ref[m, pl.ds(tokens + row, ROWS), :])
                for m in range(pieces)
            ]
        )
        for j in range(pieces):
            store(j, row, out[j])

    chunked(tokens, outer)


def halves(value):
    value = value.astype(f32)
    middle = value.shape[0] // 2
    return value[:middle], value[middle:]


def joined(re, im):
    return jnp.concatenate([re.astype(bf16), im.astype(bf16)], axis=0)


def mixed_kernel(pieces, own_ref, filt_ref, skip_ref, ahead_ref, behind_ref, *refs):
    chunks, outs, (spec_ref, held_ref, mid_ref, back_ref) = (
        refs[:pieces],
        refs[pieces : 2 * pieces],
        refs[2 * pieces :],
    )
    tokens = held_ref.shape[1]
    gathered(own_ref, chunks, held_ref)

    def load(j, row):
        return held_ref[j, pl.ds(row, ROWS), :].astype(f32)

    to_middle(load, mid_ref, tokens, pieces)

    def inner(m):
        spec = dot(ahead_ref[m], mid_ref[m])
        spec_ref[m] = spec.astype(bf16)
        (re, im), (fre, fim) = halves(spec), halves(filt_ref[m])
        back_ref[m] = dot(behind_ref[m], joined(fre * re - fim * im, fre * im + fim * re))

    each_piece(pieces, inner)
    skip = skip_ref[...]

    def store(j, row, value):
        held_ref[j, pl.ds(row, ROWS), :] = (value + skip * load(j, row)).astype(bf16)

    from_middle(back_ref, store, tokens, pieces)
    scattered(own_ref, held_ref, outs)


def input_kernel(
    pieces, own_ref, filt_ref, spec_ref, scale_ref, skip_ref, ahead_ref, behind_ref, *refs
):
    chunks, outs, (cross_ref, held_ref, mid_ref, back_ref) = (
        refs[:pieces],
        refs[pieces : 2 * pieces],
        refs[2 * pieces :],
    )
    tokens = held_ref.shape[1]
    gathered(own_ref, chunks, held_ref)

    def load(j, row):
        rows = pl.ds(row, ROWS)
        return held_ref[j, rows, :].astype(f32) * scale_ref[rows, j : j + 1]

    to_middle(load, mid_ref, tokens, pieces)

    def inner(m):
        re, im = halves(dot(ahead_ref[m], mid_ref[m]))
        (fre, fim), (xre, xim) = halves(filt_ref[m]), halves(spec_ref[m])
        cross_ref[m] = joined(xre * re + xim * im, xre * im - xim * re)
        back_ref[m] = dot(behind_ref[m], joined(fre * re + fim * im, fre * im - fim * re))

    each_piece(pieces, inner)
    skip = skip_ref[...]

    def store(j, row, value):
        held_ref[j, pl.ds(row, ROWS), :] = (value + skip * load(j, row)).astype(bf16)

    from_middle(back_ref, store, tokens, pieces)
    scattered(own_ref, held_ref, outs)


def lags_kernel(own_ref, cross_ref, behind_ref, keep_ref, send_ref, back_ref, lag_ref):
    pieces, tall, span = cross_ref.shape
    tokens = tall // 2
    held = keep_ref.shape[1] // tokens
    members = pieces // held

    def inner(m):
        back_ref[m] = dot(behind_ref[m], cross_ref[m])

    each_piece(pieces, inner)

    def store(j, row, value):
        lag_ref[j, pl.ds(row, ROWS), :] = value

    from_middle(back_ref, store, tokens, pieces)
    for j in range(held):
        part = slice(j * tokens, (j + 1) * tokens)
        keep_ref[:, part] = lag_ref[own_ref[0] * held + j].T
        for r in range(1, members):
            send_ref[r - 1, :, part] = lag_ref[relative(own_ref, r, members) * held + j].T.astype(
                bf16
            )


def gate_kernel(pieces, own_ref, grad_ref, scale_ref, *refs):
    chunks, (out_ref, held_ref) = refs[:pieces], refs[pieces:]
    _, tokens, span = held_ref.shape
    gathered(own_ref, chunks, held_ref)
    lane = lax.broadcasted_iota(jnp.int32, (tokens, pieces), 1)
    scale = jnp.sum(
        jnp.where(lane == own_ref[0], scale_ref[...], jnp.zeros((tokens, pieces), f32)),
        axis=1,
        keepdims=True,
    )
    for i in range(pieces):
        part = slice(i * span, (i + 1) * span)
        out_ref[:, part] = (
            grad_ref[:, part].astype(f32) * scale * held_ref[i].astype(f32)
        ).astype(bf16)


def input_in_kernel(pieces, own_ref, *refs):
    chunks, (out_ref, held_ref) = refs[:pieces], refs[pieces:]
    _, _, span = held_ref.shape
    gathered(own_ref, chunks, held_ref)
    for i in range(pieces):
        out_ref[:, i * span : (i + 1) * span] = held_ref[i]


def call(kernel, out, ins, scratch=(), limit=24, cost=(0, 0)):
    return pl.pallas_call(
        kernel,
        out_shape=out,
        in_specs=ins,
        out_specs=jax.tree.map(lambda _: VMEM, out),
        scratch_shapes=scratch,
        compiler_params=pltpu.CompilerParams(vmem_limit_bytes=limit << 20),
        cost_estimate=pl.CostEstimate(flops=cost[0], bytes_accessed=cost[1], transcendentals=0),
    )


def local(grad_out, saved_input, gate_value, filter_taps, skip_gain, lang_ids, doc_ids, dro_weight):
    tokens = grad_out.shape[1]
    channels = grad_out.shape[2]
    pieces = lax.axis_size("ctx")
    members = lax.axis_size("dp")
    length = tokens * pieces
    span = channels // pieces
    mean_len = length / NDOCS
    place = lax.axis_index("ctx")
    own = place.reshape(1)
    ahead, behind = inner_tables(pieces, tokens)
    skip = lax.dynamic_slice_in_dim(skip_gain, place * span, span)[None, :]

    def exchange(chunks):
        rings = [[(i, (i + r) % pieces) for i in range(pieces)] for r in range(pieces)]
        return [chunks[0]] + [lax.ppermute(chunks[r], "ctx", rings[r]) for r in range(1, pieces)]

    shape = jax.ShapeDtypeStruct
    blocks = [shape((tokens, span), bf16)] * pieces
    held = pltpu.VMEM((pieces, tokens, span), bf16)
    middle = pltpu.VMEM((pieces, 2 * tokens, span), bf16)
    back = pltpu.VMEM((pieces, 2 * tokens, span), f32)
    spectrum = shape((pieces, 2 * tokens, span), bf16)
    many = [VMEM] * pieces
    macs = pieces * (2 * tokens) ** 2 * span

    taps = exchange(
        call(
            functools.partial(taps_out_kernel, pieces, span),
            [shape((span + ROWS, tokens), bf16)] * pieces,
            [SMEM, VMEM, VMEM, VMEM],
            cost=(0, 1 << 20),
        )(own, filter_taps, doc_ids, lang_ids)
    )
    inputs = exchange(
        call(
            functools.partial(input_out_kernel, pieces, span),
            blocks,
            [SMEM, VMEM],
            [held],
            cost=(0, 1 << 20),
        )(own, saved_input[0])
    )
    grads = exchange(
        call(
            functools.partial(grad_out_kernel, pieces, span),
            blocks,
            [SMEM, VMEM, VMEM],
            [held],
            cost=(0, 1 << 20),
        )(own, grad_out[0], gate_value[0])
    )
    filt, scale = call(
        functools.partial(filter_kernel, mean_len, pieces),
        (spectrum, shape((tokens, pieces), f32)),
        [SMEM, SMEM, VMEM] + many,
        [
            pltpu.VMEM((pieces, span + ROWS, tokens), bf16),
            pltpu.VMEM((pieces, span, 2 * tokens), bf16),
            pltpu.VMEM((pieces, tokens), f32),
            pltpu.VMEM((pieces, tokens), f32),
        ],
        cost=(2 * macs, 4 << 20),
    )(own, dro_weight, ahead, *taps)
    *mixed, spec = call(
        functools.partial(mixed_kernel, pieces),
        blocks + [spectrum],
        [SMEM] + [VMEM] * 4 + many,
        [held, middle, back],
        cost=(4 * macs, 8 << 20),
    )(own, filt, skip, ahead, behind, *inputs)
    mixed = exchange(mixed)
    *d_input, cross = call(
        functools.partial(input_kernel, pieces),
        blocks + [spectrum],
        [SMEM] + [VMEM] * 6 + many,
        [held, middle, back],
        cost=(4 * macs, 8 << 20),
    )(own, filt, spec, scale, skip, ahead, behind, *grads)
    d_input = exchange(d_input)
    keep, send = call(
        lags_kernel,
        (
            shape((span, length // members), f32),
            shape((members - 1, span, length // members), bf16),
        ),
        [SMEM, VMEM, VMEM],
        [back, pltpu.VMEM((pieces, tokens, span), f32)],
        cost=(2 * macs, 6 << 20),
    )(lax.axis_index("dp").reshape(1), cross, behind)
    d_filter = keep
    for r in range(1, members):
        ring = [(d, (d + r) % members) for d in range(members)]
        d_filter = d_filter + lax.ppermute(send[r - 1], "dp", ring).astype(f32)
    token_block = shape((tokens, channels), bf16)
    d_gate = call(
        functools.partial(gate_kernel, pieces),
        token_block,
        [SMEM, VMEM, VMEM] + many,
        [held],
        cost=(0, 2 << 20),
    )(own, grad_out[0], scale, *mixed)
    d_input = call(
        functools.partial(input_in_kernel, pieces),
        token_block,
        [SMEM] + many,
        [held],
        cost=(0, 1 << 20),
    )(own, *d_input)
    return (d_input[None], d_gate[None], d_filter)


def solution(mesh):
    return jax.shard_map(
        local,
        mesh=mesh,
        in_specs=(
            P("dp", "ctx", None),
            P("dp", "ctx", None),
            P("dp", "ctx", None),
            P(None, "ctx"),
            P(),
            P("dp", "ctx"),
            P("dp", "ctx"),
            P(),
        ),
        out_specs=(P("dp", "ctx", None), P("dp", "ctx", None), P("ctx", "dp")),
        check_vma=False,
    )
```

time: 123 us -> 141 us (1.15)
  starting transfers between devices: 19.8 us -> 96.5 us
  waiting for transfers between devices: 43.2 us -> 12.6 us
  blocking collectives: 29.9 us -> 0 us
  Pallas kernels: 16.1 us -> 17.9 us
    ppermute x0 -> x76, starting transfers between devices: none -> 96.5 us  [the longest x75 95 us: exchange(): lax.ppermute(chunks[r], 'ctx', rings[r])]
    all_to_all x4 -> x0, waiting for transfers between devices: 43.2 us -> none  [the longest x1 13.5 us: local(): exchange(saved_input[0].reshape(tokens, pieces, span).transpose(1, 0, 2))]
    all_to_all x2 -> x0, blocking collectives: 29.9 us -> none  [the longest x1 19 us: local(): mixed = exchange(mixed)]
    all_to_all x4 -> x0, starting transfers between devices: 19.8 us -> none  [the longest x1 7.53 us: local(): taps = exchange(filter_taps.reshape(pieces, span, tokens))]
    ppermute x0 -> x76, waiting for transfers between devices: none -> 12.6 us  [the longest x75 12.6 us: exchange(): lax.ppermute(chunks[r], 'ctx', rings[r])]
    pallas_call x6 -> x9, Pallas kernels: 16.1 us -> 17.9 us  [the longest x1 5.15 us: local(): call(functools.partial(input_kernel, pieces), blocks + [spectrum], [SMEM]...]
    unnamed x36 -> x54, local copies, waits for them, and re-layouts: 10.2 us -> 11.1 us
  transfers between devices with their start and end apart: 4 -> 76, of which waited for: 4 -> 13; matrix products, arithmetic and copies ran while one was open for 3% -> 0% of each run, Pallas kernels for 6% -> 9%
where the time goes in v3:
time: 141 us; the launch traced here: 140 us
  starting transfers between devices  96.5 us (68%)
  Pallas kernels  17.9 us (13%)
  waiting for transfers between devices  12.6 us (9%)
  local copies, waits for them, and re-layouts  11.2 us (8%)
    ppermute x75, starting transfers between devices, exchange(): lax.ppermute(chunks[r], 'ctx', rings[r])  95 us
    ppermute x75, waiting for transfers between devices, exchange(): lax.ppermute(chunks[r], 'ctx', rings[r])  12.6 us
    unnamed x54, local copies, waits for them, and re-layouts  11.1 us
    pallas_call x1, Pallas kernels, local(): call(functools.partial(input_kernel, pieces), blocks + [spectrum], [SMEM]...  5.15 us
    pallas_call x1, Pallas kernels, local(): call(functools.partial(mixed_kernel, pieces), blocks + [spectrum], [SMEM]...  4.83 us
  transfers between devices with their start and end apart: 76, of which 13 were waited for; matrix products, arithmetic and copies ran while one was open for 0% of the time, Pallas kernels for 9%

profile of v3, /device:TPU:0, one launch (start us, length us, event | category | flops | bytes accessed | tf_op | source)
XLA Modules:
  0.0 140.1 jit_solution(7816552559117249611)
XLA Ops:
  5.9 2.5 %collective-permute-start.31 = (bf16[128,128]{1,0:T(8,128)(2,1)S(1)}, bf16[128,128]{1,0:T(8,128)(2,1)S(1)}, u32[]{:S(2)}, u32[]{:S(2)}) collective-permute-start(bf16[128,128]{1,0:T(8,128)(2,1)S(1)} %get-tuple-element.126), channel_id=1, source_target_pairs={{0,2},{1,3},{2,4},{3,5},{4,6},{5,7},{6,8},{7,9},{8,10},{9,11},{10,... | collective-permute-start | bytes 98312 | tf_op jit(solution)/shard_map/ppermute | solution.py:365
  8.4 2.4 %collective-permute-start.32 = (bf16[128,128]{1,0:T(8,128)(2,1)S(1)}, bf16[128,128]{1,0:T(8,128)(2,1)S(1)}, u32[]{:S(2)}, u32[]{:S(2)}) collective-permute-start(bf16[128,128]{1,0:T(8,128)(2,1)S(1)} %get-tuple-element.127), channel_id=1, source_target_pairs={{0,3},{1,4},{2,5},{3,6},{4,7},{5,8},{6,9},{7,10},{8,11},{9,12},{10... | collective-permute-start | bytes 98312 | tf_op jit(solution)/shard_map/ppermute | solution.py:365
  13.8 4.3 %collective-permute-start.36 = (bf16[128,128]{1,0:T(8,128)(2,1)S(1)}, bf16[128,128]{1,0:T(8,128)(2,1)S(1)}, u32[]{:S(2)}, u32[]{:S(2)}) collective-permute-start(bf16[128,128]{1,0:T(8,128)(2,1)S(1)} %get-tuple-element.131), channel_id=1, source_target_pairs={{0,7},{1,8},{2,9},{3,10},{4,11},{5,12},{6,13},{7,14},{8,15},{9,0},... | collective-permute-start | bytes 98312 | tf_op jit(solution)/shard_map/ppermute | solution.py:365
  19.6 1.6 %collective-permute-start.39 = (bf16[128,128]{1,0:T(8,128)(2,1)S(1)}, bf16[128,128]{1,0:T(8,128)(2,1)S(1)}, u32[]{:S(2)}, u32[]{:S(2)}) collective-permute-start(bf16[128,128]{1,0:T(8,128)(2,1)S(1)} %get-tuple-element.134), channel_id=1, source_target_pairs={{0,10},{1,11},{2,12},{3,13},{4,14},{5,15},{6,0},{7,1},{8,2},{9,3},... | collective-permute-start | bytes 98312 | tf_op jit(solution)/shard_map/ppermute | solution.py:365
  22.4 2.0 %collective-permute-start.15 = (bf16[128,128]{1,0:T(8,128)(2,1)S(1)}, bf16[128,128]{1,0:T(8,128)(2,1)S(1)}, u32[]{:S(2)}, u32[]{:S(2)}) collective-permute-start(bf16[128,128]{1,0:T(8,128)(2,1)S(1)} %get-tuple-element.107), channel_id=1, source_target_pairs={{0,1},{1,2},{2,3},{3,4},{4,5},{5,6},{6,7},{7,8},{8,9},{9,10},{10,1... | collective-permute-start | bytes 98312 | tf_op jit(solution)/shard_map/ppermute | solution.py:365
  28.5 1.9 %collective-permute-start.20 = (bf16[128,128]{1,0:T(8,128)(2,1)S(1)}, bf16[128,128]{1,0:T(8,128)(2,1)S(1)}, u32[]{:S(2)}, u32[]{:S(2)}) collective-permute-start(bf16[128,128]{1,0:T(8,128)(2,1)S(1)} %get-tuple-element.112), channel_id=1, source_target_pairs={{0,6},{1,7},{2,8},{3,9},{4,10},{5,11},{6,12},{7,13},{8,14},{9,15},... | collective-permute-start | bytes 98312 | tf_op jit(solution)/shard_map/ppermute | solution.py:365
  34.2 1.9 %collective-permute-start.24 = (bf16[128,128]{1,0:T(8,128)(2,1)S(1)}, bf16[128,128]{1,0:T(8,128)(2,1)S(1)}, u32[]{:S(2)}, u32[]{:S(2)}) collective-permute-start(bf16[128,128]{1,0:T(8,128)(2,1)S(1)} %get-tuple-element.116), channel_id=1, source_target_pairs={{0,10},{1,11},{2,12},{3,13},{4,14},{5,15},{6,0},{7,1},{8,2},{9,3},... | collective-permute-start | bytes 98312 | tf_op jit(solution)/shard_map/ppermute | solution.py:365
  40.6 1.6 %collective-permute-start.1 = (bf16[144,128]{1,0:T(8,128)(2,1)S(1)}, bf16[144,128]{1,0:T(8,128)(2,1)S(1)}, u32[]{:S(2)}, u32[]{:S(2)}) collective-permute-start(bf16[144,128]{1,0:T(8,128)(2,1)S(1)} %get-tuple-element.91), channel_id=1, source_target_pairs={{0,2},{1,3},{2,4},{3,5},{4,6},{5,7},{6,8},{7,9},{8,10},{9,11},{10,... | collective-permute-start | bytes 110600 | tf_op jit(solution)/shard_map/ppermute | solution.py:365
  45.2 1.7 %collective-permute-start.5 = (bf16[144,128]{1,0:T(8,128)(2,1)S(1)}, bf16[144,128]{1,0:T(8,128)(2,1)S(1)}, u32[]{:S(2)}, u32[]{:S(2)}) collective-permute-start(bf16[144,128]{1,0:T(8,128)(2,1)S(1)} %get-tuple-element.95), channel_id=1, source_target_pairs={{0,6},{1,7},{2,8},{3,9},{4,10},{5,11},{6,12},{7,13},{8,14},{9,15},... | collective-permute-start | bytes 110600 | tf_op jit(solution)/shard_map/ppermute | solution.py:365
  47.6 2.2 %collective-permute-start.6 = (bf16[144,128]{1,0:T(8,128)(2,1)S(1)}, bf16[144,128]{1,0:T(8,128)(2,1)S(1)}, u32[]{:S(2)}, u32[]{:S(2)}) collective-permute-start(bf16[144,128]{1,0:T(8,128)(2,1)S(1)} %get-tuple-element.96), channel_id=1, source_target_pairs={{0,7},{1,8},{2,9},{3,10},{4,11},{5,12},{6,13},{7,14},{8,15},{9,0},... | collective-permute-start | bytes 110600 | tf_op jit(solution)/shard_map/ppermute | solution.py:365
  49.8 1.7 %collective-permute-start.7 = (bf16[144,128]{1,0:T(8,128)(2,1)S(1)}, bf16[144,128]{1,0:T(8,128)(2,1)S(1)}, u32[]{:S(2)}, u32[]{:S(2)}) collective-permute-start(bf16[144,128]{1,0:T(8,128)(2,1)S(1)} %get-tuple-element.97), channel_id=1, source_target_pairs={{0,8},{1,9},{2,10},{3,11},{4,12},{5,13},{6,14},{7,15},{8,0},{9,1},... | collective-permute-start | bytes 110600 | tf_op jit(solution)/shard_map/ppermute | solution.py:365
  52.8 4.1 %collective-permute-start.10 = (bf16[144,128]{1,0:T(8,128)(2,1)}, bf16[144,128]{1,0:T(8,128)(2,1)S(1)}, u32[]{:S(2)}, u32[]{:S(2)}) collective-permute-start(bf16[144,128]{1,0:T(8,128)(2,1)} %get-tuple-element.100), channel_id=1, source_target_pairs={{0,11},{1,12},{2,13},{3,14},{4,15},{5,0},{6,1},{7,2},{8,3},{9,4},{... | collective-permute-start | bytes 110600 | tf_op jit(solution)/shard_map/ppermute | solution.py:365
  57.5 2.5 %collective-permute-start.13 = (bf16[144,128]{1,0:T(8,128)(2,1)S(1)}, bf16[144,128]{1,0:T(8,128)(2,1)S(1)}, u32[]{:S(2)}, u32[]{:S(2)}) collective-permute-start(bf16[144,128]{1,0:T(8,128)(2,1)S(1)} %get-tuple-element.103), channel_id=1, source_target_pairs={{0,14},{1,15},{2,0},{3,1},{4,2},{5,3},{6,4},{7,5},{8,6},{9,7},{10,... | collective-permute-start | bytes 110600 | tf_op jit(solution)/shard_map/ppermute | solution.py:365
  64.2 2.7 %collective-permute-start.28 = (bf16[128,128]{1,0:T(8,128)(2,1)}, bf16[128,128]{1,0:T(8,128)(2,1)S(1)}, u32[]{:S(2)}, u32[]{:S(2)}) collective-permute-start(bf16[128,128]{1,0:T(8,128)(2,1)} %copy-done.23), channel_id=1, source_target_pairs={{0,14},{1,15},{2,0},{3,1},{4,2},{5,3},{6,4},{7,5},{8,6},{9,7},{10,... | collective-permute-start | bytes 98312 | tf_op jit(solution)/shard_map/ppermute | solution.py:365
  67.5 1.6 %copy-done.2 = bf16[16,256,256]{2,1,0:T(8,128)(2,1)S(1)} copy-done((bf16[16,256,256]{2,1,0:T(8,128)(2,1)S(1)}, bf16[16,256,256]{2,1,0:T(8,128)(2,1)}, u32[]{:S(2)}) %copy-start.2) | copy-done | bytes 2097176
  69.1 2.8 %shard_map.122 = (bf16[16,256,128]{2,1,0:T(8,128)(2,1)S(1)}, f32[128,16]{1,0:T(8,128)S(1)}) custom-call(s32[1]{0:T(128)} %bitcast.own_ref, f32[16]{0:T(128)S(1)} %copy-done.11, bf16[16,256,256]{2,1,0:T(8,128)(2,1)S(1)} %copy-done.2, bf16[144,128]{1,0:T(8,128)(2,1)S(1)} %get-tuple-element.89.refs_0_, bf16[144,128]{1,0:T(8,128)(2,1)S(1)} %collective-permute-done.refs_1_, ...), custom_call_target="tpu_custom_call" | custom-call | flops 268435456 | bytes 4194304 | tf_op jit(solution)/shard_map/pallas_call | solution.py:402
  75.1 1.6 %collective-permute-start.43 = (bf16[128,128]{1,0:T(8,128)(2,1)S(1)}, bf16[128,128]{1,0:T(8,128)(2,1)S(1)}, u32[]{:S(2)}, u32[]{:S(2)}) collective-permute-start(bf16[128,128]{1,0:T(8,128)(2,1)S(1)} %copy-done.15), channel_id=1, source_target_pairs={{0,14},{1,15},{2,0},{3,1},{4,2},{5,3},{6,4},{7,5},{8,6},{9,7},{10,... | collective-permute-start | bytes 98312 | tf_op jit(solution)/shard_map/ppermute | solution.py:365
  76.7 1.7 %collective-permute-start.44 = (bf16[128,128]{1,0:T(8,128)(2,1)S(1)}, bf16[128,128]{1,0:T(8,128)(2,1)S(1)}, u32[]{:S(2)}, u32[]{:S(2)}) collective-permute-start(bf16[128,128]{1,0:T(8,128)(2,1)S(1)} %copy-done.13), channel_id=1, source_target_pairs={{0,15},{1,0},{2,1},{3,2},{4,3},{5,4},{6,5},{7,6},{8,7},{9,8},{10,9... | collective-permute-start | bytes 98312 | tf_op jit(solution)/shard_map/ppermute | solution.py:365
  80.0 4.8 %shard_map.124 = (bf16[128,128]{1,0:T(8,128)(2,1)S(1)}, bf16[128,128]{1,0:T(8,128)(2,1)S(1)}, bf16[128,128]{1,0:T(8,128)(2,1)S(1)}, bf16[128,128]{1,0:T(8,128)(2...) custom-call(s32[1]{0:T(128)} %bitcast.own_ref, ...), custom_call_target="tpu_custom_call" | custom-call | flops 536870912 | bytes 8388608 | tf_op jit(solution)/shard_map/pallas_call | solution.py:414
  84.9 5.2 %shard_map.126 = (bf16[128,128]{1,0:T(8,128)(2,1)S(1)}, bf16[128,128]{1,0:T(8,128)(2,1)S(1)}, bf16[128,128]{1,0:T(8,128)(2,1)S(1)}, bf16[128,128]{1,0:T(8,128)(2...) custom-call(s32[1]{0:T(128)} %bitcast.own_ref, ...), custom_call_target="tpu_custom_call" | custom-call | flops 536870912 | bytes 8388608 | tf_op jit(solution)/shard_map/pallas_call | solution.py:422
  90.2 2.1 %shard_map.129 = (f32[128,1024]{1,0:T(8,128)S(1)}, bf16[1,128,1024]{2,1,0:T(8,128)(2,1)S(1)}) custom-call(s32[1]{0:T(128)} %bitcast.7.own_ref, bf16[16,256,128]{2,1,0:T(8,128)(2,1)S(1)} %get-tuple-element.172.cross_ref, bf16[16,256,256]{2,1,0:T(8,128)(2,1)S(1)} %copy-done.1), custom_call_target="tpu_custom_call" | custom-call | flops 268435456 | bytes 6291456 | tf_op jit(solution)/shard_map/pallas_call | solution.py:430
  96.9 3.4 %collective-permute-start.50 = (bf16[128,128]{1,0:T(8,128)(2,1)S(1)}, bf16[128,128]{1,0:T(8,128)(2,1)S(1)}, u32[]{:S(2)}, u32[]{:S(2)}) collective-permute-start(bf16[128,128]{1,0:T(8,128)(2,1)S(1)} %get-tuple-element.146), channel_id=1, source_target_pairs={{0,6},{1,7},{2,8},{3,9},{4,10},{5,11},{6,12},{7,13},{8,14},{9,15},... | collective-permute-start | bytes 98312 | tf_op jit(solution)/shard_map/ppermute | solution.py:365
  101.2 2.3 %collective-permute-start.52 = (bf16[128,128]{1,0:T(8,128)(2,1)S(1)}, bf16[128,128]{1,0:T(8,128)(2,1)S(1)}, u32[]{:S(2)}, u32[]{:S(2)}) collective-permute-start(bf16[128,128]{1,0:T(8,128)(2,1)S(1)} %get-tuple-element.148), channel_id=1, source_target_pairs={{0,8},{1,9},{2,10},{3,11},{4,12},{5,13},{6,14},{7,15},{8,0},{9,1},... | collective-permute-start | bytes 98312 | tf_op jit(solution)/shard_map/ppermute | solution.py:365
  103.5 2.7 %collective-permute-start.54 = (bf16[128,128]{1,0:T(8,128)(2,1)S(1)}, bf16[128,128]{1,0:T(8,128)(2,1)S(1)}, u32[]{:S(2)}, u32[]{:S(2)}) collective-permute-start(bf16[128,128]{1,0:T(8,128)(2,1)S(1)} %get-tuple-element.150), channel_id=1, source_target_pairs={{0,10},{1,11},{2,12},{3,13},{4,14},{5,15},{6,0},{7,1},{8,2},{9,3},... | collective-permute-start | bytes 98312 | tf_op jit(solution)/shard_map/ppermute | solution.py:365
  106.2 3.2 %collective-permute-start.55 = (bf16[128,128]{1,0:T(8,128)(2,1)S(1)}, bf16[128,128]{1,0:T(8,128)(2,1)S(1)}, u32[]{:S(2)}, u32[]{:S(2)}) collective-permute-start(bf16[128,128]{1,0:T(8,128)(2,1)S(1)} %get-tuple-element.151), channel_id=1, source_target_pairs={{0,11},{1,12},{2,13},{3,14},{4,15},{5,0},{6,1},{7,2},{8,3},{9,4},{... | collective-permute-start | bytes 98312 | tf_op jit(solution)/shard_map/ppermute | solution.py:365
  110.9 3.0 %collective-permute-start.58 = (bf16[128,128]{1,0:T(8,128)(2,1)S(1)}, bf16[128,128]{1,0:T(8,128)(2,1)S(1)}, u32[]{:S(2)}, u32[]{:S(2)}) collective-permute-start(bf16[128,128]{1,0:T(8,128)(2,1)S(1)} %get-tuple-element.154), channel_id=1, source_target_pairs={{0,14},{1,15},{2,0},{3,1},{4,2},{5,3},{6,4},{7,5},{8,6},{9,7},{10,... | collective-permute-start | bytes 98312 | tf_op jit(solution)/shard_map/ppermute | solution.py:365
  114.5 2.4 %collective-permute-start.61 = (bf16[128,128]{1,0:T(8,128)(2,1)S(1)}, bf16[128,128]{1,0:T(8,128)(2,1)S(1)}, u32[]{:S(2)}, u32[]{:S(2)}) collective-permute-start(bf16[128,128]{1,0:T(8,128)(2,1)S(1)} %get-tuple-element.158), channel_id=1, source_target_pairs={{0,2},{1,3},{2,4},{3,5},{4,6},{5,7},{6,8},{7,9},{8,10},{9,11},{10,... | collective-permute-start | bytes 98312 | tf_op jit(solution)/shard_map/ppermute | solution.py:365
  118.3 1.8 %collective-permute-done.60.refs_1_ = bf16[128,128]{1,0:T(8,128)(2,1)S(1)} collective-permute-done((bf16[128,128]{1,0:T(8,128)(2,1)S(1)}, bf16[128,128]{1,0:T(8,128)(2,1)S(1)}, u32[]{:S(2)}, u32[]{:S(2)}) %collective-permute-start.60) | collective-permute-done | bytes 32800 | tf_op jit(solution)/shard_map/ppermute | solution.py:365
  122.0 1.7 %collective-permute-start.66 = (bf16[128,128]{1,0:T(8,128)(2,1)S(1)}, bf16[128,128]{1,0:T(8,128)(2,1)S(1)}, u32[]{:S(2)}, u32[]{:S(2)}) collective-permute-start(bf16[128,128]{1,0:T(8,128)(2,1)S(1)} %get-tuple-element.163), channel_id=1, source_target_pairs={{0,7},{1,8},{2,9},{3,10},{4,11},{5,12},{6,13},{7,14},{8,15},{9,0},... | collective-permute-start | bytes 98312 | tf_op jit(solution)/shard_map/ppermute | solution.py:365
  125.8 1.8 %collective-permute-done.65.refs_6_ = bf16[128,128]{1,0:T(8,128)(2,1)S(1)} collective-permute-done((bf16[128,128]{1,0:T(8,128)(2,1)S(1)}, bf16[128,128]{1,0:T(8,128)(2,1)S(1)}, u32[]{:S(2)}, u32[]{:S(2)}) %collective-permute-start.65) | collective-permute-done | bytes 32800 | tf_op jit(solution)/shard_map/ppermute | solution.py:365
  127.9 3.2 %collective-permute-start.70 = (bf16[128,128]{1,0:T(8,128)(2,1)S(1)}, bf16[128,128]{1,0:T(8,128)(2,1)S(1)}, u32[]{:S(2)}, u32[]{:S(2)}) collective-permute-start(bf16[128,128]{1,0:T(8,128)(2,1)S(1)} %get-tuple-element.167), channel_id=1, source_target_pairs={{0,11},{1,12},{2,13},{3,14},{4,15},{5,0},{6,1},{7,2},{8,3},{9,4},{... | collective-permute-start | bytes 98312 | tf_op jit(solution)/shard_map/ppermute | solution.py:365
  132.9 2.3 %collective-permute-start.73 = (bf16[128,128]{1,0:T(8,128)(2,1)S(1)}, bf16[128,128]{1,0:T(8,128)(2,1)S(1)}, u32[]{:S(2)}, u32[]{:S(2)}) collective-permute-start(bf16[128,128]{1,0:T(8,128)(2,1)S(1)} %get-tuple-element.170), channel_id=1, source_target_pairs={{0,14},{1,15},{2,0},{3,1},{4,2},{5,3},{6,4},{7,5},{8,6},{9,7},{10,... | collective-permute-start | bytes 98312 | tf_op jit(solution)/shard_map/ppermute | solution.py:365
  (185 shorter events, 58.2 us)
Async XLA Ops:
  5.9 8.0 %collective-permute-start.31 = (bf16[128,128]{1,0:T(8,128)(2,1)S(1)}, bf16[128,128]{1,0:T(8,128)(2,1)S(1)}, u32[]{:S(2)}, u32[]{:S(2)}) collective-permute-start(bf16[128,128]{1,0:T(8,128)(2,1)S(1)} %get-tuple-element.126), channel_id=1, source_target_pairs={{0,2},{1,3},{2,4},{3,5},{4,6},{5,7},{6,8},{7,9},{8,10},{9,11},{10,... | collective-permute-start | bytes 98312 | tf_op jit(solution)/shard_map/ppermute | solution.py:365
  8.4 9.7 %collective-permute-start.32 = (bf16[128,128]{1,0:T(8,128)(2,1)S(1)}, bf16[128,128]{1,0:T(8,128)(2,1)S(1)}, u32[]{:S(2)}, u32[]{:S(2)}) collective-permute-start(bf16[128,128]{1,0:T(8,128)(2,1)S(1)} %get-tuple-element.127), channel_id=1, source_target_pairs={{0,3},{1,4},{2,5},{3,6},{4,7},{5,8},{6,9},{7,10},{8,11},{9,12},{10... | collective-permute-start | bytes 98312 | tf_op jit(solution)/shard_map/ppermute | solution.py:365
  10.9 7.6 %collective-permute-start.33 = (bf16[128,128]{1,0:T(8,128)(2,1)S(1)}, bf16[128,128]{1,0:T(8,128)(2,1)S(1)}, u32[]{:S(2)}, u32[]{:S(2)}) collective-permute-start(bf16[128,128]{1,0:T(8,128)(2,1)S(1)} %get-tuple-element.128), channel_id=1, source_target_pairs={{0,4},{1,5},{2,6},{3,7},{4,8},{5,9},{6,10},{7,11},{8,12},{9,13},{1... | collective-permute-start | bytes 98312 | tf_op jit(solution)/shard_map/ppermute | solution.py:365
  12.6 9.8 %collective-permute-start.35 = (bf16[128,128]{1,0:T(8,128)(2,1)S(1)}, bf16[128,128]{1,0:T(8,128)(2,1)S(1)}, u32[]{:S(2)}, u32[]{:S(2)}) collective-permute-start(bf16[128,128]{1,0:T(8,128)(2,1)S(1)} %get-tuple-element.130), channel_id=1, source_target_pairs={{0,6},{1,7},{2,8},{3,9},{4,10},{5,11},{6,12},{7,13},{8,14},{9,15},... | collective-permute-start | bytes 98312 | tf_op jit(solution)/shard_map/ppermute | solution.py:365
  13.8 10.6 %collective-permute-start.36 = (bf16[128,128]{1,0:T(8,128)(2,1)S(1)}, bf16[128,128]{1,0:T(8,128)(2,1)S(1)}, u32[]{:S(2)}, u32[]{:S(2)}) collective-permute-start(bf16[128,128]{1,0:T(8,128)(2,1)S(1)} %get-tuple-element.131), channel_id=1, source_target_pairs={{0,7},{1,8},{2,9},{3,10},{4,11},{5,12},{6,13},{7,14},{8,15},{9,0},... | collective-permute-start | bytes 98312 | tf_op jit(solution)/shard_map/ppermute | solution.py:365
  18.5 7.5 %collective-permute-start.38 = (bf16[128,128]{1,0:T(8,128)(2,1)S(1)}, bf16[128,128]{1,0:T(8,128)(2,1)S(1)}, u32[]{:S(2)}, u32[]{:S(2)}) collective-permute-start(bf16[128,128]{1,0:T(8,128)(2,1)S(1)} %get-tuple-element.133), channel_id=1, source_target_pairs={{0,9},{1,10},{2,11},{3,12},{4,13},{5,14},{6,15},{7,0},{8,1},{9,2},... | collective-permute-start | bytes 98312 | tf_op jit(solution)/shard_map/ppermute | solution.py:365
  26.0 7.7 %collective-permute-start.18 = (bf16[128,128]{1,0:T(8,128)(2,1)S(1)}, bf16[128,128]{1,0:T(8,128)(2,1)S(1)}, u32[]{:S(2)}, u32[]{:S(2)}) collective-permute-start(bf16[128,128]{1,0:T(8,128)(2,1)S(1)} %get-tuple-element.110), channel_id=1, source_target_pairs={{0,4},{1,5},{2,6},{3,7},{4,8},{5,9},{6,10},{7,11},{8,12},{9,13},{1... | collective-permute-start | bytes 98312 | tf_op jit(solution)/shard_map/ppermute | solution.py:365
  28.5 10.6 %collective-permute-start.20 = (bf16[128,128]{1,0:T(8,128)(2,1)S(1)}, bf16[128,128]{1,0:T(8,128)(2,1)S(1)}, u32[]{:S(2)}, u32[]{:S(2)}) collective-permute-start(bf16[128,128]{1,0:T(8,128)(2,1)S(1)} %get-tuple-element.112), channel_id=1, source_target_pairs={{0,6},{1,7},{2,8},{3,9},{4,10},{5,11},{6,12},{7,13},{8,14},{9,15},... | collective-permute-start | bytes 98312 | tf_op jit(solution)/shard_map/ppermute | solution.py:365
  31.3 9.3 %collective-permute-start.21 = (bf16[128,128]{1,0:T(8,128)(2,1)S(1)}, bf16[128,128]{1,0:T(8,128)(2,1)S(1)}, u32[]{:S(2)}, u32[]{:S(2)}) collective-permute-start(bf16[128,128]{1,0:T(8,128)(2,1)S(1)} %get-tuple-element.113), channel_id=1, source_target_pairs={{0,7},{1,8},{2,9},{3,10},{4,11},{5,12},{6,13},{7,14},{8,15},{9,0},... | collective-permute-start | bytes 98312 | tf_op jit(solution)/shard_map/ppermute | solution.py:365
  32.2 10.0 %collective-permute-start.22 = (bf16[128,128]{1,0:T(8,128)(2,1)S(1)}, bf16[128,128]{1,0:T(8,128)(2,1)S(1)}, u32[]{:S(2)}, u32[]{:S(2)}) collective-permute-start(bf16[128,128]{1,0:T(8,128)(2,1)S(1)} %get-tuple-element.114), channel_id=1, source_target_pairs={{0,8},{1,9},{2,10},{3,11},{4,12},{5,13},{6,14},{7,15},{8,0},{9,1},... | collective-permute-start | bytes 98312 | tf_op jit(solution)/shard_map/ppermute | solution.py:365
  33.6 9.0 %collective-permute-start.23 = (bf16[128,128]{1,0:T(8,128)(2,1)S(1)}, bf16[128,128]{1,0:T(8,128)(2,1)S(1)}, u32[]{:S(2)}, u32[]{:S(2)}) collective-permute-start(bf16[128,128]{1,0:T(8,128)(2,1)S(1)} %get-tuple-element.115), channel_id=1, source_target_pairs={{0,9},{1,10},{2,11},{3,12},{4,13},{5,14},{6,15},{7,0},{8,1},{9,2},... | collective-permute-start | bytes 98312 | tf_op jit(solution)/shard_map/ppermute | solution.py:365
  34.2 9.9 %collective-permute-start.24 = (bf16[128,128]{1,0:T(8,128)(2,1)S(1)}, bf16[128,128]{1,0:T(8,128)(2,1)S(1)}, u32[]{:S(2)}, u32[]{:S(2)}) collective-permute-start(bf16[128,128]{1,0:T(8,128)(2,1)S(1)} %get-tuple-element.116), channel_id=1, source_target_pairs={{0,10},{1,11},{2,12},{3,13},{4,14},{5,15},{6,0},{7,1},{8,2},{9,3},... | collective-permute-start | bytes 98312 | tf_op jit(solution)/shard_map/ppermute | solution.py:365
  42.2 7.6 %collective-permute-start.2 = (bf16[144,128]{1,0:T(8,128)(2,1)S(1)}, bf16[144,128]{1,0:T(8,128)(2,1)S(1)}, u32[]{:S(2)}, u32[]{:S(2)}) collective-permute-start(bf16[144,128]{1,0:T(8,128)(2,1)S(1)} %get-tuple-element.92), channel_id=1, source_target_pairs={{0,3},{1,4},{2,5},{3,6},{4,7},{5,8},{6,9},{7,10},{8,11},{9,12},{10... | collective-permute-start | bytes 110600 | tf_op jit(solution)/shard_map/ppermute | solution.py:365
  42.7 8.8 %collective-permute-start.3 = (bf16[144,128]{1,0:T(8,128)(2,1)S(1)}, bf16[144,128]{1,0:T(8,128)(2,1)S(1)}, u32[]{:S(2)}, u32[]{:S(2)}) collective-permute-start(bf16[144,128]{1,0:T(8,128)(2,1)S(1)} %get-tuple-element.93), channel_id=1, source_target_pairs={{0,4},{1,5},{2,6},{3,7},{4,8},{5,9},{6,10},{7,11},{8,12},{9,13},{1... | collective-permute-start | bytes 110600 | tf_op jit(solution)/shard_map/ppermute | solution.py:365
  45.2 7.6 %collective-permute-start.5 = (bf16[144,128]{1,0:T(8,128)(2,1)S(1)}, bf16[144,128]{1,0:T(8,128)(2,1)S(1)}, u32[]{:S(2)}, u32[]{:S(2)}) collective-permute-start(bf16[144,128]{1,0:T(8,128)(2,1)S(1)} %get-tuple-element.95), channel_id=1, source_target_pairs={{0,6},{1,7},{2,8},{3,9},{4,10},{5,11},{6,12},{7,13},{8,14},{9,15},... | collective-permute-start | bytes 110600 | tf_op jit(solution)/shard_map/ppermute | solution.py:365
  47.6 9.3 %collective-permute-start.6 = (bf16[144,128]{1,0:T(8,128)(2,1)S(1)}, bf16[144,128]{1,0:T(8,128)(2,1)S(1)}, u32[]{:S(2)}, u32[]{:S(2)}) collective-permute-start(bf16[144,128]{1,0:T(8,128)(2,1)S(1)} %get-tuple-element.96), channel_id=1, source_target_pairs={{0,7},{1,8},{2,9},{3,10},{4,11},{5,12},{6,13},{7,14},{8,15},{9,0},... | collective-permute-start | bytes 110600 | tf_op jit(solution)/shard_map/ppermute | solution.py:365
  51.5 8.6 %collective-permute-start.9 = (bf16[144,128]{1,0:T(8,128)(2,1)S(1)}, bf16[144,128]{1,0:T(8,128)(2,1)S(1)}, u32[]{:S(2)}, u32[]{:S(2)}) collective-permute-start(bf16[144,128]{1,0:T(8,128)(2,1)S(1)} %get-tuple-element.99), channel_id=1, source_target_pairs={{0,10},{1,11},{2,12},{3,13},{4,14},{5,15},{6,0},{7,1},{8,2},{9,3},... | collective-permute-start | bytes 110600 | tf_op jit(solution)/shard_map/ppermute | solution.py:365
  52.8 8.2 %collective-permute-start.10 = (bf16[144,128]{1,0:T(8,128)(2,1)}, bf16[144,128]{1,0:T(8,128)(2,1)S(1)}, u32[]{:S(2)}, u32[]{:S(2)}) collective-permute-start(bf16[144,128]{1,0:T(8,128)(2,1)} %get-tuple-element.100), channel_id=1, source_target_pairs={{0,11},{1,12},{2,13},{3,14},{4,15},{5,0},{6,1},{7,2},{8,3},{9,4},{... | collective-permute-start | bytes 110600 | tf_op jit(solution)/shard_map/ppermute | solution.py:365
  61.0 10.9 %collective-permute-start.25 = (bf16[128,128]{1,0:T(8,128)(2,1)}, bf16[128,128]{1,0:T(8,128)(2,1)S(1)}, u32[]{:S(2)}, u32[]{:S(2)}) collective-permute-start(bf16[128,128]{1,0:T(8,128)(2,1)} %copy-done.26), channel_id=1, source_target_pairs={{0,11},{1,12},{2,13},{3,14},{4,15},{5,0},{6,1},{7,2},{8,3},{9,4},{... | collective-permute-start | bytes 98312 | tf_op jit(solution)/shard_map/ppermute | solution.py:365
  62.4 10.1 %collective-permute-start.26 = (bf16[128,128]{1,0:T(8,128)(2,1)}, bf16[128,128]{1,0:T(8,128)(2,1)S(1)}, u32[]{:S(2)}, u32[]{:S(2)}) collective-permute-start(bf16[128,128]{1,0:T(8,128)(2,1)} %copy-done.25), channel_id=1, source_target_pairs={{0,12},{1,13},{2,14},{3,15},{4,0},{5,1},{6,2},{7,3},{8,4},{9,5},{1... | collective-permute-start | bytes 98312 | tf_op jit(solution)/shard_map/ppermute | solution.py:365
  63.2 10.8 %collective-permute-start.27 = (bf16[128,128]{1,0:T(8,128)(2,1)}, bf16[128,128]{1,0:T(8,128)(2,1)S(1)}, u32[]{:S(2)}, u32[]{:S(2)}) collective-permute-start(bf16[128,128]{1,0:T(8,128)(2,1)} %copy-done.24), channel_id=1, source_target_pairs={{0,13},{1,14},{2,15},{3,0},{4,1},{5,2},{6,3},{7,4},{8,5},{9,6},{10... | collective-permute-start | bytes 98312 | tf_op jit(solution)/shard_map/ppermute | solution.py:365
  64.2 10.8 %collective-permute-start.28 = (bf16[128,128]{1,0:T(8,128)(2,1)}, bf16[128,128]{1,0:T(8,128)(2,1)S(1)}, u32[]{:S(2)}, u32[]{:S(2)}) collective-permute-start(bf16[128,128]{1,0:T(8,128)(2,1)} %copy-done.23), channel_id=1, source_target_pairs={{0,14},{1,15},{2,0},{3,1},{4,2},{5,3},{6,4},{7,5},{8,6},{9,7},{10,... | collective-permute-start | bytes 98312 | tf_op jit(solution)/shard_map/ppermute | solution.py:365
  67.0 9.7 %collective-permute-start.29 = (bf16[128,128]{1,0:T(8,128)(2,1)}, bf16[128,128]{1,0:T(8,128)(2,1)}, u32[]{:S(2)}, u32[]{:S(2)}) collective-permute-start(bf16[128,128]{1,0:T(8,128)(2,1)} %copy-done.22), channel_id=1, source_target_pairs={{0,15},{1,0},{2,1},{3,2},{4,3},{5,4},{6,5},{7,6},{8,7},{9,8},{10,9... | collective-permute-start | bytes 98312 | tf_op jit(solution)/shard_map/ppermute | solution.py:365
  71.9 13.0 %collective-permute-start.40 = (bf16[128,128]{1,0:T(8,128)(2,1)S(1)}, bf16[128,128]{1,0:T(8,128)(2,1)S(1)}, u32[]{:S(2)}, u32[]{:S(2)}) collective-permute-start(bf16[128,128]{1,0:T(8,128)(2,1)S(1)} %copy-done.21), channel_id=1, source_target_pairs={{0,11},{1,12},{2,13},{3,14},{4,15},{5,0},{6,1},{7,2},{8,3},{9,4},{... | collective-permute-start | bytes 98312 | tf_op jit(solution)/shard_map/ppermute | solution.py:365
  72.5 12.4 %collective-permute-start.41 = (bf16[128,128]{1,0:T(8,128)(2,1)S(1)}, bf16[128,128]{1,0:T(8,128)(2,1)S(1)}, u32[]{:S(2)}, u32[]{:S(2)}) collective-permute-start(bf16[128,128]{1,0:T(8,128)(2,1)S(1)} %copy-done.19), channel_id=1, source_target_pairs={{0,12},{1,13},{2,14},{3,15},{4,0},{5,1},{6,2},{7,3},{8,4},{9,5},{1... | collective-permute-start | bytes 98312 | tf_op jit(solution)/shard_map/ppermute | solution.py:365
  74.0 10.8 %collective-permute-start.42 = (bf16[128,128]{1,0:T(8,128)(2,1)S(1)}, bf16[128,128]{1,0:T(8,128)(2,1)S(1)}, u32[]{:S(2)}, u32[]{:S(2)}) collective-permute-start(bf16[128,128]{1,0:T(8,128)(2,1)S(1)} %copy-done.17), channel_id=1, source_target_pairs={{0,13},{1,14},{2,15},{3,0},{4,1},{5,2},{6,3},{7,4},{8,5},{9,6},{10... | collective-permute-start | bytes 98312 | tf_op jit(solution)/shard_map/ppermute | solution.py:365
  75.1 9.8 %collective-permute-start.43 = (bf16[128,128]{1,0:T(8,128)(2,1)S(1)}, bf16[128,128]{1,0:T(8,128)(2,1)S(1)}, u32[]{:S(2)}, u32[]{:S(2)}) collective-permute-start(bf16[128,128]{1,0:T(8,128)(2,1)S(1)} %copy-done.15), channel_id=1, source_target_pairs={{0,14},{1,15},{2,0},{3,1},{4,2},{5,3},{6,4},{7,5},{8,6},{9,7},{10,... | collective-permute-start | bytes 98312 | tf_op jit(solution)/shard_map/ppermute | solution.py:365
  76.7 8.2 %collective-permute-start.44 = (bf16[128,128]{1,0:T(8,128)(2,1)S(1)}, bf16[128,128]{1,0:T(8,128)(2,1)S(1)}, u32[]{:S(2)}, u32[]{:S(2)}) collective-permute-start(bf16[128,128]{1,0:T(8,128)(2,1)S(1)} %copy-done.13), channel_id=1, source_target_pairs={{0,15},{1,0},{2,1},{3,2},{4,3},{5,4},{6,5},{7,6},{8,7},{9,8},{10,9... | collective-permute-start | bytes 98312 | tf_op jit(solution)/shard_map/ppermute | solution.py:365
  92.3 47.0 %collective-permute-start.75 = (bf16[128,1024]{1,0:T(8,128)(2,1)S(1)}, bf16[128,1024]{1,0:T(8,128)(2,1)S(1)}, u32[]{:S(2)}, u32[]{:S(2)}) collective-permute-start(bf16[128,1024]{1,0:T(8,128)(2,1)S(1)} %bitcast.14), channel_id=1, source_target_pairs={{0,16},{16,0},{1,17},{17,1},{2,18},{18,2},{3,19},{19,3},{4,20},{20... | collective-permute-start | bytes 786440 | tf_op jit(solution)/shard_map/ppermute | solution.py:443
  101.2 8.2 %collective-permute-start.52 = (bf16[128,128]{1,0:T(8,128)(2,1)S(1)}, bf16[128,128]{1,0:T(8,128)(2,1)S(1)}, u32[]{:S(2)}, u32[]{:S(2)}) collective-permute-start(bf16[128,128]{1,0:T(8,128)(2,1)S(1)} %get-tuple-element.148), channel_id=1, source_target_pairs={{0,8},{1,9},{2,10},{3,11},{4,12},{5,13},{6,14},{7,15},{8,0},{9,1},... | collective-permute-start | bytes 98312 | tf_op jit(solution)/shard_map/ppermute | solution.py:365
  103.5 7.4 %collective-permute-start.54 = (bf16[128,128]{1,0:T(8,128)(2,1)S(1)}, bf16[128,128]{1,0:T(8,128)(2,1)S(1)}, u32[]{:S(2)}, u32[]{:S(2)}) collective-permute-start(bf16[128,128]{1,0:T(8,128)(2,1)S(1)} %get-tuple-element.150), channel_id=1, source_target_pairs={{0,10},{1,11},{2,12},{3,13},{4,14},{5,15},{6,0},{7,1},{8,2},{9,3},... | collective-permute-start | bytes 98312 | tf_op jit(solution)/shard_map/ppermute | solution.py:365
  106.2 7.7 %collective-permute-start.55 = (bf16[128,128]{1,0:T(8,128)(2,1)S(1)}, bf16[128,128]{1,0:T(8,128)(2,1)S(1)}, u32[]{:S(2)}, u32[]{:S(2)}) collective-permute-start(bf16[128,128]{1,0:T(8,128)(2,1)S(1)} %get-tuple-element.151), channel_id=1, source_target_pairs={{0,11},{1,12},{2,13},{3,14},{4,15},{5,0},{6,1},{7,2},{8,3},{9,4},{... | collective-permute-start | bytes 98312 | tf_op jit(solution)/shard_map/ppermute | solution.py:365
  (71 other events, 677.2 us)

commit v4 on v2

--- a/solution.py
+++ b/solution.py
@@ -12,6 +12,7 @@
 NDOCS = 32
 ROWS = 16
 VMEM = pl.BlockSpec(memory_space=pltpu.VMEM)
+HBM = pl.BlockSpec(memory_space=pltpu.HBM)
 SMEM = pl.BlockSpec(memory_space=pltpu.SMEM)
 f32 = jnp.float32
 bf16 = jnp.bfloat16
@@ -30,6 +31,15 @@
     )
     behind = np.swapaxes(ahead, 1, 2) * (2.0 / size)
     return jnp.asarray(ahead, bf16), jnp.asarray(behind, bf16)
+
+
+def outer_tables(pieces):
+    m = np.arange(pieces)[:, None]
+    j = np.arange(pieces)[None, :]
+    angle = math.pi / (2 * pieces) * (j * (4 * m + 1) % (4 * pieces))
+    both = np.stack([np.cos(angle), -np.sin(angle)], axis=1).reshape(2 * pieces, pieces)
+    ahead = np.kron(both, np.eye(ROWS))
+    return jnp.asarray(ahead, bf16), jnp.asarray(ahead.T, bf16)
 
 
 def turned(value, turns):
@@ -70,15 +80,6 @@
     return first + second
 
 
-def outer_forward(reals):
-    count = len(reals)
-    values = [(reals[0], jnp.zeros_like(reals[0]))]
-    for j in range(1, count):
-        angle = -math.pi * j / (2 * count)
-        values.append((reals[j] * math.cos(angle), reals[j] * math.sin(angle)))
-    return dft(values, -1.0)
-
-
 def outer_inverse(values):
     count = len(values)
     out = []
@@ -121,21 +122,93 @@
     return place, tall
 
 
+def copies(*pairs):
+    started = [pltpu.make_async_copy(*pair) for pair in pairs]
+    for copy in started:
+        copy.start()
+    return started
+
+
+def finish(*started):
+    for copy in started:
+        copy.wait()
+
+
+def id_rows(doc_ref, lang_ref, tokens):
+    tile = lax.broadcasted_iota(jnp.int32, (ROWS, tokens), 0)
+    return jnp.where(tile == 0, doc_ref[...], lang_ref[...]).astype(f32).astype(bf16)
+
+
+def gated(grad_ref, gate_ref, part):
+    return (grad_ref[:, part].astype(f32) * gate_ref[:, part].astype(f32)).astype(bf16)
+
+
 def prep_kernel(pieces, span, input_ref, grad_ref, gate_ref, taps_ref, doc_ref, lang_ref, out_ref):
     tokens = grad_ref.shape[0]
     place, tall = places(pieces, tokens, span)
-    tile = lax.broadcasted_iota(jnp.int32, (ROWS, tokens), 0)
-    ids = jnp.where(tile == 0, doc_ref[...], lang_ref[...]).astype(f32).astype(bf16)
+    ids = id_rows(doc_ref, lang_ref, tokens)
     in_row, in_lanes = place(0, span)
     grad_row, grad_lanes = place(1, span)
     for i in range(pieces):
         part = slice(i * span, (i + 1) * span)
         out_ref[i, :span, :] = taps_ref[part, :]
         out_ref[i, in_row : in_row + tokens, in_lanes] = input_ref[:, part]
-        out_ref[i, grad_row : grad_row + tokens, grad_lanes] = (
-            grad_ref[:, part].astype(f32) * gate_ref[:, part].astype(f32)
-        ).astype(bf16)
+        out_ref[i, grad_row : grad_row + tokens, grad_lanes] = gated(grad_ref, gate_ref, part)
         out_ref[i, span + tall :, :] = ids
+
+
+def prep_copy_kernel(
+    pieces,
+    span,
+    input_ref,
+    grad_ref,
+    gate_ref,
+    taps_ref,
+    doc_ref,
+    lang_ref,
+    out_ref,
+    factor_ref,
+    made_ref,
+    ids_ref,
+    in_sem,
+    out_sem,
+    made_sem,
+):
+    tokens = grad_ref.shape[0]
+    place, tall = places(pieces, tokens, span)
+    row = [place(side, span)[0] for side in (0, 1)]
+    groups = in_sem.shape[1]
+    group = pieces // groups
+    loads = []
+    for g in range(groups):
+        wide = pl.ds(g * group * span, group * span)
+        loads.append(
+            copies(
+                (grad_ref.at[:, wide], factor_ref.at[0, :, wide], in_sem.at[0, g]),
+                (gate_ref.at[:, wide], factor_ref.at[1, :, wide], in_sem.at[1, g]),
+            )
+        )
+    sent = []
+    for i in range(pieces):
+        part = pl.ds(i * span, span)
+        sent += copies(
+            (input_ref.at[:, part], out_ref.at[i, pl.ds(row[0], tokens), :], out_sem.at[i])
+        )
+    sent += copies((taps_ref, out_ref.at[:, pl.ds(0, span), :], out_sem.at[pieces]))
+    ids = id_rows(doc_ref, lang_ref, tokens)
+    for i in range(pieces):
+        ids_ref[i] = ids
+    sent += copies((ids_ref, out_ref.at[:, pl.ds(span + tall, ROWS), :], out_sem.at[pieces + 1]))
+    for g in range(groups):
+        finish(*loads[g])
+        for i in range(g * group, (g + 1) * group):
+            part = slice(i * span, (i + 1) * span)
+            made_ref[i] = gated(factor_ref.at[0], factor_ref.at[1], part)
+        these = pl.ds(g * group, group)
+        sent += copies(
+            (made_ref.at[these], out_ref.at[these, pl.ds(row[1], tokens), :], made_sem.at[g])
+        )
+    finish(*sent)
 
 
 def token_scale(message_ref, scale_ref, dro_ref, ids, mean_len, doc_ref, lang_ref):
@@ -159,50 +232,72 @@
     message_ref,
     skip_ref,
     dro_ref,
+    ahead_hbm,
+    behind_hbm,
+    outer_hbm,
+    inverse_hbm,
+    out_hbm,
+    cross_hbm,
+    scale_ref,
     ahead_ref,
     behind_ref,
+    outer_ref,
+    inverse_ref,
     out_ref,
     cross_ref,
-    scale_ref,
+    scaled_ref,
     taps_mid_ref,
     mid_ref,
     back_ref,
     doc_ref,
     lang_ref,
+    in_sem,
+    out_sem,
 ):
     pieces = message_ref.shape[0]
     tokens = message_ref.shape[2]
     span = skip_ref.shape[1]
     place, tall = places(pieces, tokens, span)
+    outer_in, ahead_in, behind_in, inverse_in = copies(
+        (outer_hbm, outer_ref, in_sem.at[0]),
+        (ahead_hbm, ahead_ref, in_sem.at[1]),
+        (behind_hbm, behind_ref, in_sem.at[2]),
+        (inverse_hbm, inverse_ref, in_sem.at[3]),
+    )
     token_scale(message_ref, scale_ref, dro_ref, span + tall, mean_len, doc_ref, lang_ref)
+    outer_in.wait()
 
     def outer_taps(row):
         rows = pl.ds(row, ROWS)
-        out = outer_forward([message_ref[j, rows, :].astype(f32) for j in range(pieces)])
-        for m, (re, im) in enumerate(out):
-            taps_mid_ref[m, rows, :tokens] = re.astype(bf16)
-            taps_mid_ref[m, rows, tokens:] = im.astype(bf16)
+        stack = jnp.concatenate([message_ref[j, rows, :] for j in range(pieces)], axis=0)
+        out = dot(outer_ref[...], stack).astype(bf16)
+        for m in range(pieces):
+            at = 2 * m * ROWS
+            taps_mid_ref[m, rows, :tokens] = out[at : at + ROWS]
+            taps_mid_ref[m, rows, tokens:] = out[at + ROWS : at + 2 * ROWS]
 
     chunked(span, outer_taps)
+    sides = (slice(0, span), slice(span, 2 * span))
 
     def load(side, j, row):
         start, lanes = place(side, span)
-        value = message_ref[j, pl.ds(start + row, ROWS), lanes].astype(f32)
-        return value * scale_ref[pl.ds(row, ROWS), j : j + 1] if side else value
-
-    sides = (slice(0, span), slice(span, 2 * span))
-
-    def outer(side):
-        def body(row):
-            out = outer_forward([load(side, j, row) for j in range(pieces)])
-            for m, (re, im) in enumerate(out):
-                mid_ref[m, pl.ds(row, ROWS), sides[side]] = re.astype(bf16)
-                mid_ref[m, pl.ds(tokens + row, ROWS), sides[side]] = im.astype(bf16)
-
-        chunked(tokens, body)
-
-    outer(0)
-    outer(1)
+        return message_ref[j, pl.ds(start + row, ROWS), lanes]
+
+    def outer(row):
+        rows = pl.ds(row, ROWS)
+        stack = []
+        for j in range(pieces):
+            scaled = (load(1, j, row).astype(f32) * scale_ref[rows, j : j + 1]).astype(bf16)
+            scaled_ref[j, rows, :] = scaled
+            stack.append(jnp.concatenate([load(0, j, row), scaled], axis=1))
+        out = dot(outer_ref[...], jnp.concatenate(stack, axis=0)).astype(bf16)
+        for m in range(pieces):
+            at = 2 * m * ROWS
+            mid_ref[m, rows, :] = out[at : at + ROWS]
+            mid_ref[m, pl.ds(tokens + row, ROWS), :] = out[at + ROWS : at + 2 * ROWS]
+
+    chunked(tokens, outer)
+    finish(ahead_in, behind_in)
 
     def inner(m):
         filt = lax.dot_general(
@@ -217,33 +312,31 @@
         mixed = jnp.concatenate([fre * xre - fim * xim, fre * xim + fim * xre], axis=0)
         back = jnp.concatenate([fre * gre + fim * gim, fre * gim - fim * gre], axis=0)
         both = jnp.concatenate([mixed.astype(bf16), back.astype(bf16)], axis=1)
-        back_ref[m] = dot(behind_ref[m], both)
+        back_ref[m] = dot(behind_ref[m], both).astype(bf16)
 
     each_piece(pieces, inner)
+    (cross_out,) = copies((cross_ref, cross_hbm, out_sem.at[0]))
+    inverse_in.wait()
     skip = skip_ref[...]
 
-    def outer_back(side):
-        start, lanes = place(side, 0)
-
-        def body(row):
-            out = outer_inverse(
-                [
-                    (
-                        back_ref[m, pl.ds(row, ROWS), sides[side]],
-                        back_ref[m, pl.ds(tokens + row, ROWS), sides[side]],
-                    )
-                    for m in range(pieces)
-                ]
-            )
-            for j in range(pieces):
+    def outer_back(row):
+        rows = pl.ds(row, ROWS)
+        stack = []
+        for m in range(pieces):
+            stack += [back_ref[m, rows, :], back_ref[m, pl.ds(tokens + row, ROWS), :]]
+        out = dot(inverse_ref[...], jnp.concatenate(stack, axis=0))
+        for j in range(pieces):
+            at = slice(j * ROWS, (j + 1) * ROWS)
+            for side in (0, 1):
+                start, lanes = place(side, 0)
+                own = load(0, j, row) if side == 0 else scaled_ref[j, rows, :]
                 out_ref[j, pl.ds(start + row, ROWS), lanes] = (
-                    out[j] + skip * load(side, j, row)
+                    out[at, sides[side]] + skip * own.astype(f32)
                 ).astype(bf16)
 
-        chunked(tokens, body)
-
-    outer_back(0)
-    outer_back(1)
+    chunked(tokens, outer_back)
+    (out_out,) = copies((out_ref, out_hbm, out_sem.at[1]))
+    finish(cross_out, out_out)
 
 
 def lags_kernel(own_ref, cross_ref, behind_ref, keep_ref, send_ref, back_ref, lag_ref):
@@ -276,17 +369,46 @@
             send_ref[r - 1, :, part] = lag_ref[other * held + j].T.astype(bf16)
 
 
+def own_scale(own_ref, scale_ref):
+    lane = lax.broadcasted_iota(jnp.int32, scale_ref.shape, 1)
+    scale = jnp.where(lane == own_ref[0], scale_ref[...], jnp.zeros(scale_ref.shape, f32))
+    return jnp.sum(scale, axis=1, keepdims=True)
+
+
+def final_copy_kernel(
+    own_ref, grad_hbm, scale_ref, message_ref, gate_hbm, input_hbm, grad_ref, gate_ref, sem, out_sem
+):
+    pieces = message_ref.shape[0]
+    tokens, channels = grad_hbm.shape
+    span = channels // pieces
+    place, _ = places(pieces, tokens, span)
+    mixed_row, back_row = place(0, 0)[0], place(1, 0)[0]
+    (grad_in,) = copies((grad_hbm, grad_ref, sem.at[0]))
+    sent = []
+    for i in range(pieces):
+        part = pl.ds(i * span, span)
+        sent += copies(
+            (message_ref.at[i, pl.ds(back_row, tokens), :], input_hbm.at[:, part], out_sem.at[i])
+        )
+    scale = own_scale(own_ref, scale_ref)
+    grad_in.wait()
+    for i in range(pieces):
+        part = slice(i * span, (i + 1) * span)
+        mixed = message_ref[i, mixed_row : mixed_row + tokens, :].astype(f32)
+        gate_ref[:, part] = (grad_ref[:, part].astype(f32) * scale * mixed).astype(bf16)
+        if (2 * (i + 1)) % pieces == 0:
+            half = (2 * (i + 1)) // pieces - 1
+            wide = pl.ds(half * (channels // 2), channels // 2)
+            sent += copies((gate_ref.at[:, wide], gate_hbm.at[:, wide], sem.at[1 + half]))
+    finish(*sent)
+
+
 def final_kernel(own_ref, grad_ref, scale_ref, message_ref, gate_ref, input_ref):
     pieces = message_ref.shape[0]
     tokens, channels = grad_ref.shape
     span = channels // pieces
     place, _ = places(pieces, tokens, span)
-    lane = lax.broadcasted_iota(jnp.int32, (tokens, pieces), 1)
-    scale = jnp.sum(
-        jnp.where(lane == own_ref[0], scale_ref[...], jnp.zeros((tokens, pieces), f32)),
-        axis=1,
-        keepdims=True,
-    )
+    scale = own_scale(own_ref, scale_ref)
     mixed_row, mixed_lanes = place(0, 0)
     back_row, back_lanes = place(1, 0)
     for i in range(pieces):
@@ -296,12 +418,12 @@
         input_ref[:, part] = message_ref[i, back_row : back_row + tokens, back_lanes]
 
 
-def call(kernel, out, ins, scratch=(), limit=24, cost=(0, 0)):
+def call(kernel, out, ins, scratch=(), outs=None, limit=24, cost=(0, 0)):
     return pl.pallas_call(
         kernel,
         out_shape=out,
         in_specs=ins,
-        out_specs=jax.tree.map(lambda _: VMEM, out),
+        out_specs=jax.tree.map(lambda _: VMEM, out) if outs is None else outs,
         scratch_shapes=scratch,
         compiler_params=pltpu.CompilerParams(vmem_limit_bytes=limit << 20),
         cost_estimate=pl.CostEstimate(flops=cost[0], bytes_accessed=cost[1], transcendentals=0),
@@ -318,6 +440,7 @@
     mean_len = length / NDOCS
     own = lax.axis_index("ctx")
     ahead, behind = inner_tables(pieces, tokens)
+    outer, inverse = outer_tables(pieces)
     skip = lax.dynamic_slice_in_dim(skip_gain, own * span, span)[None, :]
     exchange = functools.partial(
         lax.all_to_all, axis_name="ctx", split_axis=0, concat_axis=0, tiled=True
@@ -325,12 +448,33 @@
     tall = places(pieces, tokens, span)[1]
     macs = pieces * (2 * tokens) ** 2 * span
 
+    aligned = span % 128 == 0
+    dma = pltpu.SemaphoreType.DMA
+    groups = 4
     message = call(
-        functools.partial(prep_kernel, pieces, span),
+        functools.partial(prep_copy_kernel if aligned else prep_kernel, pieces, span),
         jax.ShapeDtypeStruct((pieces, span + tall + ROWS, tokens), bf16),
-        [VMEM] * 6,
+        [HBM] * 4 + [VMEM] * 2 if aligned else [VMEM] * 6,
+        [
+            pltpu.VMEM((2, tokens, channels), bf16),
+            pltpu.VMEM((pieces, tokens, span), bf16),
+            pltpu.VMEM((pieces, ROWS, tokens), bf16),
+            dma((2, groups)),
+            dma((pieces + 2,)),
+            dma((groups,)),
+        ]
+        if aligned
+        else (),
+        outs=HBM if aligned else VMEM,
         cost=(0, 4 << 20),
-    )(saved_input[0], grad_out[0], gate_value[0], filter_taps, doc_ids, lang_ids)
+    )(
+        saved_input[0],
+        grad_out[0],
+        gate_value[0],
+        filter_taps.reshape(pieces, span, tokens) if aligned else filter_taps,
+        doc_ids,
+        lang_ids,
+    )
     message = exchange(message)
     message, cross, scale = call(
         functools.partial(conv_kernel, mean_len),
@@ -339,16 +483,27 @@
             jax.ShapeDtypeStruct((pieces, 2 * tokens, span), bf16),
             jax.ShapeDtypeStruct((tokens, pieces), f32),
         ),
-        [VMEM, VMEM, SMEM, VMEM, VMEM],
+        [VMEM, VMEM, SMEM, HBM, HBM, HBM, HBM],
         [
+            pltpu.VMEM(ahead.shape, bf16),
+            pltpu.VMEM(behind.shape, bf16),
+            pltpu.VMEM(outer.shape, bf16),
+            pltpu.VMEM(inverse.shape, bf16),
+            pltpu.VMEM((pieces, tall, tokens), bf16),
+            pltpu.VMEM((pieces, 2 * tokens, span), bf16),
+            pltpu.VMEM((pieces, tokens, span), bf16),
             pltpu.VMEM((pieces, span, 2 * tokens), bf16),
             pltpu.VMEM((pieces, 2 * tokens, 2 * span), bf16),
-            pltpu.VMEM((pieces, 2 * tokens, 2 * span), f32),
+            pltpu.VMEM((pieces, 2 * tokens, 2 * span), bf16),
             pltpu.VMEM((pieces, tokens), f32),
             pltpu.VMEM((pieces, tokens), f32),
+            dma((4,)),
+            dma((2,)),
         ],
+        outs=(HBM, HBM, VMEM),
+        limit=32,
         cost=(10 * macs, 8 << 20),
-    )(message, skip, dro_weight, ahead, behind)
+    )(message, skip, dro_weight, ahead, behind, outer, inverse)
     message = exchange(message)
     keep, send = call(
         lags_kernel,
@@ -369,9 +524,18 @@
         d_filter = d_filter + lax.ppermute(send[r - 1], "dp", ring).astype(f32)
     token_block = jax.ShapeDtypeStruct((tokens, channels), bf16)
     d_gate, d_input = call(
-        final_kernel,
+        final_copy_kernel if aligned else final_kernel,
         (token_block, token_block),
-        [SMEM, VMEM, VMEM, VMEM],
+        [SMEM, HBM if aligned else VMEM, VMEM, VMEM],
+        [
+            pltpu.VMEM((tokens, channels), bf16),
+            pltpu.VMEM((tokens, channels), bf16),
+            dma((3,)),
+            dma((pieces,)),
+        ]
+        if aligned
+        else (),
+        outs=(HBM, HBM) if aligned else (VMEM, VMEM),
         cost=(0, 4 << 20),
     )(own.reshape(1), grad_out[0], scale, message)
     return (d_input[None], d_gate[None], d_filter)

time: 99.4 us -> 103 us (1.036)
  Pallas kernels: 14.8 us -> 18 us
    pallas_call x1, Pallas kernels: 11.2 us -> 13.7 us  [local(): call(functools.partial(conv_kernel, mean_len), (jax.ShapeDtypeStruct((pie...]
    unnamed x30 -> x34, local copies, waits for them, and re-layouts: 12.5 us -> 12.5 us
where the time goes in v4:
time: 103 us; the launch traced here: 101 us
  waiting for transfers between devices  50.3 us (49%)
  starting transfers between devices  18.6 us (18%)
  Pallas kernels  18 us (17%)
  local copies, waits for them, and re-layouts  12.5 us (12%)
    all_to_all x2, waiting for transfers between devices, local(): message = exchange(message)  43.2 us
    all_to_all x2, starting transfers between devices, local(): message = exchange(message)  17.1 us
    pallas_call x1, Pallas kernels, local(): call(functools.partial(conv_kernel, mean_len), (jax.ShapeDtypeStruct((pie...  13.7 us
    unnamed x34, local copies, waits for them, and re-layouts  12.5 us
    ppermute x1, waiting for transfers between devices, local(): d_filter = d_filter + lax.ppermute(send[r - 1], 'dp', ring).astype(f32)  7.15 us
  transfers between devices with their start and end apart: 3, of which 3 were waited for; matrix products, arithmetic and copies ran while one was open for 1% of the time, Pallas kernels for 2%

profile of v4, /device:TPU:0, one launch (start us, length us, event | category | flops | bytes accessed | tf_op | source)
XLA Modules:
  0.0 101.1 jit_solution(4590359607499825920)
XLA Ops:
  0.6 0.0 copy-start
  0.6 0.0 copy-start.4
  0.7 1.0 %copy-done.4 = bf16[1,128,2048]{2,1,0:T(8,128)(2,1)S(1)} copy-done((bf16[1,128,2048]{2,1,0:T(8,128)(2,1)S(1)}, bf16[1,128,2048]{2,1,0:T(8,128)(2,1)}, u32[]{:S(2)}) %copy-start.4) | copy-done | bytes 524312
  1.7 1.0 %copy-done.9 = bf16[1,128,2048]{2,1,0:T(8,128)(2,1)S(1)} copy-done((bf16[1,128,2048]{2,1,0:T(8,128)(2,1)S(1)}, bf16[1,128,2048]{2,1,0:T(8,128)(2,1)}, u32[]{:S(2)}) %copy-start.9) | copy-done | bytes 524312
  2.7 1.0 %copy-done.10 = bf16[1,128,2048]{2,1,0:T(8,128)(2,1)S(1)} copy-done((bf16[1,128,2048]{2,1,0:T(8,128)(2,1)S(1)}, bf16[1,128,2048]{2,1,0:T(8,128)(2,1)}, u32[]{:S(2)}) %copy-start.10) | copy-done | bytes 524312
  3.8 1.0 %copy-done.11 = bf16[2048,128]{1,0:T(8,128)(2,1)S(1)} copy-done((bf16[2048,128]{1,0:T(8,128)(2,1)S(1)}, bf16[2048,128]{1,0:T(8,128)(2,1)}, u32[]{:S(2)}) %copy-start.11) | copy-done | bytes 524312
  4.8 0.7 copy-done.14
  5.5 0.7 copy-done.15
  6.1 1.1 %shard_map.139 = bf16[16,400,128]{2,1,0:T(8,128)(2,1)S(1)} custom-call(bf16[128,2048]{1,0:T(8,128)(2,1)S(1)} %bitcast.13, bf16[128,2048]{1,0:T(8,128)(2,1)S(1)} %bitcast.11, bf16[128,2048]{1,0:T(8,128)(2,1)S(1)} %bitcast.14, bf16[16,128,128]{2,1,0:T(8,128)(2,1)S(1)} %bitcast.15, s32[1,128]{1,0:T(1,128)S(1)} %copy-done.14, s32[1,128]{1,0:T(1,128)S(1)} %copy-done.15), custom_call_target="tpu_custom_call" | custom-call | bytes 4194304 | tf_op jit(solution)/shard_map/pallas_call | solution.py:454
  7.2 0.0 copy-start.2
  7.2 1.2 %copy-done.2 = bf16[16,400,128]{2,1,0:T(8,128)(2,1)} copy-done((bf16[16,400,128]{2,1,0:T(8,128)(2,1)}, bf16[16,400,128]{2,1,0:T(8,128)(2,1)S(1)}, u32[]{:S(2)}) %copy-start.2) | copy-done | bytes 1638424
  8.4 7.7 %all-to-all-start = ((bf16[16,400,128]{2,1,0:T(8,128)(2,1)}), bf16[16,400,128]{2,1,0:T(8,128)(2,1)}, u32[]{:S(2)}, u32[]{:S(2)}) async-start(bf16[16,400,128]{2,1,0:T(8,128)(2,1)} %copy-done.2), calls=%async_computation | async-start | bytes 3276800 | tf_op jit(solution)/shard_map/all_to_all | solution.py:478
  16.1 0.0 copy-done
  16.1 0.1 dynamic-slice_bitcast_fusion.skip_ref
  16.2 33.1 %all-to-all-done.message_ref = bf16[16,400,128]{2,1,0:T(8,128)(2,1)} async-done(((bf16[16,400,128]{2,1,0:T(8,128)(2,1)}), bf16[16,400,128]{2,1,0:T(8,128)(2,1)}, u32[]{:S(2)}, u32[]{:S(2)}) %all-to-all-start) | async-done | bytes 1638432 | tf_op jit(solution)/shard_map/all_to_all | solution.py:478
  49.3 0.0 copy-done.1
  49.3 0.0 copy-done.12
  49.3 0.0 copy-done.13
  49.3 0.0 copy-start.3
  49.3 1.6 %copy-done.3 = bf16[16,256,256]{2,1,0:T(8,128)(2,1)S(1)} copy-done((bf16[16,256,256]{2,1,0:T(8,128)(2,1)S(1)}, bf16[16,256,256]{2,1,0:T(8,128)(2,1)}, u32[]{:S(2)}) %copy-start.3) | copy-done | bytes 2097176
  50.9 13.7 %shard_map.140 = (bf16[16,256,128]{2,1,0:T(8,128)(2,1)S(1)}, bf16[16,256,128]{2,1,0:T(8,128)(2,1)S(1)}, f32[128,16]{1,0:T(8,128)S(1)}) custom-call(bf16[16,400,128]{2,1,0:T(8,128)(2,1)} %all-to-all-done.message_ref, f32[1,128]{1,0:T(1,128)S(1)} %dynamic-slice_bitcast_fusion.skip_ref, f32[16]{0:T(128)S(1)} %copy-done.16, bf16[16,256,256]{2,1,0:T(8,128)(2,1)S(1)} %copy-done.3, ...), custom_call_target="tpu_custom_call" | custom-call | flops 1342177280 | bytes 8388608 | tf_op jit(solution)/shard_map/pallas_call | solution.py:479
  64.6 1.0 copy-done.6
  65.6 1.0 copy-done.7
  66.6 9.4 %all-to-all-start.1 = ((bf16[16,256,128]{2,1,0:T(8,128)(2,1)}), bf16[16,256,128]{2,1,0:T(8,128)(2,1)S(1)}, u32[]{:S(2)}, u32[]{:S(2)}) async-start(bf16[16,256,128]{2,1,0:T(8,128)(2,1)} %copy-done.6), calls=%async_computation.1 | async-start | bytes 2097152 | tf_op jit(solution)/shard_map/all_to_all | solution.py:507
  76.0 1.2 %copy-done.8 = bf16[16,256,128]{2,1,0:T(8,128)(2,1)S(1)} copy-done((bf16[16,256,128]{2,1,0:T(8,128)(2,1)S(1)}, bf16[16,256,128]{2,1,0:T(8,128)(2,1)}, u32[]{:S(2)}) %copy-start.8) | copy-done | bytes 1048600
  77.2 2.1 %shard_map.142 = (f32[128,1024]{1,0:T(8,128)S(1)}, bf16[1,128,1024]{2,1,0:T(8,128)(2,1)S(1)}) custom-call(s32[1]{0:T(128)} %bitcast.8.own_ref, bf16[16,256,128]{2,1,0:T(8,128)(2,1)S(1)} %copy-done.8, bf16[16,256,256]{2,1,0:T(8,128)(2,1)S(1)} %copy-done.1), custom_call_target="tpu_custom_call" | custom-call | flops 268435456 | bytes 6291456 | tf_op jit(solution)/shard_map/pallas_call | solution.py:508
  79.2 1.6 %collective-permute-start = (bf16[128,1024]{1,0:T(8,128)(2,1)S(1)}, bf16[128,1024]{1,0:T(8,128)(2,1)S(1)}, u32[]{:S(2)}, u32[]{:S(2)}) collective-permute-start(bf16[128,1024]{1,0:T(8,128)(2,1)S(1)} %bitcast.16), channel_id=1, source_target_pairs={{0,16},{16,0},{1,17},{17,1},{2,18},{18,2},{3,19},{19,3},{4,20},{20... | collective-permute-start | bytes 786440 | tf_op jit(solution)/shard_map/ppermute | solution.py:524
  80.8 7.2 %collective-permute-done = bf16[128,1024]{1,0:T(8,128)(2,1)S(1)} collective-permute-done((bf16[128,1024]{1,0:T(8,128)(2,1)S(1)}, bf16[128,1024]{1,0:T(8,128)(2,1)S(1)}, u32[]{:S(2)}, u32[]{:S(2)}) %collective-permute-start) | collective-permute-done | bytes 262176 | tf_op jit(solution)/shard_map/ppermute | solution.py:524
  88.0 0.9 convert_add_fusion
  88.8 10.1 %all-to-all-done.1.message_ref = bf16[16,256,128]{2,1,0:T(8,128)(2,1)S(1)} async-done(((bf16[16,256,128]{2,1,0:T(8,128)(2,1)}), bf16[16,256,128]{2,1,0:T(8,128)(2,1)S(1)}, u32[]{:S(2)}, u32[]{:S(2)}) %all-to-all-start.1) | async-done | bytes 1048608 | tf_op jit(solution)/shard_map/all_to_all | solution.py:507
  98.9 1.0 %copy-done.5 = bf16[1,128,2048]{2,1,0:T(8,128)(2,1)S(1)} copy-done((bf16[1,128,2048]{2,1,0:T(8,128)(2,1)S(1)}, bf16[1,128,2048]{2,1,0:T(8,128)(2,1)}, u32[]{:S(2)}) %copy-start.5) | copy-done | bytes 524312
  99.9 1.2 %shard_map.141 = (bf16[128,2048]{1,0:T(8,128)(2,1)}, bf16[128,2048]{1,0:T(8,128)(2,1)}) custom-call(s32[1]{0:T(128)} %bitcast.own_ref, bf16[128,2048]{1,0:T(8,128)(2,1)S(1)} %bitcast.12, f32[128,16]{1,0:T(8,128)S(1)} %get-tuple-element.10.scale_ref, bf16[16,256,128]{2,1,0:T(8,128)(2,1)S(1)} %all-to-all-done.1.message_ref), custom_call_target="tpu_custom_call" | custom-call | bytes 4194304 | tf_op jit(solution)/shard_map/pallas_call | solution.py:526
  (14 shorter events, 0.0 us)
Async XLA Ops:
  0.6 15.5 %copy-start = (f32[2048]{0:T(1024)S(1)}, f32[2048]{0:T(1024)}, u32[]{:S(2)}) copy-start(f32[2048]{0:T(1024)} %param.16) | copy-start | bytes 24580
  0.6 1.0 %copy-start.4 = (bf16[1,128,2048]{2,1,0:T(8,128)(2,1)S(1)}, bf16[1,128,2048]{2,1,0:T(8,128)(2,1)}, u32[]{:S(2)}) copy-start(bf16[1,128,2048]{2,1,0:T(8,128)(2,1)} %param.12) | copy-start | bytes 1572868
  1.7 1.0 %copy-start.9 = (bf16[1,128,2048]{2,1,0:T(8,128)(2,1)S(1)}, bf16[1,128,2048]{2,1,0:T(8,128)(2,1)}, u32[]{:S(2)}) copy-start(bf16[1,128,2048]{2,1,0:T(8,128)(2,1)} %param.13) | copy-start | bytes 1572868
  2.7 1.0 %copy-start.10 = (bf16[1,128,2048]{2,1,0:T(8,128)(2,1)S(1)}, bf16[1,128,2048]{2,1,0:T(8,128)(2,1)}, u32[]{:S(2)}) copy-start(bf16[1,128,2048]{2,1,0:T(8,128)(2,1)} %param.14) | copy-start | bytes 1572868
  3.8 1.0 %copy-start.11 = (bf16[2048,128]{1,0:T(8,128)(2,1)S(1)}, bf16[2048,128]{1,0:T(8,128)(2,1)}, u32[]{:S(2)}) copy-start(bf16[2048,128]{1,0:T(8,128)(2,1)} %param.15) | copy-start | bytes 1572868
  4.8 0.7 copy-start.14
  5.5 0.7 copy-start.15
  7.2 1.2 %copy-start.2 = (bf16[16,400,128]{2,1,0:T(8,128)(2,1)}, bf16[16,400,128]{2,1,0:T(8,128)(2,1)S(1)}, u32[]{:S(2)}) copy-start(bf16[16,400,128]{2,1,0:T(8,128)(2,1)S(1)} %shard_map.139) | copy-start | bytes 4915204
  8.4 40.9 %copy-start.1 = (bf16[16,256,256]{2,1,0:T(8,128)(2,1)S(1)}, bf16[16,256,256]{2,1,0:T(8,128)(2,1)}, u32[]{:S(2)}) copy-start(bf16[16,256,256]{2,1,0:T(8,128)(2,1)} %constant.24.clone.behind_hbm.behind_ref) | copy-start | bytes 6291460
  8.4 40.9 %copy-start.12 = (bf16[256,512]{1,0:T(8,128)(2,1)S(1)}, bf16[256,512]{1,0:T(8,128)(2,1)}, u32[]{:S(2)}) copy-start(bf16[256,512]{1,0:T(8,128)(2,1)} %constant.26.clone.inverse_hbm) | copy-start | bytes 786436
  8.4 40.9 %copy-start.13 = (bf16[512,256]{1,0:T(8,128)(2,1)S(1)}, bf16[512,256]{1,0:T(8,128)(2,1)}, u32[]{:S(2)}) copy-start(bf16[512,256]{1,0:T(8,128)(2,1)} %constant.25.clone.outer_hbm) | copy-start | bytes 786436
  8.4 40.9 %copy-start.16 = (f32[16]{0:T(128)S(1)}, f32[16]{0:T(128)}, u32[]{:S(2)}) copy-start(f32[16]{0:T(128)} %dro_ref.1) | copy-start | bytes 196
  8.4 40.9 %all-to-all-start = ((bf16[16,400,128]{2,1,0:T(8,128)(2,1)}), bf16[16,400,128]{2,1,0:T(8,128)(2,1)}, u32[]{:S(2)}, u32[]{:S(2)}) async-start(bf16[16,400,128]{2,1,0:T(8,128)(2,1)} %copy-done.2), calls=%async_computation | async-start | bytes 3276800 | tf_op jit(solution)/shard_map/all_to_all | solution.py:478
  49.3 1.6 %copy-start.3 = (bf16[16,256,256]{2,1,0:T(8,128)(2,1)S(1)}, bf16[16,256,256]{2,1,0:T(8,128)(2,1)}, u32[]{:S(2)}) copy-start(bf16[16,256,256]{2,1,0:T(8,128)(2,1)} %constant.23.clone.ahead_hbm) | copy-start | bytes 6291460
  64.6 1.0 copy-start.6
  65.6 1.0 copy-start.7
  66.6 32.3 %all-to-all-start.1 = ((bf16[16,256,128]{2,1,0:T(8,128)(2,1)}), bf16[16,256,128]{2,1,0:T(8,128)(2,1)S(1)}, u32[]{:S(2)}, u32[]{:S(2)}) async-start(bf16[16,256,128]{2,1,0:T(8,128)(2,1)} %copy-done.6), calls=%async_computation.1 | async-start | bytes 2097152 | tf_op jit(solution)/shard_map/all_to_all | solution.py:507
  76.0 1.2 %copy-start.8 = (bf16[16,256,128]{2,1,0:T(8,128)(2,1)S(1)}, bf16[16,256,128]{2,1,0:T(8,128)(2,1)}, u32[]{:S(2)}) copy-start(bf16[16,256,128]{2,1,0:T(8,128)(2,1)} %copy-done.7) | copy-start | bytes 3145732
  79.2 8.7 %collective-permute-start = (bf16[128,1024]{1,0:T(8,128)(2,1)S(1)}, bf16[128,1024]{1,0:T(8,128)(2,1)S(1)}, u32[]{:S(2)}, u32[]{:S(2)}) collective-permute-start(bf16[128,1024]{1,0:T(8,128)(2,1)S(1)} %bitcast.16), channel_id=1, source_target_pairs={{0,16},{16,0},{1,17},{17,1},{2,18},{18,2},{3,19},{19,3},{4,20},{20... | collective-permute-start | bytes 786440 | tf_op jit(solution)/shard_map/ppermute | solution.py:524
  98.9 1.0 %copy-start.5 = (bf16[1,128,2048]{2,1,0:T(8,128)(2,1)S(1)}, bf16[1,128,2048]{2,1,0:T(8,128)(2,1)}, u32[]{:S(2)}) copy-start(bf16[1,128,2048]{2,1,0:T(8,128)(2,1)} %param.12) | copy-start | bytes 1572868

commit v5 on v4

--- a/solution.py
+++ b/solution.py
@@ -89,7 +89,12 @@
     return out
 
 
-def chunked(total, body):
+def chunked(total, body, unrolled=False):
+    if unrolled:
+        for i in range(total // ROWS):
+            body(i * ROWS)
+        return
+
     def step(i, carry):
         body(pl.multiple_of(i * ROWS, ROWS))
         return carry
@@ -276,7 +281,7 @@
             taps_mid_ref[m, rows, :tokens] = out[at : at + ROWS]
             taps_mid_ref[m, rows, tokens:] = out[at + ROWS : at + 2 * ROWS]
 
-    chunked(span, outer_taps)
+    chunked(span, outer_taps, True)
     sides = (slice(0, span), slice(span, 2 * span))
 
     def load(side, j, row):
@@ -296,7 +301,7 @@
             mid_ref[m, rows, :] = out[at : at + ROWS]
             mid_ref[m, pl.ds(tokens + row, ROWS), :] = out[at + ROWS : at + 2 * ROWS]
 
-    chunked(tokens, outer)
+    chunked(tokens, outer, True)
     finish(ahead_in, behind_in)
 
     def inner(m):
@@ -314,7 +319,7 @@
         both = jnp.concatenate([mixed.astype(bf16), back.astype(bf16)], axis=1)
         back_ref[m] = dot(behind_ref[m], both).astype(bf16)
 
-    each_piece(pieces, inner)
+    each_piece(pieces, inner, 8)
     (cross_out,) = copies((cross_ref, cross_hbm, out_sem.at[0]))
     inverse_in.wait()
     skip = skip_ref[...]
@@ -334,7 +339,7 @@
                     out[at, sides[side]] + skip * own.astype(f32)
                 ).astype(bf16)
 
-    chunked(tokens, outer_back)
+    chunked(tokens, outer_back, True)
     (out_out,) = copies((out_ref, out_hbm, out_sem.at[1]))
     finish(cross_out, out_out)
 
@@ -418,14 +423,14 @@
         input_ref[:, part] = message_ref[i, back_row : back_row + tokens, back_lanes]
 
 
-def call(kernel, out, ins, scratch=(), outs=None, limit=24, cost=(0, 0)):
+def call(kernel, out, ins, scratch=(), outs=None, room=40 << 20, cost=(0, 0)):
     return pl.pallas_call(
         kernel,
         out_shape=out,
         in_specs=ins,
         out_specs=jax.tree.map(lambda _: VMEM, out) if outs is None else outs,
         scratch_shapes=scratch,
-        compiler_params=pltpu.CompilerParams(vmem_limit_bytes=limit << 20),
+        compiler_params=pltpu.CompilerParams(vmem_limit_bytes=(64 << 20) - room),
         cost_estimate=pl.CostEstimate(flops=cost[0], bytes_accessed=cost[1], transcendentals=0),
     )
 
@@ -466,6 +471,7 @@
         if aligned
         else (),
         outs=HBM if aligned else VMEM,
+        room=(256 << 10) if aligned else (40 << 20),
         cost=(0, 4 << 20),
     )(
         saved_input[0],
@@ -501,7 +507,7 @@
             dma((2,)),
         ],
         outs=(HBM, HBM, VMEM),
-        limit=32,
+        room=(2 << 20) if aligned else (16 << 20),
         cost=(10 * macs, 8 << 20),
     )(message, skip, dro_weight, ahead, behind, outer, inverse)
     message = exchange(message)
@@ -536,6 +542,7 @@
         if aligned
         else (),
         outs=(HBM, HBM) if aligned else (VMEM, VMEM),
+        room=(5 << 18) if aligned else (40 << 20),
         cost=(0, 4 << 20),
     )(own.reshape(1), grad_out[0], scale, message)
     return (d_input[None], d_gate[None], d_filter)

time: 103 us -> 126 us (1.22)
  Pallas kernels: 18 us -> 50.5 us
  local copies, waits for them, and re-layouts: 12.5 us -> 4 us
    pallas_call x1, Pallas kernels: 1.06 us -> 33.8 us  [local(): call(functools.partial(prep_copy_kernel if aligned else prep_kernel, piec...]
    unnamed x34 -> x10, local copies, waits for them, and re-layouts: 12.5 us -> 3.41 us
    pallas_call x1, Pallas kernels: 13.7 us -> 11.1 us  [local(): call(functools.partial(conv_kernel, mean_len), (jax.ShapeDtypeStruct((pie...]
    pallas_call x1, Pallas kernels: 1.18 us -> 3.55 us  [local(): call(final_copy_kernel if aligned else final_kernel, (token_block, token_...]
where the time goes in v5:
time: 126 us; the launch traced here: 124 us
  Pallas kernels  50.5 us (40%)
  waiting for transfers between devices  49.7 us (39%)
  starting transfers between devices  18.5 us (15%)
  local copies, waits for them, and re-layouts  4 us (3%)
    all_to_all x2, waiting for transfers between devices, local(): message = exchange(message)  42.6 us
    pallas_call x1, Pallas kernels, local(): call(functools.partial(prep_copy_kernel if aligned else prep_kernel, piec...  33.8 us
    all_to_all x2, starting transfers between devices, local(): message = exchange(message)  16.9 us
    pallas_call x1, Pallas kernels, local(): call(functools.partial(conv_kernel, mean_len), (jax.ShapeDtypeStruct((pie...  11.1 us
    ppermute x1, waiting for transfers between devices, local(): d_filter = d_filter + lax.ppermute(send[r - 1], 'dp', ring).astype(f32)  7.15 us
    pallas_call x1, Pallas kernels, local(): call(final_copy_kernel if aligned else final_kernel, (token_block, token_...  3.55 us
    unnamed x10, local copies, waits for them, and re-layouts  3.41 us
  transfers between devices with their start and end apart: 3, of which 3 were waited for; matrix products, arithmetic and copies ran while one was open for 1% of the time, Pallas kernels for 2%

profile of v5, /device:TPU:0, one launch (start us, length us, event | category | flops | bytes accessed | tf_op | source)
XLA Modules:
  0.0 124.3 jit_solution(9615670319098139415)
XLA Ops:
  0.6 0.0 copy-start
  0.6 33.8 %shard_map.139 = bf16[16,400,128]{2,1,0:T(8,128)(2,1)} custom-call(bf16[128,2048]{1,0:T(8,128)(2,1)} %bitcast.14, bf16[128,2048]{1,0:T(8,128)(2,1)} %bitcast.12, bf16[128,2048]{1,0:T(8,128)(2,1)} %bitcast.15, bf16[16,128,128]{2,1,0:T(8,128)(2,1)} %bitcast.16, s32[1,128]{1,0:T(1,128)} %doc_ref.1, s32[1,128]{1,0:T(1,128)} %lang_ref.1), custom_call_target="tpu_custom_call" | custom-call | bytes 4194304 | tf_op jit(solution)/shard_map/pallas_call | solution.py:459
  34.5 7.4 %all-to-all-start = ((bf16[16,400,128]{2,1,0:T(8,128)(2,1)}), bf16[16,400,128]{2,1,0:T(8,128)(2,1)S(1)}, u32[]{:S(2)}, u32[]{:S(2)}) async-start(bf16[16,400,128]{2,1,0:T(8,128)(2,1)} %shard_map.139), calls=%async_computation | async-start | bytes 3276800 | tf_op jit(solution)/shard_map/all_to_all | solution.py:484
  41.9 0.0 copy-done
  41.9 0.6 dynamic-slice_bitcast_fusion.skip_ref
  42.5 32.5 %all-to-all-done.message_ref = bf16[16,400,128]{2,1,0:T(8,128)(2,1)S(1)} async-done(((bf16[16,400,128]{2,1,0:T(8,128)(2,1)}), bf16[16,400,128]{2,1,0:T(8,128)(2,1)S(1)}, u32[]{:S(2)}, u32[]{:S(2)}) %all-to-all-start) | async-done | bytes 1638432 | tf_op jit(solution)/shard_map/all_to_all | solution.py:484
  75.0 0.0 copy-start.3
  75.0 1.2 copy-done.3
  76.2 11.1 %shard_map.140 = (bf16[16,256,128]{2,1,0:T(8,128)(2,1)}, bf16[16,256,128]{2,1,0:T(8,128)(2,1)}, f32[128,16]{1,0:T(8,128)}) custom-call(bf16[16,400,128]{2,1,0:T(8,128)(2,1)} %copy-done.3, f32[1,128]{1,0:T(1,128)} %dynamic-slice_bitcast_fusion.skip_ref, f32[16]{0:T(128)} %dro_ref.1, bf16[16,256,256]{2,1,0:T(8,128)(2,1)} %constant.23.clone.ahead_hbm, ...), custom_call_target="tpu_custom_call" | custom-call | flops 1342177280 | bytes 8388608 | tf_op jit(solution)/shard_map/pallas_call | solution.py:485
  87.3 0.0 copy-start.1
  87.3 9.5 %all-to-all-start.1 = ((bf16[16,256,128]{2,1,0:T(8,128)(2,1)}), bf16[16,256,128]{2,1,0:T(8,128)(2,1)S(1)}, u32[]{:S(2)}, u32[]{:S(2)}) async-start(bf16[16,256,128]{2,1,0:T(8,128)(2,1)} %get-tuple-element.11), calls=%async_computation.1 | async-start | bytes 2097152 | tf_op jit(solution)/shard_map/all_to_all | solution.py:513
  96.9 0.0 copy-done.1
  96.9 0.0 copy-start.2
  96.9 1.2 copy-done.2
  98.1 2.1 %shard_map.142 = (f32[128,1024]{1,0:T(8,128)S(1)}, bf16[1,128,1024]{2,1,0:T(8,128)(2,1)S(1)}) custom-call(s32[1]{0:T(128)} %bitcast.8.own_ref, bf16[16,256,128]{2,1,0:T(8,128)(2,1)S(1)} %copy-done.2, bf16[16,256,256]{2,1,0:T(8,128)(2,1)S(1)} %copy-done.1), custom_call_target="tpu_custom_call" | custom-call | flops 268435456 | bytes 6291456 | tf_op jit(solution)/shard_map/pallas_call | solution.py:514
  100.2 1.6 %collective-permute-start = (bf16[128,1024]{1,0:T(8,128)(2,1)S(1)}, bf16[128,1024]{1,0:T(8,128)(2,1)S(1)}, u32[]{:S(2)}, u32[]{:S(2)}) collective-permute-start(bf16[128,1024]{1,0:T(8,128)(2,1)S(1)} %bitcast.11), channel_id=1, source_target_pairs={{0,16},{16,0},{1,17},{17,1},{2,18},{18,2},{3,19},{19,3},{4,20},{20... | collective-permute-start | bytes 786440 | tf_op jit(solution)/shard_map/ppermute | solution.py:530
  101.7 7.2 %collective-permute-done = bf16[128,1024]{1,0:T(8,128)(2,1)S(1)} collective-permute-done((bf16[128,1024]{1,0:T(8,128)(2,1)S(1)}, bf16[128,1024]{1,0:T(8,128)(2,1)S(1)}, u32[]{:S(2)}, u32[]{:S(2)}) %collective-permute-start) | collective-permute-done | bytes 262176 | tf_op jit(solution)/shard_map/ppermute | solution.py:530
  108.9 0.9 convert_add_fusion
  109.7 10.1 %all-to-all-done.1.message_ref = bf16[16,256,128]{2,1,0:T(8,128)(2,1)S(1)} async-done(((bf16[16,256,128]{2,1,0:T(8,128)(2,1)}), bf16[16,256,128]{2,1,0:T(8,128)(2,1)S(1)}, u32[]{:S(2)}, u32[]{:S(2)}) %all-to-all-start.1) | async-done | bytes 1048608 | tf_op jit(solution)/shard_map/all_to_all | solution.py:513
  119.8 0.0 copy-start.4
  119.8 1.0 copy-done.4
  120.8 3.6 %shard_map.141 = (bf16[128,2048]{1,0:T(8,128)(2,1)}, bf16[128,2048]{1,0:T(8,128)(2,1)}) custom-call(s32[1]{0:T(128)} %bitcast.own_ref, bf16[128,2048]{1,0:T(8,128)(2,1)} %bitcast.13, f32[128,16]{1,0:T(8,128)} %get-tuple-element.10.scale_ref, bf16[16,256,128]{2,1,0:T(8,128)(2,1)} %copy-done.4), custom_call_target="tpu_custom_call" | custom-call | bytes 4194304 | tf_op jit(solution)/shard_map/pallas_call | solution.py:532
Async XLA Ops:
  0.6 41.3 %copy-start = (f32[2048]{0:T(1024)S(1)}, f32[2048]{0:T(1024)}, u32[]{:S(2)}) copy-start(f32[2048]{0:T(1024)} %param.16) | copy-start | bytes 24580
  34.5 40.5 %all-to-all-start = ((bf16[16,400,128]{2,1,0:T(8,128)(2,1)}), bf16[16,400,128]{2,1,0:T(8,128)(2,1)S(1)}, u32[]{:S(2)}, u32[]{:S(2)}) async-start(bf16[16,400,128]{2,1,0:T(8,128)(2,1)} %shard_map.139), calls=%async_computation | async-start | bytes 3276800 | tf_op jit(solution)/shard_map/all_to_all | solution.py:484
  75.0 1.2 copy-start.3
  87.3 9.5 %copy-start.1 = (bf16[16,256,256]{2,1,0:T(8,128)(2,1)S(1)}, bf16[16,256,256]{2,1,0:T(8,128)(2,1)}, u32[]{:S(2)}) copy-start(bf16[16,256,256]{2,1,0:T(8,128)(2,1)} %constant.24.clone.behind_hbm.behind_ref) | copy-start | bytes 6291460
  87.3 32.5 %all-to-all-start.1 = ((bf16[16,256,128]{2,1,0:T(8,128)(2,1)}), bf16[16,256,128]{2,1,0:T(8,128)(2,1)S(1)}, u32[]{:S(2)}, u32[]{:S(2)}) async-start(bf16[16,256,128]{2,1,0:T(8,128)(2,1)} %get-tuple-element.11), calls=%async_computation.1 | async-start | bytes 2097152 | tf_op jit(solution)/shard_map/all_to_all | solution.py:513
  96.9 1.2 copy-start.2
  100.2 8.7 %collective-permute-start = (bf16[128,1024]{1,0:T(8,128)(2,1)S(1)}, bf16[128,1024]{1,0:T(8,128)(2,1)S(1)}, u32[]{:S(2)}, u32[]{:S(2)}) collective-permute-start(bf16[128,1024]{1,0:T(8,128)(2,1)S(1)} %bitcast.11), channel_id=1, source_target_pairs={{0,16},{16,0},{1,17},{17,1},{2,18},{18,2},{3,19},{19,3},{4,20},{20... | collective-permute-start | bytes 786440 | tf_op jit(solution)/shard_map/ppermute | solution.py:530
  119.8 1.0 copy-start.4

commit v6 on v5

--- a/solution.py
+++ b/solution.py
@@ -139,81 +139,67 @@
         copy.wait()
 
 
-def id_rows(doc_ref, lang_ref, tokens):
+def row_copies(source, target, sems):
+    count = sems.shape[0]
+    group = source.shape[0] // count
+    rows = [pl.ds(g * group, group) for g in range(count)]
+    return copies(*[(source.at[r], target.at[r], sems.at[g]) for g, r in enumerate(rows)])
+
+
+def partner(own_ref, r):
+    return jnp.bitwise_xor(own_ref[0], r)
+
+
+def collect(own_ref, chunk_refs, held_ref, sems):
+    return copies(
+        *[(c, held_ref.at[partner(own_ref, r)], sems.at[r]) for r, c in enumerate(chunk_refs)]
+    )
+
+
+def hand_out(own_ref, held_ref, chunk_refs, sems):
+    return copies(
+        *[(held_ref.at[partner(own_ref, r)], c, sems.at[r]) for r, c in enumerate(chunk_refs)]
+    )
+
+
+def prep_kernel(
+    pieces, span, own_ref, input_hbm, grad_hbm, gate_hbm, taps_hbm, doc_ref, lang_ref, *refs
+):
+    outs, (input_ref, grad_ref, gate_ref, made_ref, in_sem, taps_sem, out_sem) = (
+        refs[:pieces],
+        refs[pieces:],
+    )
+    tokens = grad_ref.shape[0]
+    groups = in_sem.shape[1]
+    place, tall = places(pieces, tokens, span)
+    taps_in = copies((taps_hbm, made_ref.at[:, pl.ds(0, span), :], taps_sem.at[0]))
+    grad_in = row_copies(grad_hbm, grad_ref, in_sem.at[0])
+    gate_in = row_copies(gate_hbm, gate_ref, in_sem.at[1])
+    input_in = row_copies(input_hbm, input_ref, in_sem.at[2])
     tile = lax.broadcasted_iota(jnp.int32, (ROWS, tokens), 0)
-    return jnp.where(tile == 0, doc_ref[...], lang_ref[...]).astype(f32).astype(bf16)
-
-
-def gated(grad_ref, gate_ref, part):
-    return (grad_ref[:, part].astype(f32) * gate_ref[:, part].astype(f32)).astype(bf16)
-
-
-def prep_kernel(pieces, span, input_ref, grad_ref, gate_ref, taps_ref, doc_ref, lang_ref, out_ref):
-    tokens = grad_ref.shape[0]
-    place, tall = places(pieces, tokens, span)
-    ids = id_rows(doc_ref, lang_ref, tokens)
+    ids = jnp.where(tile == 0, doc_ref[...], lang_ref[...]).astype(f32).astype(bf16)
+    for i in range(pieces):
+        made_ref[i, span + tall :, :] = ids
     in_row, in_lanes = place(0, span)
     grad_row, grad_lanes = place(1, span)
-    for i in range(pieces):
-        part = slice(i * span, (i + 1) * span)
-        out_ref[i, :span, :] = taps_ref[part, :]
-        out_ref[i, in_row : in_row + tokens, in_lanes] = input_ref[:, part]
-        out_ref[i, grad_row : grad_row + tokens, grad_lanes] = gated(grad_ref, gate_ref, part)
-        out_ref[i, span + tall :, :] = ids
-
-
-def prep_copy_kernel(
-    pieces,
-    span,
-    input_ref,
-    grad_ref,
-    gate_ref,
-    taps_ref,
-    doc_ref,
-    lang_ref,
-    out_ref,
-    factor_ref,
-    made_ref,
-    ids_ref,
-    in_sem,
-    out_sem,
-    made_sem,
-):
-    tokens = grad_ref.shape[0]
-    place, tall = places(pieces, tokens, span)
-    row = [place(side, span)[0] for side in (0, 1)]
-    groups = in_sem.shape[1]
-    group = pieces // groups
-    loads = []
+    group = tokens // groups
     for g in range(groups):
-        wide = pl.ds(g * group * span, group * span)
-        loads.append(
-            copies(
-                (grad_ref.at[:, wide], factor_ref.at[0, :, wide], in_sem.at[0, g]),
-                (gate_ref.at[:, wide], factor_ref.at[1, :, wide], in_sem.at[1, g]),
-            )
-        )
-    sent = []
-    for i in range(pieces):
-        part = pl.ds(i * span, span)
-        sent += copies(
-            (input_ref.at[:, part], out_ref.at[i, pl.ds(row[0], tokens), :], out_sem.at[i])
-        )
-    sent += copies((taps_ref, out_ref.at[:, pl.ds(0, span), :], out_sem.at[pieces]))
-    ids = id_rows(doc_ref, lang_ref, tokens)
-    for i in range(pieces):
-        ids_ref[i] = ids
-    sent += copies((ids_ref, out_ref.at[:, pl.ds(span + tall, ROWS), :], out_sem.at[pieces + 1]))
+        finish(grad_in[g], gate_in[g])
+        rows = slice(g * group, (g + 1) * group)
+        at = slice(grad_row + g * group, grad_row + (g + 1) * group)
+        for i in range(pieces):
+            part = slice(i * span, (i + 1) * span)
+            made_ref[i, at, grad_lanes] = (
+                grad_ref[rows, part].astype(f32) * gate_ref[rows, part].astype(f32)
+            ).astype(bf16)
     for g in range(groups):
-        finish(*loads[g])
-        for i in range(g * group, (g + 1) * group):
-            part = slice(i * span, (i + 1) * span)
-            made_ref[i] = gated(factor_ref.at[0], factor_ref.at[1], part)
-        these = pl.ds(g * group, group)
-        sent += copies(
-            (made_ref.at[these], out_ref.at[these, pl.ds(row[1], tokens), :], made_sem.at[g])
-        )
-    finish(*sent)
+        finish(input_in[g])
+        rows = slice(g * group, (g + 1) * group)
+        at = slice(in_row + g * group, in_row + (g + 1) * group)
+        for i in range(pieces):
+            made_ref[i, at, in_lanes] = input_ref[rows, i * span : (i + 1) * span]
+    finish(*taps_in)
+    finish(*hand_out(own_ref, made_ref, outs, out_sem))
 
 
 def token_scale(message_ref, scale_ref, dro_ref, ids, mean_len, doc_ref, lang_ref):
@@ -234,43 +220,50 @@
 
 def conv_kernel(
     mean_len,
-    message_ref,
+    pieces,
+    own_ref,
+    dro_ref,
     skip_ref,
-    dro_ref,
     ahead_hbm,
     behind_hbm,
     outer_hbm,
     inverse_hbm,
-    out_hbm,
-    cross_hbm,
-    scale_ref,
-    ahead_ref,
-    behind_ref,
-    outer_ref,
-    inverse_ref,
-    out_ref,
-    cross_ref,
-    scaled_ref,
-    taps_mid_ref,
-    mid_ref,
-    back_ref,
-    doc_ref,
-    lang_ref,
-    in_sem,
-    out_sem,
+    *refs,
 ):
-    pieces = message_ref.shape[0]
+    chunks, outs = refs[:pieces], refs[pieces : 2 * pieces]
+    (
+        cross_hbm,
+        scale_ref,
+        message_ref,
+        ahead_ref,
+        behind_ref,
+        outer_ref,
+        inverse_ref,
+        out_ref,
+        cross_ref,
+        scaled_ref,
+        taps_mid_ref,
+        mid_ref,
+        back_ref,
+        doc_ref,
+        lang_ref,
+        table_sem,
+        outer_sem,
+        cross_sem,
+        chunk_sem,
+        out_sem,
+    ) = refs[2 * pieces :]
     tokens = message_ref.shape[2]
     span = skip_ref.shape[1]
     place, tall = places(pieces, tokens, span)
-    outer_in, ahead_in, behind_in, inverse_in = copies(
-        (outer_hbm, outer_ref, in_sem.at[0]),
-        (ahead_hbm, ahead_ref, in_sem.at[1]),
-        (behind_hbm, behind_ref, in_sem.at[2]),
-        (inverse_hbm, inverse_ref, in_sem.at[3]),
-    )
+    chunks_in = collect(own_ref, chunks, message_ref, chunk_sem)
+    outer_in = copies((outer_hbm, outer_ref, outer_sem.at[0]))
+    ahead_in = row_copies(ahead_hbm, ahead_ref, table_sem.at[0])
+    behind_in = row_copies(behind_hbm, behind_ref, table_sem.at[1])
+    inverse_in = copies((inverse_hbm, inverse_ref, outer_sem.at[1]))
+    finish(*chunks_in)
     token_scale(message_ref, scale_ref, dro_ref, span + tall, mean_len, doc_ref, lang_ref)
-    outer_in.wait()
+    finish(*outer_in)
 
     def outer_taps(row):
         rows = pl.ds(row, ROWS)
@@ -302,7 +295,7 @@
             mid_ref[m, pl.ds(tokens + row, ROWS), :] = out[at + ROWS : at + 2 * ROWS]
 
     chunked(tokens, outer, True)
-    finish(ahead_in, behind_in)
+    finish(*ahead_in, *behind_in)
 
     def inner(m):
         filt = lax.dot_general(
@@ -320,8 +313,8 @@
         back_ref[m] = dot(behind_ref[m], both).astype(bf16)
 
     each_piece(pieces, inner, 8)
-    (cross_out,) = copies((cross_ref, cross_hbm, out_sem.at[0]))
-    inverse_in.wait()
+    cross_out = copies((cross_ref, cross_hbm, cross_sem.at[0]))
+    finish(*inverse_in)
     skip = skip_ref[...]
 
     def outer_back(row):
@@ -340,8 +333,7 @@
                 ).astype(bf16)
 
     chunked(tokens, outer_back, True)
-    (out_out,) = copies((out_ref, out_hbm, out_sem.at[1]))
-    finish(cross_out, out_out)
+    finish(*cross_out, *hand_out(own_ref, out_ref, outs, out_sem))
 
 
 def lags_kernel(own_ref, cross_ref, behind_ref, keep_ref, send_ref, back_ref, lag_ref):
@@ -380,47 +372,49 @@
     return jnp.sum(scale, axis=1, keepdims=True)
 
 
-def final_copy_kernel(
-    own_ref, grad_hbm, scale_ref, message_ref, gate_hbm, input_hbm, grad_ref, gate_ref, sem, out_sem
-):
-    pieces = message_ref.shape[0]
-    tokens, channels = grad_hbm.shape
-    span = channels // pieces
-    place, _ = places(pieces, tokens, span)
-    mixed_row, back_row = place(0, 0)[0], place(1, 0)[0]
-    (grad_in,) = copies((grad_hbm, grad_ref, sem.at[0]))
-    sent = []
-    for i in range(pieces):
-        part = pl.ds(i * span, span)
-        sent += copies(
-            (message_ref.at[i, pl.ds(back_row, tokens), :], input_hbm.at[:, part], out_sem.at[i])
-        )
-    scale = own_scale(own_ref, scale_ref)
-    grad_in.wait()
-    for i in range(pieces):
-        part = slice(i * span, (i + 1) * span)
-        mixed = message_ref[i, mixed_row : mixed_row + tokens, :].astype(f32)
-        gate_ref[:, part] = (grad_ref[:, part].astype(f32) * scale * mixed).astype(bf16)
-        if (2 * (i + 1)) % pieces == 0:
-            half = (2 * (i + 1)) // pieces - 1
-            wide = pl.ds(half * (channels // 2), channels // 2)
-            sent += copies((gate_ref.at[:, wide], gate_hbm.at[:, wide], sem.at[1 + half]))
-    finish(*sent)
-
-
-def final_kernel(own_ref, grad_ref, scale_ref, message_ref, gate_ref, input_ref):
-    pieces = message_ref.shape[0]
+def final_kernel(pieces, own_ref, grad_hbm, scale_ref, *refs):
+    chunks = refs[:pieces]
+    (
+        gate_hbm,
+        input_hbm,
+        message_ref,
+        grad_ref,
+        gate_ref,
+        input_ref,
+        chunk_sem,
+        grad_sem,
+        out_sem,
+    ) = refs[pieces:]
     tokens, channels = grad_ref.shape
     span = channels // pieces
+    groups = grad_sem.shape[0]
+    group = tokens // groups
     place, _ = places(pieces, tokens, span)
+    chunks_in = collect(own_ref, chunks, message_ref, chunk_sem)
+    grad_in = row_copies(grad_hbm, grad_ref, grad_sem)
     scale = own_scale(own_ref, scale_ref)
     mixed_row, mixed_lanes = place(0, 0)
     back_row, back_lanes = place(1, 0)
-    for i in range(pieces):
-        part = slice(i * span, (i + 1) * span)
-        mixed = message_ref[i, mixed_row : mixed_row + tokens, mixed_lanes].astype(f32)
-        gate_ref[:, part] = (grad_ref[:, part].astype(f32) * scale * mixed).astype(bf16)
-        input_ref[:, part] = message_ref[i, back_row : back_row + tokens, back_lanes]
+    finish(*chunks_in)
+    sent = []
+    for g in range(groups):
+        finish(grad_in[g])
+        rows = slice(g * group, (g + 1) * group)
+        for i in range(pieces):
+            part = slice(i * span, (i + 1) * span)
+            start = mixed_row + g * group
+            mixed = message_ref[i, start : start + group, mixed_lanes].astype(f32)
+            gate_ref[rows, part] = (
+                grad_ref[rows, part].astype(f32) * scale[rows] * mixed
+            ).astype(bf16)
+            start = back_row + g * group
+            input_ref[rows, part] = message_ref[i, start : start + group, back_lanes]
+        rows = pl.ds(g * group, group)
+        sent += copies(
+            (gate_ref.at[rows], gate_hbm.at[rows], out_sem.at[0, g]),
+            (input_ref.at[rows], input_hbm.at[rows], out_sem.at[1, g]),
+        )
+    finish(*sent)
 
 
 def call(kernel, out, ins, scratch=(), outs=None, room=40 << 20, cost=(0, 0)):
@@ -443,59 +437,69 @@
     length = tokens * pieces
     span = channels // pieces
     mean_len = length / NDOCS
-    own = lax.axis_index("ctx")
+    place = lax.axis_index("ctx")
+    own = place.reshape(1)
     ahead, behind = inner_tables(pieces, tokens)
     outer, inverse = outer_tables(pieces)
-    skip = lax.dynamic_slice_in_dim(skip_gain, own * span, span)[None, :]
-    exchange = functools.partial(
-        lax.all_to_all, axis_name="ctx", split_axis=0, concat_axis=0, tiled=True
-    )
+    skip = lax.dynamic_slice_in_dim(skip_gain, place * span, span)[None, :]
+    def exchange(chunks):
+        half = pieces // 2
+        far = [half + (r >> 1) + (r & 1) * (half // 2) for r in range(half)]
+        near = list(range(1, half)) + [0]
+        order = [r for pair in zip(far, near) for r in pair]
+        got = {0: chunks[0]}
+        for r in order:
+            if r:
+                pairs = [(i, i ^ r) for i in range(pieces)]
+                got[r] = lax.ppermute(chunks[r], "ctx", pairs)
+        return [got[r] for r in range(pieces)]
+
+    shape = jax.ShapeDtypeStruct
+    dma = pltpu.SemaphoreType.DMA
     tall = places(pieces, tokens, span)[1]
     macs = pieces * (2 * tokens) ** 2 * span
-
-    aligned = span % 128 == 0
-    dma = pltpu.SemaphoreType.DMA
+    message = shape((span + tall + ROWS, tokens), bf16)
+    answer = shape((tall, tokens), bf16)
+    many = [HBM] * pieces
     groups = 4
-    message = call(
-        functools.partial(prep_copy_kernel if aligned else prep_kernel, pieces, span),
-        jax.ShapeDtypeStruct((pieces, span + tall + ROWS, tokens), bf16),
-        [HBM] * 4 + [VMEM] * 2 if aligned else [VMEM] * 6,
+
+    chunks = call(
+        functools.partial(prep_kernel, pieces, span),
+        [message] * pieces,
+        [SMEM] + [HBM] * 4 + [VMEM] * 2,
         [
-            pltpu.VMEM((2, tokens, channels), bf16),
-            pltpu.VMEM((pieces, tokens, span), bf16),
-            pltpu.VMEM((pieces, ROWS, tokens), bf16),
-            dma((2, groups)),
-            dma((pieces + 2,)),
-            dma((groups,)),
-        ]
-        if aligned
-        else (),
-        outs=HBM if aligned else VMEM,
-        room=(256 << 10) if aligned else (40 << 20),
+            pltpu.VMEM((tokens, channels), bf16),
+            pltpu.VMEM((tokens, channels), bf16),
+            pltpu.VMEM((tokens, channels), bf16),
+            pltpu.VMEM((pieces,) + message.shape, bf16),
+            dma((3, groups)),
+            dma((1,)),
+            dma((pieces,)),
+        ],
+        outs=many,
+        room=256 << 10,
         cost=(0, 4 << 20),
     )(
+        own,
         saved_input[0],
         grad_out[0],
         gate_value[0],
-        filter_taps.reshape(pieces, span, tokens) if aligned else filter_taps,
+        filter_taps.reshape(pieces, span, tokens),
         doc_ids,
         lang_ids,
     )
-    message = exchange(message)
-    message, cross, scale = call(
-        functools.partial(conv_kernel, mean_len),
-        (
-            jax.ShapeDtypeStruct((pieces, tall, tokens), bf16),
-            jax.ShapeDtypeStruct((pieces, 2 * tokens, span), bf16),
-            jax.ShapeDtypeStruct((tokens, pieces), f32),
-        ),
-        [VMEM, VMEM, SMEM, HBM, HBM, HBM, HBM],
+    *chunks, cross, scale = call(
+        functools.partial(conv_kernel, mean_len, pieces),
+        [answer] * pieces
+        + [shape((pieces, 2 * tokens, span), bf16), shape((tokens, pieces), f32)],
+        [SMEM, SMEM, VMEM] + [HBM] * 4 + many,
         [
+            pltpu.VMEM((pieces,) + message.shape, bf16),
             pltpu.VMEM(ahead.shape, bf16),
             pltpu.VMEM(behind.shape, bf16),
             pltpu.VMEM(outer.shape, bf16),
             pltpu.VMEM(inverse.shape, bf16),
-            pltpu.VMEM((pieces, tall, tokens), bf16),
+            pltpu.VMEM((pieces,) + answer.shape, bf16),
             pltpu.VMEM((pieces, 2 * tokens, span), bf16),
             pltpu.VMEM((pieces, tokens, span), bf16),
             pltpu.VMEM((pieces, span, 2 * tokens), bf16),
@@ -503,14 +507,17 @@
             pltpu.VMEM((pieces, 2 * tokens, 2 * span), bf16),
             pltpu.VMEM((pieces, tokens), f32),
             pltpu.VMEM((pieces, tokens), f32),
-            dma((4,)),
+            dma((2, groups)),
             dma((2,)),
+            dma((1,)),
+            dma((pieces,)),
+            dma((pieces,)),
         ],
-        outs=(HBM, HBM, VMEM),
-        room=(2 << 20) if aligned else (16 << 20),
+        outs=many + [HBM, VMEM],
+        room=2 << 20,
         cost=(10 * macs, 8 << 20),
-    )(message, skip, dro_weight, ahead, behind, outer, inverse)
-    message = exchange(message)
+    )(own, dro_weight, skip, ahead, behind, outer, inverse, *exchange(chunks))
+    chunks = exchange(chunks)
     keep, send = call(
         lags_kernel,
         (
@@ -530,21 +537,22 @@
         d_filter = d_filter + lax.ppermute(send[r - 1], "dp", ring).astype(f32)
     token_block = jax.ShapeDtypeStruct((tokens, channels), bf16)
     d_gate, d_input = call(
-        final_copy_kernel if aligned else final_kernel,
+        functools.partial(final_kernel, pieces),
         (token_block, token_block),
-        [SMEM, HBM if aligned else VMEM, VMEM, VMEM],
+        [SMEM, HBM, VMEM] + many,
         [
+            pltpu.VMEM((pieces,) + answer.shape, bf16),
             pltpu.VMEM((tokens, channels), bf16),
             pltpu.VMEM((tokens, channels), bf16),
-            dma((3,)),
+            pltpu.VMEM((tokens, channels), bf16),
             dma((pieces,)),
-        ]
-        if aligned
-        else (),
-        outs=(HBM, HBM) if aligned else (VMEM, VMEM),
-        room=(5 << 18) if aligned else (40 << 20),
+            dma((groups,)),
+            dma((2, groups)),
+        ],
+        outs=(HBM, HBM),
+        room=5 << 18,
         cost=(0, 4 << 20),
-    )(own.reshape(1), grad_out[0], scale, message)
+    )(own, grad_out[0], scale, *chunks)
     return (d_input[None], d_gate[None], d_filter)
 
 

time: 126 us -> 110 us (0.87)
  starting transfers between devices: 18.5 us -> 62.7 us
  waiting for transfers between devices: 49.7 us -> 19.2 us
  Pallas kernels: 50.5 us -> 21.5 us
    ppermute x0 -> x30, starting transfers between devices: none -> 61.2 us  [exchange(): got[r] = lax.ppermute(chunks[r], 'ctx', pairs)]
    all_to_all x2 -> x0, waiting for transfers between devices: 42.6 us -> none  [local(): message = exchange(message)]
    pallas_call x3, Pallas kernels: 48.5 us -> 19.4 us  [the longest x1 12.2 us: local(): call(functools.partial(conv_kernel, mean_len, pieces), [answer] * pieces...]
    ppermute x0 -> x30, waiting for transfers between devices: none -> 19.2 us  [exchange(): got[r] = lax.ppermute(chunks[r], 'ctx', pairs)]
    all_to_all x2 -> x0, starting transfers between devices: 16.9 us -> none  [local(): message = exchange(message)]
    ppermute x1, waiting for transfers between devices: 7.15 us -> 0.01 us  [local(): d_filter = d_filter + lax.ppermute(send[r - 1], 'dp', ring).astype(f32)]
    unnamed x10 -> x64, local copies, waits for them, and re-layouts: 3.41 us -> 3.45 us
  transfers between devices with their start and end apart: 3 -> 31, of which waited for: 3 -> 10; matrix products, arithmetic and copies ran while one was open for 1% -> 1% of each run, Pallas kernels for 2% -> 5%
where the time goes in v6:
time: 110 us; the launch traced here: 109 us
  starting transfers between devices  62.7 us (57%)
  Pallas kernels  21.5 us (20%)
  waiting for transfers between devices  19.2 us (17%)
  local copies, waits for them, and re-layouts  4.08 us (4%)
    ppermute x30, starting transfers between devices, exchange(): got[r] = lax.ppermute(chunks[r], 'ctx', pairs)  61.2 us
    ppermute x30, waiting for transfers between devices, exchange(): got[r] = lax.ppermute(chunks[r], 'ctx', pairs)  19.2 us
    pallas_call x1, Pallas kernels, local(): call(functools.partial(conv_kernel, mean_len, pieces), [answer] * pieces...  12.2 us
    pallas_call x1, Pallas kernels, local(): call(functools.partial(prep_kernel, pieces, span), [message] * pieces, [S...  3.71 us
    pallas_call x1, Pallas kernels, local(): call(functools.partial(final_kernel, pieces), (token_block, token_block),...  3.49 us
    unnamed x64, local copies, waits for them, and re-layouts  3.45 us
  transfers between devices with their start and end apart: 31, of which 10 were waited for; matrix products, arithmetic and copies ran while one was open for 1% of the time, Pallas kernels for 5%

profile of v6, /device:TPU:0, one launch (start us, length us, event | category | flops | bytes accessed | tf_op | source)
XLA Modules:
  0.0 109.3 jit_solution(13664650787827850045)
XLA Ops:
  0.7 3.7 %shard_map.139 = (bf16[400,128]{1,0:T(8,128)(2,1)}, bf16[400,128]{1,0:T(8,128)(2,1)}, bf16[400,128]{1,0:T(8,128)(2,1)}, bf16[400,128]{1,0:T(8,128)(2,1)}, bf16[4...) custom-call(s32[1]{0:T(128)} %bitcast.own_ref, ...), custom_call_target="tpu_custom_call" | custom-call | bytes 4194304 | tf_op jit(solution)/shard_map/pallas_call | solution.py:466
  4.9 2.6 %collective-permute-start.1 = (bf16[400,128]{1,0:T(8,128)(2,1)}, bf16[400,128]{1,0:T(8,128)(2,1)S(1)}, u32[]{:S(2)}, u32[]{:S(2)}) collective-permute-start(bf16[400,128]{1,0:T(8,128)(2,1)} %get-tuple-element.43), channel_id=1, source_target_pairs={{0,2},{1,3},{2,0},{3,1},{4,6},{5,7},{6,4},{7,5},{8,10},{9,11},{10,... | collective-permute-start | bytes 307208 | tf_op jit(solution)/shard_map/ppermute | solution.py:454
  7.5 1.8 %collective-permute-start.3 = (bf16[400,128]{1,0:T(8,128)(2,1)}, bf16[400,128]{1,0:T(8,128)(2,1)S(1)}, u32[]{:S(2)}, u32[]{:S(2)}) collective-permute-start(bf16[400,128]{1,0:T(8,128)(2,1)} %get-tuple-element.45), channel_id=1, source_target_pairs={{0,4},{1,5},{2,6},{3,7},{4,0},{5,1},{6,2},{7,3},{8,12},{9,13},{10,... | collective-permute-start | bytes 307208 | tf_op jit(solution)/shard_map/ppermute | solution.py:454
  9.4 2.6 %collective-permute-start.5 = (bf16[400,128]{1,0:T(8,128)(2,1)}, bf16[400,128]{1,0:T(8,128)(2,1)S(1)}, u32[]{:S(2)}, u32[]{:S(2)}) collective-permute-start(bf16[400,128]{1,0:T(8,128)(2,1)} %get-tuple-element.47), channel_id=1, source_target_pairs={{0,6},{1,7},{2,4},{3,5},{4,2},{5,3},{6,0},{7,1},{8,14},{9,15},{10,... | collective-permute-start | bytes 307208 | tf_op jit(solution)/shard_map/ppermute | solution.py:454
  12.0 1.2 %collective-permute-start.6 = (bf16[400,128]{1,0:T(8,128)(2,1)}, bf16[400,128]{1,0:T(8,128)(2,1)S(1)}, u32[]{:S(2)}, u32[]{:S(2)}) collective-permute-start(bf16[400,128]{1,0:T(8,128)(2,1)} %get-tuple-element.48), channel_id=1, source_target_pairs={{0,7},{1,6},{2,5},{3,4},{4,3},{5,2},{6,1},{7,0},{8,15},{9,14},{10,... | collective-permute-start | bytes 307208 | tf_op jit(solution)/shard_map/ppermute | solution.py:454
  13.2 2.6 %collective-permute-start.7 = (bf16[400,128]{1,0:T(8,128)(2,1)}, bf16[400,128]{1,0:T(8,128)(2,1)S(1)}, u32[]{:S(2)}, u32[]{:S(2)}) collective-permute-start(bf16[400,128]{1,0:T(8,128)(2,1)} %get-tuple-element.49), channel_id=1, source_target_pairs={{0,8},{1,9},{2,10},{3,11},{4,12},{5,13},{6,14},{7,15},{8,0},{9,1},... | collective-permute-start | bytes 307208 | tf_op jit(solution)/shard_map/ppermute | solution.py:454
  16.8 2.7 %collective-permute-start.9 = (bf16[400,128]{1,0:T(8,128)(2,1)}, bf16[400,128]{1,0:T(8,128)(2,1)S(1)}, u32[]{:S(2)}, u32[]{:S(2)}) collective-permute-start(bf16[400,128]{1,0:T(8,128)(2,1)} %get-tuple-element.51), channel_id=1, source_target_pairs={{0,10},{1,11},{2,8},{3,9},{4,14},{5,15},{6,12},{7,13},{8,2},{9,3},... | collective-permute-start | bytes 307208 | tf_op jit(solution)/shard_map/ppermute | solution.py:454
  19.5 3.4 %collective-permute-done.5.refs_6_ = bf16[400,128]{1,0:T(8,128)(2,1)S(1)} collective-permute-done((bf16[400,128]{1,0:T(8,128)(2,1)}, bf16[400,128]{1,0:T(8,128)(2,1)S(1)}, u32[]{:S(2)}, u32[]{:S(2)}) %collective-permute-start.5) | collective-permute-done | bytes 102432 | tf_op jit(solution)/shard_map/ppermute | solution.py:454
  22.9 1.3 %collective-permute-done.6.refs_7_ = bf16[400,128]{1,0:T(8,128)(2,1)S(1)} collective-permute-done((bf16[400,128]{1,0:T(8,128)(2,1)}, bf16[400,128]{1,0:T(8,128)(2,1)S(1)}, u32[]{:S(2)}, u32[]{:S(2)}) %collective-permute-start.6) | collective-permute-done | bytes 102432 | tf_op jit(solution)/shard_map/ppermute | solution.py:454
  24.2 1.5 %collective-permute-start.11 = (bf16[400,128]{1,0:T(8,128)(2,1)}, bf16[400,128]{1,0:T(8,128)(2,1)S(1)}, u32[]{:S(2)}, u32[]{:S(2)}) collective-permute-start(bf16[400,128]{1,0:T(8,128)(2,1)} %get-tuple-element.53), channel_id=1, source_target_pairs={{0,12},{1,13},{2,14},{3,15},{4,8},{5,9},{6,10},{7,11},{8,4},{9,5},... | collective-permute-start | bytes 307208 | tf_op jit(solution)/shard_map/ppermute | solution.py:454
  25.8 2.0 %collective-permute-start.12 = (bf16[400,128]{1,0:T(8,128)(2,1)}, bf16[400,128]{1,0:T(8,128)(2,1)S(1)}, u32[]{:S(2)}, u32[]{:S(2)}) collective-permute-start(bf16[400,128]{1,0:T(8,128)(2,1)} %get-tuple-element.54), channel_id=1, source_target_pairs={{0,13},{1,12},{2,15},{3,14},{4,9},{5,8},{6,11},{7,10},{8,5},{9,4},... | collective-permute-start | bytes 307208 | tf_op jit(solution)/shard_map/ppermute | solution.py:454
  27.8 10.4 %collective-permute-start.13 = (bf16[400,128]{1,0:T(8,128)(2,1)}, bf16[400,128]{1,0:T(8,128)(2,1)S(1)}, u32[]{:S(2)}, u32[]{:S(2)}) collective-permute-start(bf16[400,128]{1,0:T(8,128)(2,1)} %get-tuple-element.55), channel_id=1, source_target_pairs={{0,14},{1,15},{2,12},{3,13},{4,10},{5,11},{6,8},{7,9},{8,6},{9,7},... | collective-permute-start | bytes 307208 | tf_op jit(solution)/shard_map/ppermute | solution.py:454
  38.2 1.9 %collective-permute-start.14 = (bf16[400,128]{1,0:T(8,128)(2,1)}, bf16[400,128]{1,0:T(8,128)(2,1)S(1)}, u32[]{:S(2)}, u32[]{:S(2)}) collective-permute-start(bf16[400,128]{1,0:T(8,128)(2,1)} %get-tuple-element.56), channel_id=1, source_target_pairs={{0,15},{1,14},{2,13},{3,12},{4,11},{5,10},{6,9},{7,8},{8,7},{9,6},... | collective-permute-start | bytes 307208 | tf_op jit(solution)/shard_map/ppermute | solution.py:454
  41.6 4.2 %collective-permute-done.14.refs_15_ = bf16[400,128]{1,0:T(8,128)(2,1)S(1)} collective-permute-done((bf16[400,128]{1,0:T(8,128)(2,1)}, bf16[400,128]{1,0:T(8,128)(2,1)S(1)}, u32[]{:S(2)}, u32[]{:S(2)}) %collective-permute-start.14) | collective-permute-done | bytes 102432 | tf_op jit(solution)/shard_map/ppermute | solution.py:454
  46.4 12.2 %shard_map.140 = (bf16[256,128]{1,0:T(8,128)(2,1)}, bf16[256,128]{1,0:T(8,128)(2,1)}, bf16[256,128]{1,0:T(8,128)(2,1)}, bf16[256,128]{1,0:T(8,128)(2,1)}, bf16[2...) custom-call(s32[1]{0:T(128)} %bitcast.own_ref, ...), custom_call_target="tpu_custom_call" | custom-call | flops 1342177280 | bytes 8388608 | tf_op jit(solution)/shard_map/pallas_call | solution.py:491
  59.1 1.1 %collective-permute-start.16 = (bf16[256,128]{1,0:T(8,128)(2,1)}, bf16[256,128]{1,0:T(8,128)(2,1)S(1)}, u32[]{:S(2)}, u32[]{:S(2)}) collective-permute-start(bf16[256,128]{1,0:T(8,128)(2,1)} %get-tuple-element.60), channel_id=1, source_target_pairs={{0,2},{1,3},{2,0},{3,1},{4,6},{5,7},{6,4},{7,5},{8,10},{9,11},{10,... | collective-permute-start | bytes 196616 | tf_op jit(solution)/shard_map/ppermute | solution.py:454
  60.6 1.6 %copy-done.1 = bf16[16,256,256]{2,1,0:T(8,128)(2,1)S(1)} copy-done((bf16[16,256,256]{2,1,0:T(8,128)(2,1)S(1)}, bf16[16,256,256]{2,1,0:T(8,128)(2,1)}, u32[]{:S(2)}) %copy-start.1) | copy-done | bytes 2097176
  62.2 1.2 %copy-done.2 = bf16[16,256,128]{2,1,0:T(8,128)(2,1)S(1)} copy-done((bf16[16,256,128]{2,1,0:T(8,128)(2,1)S(1)}, bf16[16,256,128]{2,1,0:T(8,128)(2,1)}, u32[]{:S(2)}) %copy-start.2) | copy-done | bytes 1048600
  63.5 2.1 %shard_map.142 = (f32[128,1024]{1,0:T(8,128)S(1)}, bf16[1,128,1024]{2,1,0:T(8,128)(2,1)S(1)}) custom-call(s32[1]{0:T(128)} %bitcast.8.own_ref, bf16[16,256,128]{2,1,0:T(8,128)(2,1)S(1)} %copy-done.2, bf16[16,256,256]{2,1,0:T(8,128)(2,1)S(1)} %copy-done.1), custom_call_target="tpu_custom_call" | custom-call | flops 268435456 | bytes 6291456 | tf_op jit(solution)/shard_map/pallas_call | solution.py:521
  65.5 1.6 %collective-permute-start.30 = (bf16[128,1024]{1,0:T(8,128)(2,1)S(1)}, bf16[128,1024]{1,0:T(8,128)(2,1)S(1)}, u32[]{:S(2)}, u32[]{:S(2)}) collective-permute-start(bf16[128,1024]{1,0:T(8,128)(2,1)S(1)} %bitcast.11), channel_id=1, source_target_pairs={{0,16},{16,0},{1,17},{17,1},{2,18},{18,2},{3,19},{19,3},{4,20},{20... | collective-permute-start | bytes 786440 | tf_op jit(solution)/shard_map/ppermute | solution.py:537
  67.1 8.1 %collective-permute-start.18 = (bf16[256,128]{1,0:T(8,128)(2,1)S(1)}, bf16[256,128]{1,0:T(8,128)(2,1)}, u32[]{:S(2)}, u32[]{:S(2)}) collective-permute-start(bf16[256,128]{1,0:T(8,128)(2,1)S(1)} %copy-done.31), channel_id=1, source_target_pairs={{0,4},{1,5},{2,6},{3,7},{4,0},{5,1},{6,2},{7,3},{8,12},{9,13},{10,... | collective-permute-start | bytes 196616 | tf_op jit(solution)/shard_map/ppermute | solution.py:454
  75.3 2.0 %collective-permute-start.20 = (bf16[256,128]{1,0:T(8,128)(2,1)S(1)}, bf16[256,128]{1,0:T(8,128)(2,1)}, u32[]{:S(2)}, u32[]{:S(2)}) collective-permute-start(bf16[256,128]{1,0:T(8,128)(2,1)S(1)} %copy-done.29), channel_id=1, source_target_pairs={{0,6},{1,7},{2,4},{3,5},{4,2},{5,3},{6,0},{7,1},{8,14},{9,15},{10,... | collective-permute-start | bytes 196616 | tf_op jit(solution)/shard_map/ppermute | solution.py:454
  77.8 4.4 %collective-permute-start.22 = (bf16[256,128]{1,0:T(8,128)(2,1)S(1)}, bf16[256,128]{1,0:T(8,128)(2,1)}, u32[]{:S(2)}, u32[]{:S(2)}) collective-permute-start(bf16[256,128]{1,0:T(8,128)(2,1)S(1)} %copy-done.27), channel_id=1, source_target_pairs={{0,8},{1,9},{2,10},{3,11},{4,12},{5,13},{6,14},{7,15},{8,0},{9,1},... | collective-permute-start | bytes 196616 | tf_op jit(solution)/shard_map/ppermute | solution.py:454
  82.2 1.1 %collective-permute-start.23 = (bf16[256,128]{1,0:T(8,128)(2,1)S(1)}, bf16[256,128]{1,0:T(8,128)(2,1)}, u32[]{:S(2)}, u32[]{:S(2)}) collective-permute-start(bf16[256,128]{1,0:T(8,128)(2,1)S(1)} %copy-done.26), channel_id=1, source_target_pairs={{0,9},{1,8},{2,11},{3,10},{4,13},{5,12},{6,15},{7,14},{8,1},{9,0},... | collective-permute-start | bytes 196616 | tf_op jit(solution)/shard_map/ppermute | solution.py:454
  83.3 2.6 %collective-permute-start.24 = (bf16[256,128]{1,0:T(8,128)(2,1)S(1)}, bf16[256,128]{1,0:T(8,128)(2,1)}, u32[]{:S(2)}, u32[]{:S(2)}) collective-permute-start(bf16[256,128]{1,0:T(8,128)(2,1)S(1)} %copy-done.25), channel_id=1, source_target_pairs={{0,10},{1,11},{2,8},{3,9},{4,14},{5,15},{6,12},{7,13},{8,2},{9,3},... | collective-permute-start | bytes 196616 | tf_op jit(solution)/shard_map/ppermute | solution.py:454
  87.0 3.7 %collective-permute-start.26 = (bf16[256,128]{1,0:T(8,128)(2,1)S(1)}, bf16[256,128]{1,0:T(8,128)(2,1)}, u32[]{:S(2)}, u32[]{:S(2)}) collective-permute-start(bf16[256,128]{1,0:T(8,128)(2,1)S(1)} %copy-done.23), channel_id=1, source_target_pairs={{0,12},{1,13},{2,14},{3,15},{4,8},{5,9},{6,10},{7,11},{8,4},{9,5},... | collective-permute-start | bytes 196616 | tf_op jit(solution)/shard_map/ppermute | solution.py:454
  90.7 2.9 %collective-permute-done.23.refs_9_ = bf16[256,128]{1,0:T(8,128)(2,1)} collective-permute-done((bf16[256,128]{1,0:T(8,128)(2,1)S(1)}, bf16[256,128]{1,0:T(8,128)(2,1)}, u32[]{:S(2)}, u32[]{:S(2)}) %collective-permute-start.23) | collective-permute-done | bytes 65568 | tf_op jit(solution)/shard_map/ppermute | solution.py:454
  95.1 2.8 %collective-permute-start.28 = (bf16[256,128]{1,0:T(8,128)(2,1)S(1)}, bf16[256,128]{1,0:T(8,128)(2,1)}, u32[]{:S(2)}, u32[]{:S(2)}) collective-permute-start(bf16[256,128]{1,0:T(8,128)(2,1)S(1)} %copy-done.21), channel_id=1, source_target_pairs={{0,14},{1,15},{2,12},{3,13},{4,10},{5,11},{6,8},{7,9},{8,6},{9,7},... | collective-permute-start | bytes 196616 | tf_op jit(solution)/shard_map/ppermute | solution.py:454
  97.9 1.4 %collective-permute-start.29 = (bf16[256,128]{1,0:T(8,128)(2,1)S(1)}, bf16[256,128]{1,0:T(8,128)(2,1)}, u32[]{:S(2)}, u32[]{:S(2)}) collective-permute-start(bf16[256,128]{1,0:T(8,128)(2,1)S(1)} %copy-done.20), channel_id=1, source_target_pairs={{0,15},{1,14},{2,13},{3,12},{4,11},{5,10},{6,9},{7,8},{8,7},{9,6},... | collective-permute-start | bytes 196616 | tf_op jit(solution)/shard_map/ppermute | solution.py:454
  100.0 2.2 %collective-permute-done.28.refs_14_ = bf16[256,128]{1,0:T(8,128)(2,1)} collective-permute-done((bf16[256,128]{1,0:T(8,128)(2,1)S(1)}, bf16[256,128]{1,0:T(8,128)(2,1)}, u32[]{:S(2)}, u32[]{:S(2)}) %collective-permute-start.28) | collective-permute-done | bytes 65568 | tf_op jit(solution)/shard_map/ppermute | solution.py:454
  102.2 2.7 %collective-permute-done.29.refs_15_ = bf16[256,128]{1,0:T(8,128)(2,1)} collective-permute-done((bf16[256,128]{1,0:T(8,128)(2,1)S(1)}, bf16[256,128]{1,0:T(8,128)(2,1)}, u32[]{:S(2)}, u32[]{:S(2)}) %collective-permute-start.29) | collective-permute-done | bytes 65568 | tf_op jit(solution)/shard_map/ppermute | solution.py:454
  105.0 3.5 %shard_map.141 = (bf16[128,2048]{1,0:T(8,128)(2,1)}, bf16[128,2048]{1,0:T(8,128)(2,1)}) custom-call(s32[1]{0:T(128)} %bitcast.own_ref, bf16[128,2048]{1,0:T(8,128)(2,1)} %bitcast.13, f32[128,16]{1,0:T(8,128)} %get-tuple-element.57.scale_ref, bf16[256,128]{1,0:T(8,128)(2,1)} %get-tuple-element.58.refs_0_, bf16[256,128]{1,0:T(8,128)(2,1)} %copy-done.18, ...), custom_call_target="tpu_custom_call" | custom-call | bytes 4194304 | tf_op jit(solution)/shard_map/pallas_call | solution.py:539
  (100 shorter events, 9.2 us)
Async XLA Ops:
  0.6 39.4 %copy-start = (f32[2048]{0:T(1024)S(1)}, f32[2048]{0:T(1024)}, u32[]{:S(2)}) copy-start(f32[2048]{0:T(1024)} %param.16) | copy-start | bytes 24580
  4.4 5.0 %collective-permute-start = (bf16[400,128]{1,0:T(8,128)(2,1)}, bf16[400,128]{1,0:T(8,128)(2,1)S(1)}, u32[]{:S(2)}, u32[]{:S(2)}) collective-permute-start(bf16[400,128]{1,0:T(8,128)(2,1)} %get-tuple-element.42), channel_id=1, source_target_pairs={{0,1},{1,0},{2,3},{3,2},{4,5},{5,4},{6,7},{7,6},{8,9},{9,8},{10,11... | collective-permute-start | bytes 307208 | tf_op jit(solution)/shard_map/ppermute | solution.py:454
  4.9 7.1 %collective-permute-start.1 = (bf16[400,128]{1,0:T(8,128)(2,1)}, bf16[400,128]{1,0:T(8,128)(2,1)S(1)}, u32[]{:S(2)}, u32[]{:S(2)}) collective-permute-start(bf16[400,128]{1,0:T(8,128)(2,1)} %get-tuple-element.43), channel_id=1, source_target_pairs={{0,2},{1,3},{2,0},{3,1},{4,6},{5,7},{6,4},{7,5},{8,10},{9,11},{10,... | collective-permute-start | bytes 307208 | tf_op jit(solution)/shard_map/ppermute | solution.py:454
  7.5 5.7 %collective-permute-start.2 = (bf16[400,128]{1,0:T(8,128)(2,1)}, bf16[400,128]{1,0:T(8,128)(2,1)S(1)}, u32[]{:S(2)}, u32[]{:S(2)}) collective-permute-start(bf16[400,128]{1,0:T(8,128)(2,1)} %get-tuple-element.44), channel_id=1, source_target_pairs={{0,3},{1,2},{2,1},{3,0},{4,7},{5,6},{6,5},{7,4},{8,11},{9,10},{10,... | collective-permute-start | bytes 307208 | tf_op jit(solution)/shard_map/ppermute | solution.py:454
  7.5 8.3 %collective-permute-start.3 = (bf16[400,128]{1,0:T(8,128)(2,1)}, bf16[400,128]{1,0:T(8,128)(2,1)S(1)}, u32[]{:S(2)}, u32[]{:S(2)}) collective-permute-start(bf16[400,128]{1,0:T(8,128)(2,1)} %get-tuple-element.45), channel_id=1, source_target_pairs={{0,4},{1,5},{2,6},{3,7},{4,0},{5,1},{6,2},{7,3},{8,12},{9,13},{10,... | collective-permute-start | bytes 307208 | tf_op jit(solution)/shard_map/ppermute | solution.py:454
  9.3 7.5 %collective-permute-start.4 = (bf16[400,128]{1,0:T(8,128)(2,1)}, bf16[400,128]{1,0:T(8,128)(2,1)S(1)}, u32[]{:S(2)}, u32[]{:S(2)}) collective-permute-start(bf16[400,128]{1,0:T(8,128)(2,1)} %get-tuple-element.46), channel_id=1, source_target_pairs={{0,5},{1,4},{2,7},{3,6},{4,1},{5,0},{6,3},{7,2},{8,13},{9,12},{10,... | collective-permute-start | bytes 307208 | tf_op jit(solution)/shard_map/ppermute | solution.py:454
  9.4 13.6 %collective-permute-start.5 = (bf16[400,128]{1,0:T(8,128)(2,1)}, bf16[400,128]{1,0:T(8,128)(2,1)S(1)}, u32[]{:S(2)}, u32[]{:S(2)}) collective-permute-start(bf16[400,128]{1,0:T(8,128)(2,1)} %get-tuple-element.47), channel_id=1, source_target_pairs={{0,6},{1,7},{2,4},{3,5},{4,2},{5,3},{6,0},{7,1},{8,14},{9,15},{10,... | collective-permute-start | bytes 307208 | tf_op jit(solution)/shard_map/ppermute | solution.py:454
  12.0 12.2 %collective-permute-start.6 = (bf16[400,128]{1,0:T(8,128)(2,1)}, bf16[400,128]{1,0:T(8,128)(2,1)S(1)}, u32[]{:S(2)}, u32[]{:S(2)}) collective-permute-start(bf16[400,128]{1,0:T(8,128)(2,1)} %get-tuple-element.48), channel_id=1, source_target_pairs={{0,7},{1,6},{2,5},{3,4},{4,3},{5,2},{6,1},{7,0},{8,15},{9,14},{10,... | collective-permute-start | bytes 307208 | tf_op jit(solution)/shard_map/ppermute | solution.py:454
  13.2 12.6 %collective-permute-start.7 = (bf16[400,128]{1,0:T(8,128)(2,1)}, bf16[400,128]{1,0:T(8,128)(2,1)S(1)}, u32[]{:S(2)}, u32[]{:S(2)}) collective-permute-start(bf16[400,128]{1,0:T(8,128)(2,1)} %get-tuple-element.49), channel_id=1, source_target_pairs={{0,8},{1,9},{2,10},{3,11},{4,12},{5,13},{6,14},{7,15},{8,0},{9,1},... | collective-permute-start | bytes 307208 | tf_op jit(solution)/shard_map/ppermute | solution.py:454
  15.8 12.0 %collective-permute-start.8 = (bf16[400,128]{1,0:T(8,128)(2,1)}, bf16[400,128]{1,0:T(8,128)(2,1)S(1)}, u32[]{:S(2)}, u32[]{:S(2)}) collective-permute-start(bf16[400,128]{1,0:T(8,128)(2,1)} %get-tuple-element.50), channel_id=1, source_target_pairs={{0,9},{1,8},{2,11},{3,10},{4,13},{5,12},{6,15},{7,14},{8,1},{9,0},... | collective-permute-start | bytes 307208 | tf_op jit(solution)/shard_map/ppermute | solution.py:454
  16.8 21.4 %collective-permute-start.9 = (bf16[400,128]{1,0:T(8,128)(2,1)}, bf16[400,128]{1,0:T(8,128)(2,1)S(1)}, u32[]{:S(2)}, u32[]{:S(2)}) collective-permute-start(bf16[400,128]{1,0:T(8,128)(2,1)} %get-tuple-element.51), channel_id=1, source_target_pairs={{0,10},{1,11},{2,8},{3,9},{4,14},{5,15},{6,12},{7,13},{8,2},{9,3},... | collective-permute-start | bytes 307208 | tf_op jit(solution)/shard_map/ppermute | solution.py:454
  22.9 18.3 %collective-permute-start.10 = (bf16[400,128]{1,0:T(8,128)(2,1)}, bf16[400,128]{1,0:T(8,128)(2,1)S(1)}, u32[]{:S(2)}, u32[]{:S(2)}) collective-permute-start(bf16[400,128]{1,0:T(8,128)(2,1)} %get-tuple-element.52), channel_id=1, source_target_pairs={{0,11},{1,10},{2,9},{3,8},{4,15},{5,14},{6,13},{7,12},{8,3},{9,2},... | collective-permute-start | bytes 307208 | tf_op jit(solution)/shard_map/ppermute | solution.py:454
  24.2 17.0 %collective-permute-start.11 = (bf16[400,128]{1,0:T(8,128)(2,1)}, bf16[400,128]{1,0:T(8,128)(2,1)S(1)}, u32[]{:S(2)}, u32[]{:S(2)}) collective-permute-start(bf16[400,128]{1,0:T(8,128)(2,1)} %get-tuple-element.53), channel_id=1, source_target_pairs={{0,12},{1,13},{2,14},{3,15},{4,8},{5,9},{6,10},{7,11},{8,4},{9,5},... | collective-permute-start | bytes 307208 | tf_op jit(solution)/shard_map/ppermute | solution.py:454
  25.8 15.5 %collective-permute-start.12 = (bf16[400,128]{1,0:T(8,128)(2,1)}, bf16[400,128]{1,0:T(8,128)(2,1)S(1)}, u32[]{:S(2)}, u32[]{:S(2)}) collective-permute-start(bf16[400,128]{1,0:T(8,128)(2,1)} %get-tuple-element.54), channel_id=1, source_target_pairs={{0,13},{1,12},{2,15},{3,14},{4,9},{5,8},{6,11},{7,10},{8,5},{9,4},... | collective-permute-start | bytes 307208 | tf_op jit(solution)/shard_map/ppermute | solution.py:454
  27.8 13.8 %collective-permute-start.13 = (bf16[400,128]{1,0:T(8,128)(2,1)}, bf16[400,128]{1,0:T(8,128)(2,1)S(1)}, u32[]{:S(2)}, u32[]{:S(2)}) collective-permute-start(bf16[400,128]{1,0:T(8,128)(2,1)} %get-tuple-element.55), channel_id=1, source_target_pairs={{0,14},{1,15},{2,12},{3,13},{4,10},{5,11},{6,8},{7,9},{8,6},{9,7},... | collective-permute-start | bytes 307208 | tf_op jit(solution)/shard_map/ppermute | solution.py:454
  38.2 7.6 %collective-permute-start.14 = (bf16[400,128]{1,0:T(8,128)(2,1)}, bf16[400,128]{1,0:T(8,128)(2,1)S(1)}, u32[]{:S(2)}, u32[]{:S(2)}) collective-permute-start(bf16[400,128]{1,0:T(8,128)(2,1)} %get-tuple-element.56), channel_id=1, source_target_pairs={{0,15},{1,14},{2,13},{3,12},{4,11},{5,10},{6,9},{7,8},{8,7},{9,6},... | collective-permute-start | bytes 307208 | tf_op jit(solution)/shard_map/ppermute | solution.py:454
  58.6 16.6 %collective-permute-start.15 = (bf16[256,128]{1,0:T(8,128)(2,1)}, bf16[256,128]{1,0:T(8,128)(2,1)S(1)}, u32[]{:S(2)}, u32[]{:S(2)}) collective-permute-start(bf16[256,128]{1,0:T(8,128)(2,1)} %get-tuple-element.59), channel_id=1, source_target_pairs={{0,1},{1,0},{2,3},{3,2},{4,5},{5,4},{6,7},{7,6},{8,9},{9,8},{10,11... | collective-permute-start | bytes 196616 | tf_op jit(solution)/shard_map/ppermute | solution.py:454
  59.1 16.2 %collective-permute-start.16 = (bf16[256,128]{1,0:T(8,128)(2,1)}, bf16[256,128]{1,0:T(8,128)(2,1)S(1)}, u32[]{:S(2)}, u32[]{:S(2)}) collective-permute-start(bf16[256,128]{1,0:T(8,128)(2,1)} %get-tuple-element.60), channel_id=1, source_target_pairs={{0,2},{1,3},{2,0},{3,1},{4,6},{5,7},{6,4},{7,5},{8,10},{9,11},{10,... | collective-permute-start | bytes 196616 | tf_op jit(solution)/shard_map/ppermute | solution.py:454
  60.2 17.1 %collective-permute-start.17 = (bf16[256,128]{1,0:T(8,128)(2,1)}, bf16[256,128]{1,0:T(8,128)(2,1)}, u32[]{:S(2)}, u32[]{:S(2)}) collective-permute-start(bf16[256,128]{1,0:T(8,128)(2,1)} %get-tuple-element.61), channel_id=1, source_target_pairs={{0,3},{1,2},{2,1},{3,0},{4,7},{5,6},{6,5},{7,4},{8,11},{9,10},{10,... | collective-permute-start | bytes 196616 | tf_op jit(solution)/shard_map/ppermute | solution.py:454
  65.5 42.9 %collective-permute-start.30 = (bf16[128,1024]{1,0:T(8,128)(2,1)S(1)}, bf16[128,1024]{1,0:T(8,128)(2,1)S(1)}, u32[]{:S(2)}, u32[]{:S(2)}) collective-permute-start(bf16[128,1024]{1,0:T(8,128)(2,1)S(1)} %bitcast.11), channel_id=1, source_target_pairs={{0,16},{16,0},{1,17},{17,1},{2,18},{18,2},{3,19},{19,3},{4,20},{20... | collective-permute-start | bytes 786440 | tf_op jit(solution)/shard_map/ppermute | solution.py:537
  67.1 10.7 %collective-permute-start.18 = (bf16[256,128]{1,0:T(8,128)(2,1)S(1)}, bf16[256,128]{1,0:T(8,128)(2,1)}, u32[]{:S(2)}, u32[]{:S(2)}) collective-permute-start(bf16[256,128]{1,0:T(8,128)(2,1)S(1)} %copy-done.31), channel_id=1, source_target_pairs={{0,4},{1,5},{2,6},{3,7},{4,0},{5,1},{6,2},{7,3},{8,12},{9,13},{10,... | collective-permute-start | bytes 196616 | tf_op jit(solution)/shard_map/ppermute | solution.py:454
  75.2 7.0 %collective-permute-start.19 = (bf16[256,128]{1,0:T(8,128)(2,1)S(1)}, bf16[256,128]{1,0:T(8,128)(2,1)}, u32[]{:S(2)}, u32[]{:S(2)}) collective-permute-start(bf16[256,128]{1,0:T(8,128)(2,1)S(1)} %copy-done.30), channel_id=1, source_target_pairs={{0,5},{1,4},{2,7},{3,6},{4,1},{5,0},{6,3},{7,2},{8,13},{9,12},{10,... | collective-permute-start | bytes 196616 | tf_op jit(solution)/shard_map/ppermute | solution.py:454
  75.3 8.0 %collective-permute-start.20 = (bf16[256,128]{1,0:T(8,128)(2,1)S(1)}, bf16[256,128]{1,0:T(8,128)(2,1)}, u32[]{:S(2)}, u32[]{:S(2)}) collective-permute-start(bf16[256,128]{1,0:T(8,128)(2,1)S(1)} %copy-done.29), channel_id=1, source_target_pairs={{0,6},{1,7},{2,4},{3,5},{4,2},{5,3},{6,0},{7,1},{8,14},{9,15},{10,... | collective-permute-start | bytes 196616 | tf_op jit(solution)/shard_map/ppermute | solution.py:454
  77.3 8.6 %collective-permute-start.21 = (bf16[256,128]{1,0:T(8,128)(2,1)S(1)}, bf16[256,128]{1,0:T(8,128)(2,1)}, u32[]{:S(2)}, u32[]{:S(2)}) collective-permute-start(bf16[256,128]{1,0:T(8,128)(2,1)S(1)} %copy-done.28), channel_id=1, source_target_pairs={{0,7},{1,6},{2,5},{3,4},{4,3},{5,2},{6,1},{7,0},{8,15},{9,14},{10,... | collective-permute-start | bytes 196616 | tf_op jit(solution)/shard_map/ppermute | solution.py:454
  77.8 9.3 %collective-permute-start.22 = (bf16[256,128]{1,0:T(8,128)(2,1)S(1)}, bf16[256,128]{1,0:T(8,128)(2,1)}, u32[]{:S(2)}, u32[]{:S(2)}) collective-permute-start(bf16[256,128]{1,0:T(8,128)(2,1)S(1)} %copy-done.27), channel_id=1, source_target_pairs={{0,8},{1,9},{2,10},{3,11},{4,12},{5,13},{6,14},{7,15},{8,0},{9,1},... | collective-permute-start | bytes 196616 | tf_op jit(solution)/shard_map/ppermute | solution.py:454
  82.2 11.5 %collective-permute-start.23 = (bf16[256,128]{1,0:T(8,128)(2,1)S(1)}, bf16[256,128]{1,0:T(8,128)(2,1)}, u32[]{:S(2)}, u32[]{:S(2)}) collective-permute-start(bf16[256,128]{1,0:T(8,128)(2,1)S(1)} %copy-done.26), channel_id=1, source_target_pairs={{0,9},{1,8},{2,11},{3,10},{4,13},{5,12},{6,15},{7,14},{8,1},{9,0},... | collective-permute-start | bytes 196616 | tf_op jit(solution)/shard_map/ppermute | solution.py:454
  83.3 11.8 %collective-permute-start.24 = (bf16[256,128]{1,0:T(8,128)(2,1)S(1)}, bf16[256,128]{1,0:T(8,128)(2,1)}, u32[]{:S(2)}, u32[]{:S(2)}) collective-permute-start(bf16[256,128]{1,0:T(8,128)(2,1)S(1)} %copy-done.25), channel_id=1, source_target_pairs={{0,10},{1,11},{2,8},{3,9},{4,14},{5,15},{6,12},{7,13},{8,2},{9,3},... | collective-permute-start | bytes 196616 | tf_op jit(solution)/shard_map/ppermute | solution.py:454
  85.9 12.0 %collective-permute-start.25 = (bf16[256,128]{1,0:T(8,128)(2,1)S(1)}, bf16[256,128]{1,0:T(8,128)(2,1)}, u32[]{:S(2)}, u32[]{:S(2)}) collective-permute-start(bf16[256,128]{1,0:T(8,128)(2,1)S(1)} %copy-done.24), channel_id=1, source_target_pairs={{0,11},{1,10},{2,9},{3,8},{4,15},{5,14},{6,13},{7,12},{8,3},{9,2},... | collective-permute-start | bytes 196616 | tf_op jit(solution)/shard_map/ppermute | solution.py:454
  87.0 12.3 %collective-permute-start.26 = (bf16[256,128]{1,0:T(8,128)(2,1)S(1)}, bf16[256,128]{1,0:T(8,128)(2,1)}, u32[]{:S(2)}, u32[]{:S(2)}) collective-permute-start(bf16[256,128]{1,0:T(8,128)(2,1)S(1)} %copy-done.23), channel_id=1, source_target_pairs={{0,12},{1,13},{2,14},{3,15},{4,8},{5,9},{6,10},{7,11},{8,4},{9,5},... | collective-permute-start | bytes 196616 | tf_op jit(solution)/shard_map/ppermute | solution.py:454
  93.7 6.3 %collective-permute-start.27 = (bf16[256,128]{1,0:T(8,128)(2,1)S(1)}, bf16[256,128]{1,0:T(8,128)(2,1)}, u32[]{:S(2)}, u32[]{:S(2)}) collective-permute-start(bf16[256,128]{1,0:T(8,128)(2,1)S(1)} %copy-done.22), channel_id=1, source_target_pairs={{0,13},{1,12},{2,15},{3,14},{4,9},{5,8},{6,11},{7,10},{8,5},{9,4},... | collective-permute-start | bytes 196616 | tf_op jit(solution)/shard_map/ppermute | solution.py:454
  95.1 7.1 %collective-permute-start.28 = (bf16[256,128]{1,0:T(8,128)(2,1)S(1)}, bf16[256,128]{1,0:T(8,128)(2,1)}, u32[]{:S(2)}, u32[]{:S(2)}) collective-permute-start(bf16[256,128]{1,0:T(8,128)(2,1)S(1)} %copy-done.21), channel_id=1, source_target_pairs={{0,14},{1,15},{2,12},{3,13},{4,10},{5,11},{6,8},{7,9},{8,6},{9,7},... | collective-permute-start | bytes 196616 | tf_op jit(solution)/shard_map/ppermute | solution.py:454
  97.9 7.0 %collective-permute-start.29 = (bf16[256,128]{1,0:T(8,128)(2,1)S(1)}, bf16[256,128]{1,0:T(8,128)(2,1)}, u32[]{:S(2)}, u32[]{:S(2)}) collective-permute-start(bf16[256,128]{1,0:T(8,128)(2,1)S(1)} %copy-done.20), channel_id=1, source_target_pairs={{0,15},{1,14},{2,13},{3,12},{4,11},{5,10},{6,9},{7,8},{8,7},{9,6},... | collective-permute-start | bytes 196616 | tf_op jit(solution)/shard_map/ppermute | solution.py:454
  (31 other events, 570.3 us)

commit v7 on v6

--- a/solution.py
+++ b/solution.py
@@ -103,6 +103,11 @@
 
 
 def each_piece(pieces, body, group=4):
+    if group == pieces:
+        for m in range(pieces):
+            body(m)
+        return
+
     def step(i, carry):
         for g in range(group):
             body(i * group + g)
@@ -146,43 +151,52 @@
     return copies(*[(source.at[r], target.at[r], sems.at[g]) for g, r in enumerate(rows)])
 
 
-def partner(own_ref, r):
-    return jnp.bitwise_xor(own_ref[0], r)
-
-
-def collect(own_ref, chunk_refs, held_ref, sems):
-    return copies(
-        *[(c, held_ref.at[partner(own_ref, r)], sems.at[r]) for r, c in enumerate(chunk_refs)]
-    )
-
-
-def hand_out(own_ref, held_ref, chunk_refs, sems):
-    return copies(
-        *[(held_ref.at[partner(own_ref, r)], c, sems.at[r]) for r, c in enumerate(chunk_refs)]
-    )
-
-
 def prep_kernel(
-    pieces, span, own_ref, input_hbm, grad_hbm, gate_hbm, taps_hbm, doc_ref, lang_ref, *refs
+    pieces,
+    span,
+    input_hbm,
+    grad_hbm,
+    gate_hbm,
+    taps_hbm,
+    doc_ref,
+    lang_ref,
+    out_hbm,
+    input_ref,
+    grad_ref,
+    gate_ref,
+    made_ref,
+    in_sem,
+    taps_sem,
+    out_sem,
 ):
-    outs, (input_ref, grad_ref, gate_ref, made_ref, in_sem, taps_sem, out_sem) = (
-        refs[:pieces],
-        refs[pieces:],
-    )
     tokens = grad_ref.shape[0]
     groups = in_sem.shape[1]
     place, tall = places(pieces, tokens, span)
-    taps_in = copies((taps_hbm, made_ref.at[:, pl.ds(0, span), :], taps_sem.at[0]))
+    in_row, in_lanes = place(0, span)
+    grad_row, grad_lanes = place(1, span)
+
+    def send(part, start, size):
+        rows = pl.ds(start, size)
+        return copies((made_ref.at[:, rows, :], out_hbm.at[:, rows, :], out_sem.at[part]))
+
+    input_in = row_copies(input_hbm, input_ref, in_sem.at[2])
     grad_in = row_copies(grad_hbm, grad_ref, in_sem.at[0])
     gate_in = row_copies(gate_hbm, gate_ref, in_sem.at[1])
-    input_in = row_copies(input_hbm, input_ref, in_sem.at[2])
+    taps_in = copies((taps_hbm, made_ref.at[:, pl.ds(0, span), :], taps_sem.at[0]))
     tile = lax.broadcasted_iota(jnp.int32, (ROWS, tokens), 0)
     ids = jnp.where(tile == 0, doc_ref[...], lang_ref[...]).astype(f32).astype(bf16)
     for i in range(pieces):
         made_ref[i, span + tall :, :] = ids
-    in_row, in_lanes = place(0, span)
-    grad_row, grad_lanes = place(1, span)
     group = tokens // groups
+    sent = []
+    for g in range(groups):
+        finish(input_in[g])
+        rows = slice(g * group, (g + 1) * group)
+        at = slice(in_row + g * group, in_row + (g + 1) * group)
+        for i in range(pieces):
+            made_ref[i, at, in_lanes] = input_ref[rows, i * span : (i + 1) * span]
+    finish(*taps_in)
+    sent += send(0, 0, span if grad_row == in_row else grad_row)
     for g in range(groups):
         finish(grad_in[g], gate_in[g])
         rows = slice(g * group, (g + 1) * group)
@@ -192,14 +206,11 @@
             made_ref[i, at, grad_lanes] = (
                 grad_ref[rows, part].astype(f32) * gate_ref[rows, part].astype(f32)
             ).astype(bf16)
-    for g in range(groups):
-        finish(input_in[g])
-        rows = slice(g * group, (g + 1) * group)
-        at = slice(in_row + g * group, in_row + (g + 1) * group)
-        for i in range(pieces):
-            made_ref[i, at, in_lanes] = input_ref[rows, i * span : (i + 1) * span]
-    finish(*taps_in)
-    finish(*hand_out(own_ref, made_ref, outs, out_sem))
+        if g == groups // 2 - 1:
+            sent += send(1, grad_row, (g + 1) * group)
+    start = grad_row + tokens // 2
+    sent += send(2, start, span + tall + ROWS - start)
+    finish(*sent)
 
 
 def token_scale(message_ref, scale_ref, dro_ref, ids, mean_len, doc_ref, lang_ref):
@@ -220,48 +231,41 @@
 
 def conv_kernel(
     mean_len,
-    pieces,
-    own_ref,
+    message_ref,
     dro_ref,
     skip_ref,
     ahead_hbm,
     behind_hbm,
     outer_hbm,
     inverse_hbm,
-    *refs,
+    out_hbm,
+    cross_hbm,
+    scale_ref,
+    ahead_ref,
+    behind_ref,
+    outer_ref,
+    inverse_ref,
+    out_ref,
+    cross_ref,
+    scaled_ref,
+    taps_mid_ref,
+    mid_ref,
+    back_ref,
+    doc_ref,
+    lang_ref,
+    table_sem,
+    outer_sem,
+    cross_sem,
+    out_sem,
 ):
-    chunks, outs = refs[:pieces], refs[pieces : 2 * pieces]
-    (
-        cross_hbm,
-        scale_ref,
-        message_ref,
-        ahead_ref,
-        behind_ref,
-        outer_ref,
-        inverse_ref,
-        out_ref,
-        cross_ref,
-        scaled_ref,
-        taps_mid_ref,
-        mid_ref,
-        back_ref,
-        doc_ref,
-        lang_ref,
-        table_sem,
-        outer_sem,
-        cross_sem,
-        chunk_sem,
-        out_sem,
-    ) = refs[2 * pieces :]
+    pieces = message_ref.shape[0]
     tokens = message_ref.shape[2]
     span = skip_ref.shape[1]
     place, tall = places(pieces, tokens, span)
-    chunks_in = collect(own_ref, chunks, message_ref, chunk_sem)
     outer_in = copies((outer_hbm, outer_ref, outer_sem.at[0]))
     ahead_in = row_copies(ahead_hbm, ahead_ref, table_sem.at[0])
     behind_in = row_copies(behind_hbm, behind_ref, table_sem.at[1])
     inverse_in = copies((inverse_hbm, inverse_ref, outer_sem.at[1]))
-    finish(*chunks_in)
     token_scale(message_ref, scale_ref, dro_ref, span + tall, mean_len, doc_ref, lang_ref)
     finish(*outer_in)
 
@@ -312,7 +316,7 @@
         both = jnp.concatenate([mixed.astype(bf16), back.astype(bf16)], axis=1)
         back_ref[m] = dot(behind_ref[m], both).astype(bf16)
 
-    each_piece(pieces, inner, 8)
+    each_piece(pieces, inner, pieces)
     cross_out = copies((cross_ref, cross_hbm, cross_sem.at[0]))
     finish(*inverse_in)
     skip = skip_ref[...]
@@ -333,7 +337,7 @@
                 ).astype(bf16)
 
     chunked(tokens, outer_back, True)
-    finish(*cross_out, *hand_out(own_ref, out_ref, outs, out_sem))
+    finish(*cross_out, *row_copies(out_ref, out_hbm, out_sem))
 
 
 def lags_kernel(own_ref, cross_ref, behind_ref, keep_ref, send_ref, back_ref, lag_ref):
@@ -372,31 +376,39 @@
     return jnp.sum(scale, axis=1, keepdims=True)
 
 
-def final_kernel(pieces, own_ref, grad_hbm, scale_ref, *refs):
-    chunks = refs[:pieces]
-    (
-        gate_hbm,
-        input_hbm,
-        message_ref,
-        grad_ref,
-        gate_ref,
-        input_ref,
-        chunk_sem,
-        grad_sem,
-        out_sem,
-    ) = refs[pieces:]
+def final_kernel(
+    own_ref,
+    grad_hbm,
+    scale_ref,
+    message_ref,
+    gate_hbm,
+    input_hbm,
+    grad_ref,
+    gate_ref,
+    input_ref,
+    grad_sem,
+    out_sem,
+):
+    pieces = message_ref.shape[0]
     tokens, channels = grad_ref.shape
     span = channels // pieces
     groups = grad_sem.shape[0]
     group = tokens // groups
     place, _ = places(pieces, tokens, span)
-    chunks_in = collect(own_ref, chunks, message_ref, chunk_sem)
     grad_in = row_copies(grad_hbm, grad_ref, grad_sem)
-    scale = own_scale(own_ref, scale_ref)
     mixed_row, mixed_lanes = place(0, 0)
     back_row, back_lanes = place(1, 0)
-    finish(*chunks_in)
     sent = []
+    for g in range(groups):
+        rows = slice(g * group, (g + 1) * group)
+        for i in range(pieces):
+            start = back_row + g * group
+            input_ref[rows, i * span : (i + 1) * span] = message_ref[
+                i, start : start + group, back_lanes
+            ]
+        rows = pl.ds(g * group, group)
+        sent += copies((input_ref.at[rows], input_hbm.at[rows], out_sem.at[1, g]))
+    scale = own_scale(own_ref, scale_ref)
     for g in range(groups):
         finish(grad_in[g])
         rows = slice(g * group, (g + 1) * group)
@@ -407,13 +419,8 @@
             gate_ref[rows, part] = (
                 grad_ref[rows, part].astype(f32) * scale[rows] * mixed
             ).astype(bf16)
-            start = back_row + g * group
-            input_ref[rows, part] = message_ref[i, start : start + group, back_lanes]
         rows = pl.ds(g * group, group)
-        sent += copies(
-            (gate_ref.at[rows], gate_hbm.at[rows], out_sem.at[0, g]),
-            (input_ref.at[rows], input_hbm.at[rows], out_sem.at[1, g]),
-        )
+        sent += copies((gate_ref.at[rows], gate_hbm.at[rows], out_sem.at[0, g]))
     finish(*sent)
 
 
@@ -442,45 +449,34 @@
     ahead, behind = inner_tables(pieces, tokens)
     outer, inverse = outer_tables(pieces)
     skip = lax.dynamic_slice_in_dim(skip_gain, place * span, span)[None, :]
-    def exchange(chunks):
-        half = pieces // 2
-        far = [half + (r >> 1) + (r & 1) * (half // 2) for r in range(half)]
-        near = list(range(1, half)) + [0]
-        order = [r for pair in zip(far, near) for r in pair]
-        got = {0: chunks[0]}
-        for r in order:
-            if r:
-                pairs = [(i, i ^ r) for i in range(pieces)]
-                got[r] = lax.ppermute(chunks[r], "ctx", pairs)
-        return [got[r] for r in range(pieces)]
-
+    exchange = functools.partial(
+        lax.all_to_all, axis_name="ctx", split_axis=0, concat_axis=0, tiled=True
+    )
     shape = jax.ShapeDtypeStruct
     dma = pltpu.SemaphoreType.DMA
     tall = places(pieces, tokens, span)[1]
     macs = pieces * (2 * tokens) ** 2 * span
-    message = shape((span + tall + ROWS, tokens), bf16)
-    answer = shape((tall, tokens), bf16)
-    many = [HBM] * pieces
+    message = shape((pieces, span + tall + ROWS, tokens), bf16)
+    answer = shape((pieces, tall, tokens), bf16)
     groups = 4
 
-    chunks = call(
+    sent = call(
         functools.partial(prep_kernel, pieces, span),
-        [message] * pieces,
-        [SMEM] + [HBM] * 4 + [VMEM] * 2,
+        message,
+        [HBM] * 4 + [VMEM] * 2,
         [
             pltpu.VMEM((tokens, channels), bf16),
             pltpu.VMEM((tokens, channels), bf16),
             pltpu.VMEM((tokens, channels), bf16),
-            pltpu.VMEM((pieces,) + message.shape, bf16),
+            pltpu.VMEM(message.shape, bf16),
             dma((3, groups)),
             dma((1,)),
-            dma((pieces,)),
+            dma((3,)),
         ],
-        outs=many,
+        outs=HBM,
         room=256 << 10,
         cost=(0, 4 << 20),
     )(
-        own,
         saved_input[0],
         grad_out[0],
         gate_value[0],
@@ -488,18 +484,16 @@
         doc_ids,
         lang_ids,
     )
-    *chunks, cross, scale = call(
-        functools.partial(conv_kernel, mean_len, pieces),
-        [answer] * pieces
-        + [shape((pieces, 2 * tokens, span), bf16), shape((tokens, pieces), f32)],
-        [SMEM, SMEM, VMEM] + [HBM] * 4 + many,
+    sent, cross, scale = call(
+        functools.partial(conv_kernel, mean_len),
+        [answer, shape((pieces, 2 * tokens, span), bf16), shape((tokens, pieces), f32)],
+        [VMEM, SMEM, VMEM] + [HBM] * 4,
         [
-            pltpu.VMEM((pieces,) + message.shape, bf16),
             pltpu.VMEM(ahead.shape, bf16),
             pltpu.VMEM(behind.shape, bf16),
             pltpu.VMEM(outer.shape, bf16),
             pltpu.VMEM(inverse.shape, bf16),
-            pltpu.VMEM((pieces,) + answer.shape, bf16),
+            pltpu.VMEM(answer.shape, bf16),
             pltpu.VMEM((pieces, 2 * tokens, span), bf16),
             pltpu.VMEM((pieces, tokens, span), bf16),
             pltpu.VMEM((pieces, span, 2 * tokens), bf16),
@@ -510,14 +504,13 @@
             dma((2, groups)),
             dma((2,)),
             dma((1,)),
-            dma((pieces,)),
-            dma((pieces,)),
+            dma((groups,)),
         ],
-        outs=many + [HBM, VMEM],
-        room=2 << 20,
+        outs=[HBM, HBM, VMEM],
+        room=3 << 20,
         cost=(10 * macs, 8 << 20),
-    )(own, dro_weight, skip, ahead, behind, outer, inverse, *exchange(chunks))
-    chunks = exchange(chunks)
+    )(exchange(sent), dro_weight, skip, ahead, behind, outer, inverse)
+    got = exchange(sent)
     keep, send = call(
         lags_kernel,
         (
@@ -537,22 +530,20 @@
         d_filter = d_filter + lax.ppermute(send[r - 1], "dp", ring).astype(f32)
     token_block = jax.ShapeDtypeStruct((tokens, channels), bf16)
     d_gate, d_input = call(
-        functools.partial(final_kernel, pieces),
+        final_kernel,
         (token_block, token_block),
-        [SMEM, HBM, VMEM] + many,
+        [SMEM, HBM, VMEM, VMEM],
         [
-            pltpu.VMEM((pieces,) + answer.shape, bf16),
             pltpu.VMEM((tokens, channels), bf16),
             pltpu.VMEM((tokens, channels), bf16),
             pltpu.VMEM((tokens, channels), bf16),
-            dma((pieces,)),
             dma((groups,)),
             dma((2, groups)),
         ],
         outs=(HBM, HBM),
-        room=5 << 18,
+        room=1450 << 10,
         cost=(0, 4 << 20),
-    )(own, grad_out[0], scale, *chunks)
+    )(own, grad_out[0], scale, got)
     return (d_input[None], d_gate[None], d_filter)
 
 

time: 110 us -> 95.7 us (0.87)
  starting transfers between devices: 62.7 us -> 18.5 us
  waiting for transfers between devices: 19.2 us -> 49.7 us
  Pallas kernels: 21.5 us -> 20.3 us
    ppermute x30 -> x0, starting transfers between devices: 61.2 us -> none  [exchange(): got[r] = lax.ppermute(chunks[r], 'ctx', pairs)]
    all_to_all x0 -> x2, waiting for transfers between devices: none -> 42.6 us  [the longest x1 32.5 us: local(): exchange(sent)]
    ppermute x30 -> x0, waiting for transfers between devices: 19.2 us -> none  [exchange(): got[r] = lax.ppermute(chunks[r], 'ctx', pairs)]
    all_to_all x0 -> x2, starting transfers between devices: none -> 16.9 us  [the longest x1 9.52 us: local(): got = exchange(sent)]
    ppermute x1, waiting for transfers between devices: 0.01 us -> 7.15 us  [local(): d_filter = d_filter + lax.ppermute(send[r - 1], 'dp', ring).astype(f32)]
    pallas_call x3, Pallas kernels: 19.4 us -> 18.3 us  [the longest x1 11.3 us: local(): call(functools.partial(conv_kernel, mean_len), [answer, shape((pieces, 2...]
    unnamed x64 -> x10, local copies, waits for them, and re-layouts: 3.45 us -> 3.41 us
  transfers between devices with their start and end apart: 31 -> 3, of which waited for: 10 -> 3; matrix products, arithmetic and copies ran while one was open for 1% -> 2% of each run, Pallas kernels for 5% -> 2%
where the time goes in v7:
time: 95.7 us; the launch traced here: 94.1 us
  waiting for transfers between devices  49.7 us (52%)
  Pallas kernels  20.3 us (21%)
  starting transfers between devices  18.5 us (19%)
  local copies, waits for them, and re-layouts  4 us (4%)
    all_to_all x1, waiting for transfers between devices, local(): exchange(sent)  32.5 us
    pallas_call x1, Pallas kernels, local(): call(functools.partial(conv_kernel, mean_len), [answer, shape((pieces, 2...  11.3 us
    all_to_all x1, waiting for transfers between devices, local(): got = exchange(sent)  10.1 us
    all_to_all x1, starting transfers between devices, local(): got = exchange(sent)  9.52 us
    all_to_all x1, starting transfers between devices, local(): exchange(sent)  7.4 us
    ppermute x1, waiting for transfers between devices, local(): d_filter = d_filter + lax.ppermute(send[r - 1], 'dp', ring).astype(f32)  7.15 us
    pallas_call x1, Pallas kernels, local(): call(functools.partial(prep_kernel, pieces, span), message, [HBM] * 4 + [...  3.6 us
    unnamed x10, local copies, waits for them, and re-layouts  3.41 us
  transfers between devices with their start and end apart: 3, of which 3 were waited for; matrix products, arithmetic and copies ran while one was open for 2% of the time, Pallas kernels for 2%

profile of v7, /device:TPU:0, one launch (start us, length us, event | category | flops | bytes accessed | tf_op | source)
XLA Modules:
  0.0 94.1 jit_solution(10249034274018381593)
XLA Ops:
  0.6 0.0 copy-start
  0.6 3.6 %shard_map.139 = bf16[16,400,128]{2,1,0:T(8,128)(2,1)} custom-call(bf16[128,2048]{1,0:T(8,128)(2,1)} %bitcast.14, bf16[128,2048]{1,0:T(8,128)(2,1)} %bitcast.12, bf16[128,2048]{1,0:T(8,128)(2,1)} %bitcast.15, bf16[16,128,128]{2,1,0:T(8,128)(2,1)} %bitcast.16, s32[1,128]{1,0:T(1,128)} %doc_ref.1, s32[1,128]{1,0:T(1,128)} %lang_ref.1), custom_call_target="tpu_custom_call" | custom-call | bytes 4194304 | tf_op jit(solution)/shard_map/pallas_call | solution.py:463
  4.3 7.4 %all-to-all-start = ((bf16[16,400,128]{2,1,0:T(8,128)(2,1)}), bf16[16,400,128]{2,1,0:T(8,128)(2,1)S(1)}, u32[]{:S(2)}, u32[]{:S(2)}) async-start(bf16[16,400,128]{2,1,0:T(8,128)(2,1)} %shard_map.139), calls=%async_computation | async-start | bytes 3276800 | tf_op jit(solution)/shard_map/all_to_all | solution.py:512
  11.7 0.0 copy-done
  11.7 0.6 dynamic-slice_bitcast_fusion.skip_ref
  12.3 32.5 %all-to-all-done.message_ref = bf16[16,400,128]{2,1,0:T(8,128)(2,1)S(1)} async-done(((bf16[16,400,128]{2,1,0:T(8,128)(2,1)}), bf16[16,400,128]{2,1,0:T(8,128)(2,1)S(1)}, u32[]{:S(2)}, u32[]{:S(2)}) %all-to-all-start) | async-done | bytes 1638432 | tf_op jit(solution)/shard_map/all_to_all | solution.py:512
  44.8 0.0 copy-start.3
  44.8 1.2 %copy-done.3 = bf16[16,400,128]{2,1,0:T(8,128)(2,1)} copy-done((bf16[16,400,128]{2,1,0:T(8,128)(2,1)}, bf16[16,400,128]{2,1,0:T(8,128)(2,1)S(1)}, u32[]{:S(2)}) %copy-start.3) | copy-done | bytes 1638424
  46.0 11.3 %shard_map.140 = (bf16[16,256,128]{2,1,0:T(8,128)(2,1)}, bf16[16,256,128]{2,1,0:T(8,128)(2,1)}, f32[128,16]{1,0:T(8,128)}) custom-call(bf16[16,400,128]{2,1,0:T(8,128)(2,1)} %copy-done.3, f32[16]{0:T(128)} %dro_ref.1, f32[1,128]{1,0:T(1,128)} %dynamic-slice_bitcast_fusion.skip_ref, bf16[16,256,256]{2,1,0:T(8,128)(2,1)} %constant.23.clone.ahead_hbm, ...), custom_call_target="tpu_custom_call" | custom-call | flops 1342177280 | bytes 8388608 | tf_op jit(solution)/shard_map/pallas_call | solution.py:487
  57.3 0.0 copy-start.1
  57.3 9.5 %all-to-all-start.1 = ((bf16[16,256,128]{2,1,0:T(8,128)(2,1)}), bf16[16,256,128]{2,1,0:T(8,128)(2,1)S(1)}, u32[]{:S(2)}, u32[]{:S(2)}) async-start(bf16[16,256,128]{2,1,0:T(8,128)(2,1)} %get-tuple-element.11), calls=%async_computation.1 | async-start | bytes 2097152 | tf_op jit(solution)/shard_map/all_to_all | solution.py:513
  66.9 0.0 copy-done.1
  66.9 0.0 copy-start.2
  66.9 1.2 %copy-done.2 = bf16[16,256,128]{2,1,0:T(8,128)(2,1)S(1)} copy-done((bf16[16,256,128]{2,1,0:T(8,128)(2,1)S(1)}, bf16[16,256,128]{2,1,0:T(8,128)(2,1)}, u32[]{:S(2)}) %copy-start.2) | copy-done | bytes 1048600
  68.1 2.1 %shard_map.142 = (f32[128,1024]{1,0:T(8,128)S(1)}, bf16[1,128,1024]{2,1,0:T(8,128)(2,1)S(1)}) custom-call(s32[1]{0:T(128)} %bitcast.8.own_ref, bf16[16,256,128]{2,1,0:T(8,128)(2,1)S(1)} %copy-done.2, bf16[16,256,256]{2,1,0:T(8,128)(2,1)S(1)} %copy-done.1), custom_call_target="tpu_custom_call" | custom-call | flops 268435456 | bytes 6291456 | tf_op jit(solution)/shard_map/pallas_call | solution.py:514
  70.2 1.6 %collective-permute-start = (bf16[128,1024]{1,0:T(8,128)(2,1)S(1)}, bf16[128,1024]{1,0:T(8,128)(2,1)S(1)}, u32[]{:S(2)}, u32[]{:S(2)}) collective-permute-start(bf16[128,1024]{1,0:T(8,128)(2,1)S(1)} %bitcast.11), channel_id=1, source_target_pairs={{0,16},{16,0},{1,17},{17,1},{2,18},{18,2},{3,19},{19,3},{4,20},{20... | collective-permute-start | bytes 786440 | tf_op jit(solution)/shard_map/ppermute | solution.py:530
  71.7 7.2 %collective-permute-done = bf16[128,1024]{1,0:T(8,128)(2,1)S(1)} collective-permute-done((bf16[128,1024]{1,0:T(8,128)(2,1)S(1)}, bf16[128,1024]{1,0:T(8,128)(2,1)S(1)}, u32[]{:S(2)}, u32[]{:S(2)}) %collective-permute-start) | collective-permute-done | bytes 262176 | tf_op jit(solution)/shard_map/ppermute | solution.py:530
  78.9 0.9 convert_add_fusion
  79.7 10.1 %all-to-all-done.1.message_ref = bf16[16,256,128]{2,1,0:T(8,128)(2,1)S(1)} async-done(((bf16[16,256,128]{2,1,0:T(8,128)(2,1)}), bf16[16,256,128]{2,1,0:T(8,128)(2,1)S(1)}, u32[]{:S(2)}, u32[]{:S(2)}) %all-to-all-start.1) | async-done | bytes 1048608 | tf_op jit(solution)/shard_map/all_to_all | solution.py:513
  89.8 0.0 copy-start.4
  89.8 1.0 %copy-done.4 = bf16[16,256,128]{2,1,0:T(8,128)(2,1)} copy-done((bf16[16,256,128]{2,1,0:T(8,128)(2,1)}, bf16[16,256,128]{2,1,0:T(8,128)(2,1)S(1)}, u32[]{:S(2)}) %copy-start.4) | copy-done | bytes 1048600
  90.8 3.4 %shard_map.141 = (bf16[128,2048]{1,0:T(8,128)(2,1)}, bf16[128,2048]{1,0:T(8,128)(2,1)}) custom-call(s32[1]{0:T(128)} %bitcast.own_ref, bf16[128,2048]{1,0:T(8,128)(2,1)} %bitcast.13, f32[128,16]{1,0:T(8,128)} %get-tuple-element.10.scale_ref, bf16[16,256,128]{2,1,0:T(8,128)(2,1)} %copy-done.4), custom_call_target="tpu_custom_call" | custom-call | bytes 4194304 | tf_op jit(solution)/shard_map/pallas_call | solution.py:532
Async XLA Ops:
  0.6 11.0 %copy-start = (f32[2048]{0:T(1024)S(1)}, f32[2048]{0:T(1024)}, u32[]{:S(2)}) copy-start(f32[2048]{0:T(1024)} %param.16) | copy-start | bytes 24580
  4.3 40.5 %all-to-all-start = ((bf16[16,400,128]{2,1,0:T(8,128)(2,1)}), bf16[16,400,128]{2,1,0:T(8,128)(2,1)S(1)}, u32[]{:S(2)}, u32[]{:S(2)}) async-start(bf16[16,400,128]{2,1,0:T(8,128)(2,1)} %shard_map.139), calls=%async_computation | async-start | bytes 3276800 | tf_op jit(solution)/shard_map/all_to_all | solution.py:512
  44.8 1.2 %copy-start.3 = (bf16[16,400,128]{2,1,0:T(8,128)(2,1)}, bf16[16,400,128]{2,1,0:T(8,128)(2,1)S(1)}, u32[]{:S(2)}) copy-start(bf16[16,400,128]{2,1,0:T(8,128)(2,1)S(1)} %all-to-all-done.message_ref) | copy-start | bytes 4915204
  57.3 9.5 %copy-start.1 = (bf16[16,256,256]{2,1,0:T(8,128)(2,1)S(1)}, bf16[16,256,256]{2,1,0:T(8,128)(2,1)}, u32[]{:S(2)}) copy-start(bf16[16,256,256]{2,1,0:T(8,128)(2,1)} %constant.24.clone.behind_hbm.behind_ref) | copy-start | bytes 6291460
  57.3 32.5 %all-to-all-start.1 = ((bf16[16,256,128]{2,1,0:T(8,128)(2,1)}), bf16[16,256,128]{2,1,0:T(8,128)(2,1)S(1)}, u32[]{:S(2)}, u32[]{:S(2)}) async-start(bf16[16,256,128]{2,1,0:T(8,128)(2,1)} %get-tuple-element.11), calls=%async_computation.1 | async-start | bytes 2097152 | tf_op jit(solution)/shard_map/all_to_all | solution.py:513
  66.9 1.2 %copy-start.2 = (bf16[16,256,128]{2,1,0:T(8,128)(2,1)S(1)}, bf16[16,256,128]{2,1,0:T(8,128)(2,1)}, u32[]{:S(2)}) copy-start(bf16[16,256,128]{2,1,0:T(8,128)(2,1)} %get-tuple-element.14.cross_ref) | copy-start | bytes 3145732
  70.2 8.7 %collective-permute-start = (bf16[128,1024]{1,0:T(8,128)(2,1)S(1)}, bf16[128,1024]{1,0:T(8,128)(2,1)S(1)}, u32[]{:S(2)}, u32[]{:S(2)}) collective-permute-start(bf16[128,1024]{1,0:T(8,128)(2,1)S(1)} %bitcast.11), channel_id=1, source_target_pairs={{0,16},{16,0},{1,17},{17,1},{2,18},{18,2},{3,19},{19,3},{4,20},{20... | collective-permute-start | bytes 786440 | tf_op jit(solution)/shard_map/ppermute | solution.py:530
  89.8 1.0 %copy-start.4 = (bf16[16,256,128]{2,1,0:T(8,128)(2,1)}, bf16[16,256,128]{2,1,0:T(8,128)(2,1)S(1)}, u32[]{:S(2)}) copy-start(bf16[16,256,128]{2,1,0:T(8,128)(2,1)S(1)} %all-to-all-done.1.message_ref) | copy-start | bytes 3145732

commit v8 on v7

--- a/solution.py
+++ b/solution.py
@@ -30,7 +30,7 @@
         [np.concatenate([cos, sin], axis=2), np.concatenate([-sin, cos], axis=2)], axis=1
     )
     behind = np.swapaxes(ahead, 1, 2) * (2.0 / size)
-    return jnp.asarray(ahead, bf16), jnp.asarray(behind, bf16)
+    return ahead, behind
 
 
 def outer_tables(pieces):
@@ -39,7 +39,24 @@
     angle = math.pi / (2 * pieces) * (j * (4 * m + 1) % (4 * pieces))
     both = np.stack([np.cos(angle), -np.sin(angle)], axis=1).reshape(2 * pieces, pieces)
     ahead = np.kron(both, np.eye(ROWS))
-    return jnp.asarray(ahead, bf16), jnp.asarray(ahead.T, bf16)
+    return ahead, ahead.T
+
+
+def side_by_side(table, width):
+    return np.concatenate(np.split(table, table.shape[1] // width, axis=1), axis=0)
+
+
+def all_tables(pieces, tokens):
+    width = 2 * tokens
+    ahead, behind = inner_tables(pieces, tokens)
+    outer, inverse = outer_tables(pieces)
+    parts = [
+        ahead.reshape(-1, width),
+        behind.reshape(-1, width),
+        side_by_side(outer, width),
+        side_by_side(inverse, width),
+    ]
+    return jnp.asarray(np.concatenate(parts, axis=0), bf16), jnp.asarray(behind, bf16)
 
 
 def turned(value, turns):
@@ -234,17 +251,10 @@
     message_ref,
     dro_ref,
     skip_ref,
-    ahead_hbm,
-    behind_hbm,
-    outer_hbm,
-    inverse_hbm,
+    table_ref,
     out_hbm,
     cross_hbm,
     scale_ref,
-    ahead_ref,
-    behind_ref,
-    outer_ref,
-    inverse_ref,
     out_ref,
     cross_ref,
     scaled_ref,
@@ -253,8 +263,6 @@
     back_ref,
     doc_ref,
     lang_ref,
-    table_sem,
-    outer_sem,
     cross_sem,
     out_sem,
 ):
@@ -262,17 +270,29 @@
     tokens = message_ref.shape[2]
     span = skip_ref.shape[1]
     place, tall = places(pieces, tokens, span)
-    outer_in = copies((outer_hbm, outer_ref, outer_sem.at[0]))
-    ahead_in = row_copies(ahead_hbm, ahead_ref, table_sem.at[0])
-    behind_in = row_copies(behind_hbm, behind_ref, table_sem.at[1])
-    inverse_in = copies((inverse_hbm, inverse_ref, outer_sem.at[1]))
+    width = 2 * tokens
+    slab = pieces * ROWS
+
+    def ahead(m):
+        return table_ref[m * width : (m + 1) * width, :]
+
+    def behind(m):
+        return ahead(pieces + m)
+
+    def joint(start, rows, blocks):
+        parts = [slice(start + b * rows, start + (b + 1) * rows) for b in range(blocks)]
+        return jnp.concatenate([table_ref[part, :] for part in parts], axis=1)
+
+    start = 2 * pieces * width
+    outer_blocks = slab // width
+    outer_table = joint(start, 2 * slab, outer_blocks)
+    inverse_table = joint(start + 2 * slab * outer_blocks, slab, 2 * outer_blocks)
     token_scale(message_ref, scale_ref, dro_ref, span + tall, mean_len, doc_ref, lang_ref)
-    finish(*outer_in)
 
     def outer_taps(row):
         rows = pl.ds(row, ROWS)
         stack = jnp.concatenate([message_ref[j, rows, :] for j in range(pieces)], axis=0)
-        out = dot(outer_ref[...], stack).astype(bf16)
+        out = dot(outer_table, stack).astype(bf16)
         for m in range(pieces):
             at = 2 * m * ROWS
             taps_mid_ref[m, rows, :tokens] = out[at : at + ROWS]
@@ -292,20 +312,19 @@
             scaled = (load(1, j, row).astype(f32) * scale_ref[rows, j : j + 1]).astype(bf16)
             scaled_ref[j, rows, :] = scaled
             stack.append(jnp.concatenate([load(0, j, row), scaled], axis=1))
-        out = dot(outer_ref[...], jnp.concatenate(stack, axis=0)).astype(bf16)
+        out = dot(outer_table, jnp.concatenate(stack, axis=0)).astype(bf16)
         for m in range(pieces):
             at = 2 * m * ROWS
             mid_ref[m, rows, :] = out[at : at + ROWS]
             mid_ref[m, pl.ds(tokens + row, ROWS), :] = out[at + ROWS : at + 2 * ROWS]
 
     chunked(tokens, outer, True)
-    finish(*ahead_in, *behind_in)
 
     def inner(m):
         filt = lax.dot_general(
-            ahead_ref[m], taps_mid_ref[m], (((1,), (1,)), ((), ())), preferred_element_type=f32
+            ahead(m), taps_mid_ref[m], (((1,), (1,)), ((), ())), preferred_element_type=f32
         )
-        spec = dot(ahead_ref[m], mid_ref[m])
+        spec = dot(ahead(m), mid_ref[m])
         fre, fim = filt[:tokens], filt[tokens:]
         xre, xim = spec[:tokens, sides[0]], spec[tokens:, sides[0]]
         gre, gim = spec[:tokens, sides[1]], spec[tokens:, sides[1]]
@@ -314,11 +333,10 @@
         mixed = jnp.concatenate([fre * xre - fim * xim, fre * xim + fim * xre], axis=0)
         back = jnp.concatenate([fre * gre + fim * gim, fre * gim - fim * gre], axis=0)
         both = jnp.concatenate([mixed.astype(bf16), back.astype(bf16)], axis=1)
-        back_ref[m] = dot(behind_ref[m], both).astype(bf16)
+        back_ref[m] = dot(behind(m), both).astype(bf16)
 
     each_piece(pieces, inner, pieces)
     cross_out = copies((cross_ref, cross_hbm, cross_sem.at[0]))
-    finish(*inverse_in)
     skip = skip_ref[...]
 
     def outer_back(row):
@@ -326,7 +344,7 @@
         stack = []
         for m in range(pieces):
             stack += [back_ref[m, rows, :], back_ref[m, pl.ds(tokens + row, ROWS), :]]
-        out = dot(inverse_ref[...], jnp.concatenate(stack, axis=0))
+        out = dot(inverse_table, jnp.concatenate(stack, axis=0))
         for j in range(pieces):
             at = slice(j * ROWS, (j + 1) * ROWS)
             for side in (0, 1):
@@ -336,8 +354,17 @@
                     out[at, sides[side]] + skip * own.astype(f32)
                 ).astype(bf16)
 
-    chunked(tokens, outer_back, True)
-    finish(*cross_out, *row_copies(out_ref, out_hbm, out_sem))
+    sent = cross_out
+    halves = out_sem.shape[0]
+    starts = sorted({place(side, 0)[0] for side in (0, 1)})
+    for half in range(halves):
+        size = tokens // halves
+        for row in range(half * size, (half + 1) * size, ROWS):
+            outer_back(row)
+        for side, first in enumerate(starts):
+            rows = pl.ds(first + half * size, size)
+            sent += copies((out_ref.at[:, rows, :], out_hbm.at[:, rows, :], out_sem.at[half, side]))
+    finish(*sent)
 
 
 def lags_kernel(own_ref, cross_ref, behind_ref, keep_ref, send_ref, back_ref, lag_ref):
@@ -370,58 +397,24 @@
             send_ref[r - 1, :, part] = lag_ref[other * held + j].T.astype(bf16)
 
 
-def own_scale(own_ref, scale_ref):
+def scaled_kernel(own_ref, grad_ref, scale_ref, out_ref):
     lane = lax.broadcasted_iota(jnp.int32, scale_ref.shape, 1)
     scale = jnp.where(lane == own_ref[0], scale_ref[...], jnp.zeros(scale_ref.shape, f32))
-    return jnp.sum(scale, axis=1, keepdims=True)
-
-
-def final_kernel(
-    own_ref,
-    grad_hbm,
-    scale_ref,
-    message_ref,
-    gate_hbm,
-    input_hbm,
-    grad_ref,
-    gate_ref,
-    input_ref,
-    grad_sem,
-    out_sem,
-):
+    out_ref[...] = grad_ref[...].astype(f32) * jnp.sum(scale, axis=1, keepdims=True)
+
+
+def final_kernel(scaled_ref, message_ref, gate_ref, input_ref):
     pieces = message_ref.shape[0]
-    tokens, channels = grad_ref.shape
+    tokens, channels = scaled_ref.shape
     span = channels // pieces
-    groups = grad_sem.shape[0]
-    group = tokens // groups
     place, _ = places(pieces, tokens, span)
-    grad_in = row_copies(grad_hbm, grad_ref, grad_sem)
     mixed_row, mixed_lanes = place(0, 0)
     back_row, back_lanes = place(1, 0)
-    sent = []
-    for g in range(groups):
-        rows = slice(g * group, (g + 1) * group)
-        for i in range(pieces):
-            start = back_row + g * group
-            input_ref[rows, i * span : (i + 1) * span] = message_ref[
-                i, start : start + group, back_lanes
-            ]
-        rows = pl.ds(g * group, group)
-        sent += copies((input_ref.at[rows], input_hbm.at[rows], out_sem.at[1, g]))
-    scale = own_scale(own_ref, scale_ref)
-    for g in range(groups):
-        finish(grad_in[g])
-        rows = slice(g * group, (g + 1) * group)
-        for i in range(pieces):
-            part = slice(i * span, (i + 1) * span)
-            start = mixed_row + g * group
-            mixed = message_ref[i, start : start + group, mixed_lanes].astype(f32)
-            gate_ref[rows, part] = (
-                grad_ref[rows, part].astype(f32) * scale[rows] * mixed
-            ).astype(bf16)
-        rows = pl.ds(g * group, group)
-        sent += copies((gate_ref.at[rows], gate_hbm.at[rows], out_sem.at[0, g]))
-    finish(*sent)
+    for i in range(pieces):
+        part = slice(i * span, (i + 1) * span)
+        mixed = message_ref[i, mixed_row : mixed_row + tokens, mixed_lanes].astype(f32)
+        gate_ref[:, part] = (scaled_ref[:, part] * mixed).astype(bf16)
+        input_ref[:, part] = message_ref[i, back_row : back_row + tokens, back_lanes]
 
 
 def call(kernel, out, ins, scratch=(), outs=None, room=40 << 20, cost=(0, 0)):
@@ -446,8 +439,7 @@
     mean_len = length / NDOCS
     place = lax.axis_index("ctx")
     own = place.reshape(1)
-    ahead, behind = inner_tables(pieces, tokens)
-    outer, inverse = outer_tables(pieces)
+    tables, behind = all_tables(pieces, tokens)
     skip = lax.dynamic_slice_in_dim(skip_gain, place * span, span)[None, :]
     exchange = functools.partial(
         lax.all_to_all, axis_name="ctx", split_axis=0, concat_axis=0, tiled=True
@@ -487,12 +479,8 @@
     sent, cross, scale = call(
         functools.partial(conv_kernel, mean_len),
         [answer, shape((pieces, 2 * tokens, span), bf16), shape((tokens, pieces), f32)],
-        [VMEM, SMEM, VMEM] + [HBM] * 4,
+        [VMEM, SMEM, VMEM, VMEM],
         [
-            pltpu.VMEM(ahead.shape, bf16),
-            pltpu.VMEM(behind.shape, bf16),
-            pltpu.VMEM(outer.shape, bf16),
-            pltpu.VMEM(inverse.shape, bf16),
             pltpu.VMEM(answer.shape, bf16),
             pltpu.VMEM((pieces, 2 * tokens, span), bf16),
             pltpu.VMEM((pieces, tokens, span), bf16),
@@ -501,15 +489,13 @@
             pltpu.VMEM((pieces, 2 * tokens, 2 * span), bf16),
             pltpu.VMEM((pieces, tokens), f32),
             pltpu.VMEM((pieces, tokens), f32),
-            dma((2, groups)),
-            dma((2,)),
             dma((1,)),
-            dma((groups,)),
+            dma((2, 2)),
         ],
         outs=[HBM, HBM, VMEM],
-        room=3 << 20,
+        room=(8 << 20) if span % 128 == 0 else (20 << 20),
         cost=(10 * macs, 8 << 20),
-    )(exchange(sent), dro_weight, skip, ahead, behind, outer, inverse)
+    )(exchange(sent), dro_weight, skip, tables)
     got = exchange(sent)
     keep, send = call(
         lags_kernel,
@@ -529,21 +515,18 @@
         ring = [(d, (d + r) % members) for d in range(members)]
         d_filter = d_filter + lax.ppermute(send[r - 1], "dp", ring).astype(f32)
     token_block = jax.ShapeDtypeStruct((tokens, channels), bf16)
+    scaled = call(
+        scaled_kernel,
+        shape((tokens, channels), f32),
+        [SMEM, VMEM, VMEM],
+        cost=(0, 2 << 20),
+    )(own, grad_out[0], scale)
     d_gate, d_input = call(
         final_kernel,
         (token_block, token_block),
-        [SMEM, HBM, VMEM, VMEM],
-        [
-            pltpu.VMEM((tokens, channels), bf16),
-            pltpu.VMEM((tokens, channels), bf16),
-            pltpu.VMEM((tokens, channels), bf16),
-            dma((groups,)),
-            dma((2, groups)),
-        ],
-        outs=(HBM, HBM),
-        room=1450 << 10,
+        [VMEM, VMEM],
         cost=(0, 4 << 20),
-    )(own, grad_out[0], scale, got)
+    )(scaled, got)
     return (d_input[None], d_gate[None], d_filter)
 
 

time: 95.7 us -> 91.9 us (0.960)
  Pallas kernels: 20.3 us -> 17.7 us
    pallas_call x1 -> x2, Pallas kernels: 3.36 us -> 1.4 us  [the longest x1 1.25 us: local(): call(final_kernel, (token_block, token_block), [VMEM, VMEM], cost=(0, 4 <...]
    unnamed x10 -> x12, local copies, waits for them, and re-layouts: 3.41 us -> 2.81 us
where the time goes in v8:
time: 91.9 us; the launch traced here: 90.4 us
  waiting for transfers between devices  49.2 us (54%)
  starting transfers between devices  18.5 us (20%)
  Pallas kernels  17.7 us (19%)
  local copies, waits for them, and re-layouts  3.4 us (4%)
    all_to_all x1, waiting for transfers between devices, local(): exchange(sent)  32.5 us
    pallas_call x1, Pallas kernels, local(): call(functools.partial(conv_kernel, mean_len), [answer, shape((pieces, 2...  10.7 us
    all_to_all x1, waiting for transfers between devices, local(): got = exchange(sent)  9.7 us
    all_to_all x1, starting transfers between devices, local(): got = exchange(sent)  9.51 us
    all_to_all x1, starting transfers between devices, local(): exchange(sent)  7.4 us
    ppermute x1, waiting for transfers between devices, local(): d_filter = d_filter + lax.ppermute(send[r - 1], 'dp', ring).astype(f32)  6.99 us
    pallas_call x1, Pallas kernels, local(): call(functools.partial(prep_kernel, pieces, span), message, [HBM] * 4 + [...  3.58 us
    unnamed x12, local copies, waits for them, and re-layouts  2.81 us
  transfers between devices with their start and end apart: 3, of which 3 were waited for; matrix products, arithmetic and copies ran while one was open for 2% of the time, Pallas kernels for 2%

profile of v8, /device:TPU:0, one launch (start us, length us, event | category | flops | bytes accessed | tf_op | source)
XLA Modules:
  0.0 90.4 jit_solution(14653621942630641914)
XLA Ops:
  0.6 0.0 copy-start
  0.6 3.6 %shard_map.121 = bf16[16,400,128]{2,1,0:T(8,128)(2,1)} custom-call(bf16[128,2048]{1,0:T(8,128)(2,1)} %bitcast.14, bf16[128,2048]{1,0:T(8,128)(2,1)} %bitcast.11, bf16[128,2048]{1,0:T(8,128)(2,1)} %bitcast.15, bf16[16,128,128]{2,1,0:T(8,128)(2,1)} %bitcast.16, s32[1,128]{1,0:T(1,128)} %doc_ref.1, s32[1,128]{1,0:T(1,128)} %lang_ref.1), custom_call_target="tpu_custom_call" | custom-call | bytes 4194304 | tf_op jit(solution)/shard_map/pallas_call | solution.py:455
  4.2 7.4 %all-to-all-start = ((bf16[16,400,128]{2,1,0:T(8,128)(2,1)}), bf16[16,400,128]{2,1,0:T(8,128)(2,1)S(1)}, u32[]{:S(2)}, u32[]{:S(2)}) async-start(bf16[16,400,128]{2,1,0:T(8,128)(2,1)} %shard_map.121), calls=%async_computation | async-start | bytes 3276800 | tf_op jit(solution)/shard_map/all_to_all | solution.py:498
  11.6 0.0 copy-done
  11.7 0.6 dynamic-slice_bitcast_fusion.skip_ref
  12.2 32.5 %all-to-all-done.message_ref = bf16[16,400,128]{2,1,0:T(8,128)(2,1)S(1)} async-done(((bf16[16,400,128]{2,1,0:T(8,128)(2,1)}), bf16[16,400,128]{2,1,0:T(8,128)(2,1)S(1)}, u32[]{:S(2)}, u32[]{:S(2)}) %all-to-all-start) | async-done | bytes 1638432 | tf_op jit(solution)/shard_map/all_to_all | solution.py:498
  44.8 0.0 copy-start.5
  44.8 1.2 %copy-done.5 = bf16[16,400,128]{2,1,0:T(8,128)(2,1)} copy-done((bf16[16,400,128]{2,1,0:T(8,128)(2,1)}, bf16[16,400,128]{2,1,0:T(8,128)(2,1)S(1)}, u32[]{:S(2)}) %copy-start.5) | copy-done | bytes 1638424
  46.0 10.7 %shard_map.122 = (bf16[16,256,128]{2,1,0:T(8,128)(2,1)}, bf16[16,256,128]{2,1,0:T(8,128)(2,1)}, f32[128,16]{1,0:T(8,128)}) custom-call(bf16[16,400,128]{2,1,0:T(8,128)(2,1)} %copy-done.5, f32[16]{0:T(128)} %dro_ref.1, f32[1,128]{1,0:T(1,128)} %dynamic-slice_bitcast_fusion.skip_ref, bf16[9216,256]{1,0:T(8,128)(2,1)} %constant.19.clone.table_ref), custom_call_target="tpu_custom_call" | custom-call | flops 1342177280 | bytes 8388608 | tf_op jit(solution)/shard_map/pallas_call | solution.py:479
  56.7 0.0 copy-start.3
  56.7 0.0 copy-start.2
  56.7 0.0 copy-start.4
  56.7 9.5 %all-to-all-start.1 = ((bf16[16,256,128]{2,1,0:T(8,128)(2,1)}), bf16[16,256,128]{2,1,0:T(8,128)(2,1)S(1)}, u32[]{:S(2)}, u32[]{:S(2)}) async-start(bf16[16,256,128]{2,1,0:T(8,128)(2,1)} %get-tuple-element.11), calls=%async_computation.1 | async-start | bytes 2097152 | tf_op jit(solution)/shard_map/all_to_all | solution.py:499
  66.2 0.0 copy-done.3
  66.2 0.0 copy-start.1
  66.2 1.6 %copy-done.1 = bf16[16,256,256]{2,1,0:T(8,128)(2,1)S(1)} copy-done((bf16[16,256,256]{2,1,0:T(8,128)(2,1)S(1)}, bf16[16,256,256]{2,1,0:T(8,128)(2,1)}, u32[]{:S(2)}) %copy-start.1) | copy-done | bytes 2097176
  67.8 2.1 %shard_map.125 = (f32[128,1024]{1,0:T(8,128)S(1)}, bf16[1,128,1024]{2,1,0:T(8,128)(2,1)S(1)}) custom-call(s32[1]{0:T(128)} %bitcast.8.own_ref, bf16[16,256,128]{2,1,0:T(8,128)(2,1)S(1)} %copy-done.3, bf16[16,256,256]{2,1,0:T(8,128)(2,1)S(1)} %copy-done.1), custom_call_target="tpu_custom_call" | custom-call | flops 268435456 | bytes 6291456 | tf_op jit(solution)/shard_map/pallas_call | solution.py:500
  69.9 1.6 %collective-permute-start = (bf16[128,1024]{1,0:T(8,128)(2,1)S(1)}, bf16[128,1024]{1,0:T(8,128)(2,1)S(1)}, u32[]{:S(2)}, u32[]{:S(2)}) collective-permute-start(bf16[128,1024]{1,0:T(8,128)(2,1)S(1)} %bitcast.13), channel_id=1, source_target_pairs={{0,16},{16,0},{1,17},{17,1},{2,18},{18,2},{3,19},{19,3},{4,20},{20... | collective-permute-start | bytes 786440 | tf_op jit(solution)/shard_map/ppermute | solution.py:516
  71.4 0.0 copy-done.2
  71.4 0.0 copy-done.4
  71.5 0.1 shard_map.123.scaled_ref
  71.6 7.0 %collective-permute-done = bf16[128,1024]{1,0:T(8,128)(2,1)S(1)} collective-permute-done((bf16[128,1024]{1,0:T(8,128)(2,1)S(1)}, bf16[128,1024]{1,0:T(8,128)(2,1)S(1)}, u32[]{:S(2)}, u32[]{:S(2)}) %collective-permute-start) | collective-permute-done | bytes 262176 | tf_op jit(solution)/shard_map/ppermute | solution.py:516
  78.6 0.9 convert_add_fusion
  79.5 9.7 %all-to-all-done.1.message_ref = bf16[16,256,128]{2,1,0:T(8,128)(2,1)S(1)} async-done(((bf16[16,256,128]{2,1,0:T(8,128)(2,1)}), bf16[16,256,128]{2,1,0:T(8,128)(2,1)S(1)}, u32[]{:S(2)}, u32[]{:S(2)}) %all-to-all-start.1) | async-done | bytes 1048608 | tf_op jit(solution)/shard_map/all_to_all | solution.py:499
  89.2 1.2 %shard_map.124 = (bf16[128,2048]{1,0:T(8,128)(2,1)}, bf16[128,2048]{1,0:T(8,128)(2,1)}) custom-call(f32[128,2048]{1,0:T(8,128)S(1)} %shard_map.123.scaled_ref, bf16[16,256,128]{2,1,0:T(8,128)(2,1)S(1)} %all-to-all-done.1.message_ref), custom_call_target="tpu_custom_call" | custom-call | bytes 4194304 | tf_op jit(solution)/shard_map/pallas_call | solution.py:524
Async XLA Ops:
  0.6 11.0 %copy-start = (f32[2048]{0:T(1024)S(1)}, f32[2048]{0:T(1024)}, u32[]{:S(2)}) copy-start(f32[2048]{0:T(1024)} %param.14) | copy-start | bytes 24580
  4.2 40.5 %all-to-all-start = ((bf16[16,400,128]{2,1,0:T(8,128)(2,1)}), bf16[16,400,128]{2,1,0:T(8,128)(2,1)S(1)}, u32[]{:S(2)}, u32[]{:S(2)}) async-start(bf16[16,400,128]{2,1,0:T(8,128)(2,1)} %shard_map.121), calls=%async_computation | async-start | bytes 3276800 | tf_op jit(solution)/shard_map/all_to_all | solution.py:498
  44.8 1.2 %copy-start.5 = (bf16[16,400,128]{2,1,0:T(8,128)(2,1)}, bf16[16,400,128]{2,1,0:T(8,128)(2,1)S(1)}, u32[]{:S(2)}) copy-start(bf16[16,400,128]{2,1,0:T(8,128)(2,1)S(1)} %all-to-all-done.message_ref) | copy-start | bytes 4915204
  56.7 9.6 %copy-start.3 = (bf16[16,256,128]{2,1,0:T(8,128)(2,1)S(1)}, bf16[16,256,128]{2,1,0:T(8,128)(2,1)}, u32[]{:S(2)}) copy-start(bf16[16,256,128]{2,1,0:T(8,128)(2,1)} %get-tuple-element.14.cross_ref) | copy-start | bytes 3145732
  56.7 14.8 %copy-start.2 = (bf16[1,128,2048]{2,1,0:T(8,128)(2,1)S(1)}, bf16[1,128,2048]{2,1,0:T(8,128)(2,1)}, u32[]{:S(2)}) copy-start(bf16[1,128,2048]{2,1,0:T(8,128)(2,1)} %param.10) | copy-start | bytes 1572868
  56.7 14.8 %copy-start.4 = (f32[128,16]{1,0:T(8,128)S(1)}, f32[128,16]{1,0:T(8,128)}, u32[]{:S(2)}) copy-start(f32[128,16]{1,0:T(8,128)} %get-tuple-element.10.scale_ref) | copy-start | bytes 24580
  56.7 32.5 %all-to-all-start.1 = ((bf16[16,256,128]{2,1,0:T(8,128)(2,1)}), bf16[16,256,128]{2,1,0:T(8,128)(2,1)S(1)}, u32[]{:S(2)}, u32[]{:S(2)}) async-start(bf16[16,256,128]{2,1,0:T(8,128)(2,1)} %get-tuple-element.11), calls=%async_computation.1 | async-start | bytes 2097152 | tf_op jit(solution)/shard_map/all_to_all | solution.py:499
  66.2 1.6 %copy-start.1 = (bf16[16,256,256]{2,1,0:T(8,128)(2,1)S(1)}, bf16[16,256,256]{2,1,0:T(8,128)(2,1)}, u32[]{:S(2)}) copy-start(bf16[16,256,256]{2,1,0:T(8,128)(2,1)} %constant.20.clone.behind_ref) | copy-start | bytes 6291460
  69.9 8.7 %collective-permute-start = (bf16[128,1024]{1,0:T(8,128)(2,1)S(1)}, bf16[128,1024]{1,0:T(8,128)(2,1)S(1)}, u32[]{:S(2)}, u32[]{:S(2)}) collective-permute-start(bf16[128,1024]{1,0:T(8,128)(2,1)S(1)} %bitcast.13), channel_id=1, source_target_pairs={{0,16},{16,0},{1,17},{17,1},{2,18},{18,2},{3,19},{19,3},{4,20},{20... | collective-permute-start | bytes 786440 | tf_op jit(solution)/shard_map/ppermute | solution.py:516

commit v9 on v8

--- a/solution.py
+++ b/solution.py
@@ -252,19 +252,15 @@
     dro_ref,
     skip_ref,
     table_ref,
-    out_hbm,
-    cross_hbm,
-    scale_ref,
     out_ref,
     cross_ref,
+    scale_ref,
     scaled_ref,
     taps_mid_ref,
     mid_ref,
     back_ref,
     doc_ref,
     lang_ref,
-    cross_sem,
-    out_sem,
 ):
     pieces = message_ref.shape[0]
     tokens = message_ref.shape[2]
@@ -336,7 +332,6 @@
         back_ref[m] = dot(behind(m), both).astype(bf16)
 
     each_piece(pieces, inner, pieces)
-    cross_out = copies((cross_ref, cross_hbm, cross_sem.at[0]))
     skip = skip_ref[...]
 
     def outer_back(row):
@@ -354,17 +349,7 @@
                     out[at, sides[side]] + skip * own.astype(f32)
                 ).astype(bf16)
 
-    sent = cross_out
-    halves = out_sem.shape[0]
-    starts = sorted({place(side, 0)[0] for side in (0, 1)})
-    for half in range(halves):
-        size = tokens // halves
-        for row in range(half * size, (half + 1) * size, ROWS):
-            outer_back(row)
-        for side, first in enumerate(starts):
-            rows = pl.ds(first + half * size, size)
-            sent += copies((out_ref.at[:, rows, :], out_hbm.at[:, rows, :], out_sem.at[half, side]))
-    finish(*sent)
+    chunked(tokens, outer_back, True)
 
 
 def lags_kernel(own_ref, cross_ref, behind_ref, keep_ref, send_ref, back_ref, lag_ref):
@@ -481,19 +466,14 @@
         [answer, shape((pieces, 2 * tokens, span), bf16), shape((tokens, pieces), f32)],
         [VMEM, SMEM, VMEM, VMEM],
         [
-            pltpu.VMEM(answer.shape, bf16),
-            pltpu.VMEM((pieces, 2 * tokens, span), bf16),
             pltpu.VMEM((pieces, tokens, span), bf16),
             pltpu.VMEM((pieces, span, 2 * tokens), bf16),
             pltpu.VMEM((pieces, 2 * tokens, 2 * span), bf16),
             pltpu.VMEM((pieces, 2 * tokens, 2 * span), bf16),
             pltpu.VMEM((pieces, tokens), f32),
             pltpu.VMEM((pieces, tokens), f32),
-            dma((1,)),
-            dma((2, 2)),
         ],
-        outs=[HBM, HBM, VMEM],
-        room=(8 << 20) if span % 128 == 0 else (20 << 20),
+        room=(40 << 20) if span % 128 == 0 else (20 << 20),
         cost=(10 * macs, 8 << 20),
     )(exchange(sent), dro_weight, skip, tables)
     got = exchange(sent)

time: 91.9 us -> 90.3 us (0.983)
  Pallas kernels: 17.7 us -> 15 us
    pallas_call x1, Pallas kernels: 10.7 us -> 7.94 us  [local(): call(functools.partial(conv_kernel, mean_len), [answer, shape((pieces, 2...]
    unnamed x12 -> x10, local copies, waits for them, and re-layouts: 2.81 us -> 3.94 us
  transfers between devices with their start and end apart: 3 -> 3, of which waited for: 3 -> 3; matrix products, arithmetic and copies ran while one was open for 2% -> 1% of each run, Pallas kernels for 2% -> 2%
where the time goes in v9:
time: 90.3 us; the launch traced here: 88.8 us
  waiting for transfers between devices  49.7 us (55%)
  starting transfers between devices  18.5 us (20%)
  Pallas kernels  15 us (17%)
  local copies, waits for them, and re-layouts  4.02 us (4%)
    all_to_all x1, waiting for transfers between devices, local(): exchange(sent)  33 us
    all_to_all x1, waiting for transfers between devices, local(): got = exchange(sent)  9.71 us
    all_to_all x1, starting transfers between devices, local(): got = exchange(sent)  9.51 us
    pallas_call x1, Pallas kernels, local(): call(functools.partial(conv_kernel, mean_len), [answer, shape((pieces, 2...  7.94 us
    all_to_all x1, starting transfers between devices, local(): exchange(sent)  7.4 us
    ppermute x1, waiting for transfers between devices, local(): d_filter = d_filter + lax.ppermute(send[r - 1], 'dp', ring).astype(f32)  7 us
    unnamed x10, local copies, waits for them, and re-layouts  3.94 us
    pallas_call x1, Pallas kernels, local(): call(functools.partial(prep_kernel, pieces, span), message, [HBM] * 4 + [...  3.6 us
  transfers between devices with their start and end apart: 3, of which 3 were waited for; matrix products, arithmetic and copies ran while one was open for 1% of the time, Pallas kernels for 2%

profile of v9, /device:TPU:0, one launch (start us, length us, event | category | flops | bytes accessed | tf_op | source)
XLA Modules:
  0.0 88.8 jit_solution(4706814145583125551)
XLA Ops:
  0.6 0.0 copy-start
  0.6 3.6 %shard_map.121 = bf16[16,400,128]{2,1,0:T(8,128)(2,1)} custom-call(bf16[128,2048]{1,0:T(8,128)(2,1)} %bitcast.14, bf16[128,2048]{1,0:T(8,128)(2,1)} %bitcast.11, bf16[128,2048]{1,0:T(8,128)(2,1)} %bitcast.15, bf16[16,128,128]{2,1,0:T(8,128)(2,1)} %bitcast.16, s32[1,128]{1,0:T(1,128)} %doc_ref.1, s32[1,128]{1,0:T(1,128)} %lang_ref.1), custom_call_target="tpu_custom_call" | custom-call | bytes 4194304 | tf_op jit(solution)/shard_map/pallas_call | solution.py:440
  4.3 0.0 copy-start.4
  4.3 7.4 %all-to-all-start = ((bf16[16,400,128]{2,1,0:T(8,128)(2,1)}), bf16[16,400,128]{2,1,0:T(8,128)(2,1)S(1)}, u32[]{:S(2)}, u32[]{:S(2)}) async-start(bf16[16,400,128]{2,1,0:T(8,128)(2,1)} %shard_map.121), calls=%async_computation | async-start | bytes 3276800 | tf_op jit(solution)/shard_map/all_to_all | solution.py:478
  11.7 0.0 copy-done
  11.7 0.1 dynamic-slice_bitcast_fusion.skip_ref
  11.8 33.0 %all-to-all-done.message_ref = bf16[16,400,128]{2,1,0:T(8,128)(2,1)S(1)} async-done(((bf16[16,400,128]{2,1,0:T(8,128)(2,1)}), bf16[16,400,128]{2,1,0:T(8,128)(2,1)S(1)}, u32[]{:S(2)}, u32[]{:S(2)}) %all-to-all-start) | async-done | bytes 1638432 | tf_op jit(solution)/shard_map/all_to_all | solution.py:478
  44.8 0.0 copy-done.4
  44.8 0.0 copy-start.1
  44.8 2.3 %copy-done.1 = bf16[9216,256]{1,0:T(8,128)(2,1)S(1)} copy-done((bf16[9216,256]{1,0:T(8,128)(2,1)S(1)}, bf16[9216,256]{1,0:T(8,128)(2,1)}, u32[]{:S(2)}) %copy-start.1) | copy-done | bytes 4718616
  47.1 7.9 %shard_map.122 = (bf16[16,256,128]{2,1,0:T(8,128)(2,1)}, bf16[16,256,128]{2,1,0:T(8,128)(2,1)S(1)}, f32[128,16]{1,0:T(8,128)S(1)}) custom-call(bf16[16,400,128]{2,1,0:T(8,128)(2,1)S(1)} %all-to-all-done.message_ref, f32[16]{0:T(128)S(1)} %copy-done.4, f32[1,128]{1,0:T(1,128)S(1)} %dynamic-slice_bitcast_fusion.skip_ref, bf16[9216,256]{1,0:T(8,128)(2,1)S(1)} %copy-done.1), custom_call_target="tpu_custom_call" | custom-call | flops 1342177280 | bytes 8388608 | tf_op jit(solution)/shard_map/pallas_call | solution.py:464
  55.1 0.0 copy-start.3
  55.1 9.5 %all-to-all-start.1 = ((bf16[16,256,128]{2,1,0:T(8,128)(2,1)}), bf16[16,256,128]{2,1,0:T(8,128)(2,1)S(1)}, u32[]{:S(2)}, u32[]{:S(2)}) async-start(bf16[16,256,128]{2,1,0:T(8,128)(2,1)} %get-tuple-element.11), calls=%async_computation.1 | async-start | bytes 2097152 | tf_op jit(solution)/shard_map/all_to_all | solution.py:479
  64.6 0.0 copy-start.2
  64.6 1.6 %copy-done.2 = bf16[16,256,256]{2,1,0:T(8,128)(2,1)S(1)} copy-done((bf16[16,256,256]{2,1,0:T(8,128)(2,1)S(1)}, bf16[16,256,256]{2,1,0:T(8,128)(2,1)}, u32[]{:S(2)}) %copy-start.2) | copy-done | bytes 2097176
  66.2 2.1 %shard_map.125 = (f32[128,1024]{1,0:T(8,128)S(1)}, bf16[1,128,1024]{2,1,0:T(8,128)(2,1)S(1)}) custom-call(s32[1]{0:T(128)} %bitcast.8.own_ref, bf16[16,256,128]{2,1,0:T(8,128)(2,1)S(1)} %get-tuple-element.14.cross_ref, bf16[16,256,256]{2,1,0:T(8,128)(2,1)S(1)} %copy-done.2), custom_call_target="tpu_custom_call" | custom-call | flops 268435456 | bytes 6291456 | tf_op jit(solution)/shard_map/pallas_call | solution.py:480
  68.3 1.5 %collective-permute-start = (bf16[128,1024]{1,0:T(8,128)(2,1)S(1)}, bf16[128,1024]{1,0:T(8,128)(2,1)S(1)}, u32[]{:S(2)}, u32[]{:S(2)}) collective-permute-start(bf16[128,1024]{1,0:T(8,128)(2,1)S(1)} %bitcast.13), channel_id=1, source_target_pairs={{0,16},{16,0},{1,17},{17,1},{2,18},{18,2},{3,19},{19,3},{4,20},{20... | collective-permute-start | bytes 786440 | tf_op jit(solution)/shard_map/ppermute | solution.py:496
  69.8 0.0 copy-done.3
  69.8 0.1 shard_map.123.scaled_ref
  70.0 7.0 %collective-permute-done = bf16[128,1024]{1,0:T(8,128)(2,1)S(1)} collective-permute-done((bf16[128,1024]{1,0:T(8,128)(2,1)S(1)}, bf16[128,1024]{1,0:T(8,128)(2,1)S(1)}, u32[]{:S(2)}, u32[]{:S(2)}) %collective-permute-start) | collective-permute-done | bytes 262176 | tf_op jit(solution)/shard_map/ppermute | solution.py:496
  77.0 0.9 convert_add_fusion
  77.8 9.7 %all-to-all-done.1.message_ref = bf16[16,256,128]{2,1,0:T(8,128)(2,1)S(1)} async-done(((bf16[16,256,128]{2,1,0:T(8,128)(2,1)}), bf16[16,256,128]{2,1,0:T(8,128)(2,1)S(1)}, u32[]{:S(2)}, u32[]{:S(2)}) %all-to-all-start.1) | async-done | bytes 1048608 | tf_op jit(solution)/shard_map/all_to_all | solution.py:479
  87.5 1.2 %shard_map.124 = (bf16[128,2048]{1,0:T(8,128)(2,1)}, bf16[128,2048]{1,0:T(8,128)(2,1)}) custom-call(f32[128,2048]{1,0:T(8,128)S(1)} %shard_map.123.scaled_ref, bf16[16,256,128]{2,1,0:T(8,128)(2,1)S(1)} %all-to-all-done.1.message_ref), custom_call_target="tpu_custom_call" | custom-call | bytes 4194304 | tf_op jit(solution)/shard_map/pallas_call | solution.py:504
Async XLA Ops:
  0.6 11.0 %copy-start = (f32[2048]{0:T(1024)S(1)}, f32[2048]{0:T(1024)}, u32[]{:S(2)}) copy-start(f32[2048]{0:T(1024)} %param.14) | copy-start | bytes 24580
  4.3 40.5 %copy-start.4 = (f32[16]{0:T(128)S(1)}, f32[16]{0:T(128)}, u32[]{:S(2)}) copy-start(f32[16]{0:T(128)} %dro_ref.1) | copy-start | bytes 196
  4.3 40.5 %all-to-all-start = ((bf16[16,400,128]{2,1,0:T(8,128)(2,1)}), bf16[16,400,128]{2,1,0:T(8,128)(2,1)S(1)}, u32[]{:S(2)}, u32[]{:S(2)}) async-start(bf16[16,400,128]{2,1,0:T(8,128)(2,1)} %shard_map.121), calls=%async_computation | async-start | bytes 3276800 | tf_op jit(solution)/shard_map/all_to_all | solution.py:478
  44.8 2.3 %copy-start.1 = (bf16[9216,256]{1,0:T(8,128)(2,1)S(1)}, bf16[9216,256]{1,0:T(8,128)(2,1)}, u32[]{:S(2)}) copy-start(bf16[9216,256]{1,0:T(8,128)(2,1)} %constant.19.clone.table_ref) | copy-start | bytes 14155780
  55.1 14.7 %copy-start.3 = (bf16[1,128,2048]{2,1,0:T(8,128)(2,1)S(1)}, bf16[1,128,2048]{2,1,0:T(8,128)(2,1)}, u32[]{:S(2)}) copy-start(bf16[1,128,2048]{2,1,0:T(8,128)(2,1)} %param.10) | copy-start | bytes 1572868
  55.1 32.5 %all-to-all-start.1 = ((bf16[16,256,128]{2,1,0:T(8,128)(2,1)}), bf16[16,256,128]{2,1,0:T(8,128)(2,1)S(1)}, u32[]{:S(2)}, u32[]{:S(2)}) async-start(bf16[16,256,128]{2,1,0:T(8,128)(2,1)} %get-tuple-element.11), calls=%async_computation.1 | async-start | bytes 2097152 | tf_op jit(solution)/shard_map/all_to_all | solution.py:479
  64.6 1.6 %copy-start.2 = (bf16[16,256,256]{2,1,0:T(8,128)(2,1)S(1)}, bf16[16,256,256]{2,1,0:T(8,128)(2,1)}, u32[]{:S(2)}) copy-start(bf16[16,256,256]{2,1,0:T(8,128)(2,1)} %constant.20.clone.behind_ref) | copy-start | bytes 6291460
  68.3 8.7 %collective-permute-start = (bf16[128,1024]{1,0:T(8,128)(2,1)S(1)}, bf16[128,1024]{1,0:T(8,128)(2,1)S(1)}, u32[]{:S(2)}, u32[]{:S(2)}) collective-permute-start(bf16[128,1024]{1,0:T(8,128)(2,1)S(1)} %bitcast.13), channel_id=1, source_target_pairs={{0,16},{16,0},{1,17},{17,1},{2,18},{18,2},{3,19},{19,3},{4,20},{20... | collective-permute-start | bytes 786440 | tf_op jit(solution)/shard_map/ppermute | solution.py:496

commit v10 on v9

--- a/solution.py
+++ b/solution.py
@@ -137,7 +137,7 @@
     return lax.dot_general(a, b, (((1,), (0,)), ((), ())), preferred_element_type=f32)
 
 
-def places(pieces, tokens, span):
+def places(tokens, span):
     beside = max(1, tokens // span)
 
     def place(index, start):
@@ -170,7 +170,8 @@
 
 def prep_kernel(
     pieces,
-    span,
+    joint,
+    own_ref,
     input_hbm,
     grad_hbm,
     gate_hbm,
@@ -186,11 +187,15 @@
     taps_sem,
     out_sem,
 ):
-    tokens = grad_ref.shape[0]
+    tokens, channels = grad_ref.shape
     groups = in_sem.shape[1]
-    place, tall = places(pieces, tokens, span)
-    in_row, in_lanes = place(0, span)
-    grad_row, grad_lanes = place(1, span)
+    span = channels // pieces
+    share = span // joint
+    taps = share // joint
+    place, tall = places(tokens, share)
+    in_row, in_lanes = place(0, taps)
+    grad_row, grad_lanes = place(1, taps)
+    owners = [(d, i) for d in range(joint) for i in range(pieces)]
 
     def send(part, start, size):
         rows = pl.ds(start, size)
@@ -199,55 +204,67 @@
     input_in = row_copies(input_hbm, input_ref, in_sem.at[2])
     grad_in = row_copies(grad_hbm, grad_ref, in_sem.at[0])
     gate_in = row_copies(gate_hbm, gate_ref, in_sem.at[1])
-    taps_in = copies((taps_hbm, made_ref.at[:, pl.ds(0, span), :], taps_sem.at[0]))
+    taps_in = []
+    for d in range(joint):
+        start = pl.multiple_of(d * share + own_ref[0] * taps, ROWS)
+        taps_in += copies(
+            (
+                taps_hbm.at[:, pl.ds(start, taps), :],
+                made_ref.at[pl.ds(d * pieces, pieces), pl.ds(0, taps), :],
+                taps_sem.at[d],
+            )
+        )
     tile = lax.broadcasted_iota(jnp.int32, (ROWS, tokens), 0)
     ids = jnp.where(tile == 0, doc_ref[...], lang_ref[...]).astype(f32).astype(bf16)
-    for i in range(pieces):
-        made_ref[i, span + tall :, :] = ids
+    for o in range(len(owners)):
+        made_ref[o, taps + tall :, :] = ids
     group = tokens // groups
     sent = []
     for g in range(groups):
         finish(input_in[g])
         rows = slice(g * group, (g + 1) * group)
         at = slice(in_row + g * group, in_row + (g + 1) * group)
-        for i in range(pieces):
-            made_ref[i, at, in_lanes] = input_ref[rows, i * span : (i + 1) * span]
+        for o, (d, i) in enumerate(owners):
+            part = slice(i * span + d * share, i * span + (d + 1) * share)
+            made_ref[o, at, in_lanes] = input_ref[rows, part]
     finish(*taps_in)
-    sent += send(0, 0, span if grad_row == in_row else grad_row)
+    sent += send(0, 0, taps if grad_row == in_row else grad_row)
     for g in range(groups):
         finish(grad_in[g], gate_in[g])
         rows = slice(g * group, (g + 1) * group)
         at = slice(grad_row + g * group, grad_row + (g + 1) * group)
-        for i in range(pieces):
-            part = slice(i * span, (i + 1) * span)
-            made_ref[i, at, grad_lanes] = (
-                grad_ref[rows, part].astype(f32) * gate_ref[rows, part].astype(f32)
-            ).astype(bf16)
+        made = (grad_ref[rows, :].astype(f32) * gate_ref[rows, :].astype(f32)).astype(bf16)
+        for o, (d, i) in enumerate(owners):
+            part = slice(i * span + d * share, i * span + (d + 1) * share)
+            made_ref[o, at, grad_lanes] = made[:, part]
         if g == groups // 2 - 1:
             sent += send(1, grad_row, (g + 1) * group)
     start = grad_row + tokens // 2
-    sent += send(2, start, span + tall + ROWS - start)
+    sent += send(2, start, taps + tall + ROWS - start)
     finish(*sent)
 
 
-def token_scale(message_ref, scale_ref, dro_ref, ids, mean_len, doc_ref, lang_ref):
+def token_scale(message_ref, scale_ref, dro_ref, ids, pieces, mean_len, doc_ref, lang_ref):
     for j in range(message_ref.shape[0]):
         rows = message_ref[j, ids:, :].astype(f32)
         doc_ref[j : j + 1, :] = rows[0:1]
         lang_ref[j : j + 1, :] = rows[1:2]
-    docs, langs = doc_ref[...], lang_ref[...]
-    doc_len = jnp.zeros_like(docs)
-    for d in range(NDOCS):
-        hot = (docs == float(d)).astype(f32)
-        doc_len = doc_len + hot * jnp.sum(hot, axis=(0, 1), keepdims=True)
-    weight = jnp.zeros_like(langs)
-    for g in range(dro_ref.shape[0]):
-        weight = jnp.where(langs == float(g), dro_ref[g], weight)
-    scale_ref[...] = (weight * (2.0 * mean_len) / (doc_len + mean_len)).T
+    for start in range(0, message_ref.shape[0], pieces):
+        own = slice(start, start + pieces)
+        docs, langs = doc_ref[own, :], lang_ref[own, :]
+        doc_len = jnp.zeros_like(docs)
+        for d in range(NDOCS):
+            hot = (docs == float(d)).astype(f32)
+            doc_len = doc_len + hot * jnp.sum(hot, axis=(0, 1), keepdims=True)
+        weight = jnp.zeros_like(langs)
+        for g in range(dro_ref.shape[0]):
+            weight = jnp.where(langs == float(g), dro_ref[g], weight)
+        scale_ref[:, own] = (weight * (2.0 * mean_len) / (doc_len + mean_len)).T
 
 
 def conv_kernel(
     mean_len,
+    joint,
     message_ref,
     dro_ref,
     skip_ref,
@@ -255,19 +272,21 @@
     out_ref,
     cross_ref,
     scale_ref,
-    scaled_ref,
+    both_ref,
     taps_mid_ref,
     mid_ref,
     back_ref,
     doc_ref,
     lang_ref,
 ):
-    pieces = message_ref.shape[0]
+    pieces = message_ref.shape[0] // joint
     tokens = message_ref.shape[2]
-    span = skip_ref.shape[1]
-    place, tall = places(pieces, tokens, span)
+    share = skip_ref.shape[1] // 2
+    taps = share // joint
+    place, tall = places(tokens, share)
     width = 2 * tokens
     slab = pieces * ROWS
+    pair = 2 * share
 
     def ahead(m):
         return table_ref[m * width : (m + 1) * width, :]
@@ -275,39 +294,49 @@
     def behind(m):
         return ahead(pieces + m)
 
-    def joint(start, rows, blocks):
-        parts = [slice(start + b * rows, start + (b + 1) * rows) for b in range(blocks)]
+    def blocks(start, rows, count):
+        parts = [slice(start + b * rows, start + (b + 1) * rows) for b in range(count)]
         return jnp.concatenate([table_ref[part, :] for part in parts], axis=1)
 
     start = 2 * pieces * width
     outer_blocks = slab // width
-    outer_table = joint(start, 2 * slab, outer_blocks)
-    inverse_table = joint(start + 2 * slab * outer_blocks, slab, 2 * outer_blocks)
-    token_scale(message_ref, scale_ref, dro_ref, span + tall, mean_len, doc_ref, lang_ref)
-
-    def outer_taps(row):
-        rows = pl.ds(row, ROWS)
-        stack = jnp.concatenate([message_ref[j, rows, :] for j in range(pieces)], axis=0)
-        out = dot(outer_table, stack).astype(bf16)
-        for m in range(pieces):
-            at = 2 * m * ROWS
-            taps_mid_ref[m, rows, :tokens] = out[at : at + ROWS]
-            taps_mid_ref[m, rows, tokens:] = out[at + ROWS : at + 2 * ROWS]
-
-    chunked(span, outer_taps, True)
-    sides = (slice(0, span), slice(span, 2 * span))
-
-    def load(side, j, row):
-        start, lanes = place(side, span)
-        return message_ref[j, pl.ds(start + row, ROWS), lanes]
+    outer_table = blocks(start, 2 * slab, outer_blocks)
+    inverse_table = blocks(start + 2 * slab * outer_blocks, slab, 2 * outer_blocks)
+    token_scale(message_ref, scale_ref, dro_ref, taps + tall, pieces, mean_len, doc_ref, lang_ref)
+
+    for d in range(joint):
+        for row in range(0, taps, ROWS):
+            held = [message_ref[d * pieces + j, row : row + ROWS, :] for j in range(pieces)]
+            out = dot(outer_table, jnp.concatenate(held, axis=0)).astype(bf16)
+            for m in range(pieces):
+                at = 2 * m * ROWS
+                for first in (d * taps + row, share + d * taps + row):
+                    rows = slice(first, first + ROWS)
+                    taps_mid_ref[m, rows, :tokens] = out[at : at + ROWS]
+                    taps_mid_ref[m, rows, tokens:] = out[at + ROWS : at + 2 * ROWS]
+
+    lane = lax.broadcasted_iota(jnp.int32, (ROWS, pair), 1)
+
+    def load(o, row):
+        (one, one_lanes), (two, two_lanes) = place(0, taps), place(1, taps)
+        if one == two:
+            return message_ref[o, pl.ds(one + row, ROWS), slice(one_lanes.start, two_lanes.stop)]
+        return jnp.concatenate(
+            [message_ref[o, pl.ds(first + row, ROWS), :] for first in (one, two)], axis=1
+        )
 
     def outer(row):
         rows = pl.ds(row, ROWS)
         stack = []
         for j in range(pieces):
-            scaled = (load(1, j, row).astype(f32) * scale_ref[rows, j : j + 1]).astype(bf16)
-            scaled_ref[j, rows, :] = scaled
-            stack.append(jnp.concatenate([load(0, j, row), scaled], axis=1))
+            line = []
+            for d in range(joint):
+                o = d * pieces + j
+                factor = jnp.where(lane < share, 1.0, scale_ref[rows, o : o + 1])
+                made = (load(o, row).astype(f32) * factor).astype(bf16)
+                both_ref[o, rows, :] = made
+                line.append(made)
+            stack.append(jnp.concatenate(line, axis=1))
         out = dot(outer_table, jnp.concatenate(stack, axis=0)).astype(bf16)
         for m in range(pieces):
             at = 2 * m * ROWS
@@ -315,21 +344,25 @@
             mid_ref[m, pl.ds(tokens + row, ROWS), :] = out[at + ROWS : at + 2 * ROWS]
 
     chunked(tokens, outer, True)
+    sign = jnp.where(lax.broadcasted_iota(jnp.int32, (tokens, pair), 1) < share, 1.0, -1.0)
 
     def inner(m):
         filt = lax.dot_general(
             ahead(m), taps_mid_ref[m], (((1,), (1,)), ((), ())), preferred_element_type=f32
         )
         spec = dot(ahead(m), mid_ref[m])
-        fre, fim = filt[:tokens], filt[tokens:]
-        xre, xim = spec[:tokens, sides[0]], spec[tokens:, sides[0]]
-        gre, gim = spec[:tokens, sides[1]], spec[tokens:, sides[1]]
-        cross_ref[m, :tokens, :] = (xre * gre + xim * gim).astype(bf16)
-        cross_ref[m, tokens:, :] = (xre * gim - xim * gre).astype(bf16)
-        mixed = jnp.concatenate([fre * xre - fim * xim, fre * xim + fim * xre], axis=0)
-        back = jnp.concatenate([fre * gre + fim * gim, fre * gim - fim * gre], axis=0)
-        both = jnp.concatenate([mixed.astype(bf16), back.astype(bf16)], axis=1)
-        back_ref[m] = dot(behind(m), both).astype(bf16)
+        fre, fim = filt[:tokens], filt[tokens:] * sign
+        cre, cim, prods = 0.0, 0.0, []
+        for d in range(joint):
+            part = slice(d * pair, (d + 1) * pair)
+            re, im = spec[:tokens, part], spec[tokens:, part]
+            xre, gre, xim, gim = re[:, :share], re[:, share:], im[:, :share], im[:, share:]
+            cre, cim = cre + (xre * gre + xim * gim), cim + (xre * gim - xim * gre)
+            prods.append(jnp.concatenate([fre * re - fim * im, fre * im + fim * re], axis=0))
+        cross_ref[m, :tokens, :] = cre.astype(bf16)
+        cross_ref[m, tokens:, :] = cim.astype(bf16)
+        prods = jnp.concatenate([prod.astype(bf16) for prod in prods], axis=1)
+        back_ref[m] = dot(behind(m), prods).astype(bf16)
 
     each_piece(pieces, inner, pieces)
     skip = skip_ref[...]
@@ -340,14 +373,17 @@
         for m in range(pieces):
             stack += [back_ref[m, rows, :], back_ref[m, pl.ds(tokens + row, ROWS), :]]
         out = dot(inverse_table, jnp.concatenate(stack, axis=0))
+        (one, one_lanes), (two, two_lanes) = place(0, 0), place(1, 0)
         for j in range(pieces):
-            at = slice(j * ROWS, (j + 1) * ROWS)
-            for side in (0, 1):
-                start, lanes = place(side, 0)
-                own = load(0, j, row) if side == 0 else scaled_ref[j, rows, :]
-                out_ref[j, pl.ds(start + row, ROWS), lanes] = (
-                    out[at, sides[side]] + skip * own.astype(f32)
-                ).astype(bf16)
+            for d in range(joint):
+                o = d * pieces + j
+                value = out[j * ROWS : (j + 1) * ROWS, d * pair : (d + 1) * pair]
+                value = (value + skip * both_ref[o, rows, :].astype(f32)).astype(bf16)
+                if one == two:
+                    out_ref[o, rows, slice(one_lanes.start, two_lanes.stop)] = value
+                else:
+                    out_ref[o, rows, :] = value[:, :share]
+                    out_ref[o, pl.ds(two + row, ROWS), :] = value[:, share:]
 
     chunked(tokens, outer_back, True)
 
@@ -388,18 +424,22 @@
     out_ref[...] = grad_ref[...].astype(f32) * jnp.sum(scale, axis=1, keepdims=True)
 
 
-def final_kernel(scaled_ref, message_ref, gate_ref, input_ref):
-    pieces = message_ref.shape[0]
+def final_kernel(joint, scaled_ref, message_ref, gate_ref, input_ref):
+    pieces = message_ref.shape[0] // joint
     tokens, channels = scaled_ref.shape
     span = channels // pieces
-    place, _ = places(pieces, tokens, span)
+    share = span // joint
+    place, _ = places(tokens, share)
     mixed_row, mixed_lanes = place(0, 0)
     back_row, back_lanes = place(1, 0)
     for i in range(pieces):
+        owners = [d * pieces + i for d in range(joint)]
+        mixed = [message_ref[o, mixed_row : mixed_row + tokens, mixed_lanes] for o in owners]
+        back = [message_ref[o, back_row : back_row + tokens, back_lanes] for o in owners]
         part = slice(i * span, (i + 1) * span)
-        mixed = message_ref[i, mixed_row : mixed_row + tokens, mixed_lanes].astype(f32)
+        mixed = jnp.concatenate(mixed, axis=1).astype(f32)
         gate_ref[:, part] = (scaled_ref[:, part] * mixed).astype(bf16)
-        input_ref[:, part] = message_ref[i, back_row : back_row + tokens, back_lanes]
+        input_ref[:, part] = jnp.concatenate(back, axis=1)
 
 
 def call(kernel, out, ins, scratch=(), outs=None, room=40 << 20, cost=(0, 0)):
@@ -422,38 +462,49 @@
     length = tokens * pieces
     span = channels // pieces
     mean_len = length / NDOCS
+    tables, behind = all_tables(pieces, tokens)
+    share = span // members
+    joint = members if share * 2 % 128 == 0 and share // members % ROWS == 0 else 1
+    if joint == 1:
+        share = span
+    taps = share // joint
+    axes = ("dp", "ctx") if joint > 1 else "ctx"
     place = lax.axis_index("ctx")
-    own = place.reshape(1)
-    tables, behind = all_tables(pieces, tokens)
-    skip = lax.dynamic_slice_in_dim(skip_gain, place * span, span)[None, :]
+    member = lax.axis_index("dp")
+    first = place * span + (member * share if joint > 1 else 0)
+    own = (place + member * pieces if joint > 1 else place).reshape(1)
+    skip = lax.dynamic_slice_in_dim(skip_gain, first, share)
+    skip = jnp.concatenate([skip, skip])[None, :]
     exchange = functools.partial(
-        lax.all_to_all, axis_name="ctx", split_axis=0, concat_axis=0, tiled=True
+        lax.all_to_all, axis_name=axes, split_axis=0, concat_axis=0, tiled=True
     )
     shape = jax.ShapeDtypeStruct
     dma = pltpu.SemaphoreType.DMA
-    tall = places(pieces, tokens, span)[1]
+    tall = places(tokens, share)[1]
     macs = pieces * (2 * tokens) ** 2 * span
-    message = shape((pieces, span + tall + ROWS, tokens), bf16)
-    answer = shape((pieces, tall, tokens), bf16)
+    count = joint * pieces
+    message = shape((count, taps + tall + ROWS, tokens), bf16)
+    answer = shape((count, tall, tokens), bf16)
     groups = 4
 
     sent = call(
-        functools.partial(prep_kernel, pieces, span),
+        functools.partial(prep_kernel, pieces, joint),
         message,
-        [HBM] * 4 + [VMEM] * 2,
+        [SMEM] + [HBM] * 4 + [VMEM] * 2,
         [
             pltpu.VMEM((tokens, channels), bf16),
             pltpu.VMEM((tokens, channels), bf16),
             pltpu.VMEM((tokens, channels), bf16),
             pltpu.VMEM(message.shape, bf16),
             dma((3, groups)),
-            dma((1,)),
+            dma((joint,)),
             dma((3,)),
         ],
         outs=HBM,
         room=256 << 10,
         cost=(0, 4 << 20),
     )(
+        (member if joint > 1 else jnp.zeros_like(member)).reshape(1),
         saved_input[0],
         grad_out[0],
         gate_value[0],
@@ -462,16 +513,16 @@
         lang_ids,
     )
     sent, cross, scale = call(
-        functools.partial(conv_kernel, mean_len),
-        [answer, shape((pieces, 2 * tokens, span), bf16), shape((tokens, pieces), f32)],
+        functools.partial(conv_kernel, mean_len, joint),
+        [answer, shape((pieces, 2 * tokens, share), bf16), shape((tokens, count), f32)],
         [VMEM, SMEM, VMEM, VMEM],
         [
-            pltpu.VMEM((pieces, tokens, span), bf16),
-            pltpu.VMEM((pieces, span, 2 * tokens), bf16),
-            pltpu.VMEM((pieces, 2 * tokens, 2 * span), bf16),
-            pltpu.VMEM((pieces, 2 * tokens, 2 * span), bf16),
-            pltpu.VMEM((pieces, tokens), f32),
-            pltpu.VMEM((pieces, tokens), f32),
+            pltpu.VMEM((count, tokens, 2 * share), bf16),
+            pltpu.VMEM((pieces, 2 * share, 2 * tokens), bf16),
+            pltpu.VMEM((pieces, 2 * tokens, 2 * share * joint), bf16),
+            pltpu.VMEM((pieces, 2 * tokens, 2 * share * joint), bf16),
+            pltpu.VMEM((count, tokens), f32),
+            pltpu.VMEM((count, tokens), f32),
         ],
         room=(40 << 20) if span % 128 == 0 else (20 << 20),
         cost=(10 * macs, 8 << 20),
@@ -480,20 +531,28 @@
     keep, send = call(
         lags_kernel,
         (
-            jax.ShapeDtypeStruct((span, length // members), f32),
-            jax.ShapeDtypeStruct((members - 1, span, length // members), bf16),
+            shape((share, length // members), f32),
+            shape((members - 1, share, length // members), bf16),
         ),
         [SMEM, VMEM, VMEM],
         [
-            pltpu.VMEM((pieces, 2 * tokens, span), f32),
-            pltpu.VMEM((pieces, tokens, span), f32),
+            pltpu.VMEM((pieces, 2 * tokens, share), f32),
+            pltpu.VMEM((pieces, tokens, share), f32),
         ],
         cost=(2 * macs, 6 << 20),
-    )(lax.axis_index("dp").reshape(1), cross, behind)
-    d_filter = keep
-    for r in range(1, members):
-        ring = [(d, (d + r) % members) for d in range(members)]
-        d_filter = d_filter + lax.ppermute(send[r - 1], "dp", ring).astype(f32)
+    )(member.reshape(1), cross, behind)
+    rings = [[(d, (d + r) % members) for d in range(members)] for r in range(members)]
+    came = [lax.ppermute(send[r - 1], "dp", rings[r]).astype(f32) for r in range(1, members)]
+    if joint > 1:
+        came = jnp.stack([keep] + came)
+        d_filter = jnp.concatenate(
+            [
+                lax.dynamic_index_in_dim(came, (member - d) % members, 0, keepdims=False)
+                for d in range(members)
+            ]
+        )
+    else:
+        d_filter = sum(came, keep)
     token_block = jax.ShapeDtypeStruct((tokens, channels), bf16)
     scaled = call(
         scaled_kernel,
@@ -502,7 +561,7 @@
         cost=(0, 2 << 20),
     )(own, grad_out[0], scale)
     d_gate, d_input = call(
-        final_kernel,
+        functools.partial(final_kernel, joint),
         (token_block, token_block),
         [VMEM, VMEM],
         cost=(0, 4 << 20),

time: 90.3 us -> 91.3 us (1.011); the launches traced: 88.8 us -> 90.9 us
  starting transfers between devices: 18.5 us -> 11.8 us
  waiting for transfers between devices: 49.7 us -> 55.6 us
  local copies, waits for them, and re-layouts: 4.02 us -> 5.7 us
  Pallas kernels: 15 us -> 16 us
    all_to_all x1, starting transfers between devices: 9.51 us -> 2.78 us  [local(): got = exchange(sent)]
    all_to_all x1, waiting for transfers between devices: 9.71 us -> 13.5 us  [local(): got = exchange(sent)]
    all_to_all x1, waiting for transfers between devices: 33 us -> 35 us  [local(): exchange(sent)]
    pallas_call x4, Pallas kernels: 14.8 us -> 15.9 us  [the longest x1 8.7 us: local(): call(functools.partial(conv_kernel, mean_len, joint), [answer, shape((pie...]
    unnamed x10 -> x12, local copies, waits for them, and re-layouts: 3.94 us -> 4.93 us
  transfers between devices with their start and end apart: 3 -> 3, of which waited for: 3 -> 3; matrix products, arithmetic and copies ran while one was open for 1% -> 2% of each run, Pallas kernels for 2% -> 2%
where the time goes in v10:
time: 91.3 us; the launch traced here: 90.9 us
  waiting for transfers between devices  55.6 us (61%)
  Pallas kernels  16 us (18%)
  starting transfers between devices  11.8 us (13%)
  local copies, waits for them, and re-layouts  5.7 us (6%)
  other arithmetic  1.04 us (1%)
    all_to_all x1, waiting for transfers between devices, local(): exchange(sent)  35 us
    all_to_all x1, waiting for transfers between devices, local(): got = exchange(sent)  13.5 us
    pallas_call x1, Pallas kernels, local(): call(functools.partial(conv_kernel, mean_len, joint), [answer, shape((pie...  8.7 us
    all_to_all x1, starting transfers between devices, local(): exchange(sent)  7.3 us
    ppermute x1, waiting for transfers between devices, local(): lax.ppermute(send[r - 1], 'dp', rings[r]).astype(f32)  7.19 us
    unnamed x12, local copies, waits for them, and re-layouts  4.93 us
    pallas_call x1, Pallas kernels, local(): call(functools.partial(prep_kernel, pieces, joint), message, [SMEM] + [HB...  3.74 us
    all_to_all x1, starting transfers between devices, local(): got = exchange(sent)  2.78 us
  transfers between devices with their start and end apart: 3, of which 3 were waited for; matrix products, arithmetic and copies ran while one was open for 2% of the time, Pallas kernels for 2%

profile of v10, /device:TPU:0, one launch (start us, length us, event | category | flops | bytes accessed | tf_op | source)
XLA Modules:
  0.0 90.9 jit_solution(2766304377197420778)
XLA Ops:
  0.6 3.7 %shard_map.121 = bf16[32,176,128]{2,1,0:T(8,128)(2,1)} custom-call(s32[1]{0:T(128)} %bitcast.2.own_ref, bf16[128,2048]{1,0:T(8,128)(2,1)} %bitcast.23, bf16[128,2048]{1,0:T(8,128)(2,1)} %bitcast.19, bf16[128,2048]{1,0:T(8,128)(2,1)} %bitcast.24, bf16[16,128,128]{2,1,0:T(8,128)(2,1)} %bitcast.25, s32[1,128]{1,0:T(1,128)} %doc_ref.1, s32[1,128]{1,0:T(1,128)} %lang_ref.1), custom_call_target="tpu_custom_call" | custom-call | bytes 4194304 | tf_op jit(solution)/shard_map/pallas_call | solution.py:490
  4.4 0.0 copy-start.5
  4.4 7.3 %all-to-all-start = ((bf16[32,176,128]{2,1,0:T(8,128)(2,1)}), bf16[32,176,128]{2,1,0:T(8,128)(2,1)S(1)}, u32[]{:S(2)}, u32[]{:S(2)}) async-start(bf16[32,176,128]{2,1,0:T(8,128)(2,1)} %shard_map.121), calls=%async_computation | async-start | bytes 2883584 | tf_op jit(solution)/shard_map/all_to_all | solution.py:529
  11.7 0.8 dynamic_slice.10
  12.5 0.1 maximum_bitcast_fusion.skip_ref
  12.6 35.0 %all-to-all-done.message_ref = bf16[32,176,128]{2,1,0:T(8,128)(2,1)S(1)} async-done(((bf16[32,176,128]{2,1,0:T(8,128)(2,1)}), bf16[32,176,128]{2,1,0:T(8,128)(2,1)S(1)}, u32[]{:S(2)}, u32[]{:S(2)}) %all-to-all-start) | async-done | bytes 1441824 | tf_op jit(solution)/shard_map/all_to_all | solution.py:529
  47.5 0.0 copy-done.5
  47.5 0.0 copy-start
  47.5 2.3 %copy-done = bf16[9216,256]{1,0:T(8,128)(2,1)S(1)} copy-done((bf16[9216,256]{1,0:T(8,128)(2,1)S(1)}, bf16[9216,256]{1,0:T(8,128)(2,1)}, u32[]{:S(2)}) %copy-start) | copy-done | bytes 4718616
  49.8 8.7 %shard_map.122 = (bf16[32,128,128]{2,1,0:T(8,128)(2,1)}, bf16[16,256,64]{2,1,0:T(8,128)(2,1)S(1)}, f32[128,32]{1,0:T(8,128)S(1)}) custom-call(bf16[32,176,128]{2,1,0:T(8,128)(2,1)S(1)} %all-to-all-done.message_ref, f32[16]{0:T(128)S(1)} %copy-done.5, f32[1,128]{1,0:T(1,128)S(1)} %maximum_bitcast_fusion.skip_ref, bf16[9216,256]{1,0:T(8,128)(2,1)S(1)} %copy-done), custom_call_target="tpu_custom_call" | custom-call | flops 1342177280 | bytes 8388608 | tf_op jit(solution)/shard_map/pallas_call | solution.py:515
  58.5 0.0 copy-start.3
  58.6 1.0 %copy-done.3 = bf16[16,256,64]{2,1,0:T(8,128)(2,1)} copy-done((bf16[16,256,64]{2,1,0:T(8,128)(2,1)}, bf16[16,256,64]{2,1,0:T(8,128)(2,1)S(1)}, u32[]{:S(2)}) %copy-start.3) | copy-done | bytes 524312
  59.5 0.0 copy-start.4
  59.5 2.8 %all-to-all-start.1 = ((bf16[32,128,128]{2,1,0:T(8,128)(2,1)}), bf16[32,128,128]{2,1,0:T(8,128)(2,1)S(1)}, u32[]{:S(2)}, u32[]{:S(2)}) async-start(bf16[32,128,128]{2,1,0:T(8,128)(2,1)} %get-tuple-element.11), calls=%async_computation.1 | async-start | bytes 2097152 | tf_op jit(solution)/shard_map/all_to_all | solution.py:530
  62.3 0.0 copy-done.4
  62.3 0.0 copy-start.1
  62.4 1.6 %copy-done.1 = bf16[16,256,256]{2,1,0:T(8,128)(2,1)S(1)} copy-done((bf16[16,256,256]{2,1,0:T(8,128)(2,1)S(1)}, bf16[16,256,256]{2,1,0:T(8,128)(2,1)}, u32[]{:S(2)}) %copy-start.1) | copy-done | bytes 2097176
  63.9 0.0 copy-start.2
  63.9 2.1 %shard_map.125 = (f32[64,1024]{1,0:T(8,128)S(1)}, bf16[1,64,1024]{2,1,0:T(8,128)(2,1)S(1)}) custom-call(s32[1]{0:T(128)} %bitcast.2.own_ref, bf16[16,256,64]{2,1,0:T(8,128)(2,1)S(1)} %copy-done.4, bf16[16,256,256]{2,1,0:T(8,128)(2,1)S(1)} %copy-done.1), custom_call_target="tpu_custom_call" | custom-call | flops 268435456 | bytes 6291456 | tf_op jit(solution)/shard_map/pallas_call | solution.py:531
  66.0 1.7 %collective-permute-start = (bf16[64,1024]{1,0:T(8,128)(2,1)S(1)}, bf16[64,1024]{1,0:T(8,128)(2,1)S(1)}, u32[]{:S(2)}, u32[]{:S(2)}) collective-permute-start(bf16[64,1024]{1,0:T(8,128)(2,1)S(1)} %bitcast.22), channel_id=1, source_target_pairs={{0,16},{16,0},{1,17},{17,1},{2,18},{18,2},{3,19},{19,3},{4,20},{20... | collective-permute-start | bytes 393224 | tf_op jit(solution)/shard_map/ppermute | solution.py:545
  67.7 0.0 copy-done.2
  67.7 0.1 shard_map.123.scaled_ref
  67.9 7.2 %collective-permute-done = bf16[64,1024]{1,0:T(8,128)(2,1)S(1)} collective-permute-done((bf16[64,1024]{1,0:T(8,128)(2,1)S(1)}, bf16[64,1024]{1,0:T(8,128)(2,1)S(1)}, u32[]{:S(2)}, u32[]{:S(2)}) %collective-permute-start) | collective-permute-done | bytes 131104 | tf_op jit(solution)/shard_map/ppermute | solution.py:545
  75.1 0.1 fusion.3
  75.2 0.8 pad_maximum_fusion
  76.0 13.5 %all-to-all-done.1.message_ref = bf16[32,128,128]{2,1,0:T(8,128)(2,1)S(1)} async-done(((bf16[32,128,128]{2,1,0:T(8,128)(2,1)}), bf16[32,128,128]{2,1,0:T(8,128)(2,1)S(1)}, u32[]{:S(2)}, u32[]{:S(2)}) %all-to-all-start.1) | async-done | bytes 1048608 | tf_op jit(solution)/shard_map/all_to_all | solution.py:530
  89.5 1.4 %shard_map.124 = (bf16[128,2048]{1,0:T(8,128)(2,1)}, bf16[128,2048]{1,0:T(8,128)(2,1)}) custom-call(f32[128,2048]{1,0:T(8,128)S(1)} %shard_map.123.scaled_ref, bf16[32,128,128]{2,1,0:T(8,128)(2,1)S(1)} %all-to-all-done.1.message_ref), custom_call_target="tpu_custom_call" | custom-call | bytes 4194304 | tf_op jit(solution)/shard_map/pallas_call | solution.py:563
  (1 shorter events, 0.0 us)
Async XLA Ops:
  4.4 43.1 %copy-start.5 = (f32[16]{0:T(128)S(1)}, f32[16]{0:T(128)}, u32[]{:S(2)}) copy-start(f32[16]{0:T(128)} %dro_ref.1) | copy-start | bytes 196
  4.4 43.1 %all-to-all-start = ((bf16[32,176,128]{2,1,0:T(8,128)(2,1)}), bf16[32,176,128]{2,1,0:T(8,128)(2,1)S(1)}, u32[]{:S(2)}, u32[]{:S(2)}) async-start(bf16[32,176,128]{2,1,0:T(8,128)(2,1)} %shard_map.121), calls=%async_computation | async-start | bytes 2883584 | tf_op jit(solution)/shard_map/all_to_all | solution.py:529
  47.5 2.3 %copy-start = (bf16[9216,256]{1,0:T(8,128)(2,1)S(1)}, bf16[9216,256]{1,0:T(8,128)(2,1)}, u32[]{:S(2)}) copy-start(bf16[9216,256]{1,0:T(8,128)(2,1)} %constant.48.clone.table_ref) | copy-start | bytes 14155780
  58.5 1.0 %copy-start.3 = (bf16[16,256,64]{2,1,0:T(8,128)(2,1)}, bf16[16,256,64]{2,1,0:T(8,128)(2,1)S(1)}, u32[]{:S(2)}) copy-start(bf16[16,256,64]{2,1,0:T(8,128)(2,1)S(1)} %get-tuple-element.14.cross_ref) | copy-start | bytes 1572868
  59.5 2.8 %copy-start.4 = (bf16[16,256,64]{2,1,0:T(8,128)(2,1)S(1)}, bf16[16,256,64]{2,1,0:T(8,128)(2,1)}, u32[]{:S(2)}) copy-start(bf16[16,256,64]{2,1,0:T(8,128)(2,1)} %copy-done.3) | copy-start | bytes 1572868
  59.5 30.0 %all-to-all-start.1 = ((bf16[32,128,128]{2,1,0:T(8,128)(2,1)}), bf16[32,128,128]{2,1,0:T(8,128)(2,1)S(1)}, u32[]{:S(2)}, u32[]{:S(2)}) async-start(bf16[32,128,128]{2,1,0:T(8,128)(2,1)} %get-tuple-element.11), calls=%async_computation.1 | async-start | bytes 2097152 | tf_op jit(solution)/shard_map/all_to_all | solution.py:530
  62.3 1.6 %copy-start.1 = (bf16[16,256,256]{2,1,0:T(8,128)(2,1)S(1)}, bf16[16,256,256]{2,1,0:T(8,128)(2,1)}, u32[]{:S(2)}) copy-start(bf16[16,256,256]{2,1,0:T(8,128)(2,1)} %constant.49.clone.behind_ref) | copy-start | bytes 6291460
  63.9 3.8 %copy-start.2 = (bf16[1,128,2048]{2,1,0:T(8,128)(2,1)S(1)}, bf16[1,128,2048]{2,1,0:T(8,128)(2,1)}, u32[]{:S(2)}) copy-start(bf16[1,128,2048]{2,1,0:T(8,128)(2,1)} %param.10) | copy-start | bytes 1572868
  66.0 9.0 %collective-permute-start = (bf16[64,1024]{1,0:T(8,128)(2,1)S(1)}, bf16[64,1024]{1,0:T(8,128)(2,1)S(1)}, u32[]{:S(2)}, u32[]{:S(2)}) collective-permute-start(bf16[64,1024]{1,0:T(8,128)(2,1)S(1)} %bitcast.22), channel_id=1, source_target_pairs={{0,16},{16,0},{1,17},{17,1},{2,18},{18,2},{3,19},{19,3},{4,20},{20... | collective-permute-start | bytes 393224 | tf_op jit(solution)/shard_map/ppermute | solution.py:545

commit v11 on v10

--- a/solution.py
+++ b/solution.py
@@ -52,7 +52,6 @@
     outer, inverse = outer_tables(pieces)
     parts = [
         ahead.reshape(-1, width),
-        behind.reshape(-1, width),
         side_by_side(outer, width),
         side_by_side(inverse, width),
     ]
@@ -195,11 +194,11 @@
     place, tall = places(tokens, share)
     in_row, in_lanes = place(0, taps)
     grad_row, grad_lanes = place(1, taps)
-    owners = [(d, i) for d in range(joint) for i in range(pieces)]
+    owners = [(i, d) for i in range(pieces) for d in range(joint)]
 
     def send(part, start, size):
         rows = pl.ds(start, size)
-        return copies((made_ref.at[:, rows, :], out_hbm.at[:, rows, :], out_sem.at[part]))
+        return copies((made_ref.at[:, :, rows, :], out_hbm.at[:, :, rows, :], out_sem.at[part]))
 
     input_in = row_copies(input_hbm, input_ref, in_sem.at[2])
     grad_in = row_copies(grad_hbm, grad_ref, in_sem.at[0])
@@ -210,23 +209,23 @@
         taps_in += copies(
             (
                 taps_hbm.at[:, pl.ds(start, taps), :],
-                made_ref.at[pl.ds(d * pieces, pieces), pl.ds(0, taps), :],
+                made_ref.at[:, d, pl.ds(0, taps), :],
                 taps_sem.at[d],
             )
         )
     tile = lax.broadcasted_iota(jnp.int32, (ROWS, tokens), 0)
     ids = jnp.where(tile == 0, doc_ref[...], lang_ref[...]).astype(f32).astype(bf16)
-    for o in range(len(owners)):
-        made_ref[o, taps + tall :, :] = ids
+    for i, d in owners:
+        made_ref[i, d, taps + tall :, :] = ids
     group = tokens // groups
     sent = []
     for g in range(groups):
         finish(input_in[g])
         rows = slice(g * group, (g + 1) * group)
         at = slice(in_row + g * group, in_row + (g + 1) * group)
-        for o, (d, i) in enumerate(owners):
+        for i, d in owners:
             part = slice(i * span + d * share, i * span + (d + 1) * share)
-            made_ref[o, at, in_lanes] = input_ref[rows, part]
+            made_ref[i, d, at, in_lanes] = input_ref[rows, part]
     finish(*taps_in)
     sent += send(0, 0, taps if grad_row == in_row else grad_row)
     for g in range(groups):
@@ -234,9 +233,9 @@
         rows = slice(g * group, (g + 1) * group)
         at = slice(grad_row + g * group, grad_row + (g + 1) * group)
         made = (grad_ref[rows, :].astype(f32) * gate_ref[rows, :].astype(f32)).astype(bf16)
-        for o, (d, i) in enumerate(owners):
+        for i, d in owners:
             part = slice(i * span + d * share, i * span + (d + 1) * share)
-            made_ref[o, at, grad_lanes] = made[:, part]
+            made_ref[i, d, at, grad_lanes] = made[:, part]
         if g == groups // 2 - 1:
             sent += send(1, grad_row, (g + 1) * group)
     start = grad_row + tokens // 2
@@ -245,10 +244,12 @@
 
 
 def token_scale(message_ref, scale_ref, dro_ref, ids, pieces, mean_len, doc_ref, lang_ref):
-    for j in range(message_ref.shape[0]):
-        rows = message_ref[j, ids:, :].astype(f32)
-        doc_ref[j : j + 1, :] = rows[0:1]
-        lang_ref[j : j + 1, :] = rows[1:2]
+    joint = message_ref.shape[0] // pieces
+    for o in range(message_ref.shape[0]):
+        rows = message_ref[o, ids:, :].astype(f32)
+        at = (o % joint) * pieces + o // joint
+        doc_ref[at : at + 1, :] = rows[0:1]
+        lang_ref[at : at + 1, :] = rows[1:2]
     for start in range(0, message_ref.shape[0], pieces):
         own = slice(start, start + pieces)
         docs, langs = doc_ref[own, :], lang_ref[own, :]
@@ -269,6 +270,7 @@
     dro_ref,
     skip_ref,
     table_ref,
+    behind_ref,
     out_ref,
     cross_ref,
     scale_ref,
@@ -291,14 +293,11 @@
     def ahead(m):
         return table_ref[m * width : (m + 1) * width, :]
 
-    def behind(m):
-        return ahead(pieces + m)
-
     def blocks(start, rows, count):
         parts = [slice(start + b * rows, start + (b + 1) * rows) for b in range(count)]
         return jnp.concatenate([table_ref[part, :] for part in parts], axis=1)
 
-    start = 2 * pieces * width
+    start = pieces * width
     outer_blocks = slab // width
     outer_table = blocks(start, 2 * slab, outer_blocks)
     inverse_table = blocks(start + 2 * slab * outer_blocks, slab, 2 * outer_blocks)
@@ -306,7 +305,7 @@
 
     for d in range(joint):
         for row in range(0, taps, ROWS):
-            held = [message_ref[d * pieces + j, row : row + ROWS, :] for j in range(pieces)]
+            held = [message_ref[j * joint + d, row : row + ROWS, :] for j in range(pieces)]
             out = dot(outer_table, jnp.concatenate(held, axis=0)).astype(bf16)
             for m in range(pieces):
                 at = 2 * m * ROWS
@@ -331,8 +330,9 @@
         for j in range(pieces):
             line = []
             for d in range(joint):
-                o = d * pieces + j
-                factor = jnp.where(lane < share, 1.0, scale_ref[rows, o : o + 1])
+                o = j * joint + d
+                at = d * pieces + j
+                factor = jnp.where(lane < share, 1.0, scale_ref[rows, at : at + 1])
                 made = (load(o, row).astype(f32) * factor).astype(bf16)
                 both_ref[o, rows, :] = made
                 line.append(made)
@@ -362,7 +362,7 @@
         cross_ref[m, :tokens, :] = cre.astype(bf16)
         cross_ref[m, tokens:, :] = cim.astype(bf16)
         prods = jnp.concatenate([prod.astype(bf16) for prod in prods], axis=1)
-        back_ref[m] = dot(behind(m), prods).astype(bf16)
+        back_ref[m] = dot(behind_ref[m], prods).astype(bf16)
 
     each_piece(pieces, inner, pieces)
     skip = skip_ref[...]
@@ -376,7 +376,7 @@
         (one, one_lanes), (two, two_lanes) = place(0, 0), place(1, 0)
         for j in range(pieces):
             for d in range(joint):
-                o = d * pieces + j
+                o = j * joint + d
                 value = out[j * ROWS : (j + 1) * ROWS, d * pair : (d + 1) * pair]
                 value = (value + skip * both_ref[o, rows, :].astype(f32)).astype(bf16)
                 if one == two:
@@ -433,7 +433,7 @@
     mixed_row, mixed_lanes = place(0, 0)
     back_row, back_lanes = place(1, 0)
     for i in range(pieces):
-        owners = [d * pieces + i for d in range(joint)]
+        owners = [i * joint + d for d in range(joint)]
         mixed = [message_ref[o, mixed_row : mixed_row + tokens, mixed_lanes] for o in owners]
         back = [message_ref[o, back_row : back_row + tokens, back_lanes] for o in owners]
         part = slice(i * span, (i + 1) * span)
@@ -468,7 +468,7 @@
     if joint == 1:
         share = span
     taps = share // joint
-    axes = ("dp", "ctx") if joint > 1 else "ctx"
+    axes = ("ctx", "dp") if joint > 1 else "ctx"
     place = lax.axis_index("ctx")
     member = lax.axis_index("dp")
     first = place * span + (member * share if joint > 1 else 0)
@@ -483,7 +483,7 @@
     tall = places(tokens, share)[1]
     macs = pieces * (2 * tokens) ** 2 * span
     count = joint * pieces
-    message = shape((count, taps + tall + ROWS, tokens), bf16)
+    message = shape((pieces, joint, taps + tall + ROWS, tokens), bf16)
     answer = shape((count, tall, tokens), bf16)
     groups = 4
 
@@ -515,7 +515,7 @@
     sent, cross, scale = call(
         functools.partial(conv_kernel, mean_len, joint),
         [answer, shape((pieces, 2 * tokens, share), bf16), shape((tokens, count), f32)],
-        [VMEM, SMEM, VMEM, VMEM],
+        [VMEM, SMEM, VMEM, VMEM, VMEM],
         [
             pltpu.VMEM((count, tokens, 2 * share), bf16),
             pltpu.VMEM((pieces, 2 * share, 2 * tokens), bf16),
@@ -526,7 +526,7 @@
         ],
         room=(40 << 20) if span % 128 == 0 else (20 << 20),
         cost=(10 * macs, 8 << 20),
-    )(exchange(sent), dro_weight, skip, tables)
+    )(exchange(sent.reshape(count, -1, tokens)), dro_weight, skip, tables, behind)
     got = exchange(sent)
     keep, send = call(
         lags_kernel,

time: 91.3 us -> 90.1 us (0.987)
  waiting for transfers between devices: 55.6 us -> 52.2 us
  local copies, waits for them, and re-layouts: 5.7 us -> 7.39 us
    all_to_all x1, waiting for transfers between devices: 13.5 us -> 11.2 us  [local(): got = exchange(sent)]
    unnamed x12 -> x18, local copies, waits for them, and re-layouts: 4.93 us -> 6.62 us
    all_to_all x1, waiting for transfers between devices: 35 us -> 33.8 us  [local(): exchange(sent.reshape(count, -1, tokens))]
    pallas_call x1, Pallas kernels: 8.7 us -> 7.66 us  [local(): call(functools.partial(conv_kernel, mean_len, joint), [answer, shape((pie...]
  transfers between devices with their start and end apart: 3 -> 3, of which waited for: 3 -> 3; matrix products, arithmetic and copies ran while one was open for 2% -> 2% of each run, Pallas kernels for 2% -> 3%
where the time goes in v11:
time: 90.1 us; the launch traced here: 89.6 us
  waiting for transfers between devices  52.2 us (58%)
  Pallas kernels  15.6 us (17%)
  starting transfers between devices  12.7 us (14%)
  local copies, waits for them, and re-layouts  7.39 us (8%)
  other arithmetic  1.04 us (1%)
    all_to_all x1, waiting for transfers between devices, local(): exchange(sent.reshape(count, -1, tokens))  33.8 us
    all_to_all x1, waiting for transfers between devices, local(): got = exchange(sent)  11.2 us
    pallas_call x1, Pallas kernels, local(): call(functools.partial(conv_kernel, mean_len, joint), [answer, shape((pie...  7.66 us
    all_to_all x1, starting transfers between devices, local(): exchange(sent.reshape(count, -1, tokens))  7.3 us
    ppermute x1, waiting for transfers between devices, local(): lax.ppermute(send[r - 1], 'dp', rings[r]).astype(f32)  7.18 us
    unnamed x18, local copies, waits for them, and re-layouts  6.62 us
    pallas_call x1, Pallas kernels, local(): call(functools.partial(prep_kernel, pieces, joint), message, [SMEM] + [HB...  3.72 us
    all_to_all x1, starting transfers between devices, local(): got = exchange(sent)  3.62 us
  transfers between devices with their start and end apart: 3, of which 3 were waited for; matrix products, arithmetic and copies ran while one was open for 2% of the time, Pallas kernels for 3%

profile of v11, /device:TPU:0, one launch (start us, length us, event | category | flops | bytes accessed | tf_op | source)
XLA Modules:
  0.0 89.6 jit_solution(12989297136814781038)
XLA Ops:
  0.6 3.7 %shard_map.121 = bf16[16,2,176,128]{3,2,1,0:T(8,128)(2,1)} custom-call(s32[1]{0:T(128)} %bitcast.2.own_ref, bf16[128,2048]{1,0:T(8,128)(2,1)} %bitcast.24, bf16[128,2048]{1,0:T(8,128)(2,1)} %bitcast.20, bf16[128,2048]{1,0:T(8,128)(2,1)} %bitcast.25, bf16[16,128,128]{2,1,0:T(8,128)(2,1)} %bitcast.26, s32[1,128]{1,0:T(1,128)} %doc_ref.1, s32[1,128]{1,0:T(1,128)} %lang_ref.1), custom_call_target="tpu_custom_call" | custom-call | bytes 4194304 | tf_op jit(solution)/shard_map/pallas_call | solution.py:490
  4.4 0.0 copy-start
  4.4 0.0 copy-start.8
  4.4 7.3 %all-to-all-start = ((bf16[32,176,128]{2,1,0:T(8,128)(2,1)}), bf16[32,176,128]{2,1,0:T(8,128)(2,1)S(1)}, u32[]{:S(2)}, u32[]{:S(2)}) async-start(bf16[32,176,128]{2,1,0:T(8,128)(2,1)} %bitcast.23), calls=%async_computation | async-start | bytes 2883584 | tf_op jit(solution)/shard_map/all_to_all | solution.py:529
  11.7 0.8 dynamic_slice.10
  12.5 0.1 maximum_bitcast_fusion.skip_ref
  12.6 33.8 %all-to-all-done.message_ref = bf16[32,176,128]{2,1,0:T(8,128)(2,1)S(1)} async-done(((bf16[32,176,128]{2,1,0:T(8,128)(2,1)}), bf16[32,176,128]{2,1,0:T(8,128)(2,1)S(1)}, u32[]{:S(2)}, u32[]{:S(2)}) %all-to-all-start) | async-done | bytes 1441824 | tf_op jit(solution)/shard_map/all_to_all | solution.py:529
  46.4 0.0 copy-done
  46.4 0.0 copy-done.8
  46.4 0.0 copy-start.1
  46.4 1.7 %copy-done.1 = bf16[5120,256]{1,0:T(8,128)(2,1)S(1)} copy-done((bf16[5120,256]{1,0:T(8,128)(2,1)S(1)}, bf16[5120,256]{1,0:T(8,128)(2,1)}, u32[]{:S(2)}) %copy-start.1) | copy-done | bytes 2621464
  48.1 7.7 %shard_map.122 = (bf16[32,128,128]{2,1,0:T(8,128)(2,1)S(1)}, bf16[16,256,64]{2,1,0:T(8,128)(2,1)S(1)}, f32[128,32]{1,0:T(8,128)S(1)}) custom-call(bf16[32,176,128]{2,1,0:T(8,128)(2,1)S(1)} %all-to-all-done.message_ref, f32[16]{0:T(128)S(1)} %copy-done.8, f32[1,128]{1,0:T(1,128)S(1)} %maximum_bitcast_fusion.skip_ref, bf16[5120,256]{1,0:T(8,128)(2,1)S(1)} %copy-done.1, ...), custom_call_target="tpu_custom_call" | custom-call | flops 1342177280 | bytes 8388608 | tf_op jit(solution)/shard_map/pallas_call | solution.py:515
  55.8 0.0 copy-start.3
  55.8 1.0 %copy-done.3 = bf16[32,128,128]{2,1,0:T(8,128)(2,1)} copy-done((bf16[32,128,128]{2,1,0:T(8,128)(2,1)}, bf16[32,128,128]{2,1,0:T(8,128)(2,1)S(1)}, u32[]{:S(2)}) %copy-start.3) | copy-done | bytes 1048600
  56.8 0.0 copy-start.4
  56.8 1.0 %copy-done.4 = bf16[16,256,64]{2,1,0:T(8,128)(2,1)} copy-done((bf16[16,256,64]{2,1,0:T(8,128)(2,1)}, bf16[16,256,64]{2,1,0:T(8,128)(2,1)S(1)}, u32[]{:S(2)}) %copy-start.4) | copy-done | bytes 524312
  57.8 0.0 copy-start.6
  57.8 0.6 copy-done.6
  58.4 3.6 %all-to-all-start.1 = ((bf16[32,128,128]{2,1,0:T(8,128)(2,1)}), bf16[32,128,128]{2,1,0:T(8,128)(2,1)S(1)}, u32[]{:S(2)}, u32[]{:S(2)}) async-start(bf16[32,128,128]{2,1,0:T(8,128)(2,1)} %copy-done.3), calls=%async_computation.1 | async-start | bytes 2097152 | tf_op jit(solution)/shard_map/all_to_all | solution.py:530
  62.0 0.0 copy-start.5
  62.0 1.2 %copy-done.5 = bf16[16,256,64]{2,1,0:T(8,128)(2,1)S(1)} copy-done((bf16[16,256,64]{2,1,0:T(8,128)(2,1)S(1)}, bf16[16,256,64]{2,1,0:T(8,128)(2,1)}, u32[]{:S(2)}) %copy-start.5) | copy-done | bytes 524312
  63.2 0.0 copy-start.7
  63.3 2.7 %shard_map.125 = (f32[64,1024]{1,0:T(8,128)S(1)}, bf16[1,64,1024]{2,1,0:T(8,128)(2,1)}) custom-call(s32[1]{0:T(128)} %bitcast.2.own_ref, bf16[16,256,64]{2,1,0:T(8,128)(2,1)S(1)} %copy-done.5, bf16[16,256,256]{2,1,0:T(8,128)(2,1)S(1)} %copy-done), custom_call_target="tpu_custom_call" | custom-call | flops 268435456 | bytes 6291456 | tf_op jit(solution)/shard_map/pallas_call | solution.py:531
  66.0 1.8 %collective-permute-start = (bf16[64,1024]{1,0:T(8,128)(2,1)}, bf16[64,1024]{1,0:T(8,128)(2,1)S(1)}, u32[]{:S(2)}, u32[]{:S(2)}) collective-permute-start(bf16[64,1024]{1,0:T(8,128)(2,1)} %bitcast.11), channel_id=1, source_target_pairs={{0,16},{16,0},{1,17},{17,1},{2,18},{18,2},{3,19},{19,3},{4,20},{20... | collective-permute-start | bytes 393224 | tf_op jit(solution)/shard_map/ppermute | solution.py:545
  67.7 0.0 copy-done.7
  67.7 1.0 %copy-done.2 = bf16[1,128,2048]{2,1,0:T(8,128)(2,1)S(1)} copy-done((bf16[1,128,2048]{2,1,0:T(8,128)(2,1)S(1)}, bf16[1,128,2048]{2,1,0:T(8,128)(2,1)}, u32[]{:S(2)}) %copy-start.2) | copy-done | bytes 524312
  68.8 0.1 shard_map.123.scaled_ref
  68.9 7.2 %collective-permute-done = bf16[64,1024]{1,0:T(8,128)(2,1)S(1)} collective-permute-done((bf16[64,1024]{1,0:T(8,128)(2,1)}, bf16[64,1024]{1,0:T(8,128)(2,1)S(1)}, u32[]{:S(2)}, u32[]{:S(2)}) %collective-permute-start) | collective-permute-done | bytes 131104 | tf_op jit(solution)/shard_map/ppermute | solution.py:545
  76.1 0.1 fusion.3
  76.3 0.8 pad_maximum_fusion
  77.1 11.2 %all-to-all-done.1.message_ref = bf16[32,128,128]{2,1,0:T(8,128)(2,1)S(1)} async-done(((bf16[32,128,128]{2,1,0:T(8,128)(2,1)}), bf16[32,128,128]{2,1,0:T(8,128)(2,1)S(1)}, u32[]{:S(2)}, u32[]{:S(2)}) %all-to-all-start.1) | async-done | bytes 1048608 | tf_op jit(solution)/shard_map/all_to_all | solution.py:530
  88.3 1.4 %shard_map.124 = (bf16[128,2048]{1,0:T(8,128)(2,1)}, bf16[128,2048]{1,0:T(8,128)(2,1)}) custom-call(f32[128,2048]{1,0:T(8,128)S(1)} %shard_map.123.scaled_ref, bf16[32,128,128]{2,1,0:T(8,128)(2,1)S(1)} %all-to-all-done.1.message_ref), custom_call_target="tpu_custom_call" | custom-call | bytes 4194304 | tf_op jit(solution)/shard_map/pallas_call | solution.py:563
  (2 shorter events, 0.0 us)
Async XLA Ops:
  4.4 42.0 %copy-start = (bf16[16,256,256]{2,1,0:T(8,128)(2,1)S(1)}, bf16[16,256,256]{2,1,0:T(8,128)(2,1)}, u32[]{:S(2)}) copy-start(bf16[16,256,256]{2,1,0:T(8,128)(2,1)} %constant.49.clone.behind_ref) | copy-start | bytes 6291460
  4.4 42.0 %copy-start.8 = (f32[16]{0:T(128)S(1)}, f32[16]{0:T(128)}, u32[]{:S(2)}) copy-start(f32[16]{0:T(128)} %dro_ref.1) | copy-start | bytes 196
  4.4 42.0 %all-to-all-start = ((bf16[32,176,128]{2,1,0:T(8,128)(2,1)}), bf16[32,176,128]{2,1,0:T(8,128)(2,1)S(1)}, u32[]{:S(2)}, u32[]{:S(2)}) async-start(bf16[32,176,128]{2,1,0:T(8,128)(2,1)} %bitcast.23), calls=%async_computation | async-start | bytes 2883584 | tf_op jit(solution)/shard_map/all_to_all | solution.py:529
  46.4 1.7 %copy-start.1 = (bf16[5120,256]{1,0:T(8,128)(2,1)S(1)}, bf16[5120,256]{1,0:T(8,128)(2,1)}, u32[]{:S(2)}) copy-start(bf16[5120,256]{1,0:T(8,128)(2,1)} %constant.48.clone.table_ref) | copy-start | bytes 7864324
  55.8 1.0 %copy-start.3 = (bf16[32,128,128]{2,1,0:T(8,128)(2,1)}, bf16[32,128,128]{2,1,0:T(8,128)(2,1)S(1)}, u32[]{:S(2)}) copy-start(bf16[32,128,128]{2,1,0:T(8,128)(2,1)S(1)} %get-tuple-element.11) | copy-start | bytes 3145732
  56.8 1.0 %copy-start.4 = (bf16[16,256,64]{2,1,0:T(8,128)(2,1)}, bf16[16,256,64]{2,1,0:T(8,128)(2,1)S(1)}, u32[]{:S(2)}) copy-start(bf16[16,256,64]{2,1,0:T(8,128)(2,1)S(1)} %get-tuple-element.14.cross_ref) | copy-start | bytes 1572868
  57.8 0.6 copy-start.6
  58.4 29.9 %all-to-all-start.1 = ((bf16[32,128,128]{2,1,0:T(8,128)(2,1)}), bf16[32,128,128]{2,1,0:T(8,128)(2,1)S(1)}, u32[]{:S(2)}, u32[]{:S(2)}) async-start(bf16[32,128,128]{2,1,0:T(8,128)(2,1)} %copy-done.3), calls=%async_computation.1 | async-start | bytes 2097152 | tf_op jit(solution)/shard_map/all_to_all | solution.py:530
  62.0 1.2 %copy-start.5 = (bf16[16,256,64]{2,1,0:T(8,128)(2,1)S(1)}, bf16[16,256,64]{2,1,0:T(8,128)(2,1)}, u32[]{:S(2)}) copy-start(bf16[16,256,64]{2,1,0:T(8,128)(2,1)} %copy-done.4) | copy-start | bytes 1572868
  63.2 4.5 %copy-start.7 = (f32[128,32]{1,0:T(8,128)S(1)}, f32[128,32]{1,0:T(8,128)}, u32[]{:S(2)}) copy-start(f32[128,32]{1,0:T(8,128)} %copy-done.6) | copy-start | bytes 49156
  66.0 10.1 %collective-permute-start = (bf16[64,1024]{1,0:T(8,128)(2,1)}, bf16[64,1024]{1,0:T(8,128)(2,1)S(1)}, u32[]{:S(2)}, u32[]{:S(2)}) collective-permute-start(bf16[64,1024]{1,0:T(8,128)(2,1)} %bitcast.11), channel_id=1, source_target_pairs={{0,16},{16,0},{1,17},{17,1},{2,18},{18,2},{3,19},{19,3},{4,20},{20... | collective-permute-start | bytes 393224 | tf_op jit(solution)/shard_map/ppermute | solution.py:545
  67.7 1.0 %copy-start.2 = (bf16[1,128,2048]{2,1,0:T(8,128)(2,1)S(1)}, bf16[1,128,2048]{2,1,0:T(8,128)(2,1)}, u32[]{:S(2)}) copy-start(bf16[1,128,2048]{2,1,0:T(8,128)(2,1)} %param.10) | copy-start | bytes 1572868

commit v12 on v11

--- a/solution.py
+++ b/solution.py
@@ -524,7 +524,7 @@
             pltpu.VMEM((count, tokens), f32),
             pltpu.VMEM((count, tokens), f32),
         ],
-        room=(40 << 20) if span % 128 == 0 else (20 << 20),
+        room=(14 << 20) if span % 128 == 0 else (20 << 20),
         cost=(10 * macs, 8 << 20),
     )(exchange(sent.reshape(count, -1, tokens)), dro_weight, skip, tables, behind)
     got = exchange(sent)

time: 90.1 us -> 89.4 us (level)
  local copies, waits for them, and re-layouts: 7.39 us -> 5 us
  Pallas kernels: 15.6 us -> 17.4 us
    unnamed x18 -> x12, local copies, waits for them, and re-layouts: 6.62 us -> 4.24 us
    pallas_call x1, Pallas kernels: 7.66 us -> 9.41 us  [local(): call(functools.partial(conv_kernel, mean_len, joint), [answer, shape((pie...]
where the time goes in v12:
time: 89.4 us; the launch traced here: 89 us
  waiting for transfers between devices  52.2 us (58%)
  Pallas kernels  17.4 us (19%)
  starting transfers between devices  12.7 us (14%)
  local copies, waits for them, and re-layouts  5 us (6%)
  other arithmetic  1.04 us (1%)
    all_to_all x1, waiting for transfers between devices, local(): exchange(sent.reshape(count, -1, tokens))  33.8 us
    all_to_all x1, waiting for transfers between devices, local(): got = exchange(sent)  11.2 us
    pallas_call x1, Pallas kernels, local(): call(functools.partial(conv_kernel, mean_len, joint), [answer, shape((pie...  9.41 us
    all_to_all x1, starting transfers between devices, local(): exchange(sent.reshape(count, -1, tokens))  7.3 us
    ppermute x1, waiting for transfers between devices, local(): lax.ppermute(send[r - 1], 'dp', rings[r]).astype(f32)  7.18 us
    unnamed x12, local copies, waits for them, and re-layouts  4.24 us
    pallas_call x1, Pallas kernels, local(): call(functools.partial(prep_kernel, pieces, joint), message, [SMEM] + [HB...  3.74 us
    all_to_all x1, starting transfers between devices, local(): got = exchange(sent)  3.62 us
  transfers between devices with their start and end apart: 3, of which 3 were waited for; matrix products, arithmetic and copies ran while one was open for 2% of the time, Pallas kernels for 3%

profile of v12, /device:TPU:0, one launch (start us, length us, event | category | flops | bytes accessed | tf_op | source)
XLA Modules:
  0.0 89.0 jit_solution(2632058596997471686)
XLA Ops:
  0.6 3.7 %shard_map.121 = bf16[16,2,176,128]{3,2,1,0:T(8,128)(2,1)} custom-call(s32[1]{0:T(128)} %bitcast.2.own_ref, bf16[128,2048]{1,0:T(8,128)(2,1)} %bitcast.24, bf16[128,2048]{1,0:T(8,128)(2,1)} %bitcast.20, bf16[128,2048]{1,0:T(8,128)(2,1)} %bitcast.25, bf16[16,128,128]{2,1,0:T(8,128)(2,1)} %bitcast.26, s32[1,128]{1,0:T(1,128)} %doc_ref.1, s32[1,128]{1,0:T(1,128)} %lang_ref.1), custom_call_target="tpu_custom_call" | custom-call | bytes 4194304 | tf_op jit(solution)/shard_map/pallas_call | solution.py:490
  4.4 0.0 copy-start.5
  4.4 7.3 %all-to-all-start = ((bf16[32,176,128]{2,1,0:T(8,128)(2,1)}), bf16[32,176,128]{2,1,0:T(8,128)(2,1)S(1)}, u32[]{:S(2)}, u32[]{:S(2)}) async-start(bf16[32,176,128]{2,1,0:T(8,128)(2,1)} %bitcast.23), calls=%async_computation | async-start | bytes 2883584 | tf_op jit(solution)/shard_map/all_to_all | solution.py:529
  11.7 0.8 dynamic_slice.10
  12.5 0.1 maximum_bitcast_fusion.skip_ref
  12.6 33.8 %all-to-all-done.message_ref = bf16[32,176,128]{2,1,0:T(8,128)(2,1)S(1)} async-done(((bf16[32,176,128]{2,1,0:T(8,128)(2,1)}), bf16[32,176,128]{2,1,0:T(8,128)(2,1)S(1)}, u32[]{:S(2)}, u32[]{:S(2)}) %all-to-all-start) | async-done | bytes 1441824 | tf_op jit(solution)/shard_map/all_to_all | solution.py:529
  46.4 0.0 copy-done.5
  46.4 9.4 %shard_map.122 = (bf16[32,128,128]{2,1,0:T(8,128)(2,1)S(1)}, bf16[16,256,64]{2,1,0:T(8,128)(2,1)S(1)}, f32[128,32]{1,0:T(8,128)S(1)}) custom-call(bf16[32,176,128]{2,1,0:T(8,128)(2,1)S(1)} %all-to-all-done.message_ref, f32[16]{0:T(128)S(1)} %copy-done.5, f32[1,128]{1,0:T(1,128)S(1)} %maximum_bitcast_fusion.skip_ref, ...), custom_call_target="tpu_custom_call" | custom-call | flops 1342177280 | bytes 8388608 | tf_op jit(solution)/shard_map/pallas_call | solution.py:515
  55.8 0.0 copy-start.2
  55.8 1.0 %copy-done.2 = bf16[32,128,128]{2,1,0:T(8,128)(2,1)} copy-done((bf16[32,128,128]{2,1,0:T(8,128)(2,1)}, bf16[32,128,128]{2,1,0:T(8,128)(2,1)S(1)}, u32[]{:S(2)}) %copy-start.2) | copy-done | bytes 1048600
  56.8 0.0 copy-start.3
  56.8 1.0 %copy-done.3 = bf16[16,256,64]{2,1,0:T(8,128)(2,1)} copy-done((bf16[16,256,64]{2,1,0:T(8,128)(2,1)}, bf16[16,256,64]{2,1,0:T(8,128)(2,1)S(1)}, u32[]{:S(2)}) %copy-start.3) | copy-done | bytes 524312
  57.8 0.0 copy-start
  57.8 3.6 %all-to-all-start.1 = ((bf16[32,128,128]{2,1,0:T(8,128)(2,1)}), bf16[32,128,128]{2,1,0:T(8,128)(2,1)S(1)}, u32[]{:S(2)}, u32[]{:S(2)}) async-start(bf16[32,128,128]{2,1,0:T(8,128)(2,1)} %copy-done.2), calls=%async_computation.1 | async-start | bytes 2097152 | tf_op jit(solution)/shard_map/all_to_all | solution.py:530
  61.4 0.0 copy-done
  61.4 0.0 copy-start.4
  61.4 1.2 %copy-done.4 = bf16[16,256,64]{2,1,0:T(8,128)(2,1)S(1)} copy-done((bf16[16,256,64]{2,1,0:T(8,128)(2,1)S(1)}, bf16[16,256,64]{2,1,0:T(8,128)(2,1)}, u32[]{:S(2)}) %copy-start.4) | copy-done | bytes 524312
  62.6 2.7 %shard_map.125 = (f32[64,1024]{1,0:T(8,128)S(1)}, bf16[1,64,1024]{2,1,0:T(8,128)(2,1)}) custom-call(s32[1]{0:T(128)} %bitcast.2.own_ref, bf16[16,256,64]{2,1,0:T(8,128)(2,1)S(1)} %copy-done.4, bf16[16,256,256]{2,1,0:T(8,128)(2,1)S(1)} %copy-done), custom_call_target="tpu_custom_call" | custom-call | flops 268435456 | bytes 6291456 | tf_op jit(solution)/shard_map/pallas_call | solution.py:531
  65.4 1.8 %collective-permute-start = (bf16[64,1024]{1,0:T(8,128)(2,1)}, bf16[64,1024]{1,0:T(8,128)(2,1)S(1)}, u32[]{:S(2)}, u32[]{:S(2)}) collective-permute-start(bf16[64,1024]{1,0:T(8,128)(2,1)} %bitcast.11), channel_id=1, source_target_pairs={{0,16},{16,0},{1,17},{17,1},{2,18},{18,2},{3,19},{19,3},{4,20},{20... | collective-permute-start | bytes 393224 | tf_op jit(solution)/shard_map/ppermute | solution.py:545
  67.1 0.0 copy-start.1
  67.1 1.0 %copy-done.1 = bf16[1,128,2048]{2,1,0:T(8,128)(2,1)S(1)} copy-done((bf16[1,128,2048]{2,1,0:T(8,128)(2,1)S(1)}, bf16[1,128,2048]{2,1,0:T(8,128)(2,1)}, u32[]{:S(2)}) %copy-start.1) | copy-done | bytes 524312
  68.2 0.1 shard_map.123.scaled_ref
  68.3 7.2 %collective-permute-done = bf16[64,1024]{1,0:T(8,128)(2,1)S(1)} collective-permute-done((bf16[64,1024]{1,0:T(8,128)(2,1)}, bf16[64,1024]{1,0:T(8,128)(2,1)S(1)}, u32[]{:S(2)}, u32[]{:S(2)}) %collective-permute-start) | collective-permute-done | bytes 131104 | tf_op jit(solution)/shard_map/ppermute | solution.py:545
  75.5 0.1 fusion.3
  75.6 0.8 pad_maximum_fusion
  76.5 11.2 %all-to-all-done.1.message_ref = bf16[32,128,128]{2,1,0:T(8,128)(2,1)S(1)} async-done(((bf16[32,128,128]{2,1,0:T(8,128)(2,1)}), bf16[32,128,128]{2,1,0:T(8,128)(2,1)S(1)}, u32[]{:S(2)}, u32[]{:S(2)}) %all-to-all-start.1) | async-done | bytes 1048608 | tf_op jit(solution)/shard_map/all_to_all | solution.py:530
  87.6 1.4 %shard_map.124 = (bf16[128,2048]{1,0:T(8,128)(2,1)}, bf16[128,2048]{1,0:T(8,128)(2,1)}) custom-call(f32[128,2048]{1,0:T(8,128)S(1)} %shard_map.123.scaled_ref, bf16[32,128,128]{2,1,0:T(8,128)(2,1)S(1)} %all-to-all-done.1.message_ref), custom_call_target="tpu_custom_call" | custom-call | bytes 4194304 | tf_op jit(solution)/shard_map/pallas_call | solution.py:563
  (1 shorter events, 0.0 us)
Async XLA Ops:
  4.4 42.0 %copy-start.5 = (f32[16]{0:T(128)S(1)}, f32[16]{0:T(128)}, u32[]{:S(2)}) copy-start(f32[16]{0:T(128)} %dro_ref.1) | copy-start | bytes 196
  4.4 42.0 %all-to-all-start = ((bf16[32,176,128]{2,1,0:T(8,128)(2,1)}), bf16[32,176,128]{2,1,0:T(8,128)(2,1)S(1)}, u32[]{:S(2)}, u32[]{:S(2)}) async-start(bf16[32,176,128]{2,1,0:T(8,128)(2,1)} %bitcast.23), calls=%async_computation | async-start | bytes 2883584 | tf_op jit(solution)/shard_map/all_to_all | solution.py:529
  55.8 1.0 %copy-start.2 = (bf16[32,128,128]{2,1,0:T(8,128)(2,1)}, bf16[32,128,128]{2,1,0:T(8,128)(2,1)S(1)}, u32[]{:S(2)}) copy-start(bf16[32,128,128]{2,1,0:T(8,128)(2,1)S(1)} %get-tuple-element.11) | copy-start | bytes 3145732
  56.8 1.0 %copy-start.3 = (bf16[16,256,64]{2,1,0:T(8,128)(2,1)}, bf16[16,256,64]{2,1,0:T(8,128)(2,1)S(1)}, u32[]{:S(2)}) copy-start(bf16[16,256,64]{2,1,0:T(8,128)(2,1)S(1)} %get-tuple-element.14.cross_ref) | copy-start | bytes 1572868
  57.8 3.6 %copy-start = (bf16[16,256,256]{2,1,0:T(8,128)(2,1)S(1)}, bf16[16,256,256]{2,1,0:T(8,128)(2,1)}, u32[]{:S(2)}) copy-start(bf16[16,256,256]{2,1,0:T(8,128)(2,1)} %constant.49.clone.behind_ref) | copy-start | bytes 6291460
  57.8 29.9 %all-to-all-start.1 = ((bf16[32,128,128]{2,1,0:T(8,128)(2,1)}), bf16[32,128,128]{2,1,0:T(8,128)(2,1)S(1)}, u32[]{:S(2)}, u32[]{:S(2)}) async-start(bf16[32,128,128]{2,1,0:T(8,128)(2,1)} %copy-done.2), calls=%async_computation.1 | async-start | bytes 2097152 | tf_op jit(solution)/shard_map/all_to_all | solution.py:530
  61.4 1.2 %copy-start.4 = (bf16[16,256,64]{2,1,0:T(8,128)(2,1)S(1)}, bf16[16,256,64]{2,1,0:T(8,128)(2,1)}, u32[]{:S(2)}) copy-start(bf16[16,256,64]{2,1,0:T(8,128)(2,1)} %copy-done.3) | copy-start | bytes 1572868
  65.4 10.1 %collective-permute-start = (bf16[64,1024]{1,0:T(8,128)(2,1)}, bf16[64,1024]{1,0:T(8,128)(2,1)S(1)}, u32[]{:S(2)}, u32[]{:S(2)}) collective-permute-start(bf16[64,1024]{1,0:T(8,128)(2,1)} %bitcast.11), channel_id=1, source_target_pairs={{0,16},{16,0},{1,17},{17,1},{2,18},{18,2},{3,19},{19,3},{4,20},{20... | collective-permute-start | bytes 393224 | tf_op jit(solution)/shard_map/ppermute | solution.py:545
  67.1 1.0 %copy-start.1 = (bf16[1,128,2048]{2,1,0:T(8,128)(2,1)S(1)}, bf16[1,128,2048]{2,1,0:T(8,128)(2,1)}, u32[]{:S(2)}) copy-start(bf16[1,128,2048]{2,1,0:T(8,128)(2,1)} %param.10) | copy-start | bytes 1572868

commit v13 on v12

--- a/solution.py
+++ b/solution.py
@@ -524,7 +524,7 @@
             pltpu.VMEM((count, tokens), f32),
             pltpu.VMEM((count, tokens), f32),
         ],
-        room=(14 << 20) if span % 128 == 0 else (20 << 20),
+        room=(10 << 20) if span % 128 == 0 else (20 << 20),
         cost=(10 * macs, 8 << 20),
     )(exchange(sent.reshape(count, -1, tokens)), dro_weight, skip, tables, behind)
     got = exchange(sent)

time: 89.4 us -> 89.9 us (level)
  Pallas kernels: 17.4 us -> 18.8 us
    pallas_call x1, Pallas kernels: 9.41 us -> 10.8 us  [local(): call(functools.partial(conv_kernel, mean_len, joint), [answer, shape((pie...]
    unnamed x12 -> x10, local copies, waits for them, and re-layouts: 4.24 us -> 3.38 us
  transfers between devices with their start and end apart: 3 -> 3, of which waited for: 3 -> 3; matrix products, arithmetic and copies ran while one was open for 2% -> 3% of each run, Pallas kernels for 3% -> 3%
where the time goes in v13:
time: 89.9 us; the launch traced here: 89.5 us
  waiting for transfers between devices  51.6 us (57%)
  Pallas kernels  18.8 us (21%)
  starting transfers between devices  12.7 us (14%)
  local copies, waits for them, and re-layouts  4.15 us (5%)
  other arithmetic  1.55 us (2%)
    all_to_all x1, waiting for transfers between devices, local(): exchange(sent.reshape(count, -1, tokens))  33.3 us
    all_to_all x1, waiting for transfers between devices, local(): got = exchange(sent)  11.2 us
    pallas_call x1, Pallas kernels, local(): call(functools.partial(conv_kernel, mean_len, joint), [answer, shape((pie...  10.8 us
    all_to_all x1, starting transfers between devices, local(): exchange(sent.reshape(count, -1, tokens))  7.3 us
    ppermute x1, waiting for transfers between devices, local(): lax.ppermute(send[r - 1], 'dp', rings[r]).astype(f32)  7.17 us
    pallas_call x1, Pallas kernels, local(): call(functools.partial(prep_kernel, pieces, joint), message, [SMEM] + [HB...  3.73 us
    all_to_all x1, starting transfers between devices, local(): got = exchange(sent)  3.61 us
    unnamed x10, local copies, waits for them, and re-layouts  3.38 us
  transfers between devices with their start and end apart: 3, of which 3 were waited for; matrix products, arithmetic and copies ran while one was open for 3% of the time, Pallas kernels for 3%

profile of v13, /device:TPU:0, one launch (start us, length us, event | category | flops | bytes accessed | tf_op | source)
XLA Modules:
  0.0 89.5 jit_solution(5074016434860304519)
XLA Ops:
  0.6 3.7 %shard_map.121 = bf16[16,2,176,128]{3,2,1,0:T(8,128)(2,1)} custom-call(s32[1]{0:T(128)} %bitcast.2.own_ref, bf16[128,2048]{1,0:T(8,128)(2,1)} %bitcast.24, bf16[128,2048]{1,0:T(8,128)(2,1)} %bitcast.20, bf16[128,2048]{1,0:T(8,128)(2,1)} %bitcast.25, bf16[16,128,128]{2,1,0:T(8,128)(2,1)} %bitcast.26, s32[1,128]{1,0:T(1,128)} %doc_ref.1, s32[1,128]{1,0:T(1,128)} %lang_ref.1), custom_call_target="tpu_custom_call" | custom-call | bytes 4194304 | tf_op jit(solution)/shard_map/pallas_call | solution.py:490
  4.4 7.3 %all-to-all-start = ((bf16[32,176,128]{2,1,0:T(8,128)(2,1)}), bf16[32,176,128]{2,1,0:T(8,128)(2,1)S(1)}, u32[]{:S(2)}, u32[]{:S(2)}) async-start(bf16[32,176,128]{2,1,0:T(8,128)(2,1)} %bitcast.23), calls=%async_computation | async-start | bytes 2883584 | tf_op jit(solution)/shard_map/all_to_all | solution.py:529
  11.7 0.8 dynamic_slice.10
  12.5 0.6 maximum_bitcast_fusion.skip_ref
  13.0 33.3 %all-to-all-done.message_ref = bf16[32,176,128]{2,1,0:T(8,128)(2,1)S(1)} async-done(((bf16[32,176,128]{2,1,0:T(8,128)(2,1)}), bf16[32,176,128]{2,1,0:T(8,128)(2,1)S(1)}, u32[]{:S(2)}, u32[]{:S(2)}) %all-to-all-start) | async-done | bytes 1441824 | tf_op jit(solution)/shard_map/all_to_all | solution.py:529
  46.4 0.0 copy-start.4
  46.4 1.1 %copy-done.4 = bf16[32,176,128]{2,1,0:T(8,128)(2,1)} copy-done((bf16[32,176,128]{2,1,0:T(8,128)(2,1)}, bf16[32,176,128]{2,1,0:T(8,128)(2,1)S(1)}, u32[]{:S(2)}) %copy-start.4) | copy-done | bytes 1441816
  47.5 10.8 %shard_map.122 = (bf16[32,128,128]{2,1,0:T(8,128)(2,1)}, bf16[16,256,64]{2,1,0:T(8,128)(2,1)}, f32[128,32]{1,0:T(8,128)}) custom-call(bf16[32,176,128]{2,1,0:T(8,128)(2,1)} %copy-done.4, f32[16]{0:T(128)} %dro_ref.1, f32[1,128]{1,0:T(1,128)} %maximum_bitcast_fusion.skip_ref, bf16[5120,256]{1,0:T(8,128)(2,1)} %constant.48.clone.table_ref, ...), custom_call_target="tpu_custom_call" | custom-call | flops 1342177280 | bytes 8388608 | tf_op jit(solution)/shard_map/pallas_call | solution.py:515
  58.3 0.0 copy-start
  58.3 3.6 %all-to-all-start.1 = ((bf16[32,128,128]{2,1,0:T(8,128)(2,1)}), bf16[32,128,128]{2,1,0:T(8,128)(2,1)S(1)}, u32[]{:S(2)}, u32[]{:S(2)}) async-start(bf16[32,128,128]{2,1,0:T(8,128)(2,1)} %get-tuple-element.11), calls=%async_computation.1 | async-start | bytes 2097152 | tf_op jit(solution)/shard_map/all_to_all | solution.py:530
  61.9 0.0 copy-done
  61.9 0.0 copy-start.2
  62.0 1.2 %copy-done.2 = bf16[16,256,64]{2,1,0:T(8,128)(2,1)S(1)} copy-done((bf16[16,256,64]{2,1,0:T(8,128)(2,1)S(1)}, bf16[16,256,64]{2,1,0:T(8,128)(2,1)}, u32[]{:S(2)}) %copy-start.2) | copy-done | bytes 524312
  63.2 0.0 copy-start.3
  63.2 2.7 %shard_map.125 = (f32[64,1024]{1,0:T(8,128)S(1)}, bf16[1,64,1024]{2,1,0:T(8,128)(2,1)}) custom-call(s32[1]{0:T(128)} %bitcast.2.own_ref, bf16[16,256,64]{2,1,0:T(8,128)(2,1)S(1)} %copy-done.2, bf16[16,256,256]{2,1,0:T(8,128)(2,1)S(1)} %copy-done), custom_call_target="tpu_custom_call" | custom-call | flops 268435456 | bytes 6291456 | tf_op jit(solution)/shard_map/pallas_call | solution.py:531
  65.9 1.8 %collective-permute-start = (bf16[64,1024]{1,0:T(8,128)(2,1)}, bf16[64,1024]{1,0:T(8,128)(2,1)S(1)}, u32[]{:S(2)}, u32[]{:S(2)}) collective-permute-start(bf16[64,1024]{1,0:T(8,128)(2,1)} %bitcast.11), channel_id=1, source_target_pairs={{0,16},{16,0},{1,17},{17,1},{2,18},{18,2},{3,19},{19,3},{4,20},{20... | collective-permute-start | bytes 393224 | tf_op jit(solution)/shard_map/ppermute | solution.py:545
  67.7 0.0 copy-done.3
  67.7 0.0 copy-start.1
  67.7 1.0 %copy-done.1 = bf16[1,128,2048]{2,1,0:T(8,128)(2,1)S(1)} copy-done((bf16[1,128,2048]{2,1,0:T(8,128)(2,1)S(1)}, bf16[1,128,2048]{2,1,0:T(8,128)(2,1)}, u32[]{:S(2)}) %copy-start.1) | copy-done | bytes 524312
  68.7 0.1 shard_map.123.scaled_ref
  68.9 7.2 %collective-permute-done = bf16[64,1024]{1,0:T(8,128)(2,1)S(1)} collective-permute-done((bf16[64,1024]{1,0:T(8,128)(2,1)}, bf16[64,1024]{1,0:T(8,128)(2,1)S(1)}, u32[]{:S(2)}, u32[]{:S(2)}) %collective-permute-start) | collective-permute-done | bytes 131104 | tf_op jit(solution)/shard_map/ppermute | solution.py:545
  76.1 0.1 fusion.3
  76.2 0.8 pad_maximum_fusion
  77.0 11.2 %all-to-all-done.1.message_ref = bf16[32,128,128]{2,1,0:T(8,128)(2,1)S(1)} async-done(((bf16[32,128,128]{2,1,0:T(8,128)(2,1)}), bf16[32,128,128]{2,1,0:T(8,128)(2,1)S(1)}, u32[]{:S(2)}, u32[]{:S(2)}) %all-to-all-start.1) | async-done | bytes 1048608 | tf_op jit(solution)/shard_map/all_to_all | solution.py:530
  88.2 1.4 %shard_map.124 = (bf16[128,2048]{1,0:T(8,128)(2,1)}, bf16[128,2048]{1,0:T(8,128)(2,1)}) custom-call(f32[128,2048]{1,0:T(8,128)S(1)} %shard_map.123.scaled_ref, bf16[32,128,128]{2,1,0:T(8,128)(2,1)S(1)} %all-to-all-done.1.message_ref), custom_call_target="tpu_custom_call" | custom-call | bytes 4194304 | tf_op jit(solution)/shard_map/pallas_call | solution.py:563
  (1 shorter events, 0.0 us)
Async XLA Ops:
  4.4 42.0 %all-to-all-start = ((bf16[32,176,128]{2,1,0:T(8,128)(2,1)}), bf16[32,176,128]{2,1,0:T(8,128)(2,1)S(1)}, u32[]{:S(2)}, u32[]{:S(2)}) async-start(bf16[32,176,128]{2,1,0:T(8,128)(2,1)} %bitcast.23), calls=%async_computation | async-start | bytes 2883584 | tf_op jit(solution)/shard_map/all_to_all | solution.py:529
  46.4 1.1 %copy-start.4 = (bf16[32,176,128]{2,1,0:T(8,128)(2,1)}, bf16[32,176,128]{2,1,0:T(8,128)(2,1)S(1)}, u32[]{:S(2)}) copy-start(bf16[32,176,128]{2,1,0:T(8,128)(2,1)S(1)} %all-to-all-done.message_ref) | copy-start | bytes 4325380
  58.3 3.6 %copy-start = (bf16[16,256,256]{2,1,0:T(8,128)(2,1)S(1)}, bf16[16,256,256]{2,1,0:T(8,128)(2,1)}, u32[]{:S(2)}) copy-start(bf16[16,256,256]{2,1,0:T(8,128)(2,1)} %constant.49.clone.behind_ref) | copy-start | bytes 6291460
  58.3 29.9 %all-to-all-start.1 = ((bf16[32,128,128]{2,1,0:T(8,128)(2,1)}), bf16[32,128,128]{2,1,0:T(8,128)(2,1)S(1)}, u32[]{:S(2)}, u32[]{:S(2)}) async-start(bf16[32,128,128]{2,1,0:T(8,128)(2,1)} %get-tuple-element.11), calls=%async_computation.1 | async-start | bytes 2097152 | tf_op jit(solution)/shard_map/all_to_all | solution.py:530
  61.9 1.2 %copy-start.2 = (bf16[16,256,64]{2,1,0:T(8,128)(2,1)S(1)}, bf16[16,256,64]{2,1,0:T(8,128)(2,1)}, u32[]{:S(2)}) copy-start(bf16[16,256,64]{2,1,0:T(8,128)(2,1)} %get-tuple-element.14.cross_ref) | copy-start | bytes 1572868
  63.2 4.5 %copy-start.3 = (f32[128,32]{1,0:T(8,128)S(1)}, f32[128,32]{1,0:T(8,128)}, u32[]{:S(2)}) copy-start(f32[128,32]{1,0:T(8,128)} %get-tuple-element.10.scale_ref) | copy-start | bytes 49156
  65.9 10.1 %collective-permute-start = (bf16[64,1024]{1,0:T(8,128)(2,1)}, bf16[64,1024]{1,0:T(8,128)(2,1)S(1)}, u32[]{:S(2)}, u32[]{:S(2)}) collective-permute-start(bf16[64,1024]{1,0:T(8,128)(2,1)} %bitcast.11), channel_id=1, source_target_pairs={{0,16},{16,0},{1,17},{17,1},{2,18},{18,2},{3,19},{19,3},{4,20},{20... | collective-permute-start | bytes 393224 | tf_op jit(solution)/shard_map/ppermute | solution.py:545
  67.7 1.0 %copy-start.1 = (bf16[1,128,2048]{2,1,0:T(8,128)(2,1)S(1)}, bf16[1,128,2048]{2,1,0:T(8,128)(2,1)}, u32[]{:S(2)}) copy-start(bf16[1,128,2048]{2,1,0:T(8,128)(2,1)} %param.10) | copy-start | bytes 1572868
